TPU v7x, 128 devices: a whole 4x4x4 slice. The times are simulated.
128 devices in a mesh: shard: 64 (over z, y, x), basis: 2 (over core).
Axes of the slice: x: 4, y: 4, z: 4, core: 2. Of those that a mesh axis runs over, the one named last changes fastest.
Arguments:
- features: bfloat16 [393216, 1024], P('shard', 'basis'), may hold values from -6 to 6
- bases: bfloat16 [2, 1024, 1024], P('basis'), may hold values from -0.1875 to 0.1875
- coeffs: float32 [14824, 2], replicated, may hold values from -3 to 3
- block_lists: int32 [64, 64, 1], P('shard'), may hold values from 0 to 47
- block_counts: int32 [64, 64], P('shard'), may hold values from 0 to 1, as said below
- tile_rel: int32 [64, 52], P('shard'), may hold values from 0 to 14823
- dest_ids: int32 [64, 3328], P('shard'), may hold values from 0 to 127
Outputs:
- aggregated: bfloat16 [16384, 1024], P(('shard', 'basis'))
Inputs may be any that keep to these rules, and one draw needn't show every extreme that they name: `block_counts`: each row g sums to exactly 26; one owner, the same in every row, has count 1 in every row. `block_lists`: slots at or beyond the count hold valid block numbers that are not used.
All inputs are finite; a program needn't handle non-finite values.
Results may differ from a plain program's by a relative error of at most 0.0049.
Values may be sent and summed in bfloat16 or wider, within the bound.
No kernel may reach another device: no remote copies, remote signals or barrier semaphores. Data moves between devices by JAX's collectives and lax.ppermute only.
A program may use at most 128 MiB of HBM per device.

v0:
```python
import jax
import jax.numpy as jnp
from jax import lax
from jax.sharding import PartitionSpec as P

BROWS = 128
TILE = 64
DST_DEV = 128


def select_slots(count_row, block_total, slot_cap):
    slot_ids = jnp.arange(count_row.shape[0] * slot_cap, dtype=jnp.int32)
    live_slot = slot_ids % slot_cap < count_row[slot_ids // slot_cap]
    position = jnp.cumsum(live_slot.astype(jnp.int32)) - 1
    wanted_pos = jnp.arange(block_total, dtype=jnp.int32)
    match_hit = live_slot[None, :] & (position[None, :] == wanted_pos[:, None])
    return jnp.sum(jnp.where(match_hit, slot_ids[None, :], 0), axis=1)


def body(features, bases, coeffs, block_lists, block_counts, tile_rel, dest_ids):
    peer_count = lax.axis_size("shard")
    group_count = lax.axis_size("basis")
    basis_index = lax.axis_index("basis")
    slot_cap = block_lists.shape[2]
    col_width = features.shape[1]
    block_total = tile_rel.shape[1] * TILE // BROWS
    group_size = block_total * BROWS
    rows_dev = group_size // group_count
    local_blocks = features.reshape(-1, BROWS, col_width)
    wanted = lax.all_to_all(block_lists, "shard", split_axis=1, concat_axis=0, tiled=True)
    picked = local_blocks[wanted.reshape(peer_count, slot_cap)]
    arrived = lax.all_to_all(picked, "shard", split_axis=0, concat_axis=0, tiled=True)
    chosen = select_slots(block_counts[0], block_total, slot_cap)
    fetched = arrived.reshape(peer_count * slot_cap, BROWS, col_width)[chosen].reshape(
        group_size, col_width
    )
    projected = jnp.einsum(
        "rc,kcd->rkd",
        lax.all_gather(fetched, "basis", axis=1, tiled=True),
        bases,
        preferred_element_type=jnp.float32,
    ).astype(jnp.bfloat16)
    row_coef = jnp.repeat(coeffs[tile_rel[0]], TILE, axis=0)
    dest_rows = dest_ids[0]
    my_dests = lax.dynamic_slice_in_dim(dest_rows, basis_index * rows_dev, rows_dev)
    indegree = jax.ops.segment_sum(
        jnp.ones((rows_dev,), jnp.float32), my_dests, num_segments=DST_DEV
    )
    my_coef = lax.dynamic_slice_in_dim(row_coef, basis_index * rows_dev, rows_dev, 0)
    mixture = jnp.sum(
        my_coef[:, :, None]
        * lax.all_to_all(projected, "basis", split_axis=0, concat_axis=1, tiled=True).astype(
            jnp.float32
        ),
        axis=1,
    )
    summed = jax.ops.segment_sum(mixture, my_dests, num_segments=DST_DEV)
    return (summed / jnp.maximum(indegree, 1.0)[:, None]).astype(jnp.bfloat16)


def solution(mesh):
    placed = (
        P("shard", "basis"),
        P("basis", None, None),
        P(),
        P("shard", None, None),
        P("shard", None),
        P("shard", None),
        P("shard", None),
    )
    return jax.shard_map(
        body, mesh=mesh, in_specs=placed, out_specs=P(("shard", "basis"), None), check_vma=False
    )
```

profile of v0, /device:TPU:1, one launch (start us, length us, event | category | flops | bytes accessed | tf_op | source)
XLA Modules:
  0.0 307.2 jit_solution(18364889435645601740)
XLA Ops:
  6.5 0.9 copy.26
  7.4 20.2 %all_to_all.23 = s32[1,64,1]{2,0,1:T(1,128)S(1)} all-to-all(s32[1,64,1]{2,0,1:T(1,128)S(1)} %copy.26), channel_id=1, replica_groups=mesh['shard'=64,'basis'=2] {'shard'}, dimensions={1} | all-to-all | bytes 512 | tf_op jit(solution)/shard_map/all_to_all | solution.py:30
  27.6 1.2 reduce.1
  28.8 8.3 %gather_fusion.1 = bf16[64,128,512]{2,1,0:T(8,128)(2,1)} fusion(bf16[48,128,512]{2,1,0:T(8,128)(2,1)} %bitcast.39, s32[1024]{0:T(1024)S(1)} %pad_clamp_fusion.2), kind=kCustom, calls=%fused_computation.1 | custom fusion | bytes 16777472 | tf_op jit(solution)/shard_map/gather | solution.py:31
  37.1 5.9 %all-to-all-start.1 = ((bf16[64,1,128,512]{3,2,1,0:T(8,128)(2,1)}), bf16[64,1,128,512]{3,2,1,0:T(8,128)(2,1)}, u32[]{:S(2)}, u32[]{:S(2)}) async-start(bf16[64,1,128,512]{3,2,1,0:T(8,128)(2,1)} %bitcast.37), calls=%async_computation.1 | async-start | bytes 16777216 | tf_op jit(solution)/shard_map/all_to_all | solution.py:32
  43.1 0.8 gather_fusion.2
  44.1 0.1 add_reduce_fusion
  44.2 0.1 select_reduce_fusion
  44.4 105.9 %all-to-all-done.1 = bf16[64,1,128,512]{3,2,1,0:T(8,128)(2,1)} async-done(((bf16[64,1,128,512]{3,2,1,0:T(8,128)(2,1)}), bf16[64,1,128,512]{3,2,1,0:T(8,128)(2,1)}, u32[]{:S(2)}, u32[]{:S(2)}) %all-to-all-start.1) | async-done | bytes 8388640 | tf_op jit(solution)/shard_map/all_to_all | solution.py:32
  150.3 5.9 %gather_fusion.3 = bf16[26,128,512]{2,1,0:T(8,128)(2,1)} fusion(bf16[64,128,512]{2,1,0:T(8,128)(2,1)} %bitcast.5, s32[1024]{0:T(1024)S(1)} %pad_clamp_fusion), kind=kCustom, calls=%fused_computation.3 | custom fusion | bytes 6815848 | tf_op jit(solution)/shard_map/gather | solution.py:34
  156.2 4.7 %copy.24 = f32[14824,2]{1,0:T(8,128)} copy(f32[14824,2]{0,1:T(2,128)S(1)} %copy-done.3) | data formatting | bytes 237184 | tf_op args[2]
  160.9 3.7 %gather_fusion = f32[52,2]{1,0:T(8,128)S(1)} fusion(f32[14824,2]{1,0:T(8,128)} %copy.24, s32[1024]{0:T(1024)S(1)} %pad_clamp_fusion.3), kind=kCustom, calls=%fused_computation | custom fusion | bytes 1040 | tf_op jit(solution)/shard_map/gather | solution.py:43
  165.0 12.9 %scatter_custom_fusion.1 = f32[128]{0:T(128)S(1)} fusion(s32[1664]{0:T(1024)S(1)} %dynamic-slice_reduce_fusion, f32[1664]{0:T(1024)S(1)} %broadcast.136, f32[]{:T(128)} %constant.30.clone.1), kind=kCustom, calls=%fused_computation.33 | custom fusion | flops 1664 | bytes 516 | tf_op jit(solution)/shard_map/scatter-add | solution.py:46
  177.9 12.1 %all-gather.2.cloned.1.call-done = bf16[3328,1024]{1,0:T(8,128)(2,1)} async-done(((bf16[3328,512]{1,0:T(8,128)(2,1)}), bf16[3328,1024]{1,0:T(8,128)(2,1)}) %all-gather.2.cloned.1.call-update) | async-done | bytes 6815760 | tf_op jit(solution)/shard_map/all_gather | solution.py:39
  190.0 12.2 %fusion.1 = bf16[3328,1,1024]{2,0,1:T(8,128)(2,1)} fusion(bf16[3328,1024]{1,0:T(8,128)(2,1)} %all-gather.2.cloned.1.call-done, bf16[1,1024,1024]{2,1,0:T(8,128)(2,1)S(1)} %copy-done), kind=kOutput, calls=%fused_computation.10 | convolution fusion | flops 6982729728 | bytes 15728640 | tf_op jit(solution)/shard_map/rc,kcd->rkd/dot_general | solution.py:37
  202.2 0.5 broadcast.158
  202.7 10.8 %reduce.5 = bf16[3328,1024]{1,0:T(8,128)(2,1)} reduce(bf16[3328,1,1024]{2,0,1:T(8,128)(2,1)} %fusion.1, bf16[]{:T(256)} %broadcast.158), dimensions={1}, to_apply=%copy.28.reduce_sub_computation | reduce | bytes 13631490 | tf_op jit(solution)/shard_map/convert_element_type | solution.py:42
  213.5 8.6 %reshape.219 = bf16[2,2,851968]{2,1,0:T(2,128)(2,1)} reshape(bf16[3328,1024]{1,0:T(8,128)(2,1)} %reduce.5) | data formatting | bytes 13631488
  222.1 15.9 %all_to_all.24 = bf16[2,2,851968]{2,1,0:T(2,128)(2,1)} all-to-all(bf16[2,2,851968]{2,1,0:T(2,128)(2,1)} %reshape.219), channel_id=1, replica_groups=mesh['shard'=64,'basis'=2] {'basis'}, dimensions={0} | all-to-all | bytes 13631488 | tf_op jit(solution)/shard_map/all_to_all | solution.py:52
  238.0 15.3 %reshape.220 = bf16[3328,1,1024]{2,1,0:T(2,128)(2,1)} reshape(bf16[2,2,851968]{2,1,0:T(2,128)(2,1)} %all_to_all.24) | data formatting | bytes 13631488
  253.2 16.7 %convert_bitcast_fusion = f32[1664,2,1,1024]{3,2,0,1:T(1,128)} fusion(bf16[2,1664,1,1024]{3,2,1,0:T(2,128)(2,1)} %bitcast.36), kind=kLoop, calls=%fused_computation.8 | loop fusion | flops 3407872 | bytes 20447232 | tf_op jit(solution)/shard_map/convert_element_type | solution.py:52
  269.9 10.5 %fusion = f32[1664,1024]{1,0:T(8,128)} fusion(f32[1664,2,1,1024]{3,2,0,1:T(1,128)} %convert_bitcast_fusion, f32[1664,2]{0,1:T(2,128)S(1)} %constant_dynamic-slice_fusion), kind=kLoop, calls=%fused_computation.7 | loop fusion | flops 5111808 | bytes 20460544 | tf_op jit(solution)/shard_map/reduce_sum | solution.py:50
  280.5 19.1 %scatter_custom_fusion = f32[128,1024]{1,0:T(8,128)S(1)} fusion(s32[1664]{0:T(1024)S(1)} %dynamic-slice_reduce_fusion, f32[1664,1024]{1,0:T(8,128)} %fusion, f32[]{:T(128)} %constant.30.clone.1), kind=kCustom, calls=%fused_computation.13 | custom fusion | flops 1703936 | bytes 524800 | tf_op jit(solution)/shard_map/scatter-add | solution.py:57
  299.6 0.8 divide_convert_fusion
  (32 shorter events, 0.6 us)
Async XLA Ops:
  6.5 183.4 %copy-start = (bf16[1,1024,1024]{2,1,0:T(8,128)(2,1)S(1)}, bf16[1,1024,1024]{2,1,0:T(8,128)(2,1)}, u32[]{:S(2)}) copy-start(bf16[1,1024,1024]{2,1,0:T(8,128)(2,1)} %param.8) | copy-start | bytes 6291460
  37.1 6.0 %copy-start.2 = (s32[1,64]{1,0:T(1,128)S(1)}, s32[1,64]{1,0:T(1,128)}, u32[]{:S(2)}) copy-start(s32[1,64]{1,0:T(1,128)} %param.11) | copy-start | bytes 772
  37.1 113.1 %all-to-all-start.1 = ((bf16[64,1,128,512]{3,2,1,0:T(8,128)(2,1)}), bf16[64,1,128,512]{3,2,1,0:T(8,128)(2,1)}, u32[]{:S(2)}, u32[]{:S(2)}) async-start(bf16[64,1,128,512]{3,2,1,0:T(8,128)(2,1)} %bitcast.37), calls=%async_computation.1 | async-start | bytes 16777216 | tf_op jit(solution)/shard_map/all_to_all | solution.py:32
  43.0 113.2 %copy-start.3 = (f32[14824,2]{0,1:T(2,128)S(1)}, f32[14824,2]{0,1:T(2,128)}, u32[]{:S(2)}) copy-start(f32[14824,2]{0,1:T(2,128)} %param.9) | copy-start | bytes 355780
  43.0 146.9 %all-gather.2.cloned.1.call-start = ((), (), s32[]{:S(2)}) async-start(), calls=%async_computation.3 | async-start | bytes 10223616 | tf_op jit(solution)/shard_map/all_gather | solution.py:39
  156.2 4.7 %copy-start.5 = (s32[1,52]{1,0:T(1,128)S(1)}, s32[1,52]{1,0:T(1,128)}, u32[]{:S(2)}) copy-start(s32[1,52]{1,0:T(1,128)} %param.12) | copy-start | bytes 628
  156.2 8.7 %copy-start.4 = (s32[1,3328]{1,0:T(1,128)S(1)}, s32[1,3328]{1,0:T(1,128)}, u32[]{:S(2)}) copy-start(s32[1,3328]{1,0:T(1,128)} %param.13) | copy-start | bytes 39940
  253.2 47.1 %copy-start.1 = (bf16[1,1024,1024]{2,1,0:T(8,128)(2,1)S(1)}, bf16[1,1024,1024]{2,1,0:T(8,128)(2,1)}, u32[]{:S(2)}) copy-start(bf16[1,1024,1024]{2,1,0:T(8,128)(2,1)} %param.8) | copy-start | bytes 6291460
Sparse Core Ops, SparseCore 0:
  156.3 33.6 all-gather.1
where the time goes:
time: 313 us; the launch traced here: 307 us
  waiting for transfers between devices  118 us (38%)
  other arithmetic  72.4 us (23%)
  local copies, waits for them, and re-layouts  49.1 us (16%)
  blocking collectives  36.1 us (12%)
  between operations  13.6 us (4%)
  matrix products  12.2 us (4%)
  starting transfers between devices  5.92 us (2%)
    all_to_all x1, waiting for transfers between devices, body(): lax.all_to_all(picked, 'shard', split_axis=0, concat_axis=0, tiled=True)  106 us
    unnamed x16, local copies, waits for them, and re-layouts  29.4 us
    all_to_all x1, blocking collectives, body(): lax.all_to_all(block_lists, 'shard', split_axis=1, concat_axis=0, tiled=T...  20.2 us
    scatter-add x1, other arithmetic, body(): summed = jax.ops.segment_sum(mixture, my_dests, num_segments=DST_DEV)  19.1 us
    convert_element_type x1, other arithmetic, body(): lax.all_to_all(projected, 'basis', split_axis=0, concat_axis=1, tiled=True)  16.7 us
    all_to_all x1, blocking collectives, body(): lax.all_to_all(projected, 'basis', split_axis=0, concat_axis=1, tiled=True)  15.9 us
    scatter-add x1, other arithmetic, body(): jax.ops.segment_sum(jnp.ones((rows_dev,), jnp.float32), my_dests, num_seg...  12.9 us
    dot_general x1, matrix products, body(): jnp.einsum('rc,kcd->rkd', lax.all_gather(fetched, 'basis', axis=1, tiled=...  12.2 us
  transfers between devices with their start and end apart: 2, of which 2 were waited for; matrix products, arithmetic and copies ran while one was open for 7% of the time, Pallas kernels for 0%

commit v1 on v0

v1 whole, which is shorter than its diff:
```python
import functools

import jax
import jax.numpy as jnp
from jax import lax
from jax.experimental import pallas as pl
from jax.experimental.pallas import tpu as pltpu
from jax.sharding import PartitionSpec as P

BROWS = 128
TILE = 64
DST = 128
SIDE = 4
CHIPS = SIDE**3
AXES = ("shard", "basis")
HOP2 = (2, 1, 3, 0)
BF16 = jnp.bfloat16
F32 = jnp.float32
VMEM_LIMIT = 48 * 1024 * 1024


def device_id(x, y, z, core):
    return ((z % SIDE * SIDE + y % SIDE) * SIDE + x % SIDE) * 2 + core


def pairs(target):
    found = []
    for z in range(SIDE):
        for y in range(SIDE):
            for x in range(SIDE):
                for core in range(2):
                    found.append((device_id(x, y, z, core), device_id(*target(x, y, z, core))))
    assert len({to for _, to in found}) == len(found)
    return found


def hop1_pairs(step, crossed):
    def target(x, y, z, core):
        kind = 1 - core if crossed else core
        return (x + step, y, z, 0) if kind == 0 else (x, y + step, z, 1)

    return pairs(target)


def hop2_pairs(step):
    return pairs(lambda x, y, z, core: (x, y, z + step, core))


MATCHED = ((0, 0), (2, 1), (2, 0), (0, 1))
UNMATCHED = ((1, 1), (1, 0), (3, 1), (3, 0))


def hop3_pairs(send):
    def target(x, y, z, core):
        step, half = (MATCHED if (x + y + z) % 2 == core else UNMATCHED)[send]
        return (x, y + step, z, half) if core == 0 else (x + step, y, z, half)

    return pairs(target)


def coordinates():
    chip = lax.axis_index("shard")
    return chip % SIDE, chip // SIDE % SIDE, chip // (SIDE * SIDE), lax.axis_index("basis")


def group_of(x, y, z, kind, which):
    y_end = 2 * which + (x + z) % 2
    x_end = 2 * which + (y + z + 1) % 2
    return jnp.where(kind == 0, (z * SIDE + y_end) * SIDE + x, (z * SIDE + y) * SIDE + x_end)


def notes_kernel(kind_ref, counts_ref, dests_ref, rels_ref, lists_ref, out_ref):
    rows = CHIPS * 8
    blocks = dests_ref.shape[0]
    counts = counts_ref[...]
    before = (
        lax.broadcasted_iota(jnp.int32, (CHIPS, CHIPS), 0)
        < lax.broadcasted_iota(jnp.int32, (CHIPS, CHIPS), 1)
    ).astype(F32)
    used = counts.astype(F32)
    rank = jnp.dot(jnp.broadcast_to(used, (8, CHIPS)), before, preferred_element_type=F32)[:1]
    where = jnp.where(counts > 0, rank, -1.0)
    row = lax.broadcasted_iota(jnp.int32, (rows, 1), 0)
    slot, place = row // 8, row % 8
    line = place % SIDE
    owner = jnp.where(
        kind_ref[0] == 0, slot // SIDE * SIDE + line, slot // 16 * 16 + line * SIDE + slot % SIDE
    )
    lane = lax.broadcasted_iota(jnp.int32, (rows, CHIPS), 1)
    position = jnp.sum(jnp.where(lane == owner, where, 0.0), axis=1, keepdims=True)
    hit = position == lax.broadcasted_iota(jnp.int32, (rows, blocks), 1).astype(F32)
    hit = hit.astype(BF16)
    dests = jnp.dot(hit, dests_ref[...].astype(BF16), preferred_element_type=F32)
    rels = jnp.dot(hit, rels_ref[...].astype(BF16), preferred_element_type=F32)
    codes = jnp.where(position < 0, -1.0, dests + jnp.where(position >= blocks // 2, float(DST), 0.0))
    wanted = jnp.where(counts > 0, lists_ref[...], -1).astype(F32)
    block = jnp.sum(jnp.where(lane == slot, wanted, 0.0), axis=1, keepdims=True)
    other = jnp.where(lax.broadcasted_iota(jnp.int32, (rows, DST), 1) == 4, block, rels)
    out_ref[...] = jnp.where(place < SIDE, codes, other).astype(jnp.int32)


def make_notes(kind, counts, dests, rels, lists):
    blocks = dests.shape[0]
    halves = jnp.concatenate([rels // DST, rels % DST], axis=1)
    halves = jnp.pad(halves, ((0, 0), (0, DST - halves.shape[1])))
    vmem = pl.BlockSpec(memory_space=pltpu.VMEM)
    return pl.pallas_call(
        notes_kernel,
        out_shape=jax.ShapeDtypeStruct((CHIPS * 8, DST), jnp.int32),
        in_specs=[pl.BlockSpec(memory_space=pltpu.SMEM)] + [vmem] * 4,
        out_specs=vmem,
        name="notes",
    )(kind.reshape(1), counts.reshape(1, CHIPS), dests, halves, lists.reshape(1, CHIPS)).reshape(CHIPS, 8, DST)


SENDS = ((1, False), (3, False), (1, True), (3, True), (2, False), (2, True), (0, True))


def pick_kernel(step_z, wanted_ref, table_ref, *rest):
    outs, sems = rest[:-1], rest[-1]
    x, y, z, core = coordinates()
    copies = []
    for send, (step, crossed) in enumerate(SENDS):
        kind = 1 - core if crossed else core
        x_to = jnp.where(kind == 0, (x + step) % SIDE, x)
        y_to = jnp.where(kind == 0, y, (y + step) % SIDE)
        for which in range(2):
            block = wanted_ref[group_of(x_to, y_to, (z + step_z) % SIDE, kind, which)]
            start = pl.multiple_of(jnp.maximum(block, 0) * BROWS, BROWS)
            copies.append(
                (
                    block >= 0,
                    pltpu.make_async_copy(
                        table_ref.at[pl.ds(start, BROWS)], outs[send].at[which], sems.at[send, which]
                    ),
                )
            )
    for live, copy in copies:
        pl.when(live)(copy.start)
    for live, copy in copies:
        pl.when(live)(copy.wait)


def pick(step_z, wanted, table):
    width = table.shape[1]
    anywhere = pl.BlockSpec(memory_space=pl.ANY)
    return pl.pallas_call(
        functools.partial(pick_kernel, step_z),
        out_shape=[jax.ShapeDtypeStruct((2, BROWS, width), BF16)] * len(SENDS),
        in_specs=[pl.BlockSpec(memory_space=pltpu.SMEM), anywhere],
        out_specs=[anywhere] * len(SENDS),
        scratch_shapes=[pltpu.SemaphoreType.DMA((len(SENDS), 2))],
        cost_estimate=pl.CostEstimate(
            flops=0, bytes_accessed=4 * len(SENDS) * 2 * BROWS * width, transcendentals=0
        ),
        name="pick",
    )(wanted, table)


def project_kernel(step_z, codes_ref, wanted_ref, coef_ref, notes_ref, table_ref, *rest):
    received = rest[: len(SENDS)]
    own_basis, other_basis, out_ref, rows, notes, total, basis, sems, more_sems = rest[len(SENDS) :]
    x, y, z, core = coordinates()
    width = table_ref.shape[1]
    along = jnp.where(core == 0, x, y)
    lookup = {sent: received[i] for i, sent in enumerate(SENDS)}
    loads = [
        pltpu.make_async_copy(own_basis, basis.at[0], more_sems.at[0]),
        pltpu.make_async_copy(other_basis, basis.at[1], more_sems.at[1]),
    ]
    pieces, note_loads = [], []
    for which in range(2):
        group = group_of(x, y, (z + step_z) % SIDE, core, which)
        note_loads.append(pltpu.make_async_copy(notes_ref.at[group], notes.at[which], more_sems.at[2 + which]))
        note_loads[-1].start()
        for step in range(SIDE):
            line = (along - step) % SIDE
            code = codes_ref[group * SIDE + line]
            copies = []
            for part, crossed in enumerate((False, True)):
                if step == 0 and not crossed:
                    start = pl.multiple_of(jnp.maximum(wanted_ref[group], 0) * BROWS, BROWS)
                    source = table_ref.at[pl.ds(start, BROWS)]
                else:
                    source = lookup[(step, crossed)].at[which]
                copies.append(
                    pltpu.make_async_copy(source, rows.at[which, step, part], sems.at[which, step, part])
                )
            pl.when(code >= 0)(lambda copies=copies: [c.start() for c in copies] and None)
            pieces.append((which, step, line, code, copies))
    for load in loads:
        load.start()
    total[...] = jnp.zeros_like(total)
    for load in note_loads:
        load.wait()
    first_tile = lax.broadcasted_iota(jnp.int32, (1, BROWS), 1) < TILE
    dest = lax.broadcasted_iota(jnp.int32, (DST, BROWS), 0)
    for which, step, line, code, copies in pieces:

        @pl.when(code >= 0)
        def _(which=which, step=step, line=line, code=code, copies=copies):
            half = jnp.where(code >= DST, 1, 0)
            hit = notes[which, pl.ds(line, 1), :] - half * DST == dest
            chosen = []
            at = ((which * SIDE + step) * (BROWS // TILE)) * 2
            for k in range(2):
                weight = jnp.where(first_tile, coef_ref[at + k], coef_ref[at + 2 + k])
                high = weight.astype(BF16).astype(F32)
                high, low = jnp.where(hit, high, 0.0), jnp.where(hit, weight - high, 0.0)
                chosen.append(jnp.concatenate([high, low], axis=1))
            chosen = jnp.concatenate(chosen, axis=0).astype(BF16)
            for part in range(2):
                copies[part].wait()
                block = rows[which, step, part]
                added = jnp.dot(
                    chosen, jnp.concatenate([block, block], axis=0), preferred_element_type=F32
                )
                column = pl.multiple_of(jnp.where(core == part, 0, width), width)
                total[which, half, :, pl.ds(column, width)] += added

    for load in loads:
        load.wait()
    summed = [
        total[:, :, k * DST : (k + 1) * DST, :].reshape(4 * DST, 2 * width).astype(BF16) for k in range(2)
    ]
    wide = basis.shape[2]
    tile = 256
    for start in range(0, wide, tile):
        result = jnp.dot(summed[0], basis[0, :, start : start + tile], preferred_element_type=F32)
        result += jnp.dot(summed[1], basis[1, :, start : start + tile], preferred_element_type=F32)
        out_ref[:, :, start : start + tile] = result.reshape(4, DST, tile).astype(BF16)


def project(step_z, codes, wanted, coef, notes, table, received, own_basis, other_basis):
    width = table.shape[1]
    wide = own_basis.shape[1]
    anywhere = pl.BlockSpec(memory_space=pl.ANY)
    smem = pl.BlockSpec(memory_space=pltpu.SMEM)
    return pl.pallas_call(
        functools.partial(project_kernel, step_z),
        out_shape=jax.ShapeDtypeStruct((4, DST, wide), BF16),
        in_specs=[smem] * 3 + [anywhere] * (4 + len(SENDS)),
        out_specs=pl.BlockSpec(memory_space=pltpu.VMEM),
        scratch_shapes=[
            pltpu.VMEM((2, SIDE, 2, BROWS, width), BF16),
            pltpu.VMEM((2, 8, DST), jnp.int32),
            pltpu.VMEM((2, 2, 2 * DST, 2 * width), F32),
            pltpu.VMEM((2, 2 * width, wide), BF16),
            pltpu.SemaphoreType.DMA((2, SIDE, 2)),
            pltpu.SemaphoreType.DMA((4,)),
        ],
        cost_estimate=pl.CostEstimate(
            flops=2 * 4 * DST * 4 * width * wide, bytes_accessed=8 * 2**20, transcendentals=0
        ),
        compiler_params=pltpu.CompilerParams(vmem_limit_bytes=VMEM_LIMIT),
        name="project",
    )(codes, wanted, coef, notes, table, *received, own_basis, other_basis)


def merge_kernel(order_ref, *refs):
    ins, outs = refs[:SIDE], refs[SIDE:]
    for send in range(4):
        at = order_ref[send]
        result = ins[0][at].astype(F32)
        for other in ins[1:]:
            result += other[at].astype(F32)
        outs[send][...] = result.astype(BF16)


def merge(order, parts):
    wide = parts[0].shape[2]
    slab = 32
    return pl.pallas_call(
        merge_kernel,
        out_shape=[jax.ShapeDtypeStruct((DST, wide), BF16)] * 4,
        grid_spec=pltpu.PrefetchScalarGridSpec(
            num_scalar_prefetch=1,
            grid=(DST // slab,),
            in_specs=[pl.BlockSpec((4, slab, wide), lambda i, order: (0, i, 0))] * SIDE,
            out_specs=[pl.BlockSpec((slab, wide), lambda i, order: (i, 0))] * 4,
        ),
        compiler_params=pltpu.CompilerParams(vmem_limit_bytes=VMEM_LIMIT),
        name="merge",
    )(order, *parts)


def body(features, bases, coeffs, block_lists, block_counts, tile_rel, dest_ids):
    x, y, z, core = coordinates()
    blocks = tile_rel.shape[1] * TILE // BROWS
    other_basis = lax.ppermute(bases[0], "basis", [(0, 1), (1, 0)])

    sent = make_notes(
        (x + y + z) % 2,
        block_counts[0],
        dest_ids[0].reshape(blocks, BROWS),
        tile_rel[0].reshape(blocks, BROWS // TILE),
        block_lists[0, :, 0],
    )
    notes = lax.all_to_all(sent, "shard", split_axis=0, concat_axis=0, tiled=True)
    wanted = notes[:, SIDE, 4]
    codes = notes[:, :SIDE, 0].reshape(-1)
    along = jnp.where(core == 0, x, y)

    arrived = []
    for step_z in HOP2:
        picked = pick(step_z, wanted, features)
        arrived.append([lax.ppermute(buf, AXES, hop1_pairs(*send)) for buf, send in zip(picked, SENDS)])

    groups = jnp.stack([group_of(x, y, (z + s) % SIDE, core, w) for s in HOP2 for w in range(2)])
    lines = (along - jnp.arange(SIDE, dtype=jnp.int32)) % SIDE
    told = notes[groups[:, None], SIDE + lines[None, :], :4]
    coef = coeffs[told[..., :2] * DST + told[..., 2:]]
    coef = jnp.where(core == 0, coef, coef[..., ::-1]).reshape(len(HOP2), -1)

    parts = []
    for i, step_z in enumerate(HOP2):
        part = project(
            step_z, codes, wanted, coef[i], notes, features, arrived[i], bases[0], other_basis
        )
        parts.append(part if step_z == 0 else lax.ppermute(part, AXES, hop2_pairs(step_z)))

    last = jnp.where(core == 0, y, x)
    matched = (x + y + z) % 2 == core
    order = jnp.stack(
        [
            jnp.where(matched, (last + a) % SIDE // 2 * 2 + b, (last + c) % SIDE // 2 * 2 + d)
            for (a, b), (c, d) in zip(MATCHED, UNMATCHED)
        ]
    )
    merged = merge(order, parts)
    ends = [lax.ppermute(buf, AXES, hop3_pairs(send)) for send, buf in enumerate(merged)]
    summed = sum(end.astype(F32) for end in ends)

    rows_dev = blocks // 2 * BROWS
    my_dests = lax.dynamic_slice_in_dim(dest_ids[0], core * rows_dev, rows_dev)
    indegree = jnp.sum(
        (my_dests[None, :] == jnp.arange(DST, dtype=jnp.int32)[:, None]).astype(F32), axis=1
    )
    return (summed / jnp.maximum(indegree, 1.0)[:, None]).astype(BF16)


def solution(mesh):
    placed = (
        P("shard", "basis"),
        P("basis", None, None),
        P(),
        P("shard", None, None),
        P("shard", None),
        P("shard", None),
        P("shard", None),
    )
    return jax.shard_map(
        body, mesh=mesh, in_specs=placed, out_specs=P(("shard", "basis"), None), check_vma=False
    )
```

time: 313 us -> 389 us (1.24); the launches traced: 307 us -> 388 us
  starting transfers between devices: 5.92 us -> 193 us
  Pallas kernels: 0 us -> 122 us
  waiting for transfers between devices: 118 us -> 32.8 us
  other arithmetic: 72.4 us -> 4.08 us
  blocking collectives: 36.1 us -> 0 us
  local copies, waits for them, and re-layouts: 49.1 us -> 34.3 us
  between operations: 13.6 us -> 0.92 us
  matrix products: 12.2 us -> 0 us
    ppermute x0 -> x36, starting transfers between devices: none -> 182 us  [the longest x28 129 us: body(): lax.ppermute(buf, AXES, hop1_pairs(*send))]
    pallas_call x0 -> x10, Pallas kernels: none -> 122 us  [the longest x4 87.7 us: pick(): pl.pallas_call(functools.partial(pick_kernel, step_z), out_shape=[jax.Sha...]
    all_to_all x1, waiting for transfers between devices: 106 us -> 8.48 us  [body(): lax.all_to_all(sent, 'shard', split_axis=0, concat_axis=0, tiled=True)]
    all_to_all x2 -> x0, blocking collectives: 36.1 us -> none  [the longest x1 20.2 us: body(): lax.all_to_all(block_lists, 'shard', split_axis=1, concat_axis=0, tiled=T...]
    scatter-add x2 -> x0, other arithmetic: 32 us -> none  [the longest x1 19.1 us: body(): summed = jax.ops.segment_sum(mixture, my_dests, num_segments=DST_DEV)]
    convert_element_type x3 -> x1, other arithmetic: 28.3 us -> 0.89 us  [body(): return (summed / jnp.maximum(indegree, 1.0)[:, None]).astype(BF16)]
    ppermute x0 -> x36, waiting for transfers between devices: none -> 24.3 us  [the longest x28 15.3 us: body(): lax.ppermute(buf, AXES, hop1_pairs(*send))]
    dot_general x1 -> x0, matrix products: 12.2 us -> none  [body(): jnp.einsum('rc,kcd->rkd', lax.all_gather(fetched, 'basis', axis=1, tiled=...]
  transfers between devices with their start and end apart: 2 -> 37, of which waited for: 2 -> 8; matrix products, arithmetic and copies ran while one was open for 7% -> 4% of each run, Pallas kernels for 0% -> 30%
where the time goes in v1:
time: 389 us; the launch traced here: 388 us
  starting transfers between devices  193 us (50%)
  Pallas kernels  122 us (31%)
  local copies, waits for them, and re-layouts  34.3 us (9%)
  waiting for transfers between devices  32.8 us (8%)
  other arithmetic  4.08 us (1%)
    ppermute x28, starting transfers between devices, body(): lax.ppermute(buf, AXES, hop1_pairs(*send))  129 us
    pallas_call x4, Pallas kernels, pick(): pl.pallas_call(functools.partial(pick_kernel, step_z), out_shape=[jax.Sha...  87.7 us
    ppermute x3, starting transfers between devices, body(): lax.ppermute(part, AXES, hop2_pairs(step_z))  42.2 us
    pallas_call x4, Pallas kernels, project(): pl.pallas_call(functools.partial(project_kernel, step_z), out_shape=jax.S...  29.1 us
    unnamed x96, local copies, waits for them, and re-layouts  21.6 us
    ppermute x28, waiting for transfers between devices, body(): lax.ppermute(buf, AXES, hop1_pairs(*send))  15.3 us
    all_to_all x1, starting transfers between devices, body(): lax.all_to_all(sent, 'shard', split_axis=0, concat_axis=0, tiled=True)  12 us
    ppermute x4, waiting for transfers between devices, body(): lax.ppermute(buf, AXES, hop3_pairs(send))  8.98 us
  transfers between devices with their start and end apart: 37, of which 8 were waited for; matrix products, arithmetic and copies ran while one was open for 4% of the time, Pallas kernels for 30%

profile of v1, /device:TPU:1, one launch (start us, length us, event | category | flops | bytes accessed | tf_op | source)
XLA Modules:
  0.0 387.8 jit_solution(8203745667923668790)
XLA Ops:
  5.9 12.0 %all-to-all-start = ((s32[64,8,128]{2,1,0:T(8,128)}), s32[64,8,128]{2,1,0:T(8,128)S(1)}, u32[]{:S(2)}, u32[]{:S(2)}) async-start(s32[64,8,128]{2,1,0:T(8,128)} %bitcast.31), calls=%async_computation | async-start | bytes 524288 | tf_op jit(solution)/shard_map/all_to_all | solution.py:299
  18.9 8.5 %all-to-all-done.notes_ref = s32[64,8,128]{2,1,0:T(8,128)S(1)} async-done(((s32[64,8,128]{2,1,0:T(8,128)}), s32[64,8,128]{2,1,0:T(8,128)S(1)}, u32[]{:S(2)}, u32[]{:S(2)}) %all-to-all-start) | async-done | bytes 262176 | tf_op jit(solution)/shard_map/all_to_all | solution.py:299
  29.2 18.0 %pick.4 = (bf16[2,128,512]{2,1,0:T(8,128)(2,1)}, bf16[2,128,512]{2,1,0:T(8,128)(2,1)}, bf16[2,128,512]{2,1,0:T(8,128)(2,1)}, bf16[2,128,512]{2,1,0:T(8,128)(2,1)...) custom-call(s32[64]{0:T(128)} %slice_reduce_fusion.1.wanted_ref, ...), custom_call_target="tpu_custom_call" | custom-call | bytes 3670016 | tf_op jit(solution)/shard_map/pick/pallas_call | solution.py:147
  47.3 16.2 %collective-permute-start = (bf16[2,128,512]{2,1,0:T(8,128)(2,1)}, bf16[2,128,512]{2,1,0:T(8,128)(2,1)S(1)}, u32[]{:S(2)}, u32[]{:S(2)}) collective-permute-start(bf16[2,128,512]{2,1,0:T(8,128)(2,1)} %get-tuple-element.37), channel_id=1, source_target_pairs={{0,2},{1,9},{2,4},{3,11},{4,6},{5,13},{6,0},{7,15},{8,10},{9,17},{... | collective-permute-start | bytes 786440 | tf_op jit(solution)/shard_map/ppermute | solution.py:307
  69.4 21.9 %pick.5 = (bf16[2,128,512]{2,1,0:T(8,128)(2,1)}, bf16[2,128,512]{2,1,0:T(8,128)(2,1)}, bf16[2,128,512]{2,1,0:T(8,128)(2,1)}, bf16[2,128,512]{2,1,0:T(8,128)(2,1)...) custom-call(s32[64]{0:T(128)} %slice_reduce_fusion.1.wanted_ref, ...), custom_call_target="tpu_custom_call" | custom-call | bytes 3670016 | tf_op jit(solution)/shard_map/pick/pallas_call | solution.py:147
  91.6 16.1 %collective-permute-start.9 = (bf16[2,128,512]{2,1,0:T(8,128)(2,1)}, bf16[2,128,512]{2,1,0:T(8,128)(2,1)S(1)}, u32[]{:S(2)}, u32[]{:S(2)}) collective-permute-start(bf16[2,128,512]{2,1,0:T(8,128)(2,1)} %get-tuple-element.44), channel_id=1, source_target_pairs={{0,2},{1,9},{2,4},{3,11},{4,6},{5,13},{6,0},{7,15},{8,10},{9,17},{... | collective-permute-start | bytes 786440 | tf_op jit(solution)/shard_map/ppermute | solution.py:307
  107.8 4.7 %copy.33 = f32[14824,2]{1,0:T(8,128)} copy(f32[14824,2]{0,1:T(2,128)S(1)} %copy-done.36) | data formatting | bytes 237184 | tf_op args[2]
  127.1 14.1 %pick.6 = (bf16[2,128,512]{2,1,0:T(8,128)(2,1)}, bf16[2,128,512]{2,1,0:T(8,128)(2,1)}, bf16[2,128,512]{2,1,0:T(8,128)(2,1)}, bf16[2,128,512]{2,1,0:T(8,128)(2,1)...) custom-call(s32[64]{0:T(128)} %slice_reduce_fusion.1.wanted_ref, ...), custom_call_target="tpu_custom_call" | custom-call | bytes 3670016 | tf_op jit(solution)/shard_map/pick/pallas_call | solution.py:147
  143.4 8.2 %collective-permute-start.17 = (bf16[2,128,512]{2,1,0:T(8,128)(2,1)}, bf16[2,128,512]{2,1,0:T(8,128)(2,1)}, u32[]{:S(2)}, u32[]{:S(2)}) collective-permute-start(bf16[2,128,512]{2,1,0:T(8,128)(2,1)} %get-tuple-element.51), channel_id=1, source_target_pairs={{0,2},{1,9},{2,4},{3,11},{4,6},{5,13},{6,0},{7,15},{8,10},{9,17},{... | collective-permute-start | bytes 786440 | tf_op jit(solution)/shard_map/ppermute | solution.py:307
  151.6 5.0 %collective-permute-start.18 = (bf16[2,128,512]{2,1,0:T(8,128)(2,1)}, bf16[2,128,512]{2,1,0:T(8,128)(2,1)}, u32[]{:S(2)}, u32[]{:S(2)}) collective-permute-start(bf16[2,128,512]{2,1,0:T(8,128)(2,1)} %get-tuple-element.52), channel_id=1, source_target_pairs={{0,6},{1,25},{2,0},{3,27},{4,2},{5,29},{6,4},{7,31},{8,14},{9,1},{... | collective-permute-start | bytes 786440 | tf_op jit(solution)/shard_map/ppermute | solution.py:307
  156.6 24.3 %collective-permute-start.19 = (bf16[2,128,512]{2,1,0:T(8,128)(2,1)}, bf16[2,128,512]{2,1,0:T(8,128)(2,1)}, u32[]{:S(2)}, u32[]{:S(2)}) collective-permute-start(bf16[2,128,512]{2,1,0:T(8,128)(2,1)} %get-tuple-element.53), channel_id=1, source_target_pairs={{0,9},{1,2},{2,11},{3,4},{4,13},{5,6},{6,15},{7,0},{8,17},{9,10},{... | collective-permute-start | bytes 786440 | tf_op jit(solution)/shard_map/ppermute | solution.py:307
  182.0 33.8 %pick.7 = (bf16[2,128,512]{2,1,0:T(8,128)(2,1)}, bf16[2,128,512]{2,1,0:T(8,128)(2,1)}, bf16[2,128,512]{2,1,0:T(8,128)(2,1)}, bf16[2,128,512]{2,1,0:T(8,128)(2,1)...) custom-call(s32[64]{0:T(128)} %slice_reduce_fusion.1.wanted_ref, ...), custom_call_target="tpu_custom_call" | custom-call | bytes 3670016 | tf_op jit(solution)/shard_map/pick/pallas_call | solution.py:147
  227.0 8.5 %project.4 = bf16[4,128,1024]{2,1,0:T(8,128)(2,1)S(1)} custom-call(s32[256]{0:T(256)S(1)} %reshape_squeeze.15.codes_ref, s32[64]{0:T(128)S(1)} %copy-done.35, f32[32]{0:T(128)S(1)} %squeeze.24.coef_ref, s32[64,8,128]{2,1,0:T(8,128)S(1)} %all-to-all-done.notes_ref, bf16[6144,512]{1,0:T(8,128)(2,1)} %table_ref.15, bf16[2,128,512]{2,1,0:T(8,128)(2,1)S(1)} %copy-done.2, ...), custom_call_target="tpu_custom_call" | custom-call | flops 2147483648 | bytes 8388608 | tf_op jit(solution)/shard_map/project/pallas_call | solution.py:239
  235.7 6.3 %project.5 = bf16[4,128,1024]{2,1,0:T(8,128)(2,1)} custom-call(s32[256]{0:T(256)S(1)} %reshape_squeeze.15.codes_ref, s32[64]{0:T(128)S(1)} %copy-done.35, f32[32]{0:T(128)S(1)} %squeeze.26.coef_ref, s32[64,8,128]{2,1,0:T(8,128)S(1)} %all-to-all-done.notes_ref, bf16[6144,512]{1,0:T(8,128)(2,1)} %table_ref.15, bf16[2,128,512]{2,1,0:T(8,128)(2,1)S(1)} %copy-done.24, ...), custom_call_target="tpu_custom_call" | custom-call | flops 2147483648 | bytes 8388608 | tf_op jit(solution)/shard_map/project/pallas_call | solution.py:239
  242.0 40.0 %collective-permute-start.8 = (bf16[4,128,1024]{2,1,0:T(8,128)(2,1)S(1)}, bf16[4,128,1024]{2,1,0:T(8,128)(2,1)}, u32[]{:S(2)}, u32[]{:S(2)}) collective-permute-start(bf16[4,128,1024]{2,1,0:T(8,128)(2,1)S(1)} %project.4), channel_id=1, source_target_pairs={{0,64},{1,65},{2,66},{3,67},{4,68},{5,69},{6,70},{7,71},{8,72},{9,... | collective-permute-start | bytes 3145736 | tf_op jit(solution)/shard_map/ppermute | solution.py:320
  282.0 8.0 %project.6 = bf16[4,128,1024]{2,1,0:T(8,128)(2,1)} custom-call(s32[256]{0:T(256)S(1)} %reshape_squeeze.15.codes_ref, s32[64]{0:T(128)S(1)} %copy-done.35, f32[32]{0:T(128)S(1)} %squeeze.27.coef_ref, s32[64,8,128]{2,1,0:T(8,128)S(1)} %all-to-all-done.notes_ref, bf16[6144,512]{1,0:T(8,128)(2,1)} %table_ref.15, ...), custom_call_target="tpu_custom_call" | custom-call | flops 2147483648 | bytes 8388608 | tf_op jit(solution)/shard_map/project/pallas_call | solution.py:239
  293.0 9.0 %collective-permute-start.27 = (bf16[2,128,512]{2,1,0:T(8,128)(2,1)S(1)}, bf16[2,128,512]{2,1,0:T(8,128)(2,1)S(1)}, u32[]{:S(2)}, u32[]{:S(2)}) collective-permute-start(bf16[2,128,512]{2,1,0:T(8,128)(2,1)S(1)} %copy-done.44), channel_id=1, source_target_pairs={{0,9},{1,2},{2,11},{3,4},{4,13},{5,6},{6,15},{7,0},{8,17},{9,10},{... | collective-permute-start | bytes 786440 | tf_op jit(solution)/shard_map/ppermute | solution.py:307
  302.7 32.8 %collective-permute-start.28 = (bf16[2,128,512]{2,1,0:T(8,128)(2,1)S(1)}, bf16[2,128,512]{2,1,0:T(8,128)(2,1)S(1)}, u32[]{:S(2)}, u32[]{:S(2)}) collective-permute-start(bf16[2,128,512]{2,1,0:T(8,128)(2,1)S(1)} %copy-done.43), channel_id=1, source_target_pairs={{0,25},{1,6},{2,27},{3,0},{4,29},{5,2},{6,31},{7,4},{8,1},{9,14},{... | collective-permute-start | bytes 786440 | tf_op jit(solution)/shard_map/ppermute | solution.py:307
  337.8 4.0 %collective-permute-start.29 = (bf16[2,128,512]{2,1,0:T(8,128)(2,1)S(1)}, bf16[2,128,512]{2,1,0:T(8,128)(2,1)S(1)}, u32[]{:S(2)}, u32[]{:S(2)}) collective-permute-start(bf16[2,128,512]{2,1,0:T(8,128)(2,1)S(1)} %copy-done.42), channel_id=1, source_target_pairs={{0,4},{1,17},{2,6},{3,19},{4,0},{5,21},{6,2},{7,23},{8,12},{9,25},... | collective-permute-start | bytes 786440 | tf_op jit(solution)/shard_map/ppermute | solution.py:307
  341.8 4.1 %collective-permute-done.28.rest_3_ = bf16[2,128,512]{2,1,0:T(8,128)(2,1)S(1)} collective-permute-done((bf16[2,128,512]{2,1,0:T(8,128)(2,1)S(1)}, bf16[2,128,512]{2,1,0:T(8,128)(2,1)S(1)}, u32[]{:S(2)}, u32[]{:S(2)}) %collective-permute-start.28) | collective-permute-done | bytes 262176 | tf_op jit(solution)/shard_map/ppermute | solution.py:307
  348.2 6.0 %collective-permute-done.30.rest_5_ = bf16[2,128,512]{2,1,0:T(8,128)(2,1)} collective-permute-done((bf16[2,128,512]{2,1,0:T(8,128)(2,1)}, bf16[2,128,512]{2,1,0:T(8,128)(2,1)}, u32[]{:S(2)}, u32[]{:S(2)}) %collective-permute-start.30) | collective-permute-done | bytes 262176 | tf_op jit(solution)/shard_map/ppermute | solution.py:307
  359.0 6.4 %project.7.refs_3_ = bf16[4,128,1024]{2,1,0:T(8,128)(2,1)S(1)} custom-call(s32[256]{0:T(256)S(1)} %reshape_squeeze.15.codes_ref, s32[64]{0:T(128)S(1)} %copy-done.35, f32[32]{0:T(128)S(1)} %squeeze.28.coef_ref, s32[64,8,128]{2,1,0:T(8,128)S(1)} %all-to-all-done.notes_ref, bf16[6144,512]{1,0:T(8,128)(2,1)} %table_ref.15, bf16[2,128,512]{2,1,0:T(8,128)(2,1)S(1)} %copy-done.4, ...), custom_call_target="tpu_custom_call" | custom-call | flops 2147483648 | bytes 8388608 | tf_op jit(solution)/shard_map/project/pallas_call | solution.py:239
  372.9 4.8 %collective-permute-start.32 = (bf16[128,1024]{1,0:T(8,128)(2,1)S(1)}, bf16[128,1024]{1,0:T(8,128)(2,1)S(1)}, u32[]{:S(2)}, u32[]{:S(2)}) collective-permute-start(bf16[128,1024]{1,0:T(8,128)(2,1)S(1)} %get-tuple-element.65), channel_id=1, source_target_pairs={{0,0},{1,3},{2,11},{3,2},{4,4},{5,7},{6,15},{7,6},{8,17},{9,8},{10... | collective-permute-start | bytes 786440 | tf_op jit(solution)/shard_map/ppermute | solution.py:331
  383.0 3.9 collective-permute-done.32
  (207 shorter events, 70.4 us)
Async XLA Ops:
  17.9 199.1 %collective-permute-start.7 = (bf16[1024,1024]{1,0:T(8,128)(2,1)}, bf16[1024,1024]{1,0:T(8,128)(2,1)}, u32[]{:S(2)}, u32[]{:S(2)}) collective-permute-start(bf16[1024,1024]{1,0:T(8,128)(2,1)} %bitcast.26), channel_id=1, source_target_pairs={{0,1},{1,0},{2,3},{3,2},{4,5},{5,4},{6,7},{7,6},{8,9},{9,8},{10,11... | collective-permute-start | bytes 6291464 | tf_op jit(solution)/shard_map/ppermute | solution.py:290
  63.8 27.5 %collective-permute-start.1 = (bf16[2,128,512]{2,1,0:T(8,128)(2,1)}, bf16[2,128,512]{2,1,0:T(8,128)(2,1)S(1)}, u32[]{:S(2)}, u32[]{:S(2)}) collective-permute-start(bf16[2,128,512]{2,1,0:T(8,128)(2,1)} %get-tuple-element.38), channel_id=1, source_target_pairs={{0,6},{1,25},{2,0},{3,27},{4,2},{5,29},{6,4},{7,31},{8,14},{9,1},{... | collective-permute-start | bytes 786440 | tf_op jit(solution)/shard_map/ppermute | solution.py:307
  64.2 27.3 %collective-permute-start.2 = (bf16[2,128,512]{2,1,0:T(8,128)(2,1)}, bf16[2,128,512]{2,1,0:T(8,128)(2,1)S(1)}, u32[]{:S(2)}, u32[]{:S(2)}) collective-permute-start(bf16[2,128,512]{2,1,0:T(8,128)(2,1)} %get-tuple-element.39), channel_id=1, source_target_pairs={{0,9},{1,2},{2,11},{3,4},{4,13},{5,6},{6,15},{7,0},{8,17},{9,10},{... | collective-permute-start | bytes 786440 | tf_op jit(solution)/shard_map/ppermute | solution.py:307
  64.2 27.4 %collective-permute-start.3 = (bf16[2,128,512]{2,1,0:T(8,128)(2,1)}, bf16[2,128,512]{2,1,0:T(8,128)(2,1)S(1)}, u32[]{:S(2)}, u32[]{:S(2)}) collective-permute-start(bf16[2,128,512]{2,1,0:T(8,128)(2,1)} %get-tuple-element.40), channel_id=1, source_target_pairs={{0,25},{1,6},{2,27},{3,0},{4,29},{5,2},{6,31},{7,4},{8,1},{9,14},{... | collective-permute-start | bytes 786440 | tf_op jit(solution)/shard_map/ppermute | solution.py:307
  67.7 40.0 %collective-permute-start.4 = (bf16[2,128,512]{2,1,0:T(8,128)(2,1)}, bf16[2,128,512]{2,1,0:T(8,128)(2,1)S(1)}, u32[]{:S(2)}, u32[]{:S(2)}) collective-permute-start(bf16[2,128,512]{2,1,0:T(8,128)(2,1)} %get-tuple-element.41), channel_id=1, source_target_pairs={{0,4},{1,17},{2,6},{3,19},{4,0},{5,21},{6,2},{7,23},{8,12},{9,25},... | collective-permute-start | bytes 786440 | tf_op jit(solution)/shard_map/ppermute | solution.py:307
  91.6 29.3 %collective-permute-start.9 = (bf16[2,128,512]{2,1,0:T(8,128)(2,1)}, bf16[2,128,512]{2,1,0:T(8,128)(2,1)S(1)}, u32[]{:S(2)}, u32[]{:S(2)}) collective-permute-start(bf16[2,128,512]{2,1,0:T(8,128)(2,1)} %get-tuple-element.44), channel_id=1, source_target_pairs={{0,2},{1,9},{2,4},{3,11},{4,6},{5,13},{6,0},{7,15},{8,10},{9,17},{... | collective-permute-start | bytes 786440 | tf_op jit(solution)/shard_map/ppermute | solution.py:307
  116.2 25.0 %collective-permute-start.11 = (bf16[2,128,512]{2,1,0:T(8,128)(2,1)}, bf16[2,128,512]{2,1,0:T(8,128)(2,1)S(1)}, u32[]{:S(2)}, u32[]{:S(2)}) collective-permute-start(bf16[2,128,512]{2,1,0:T(8,128)(2,1)} %get-tuple-element.46), channel_id=1, source_target_pairs={{0,9},{1,2},{2,11},{3,4},{4,13},{5,6},{6,15},{7,0},{8,17},{9,10},{... | collective-permute-start | bytes 786440 | tf_op jit(solution)/shard_map/ppermute | solution.py:307
  117.1 26.3 %collective-permute-start.12 = (bf16[2,128,512]{2,1,0:T(8,128)(2,1)}, bf16[2,128,512]{2,1,0:T(8,128)(2,1)S(1)}, u32[]{:S(2)}, u32[]{:S(2)}) collective-permute-start(bf16[2,128,512]{2,1,0:T(8,128)(2,1)} %get-tuple-element.47), channel_id=1, source_target_pairs={{0,25},{1,6},{2,27},{3,0},{4,29},{5,2},{6,31},{7,4},{8,1},{9,14},{... | collective-permute-start | bytes 786440 | tf_op jit(solution)/shard_map/ppermute | solution.py:307
  121.6 30.0 %collective-permute-start.13 = (bf16[2,128,512]{2,1,0:T(8,128)(2,1)}, bf16[2,128,512]{2,1,0:T(8,128)(2,1)S(1)}, u32[]{:S(2)}, u32[]{:S(2)}) collective-permute-start(bf16[2,128,512]{2,1,0:T(8,128)(2,1)} %get-tuple-element.48), channel_id=1, source_target_pairs={{0,4},{1,17},{2,6},{3,19},{4,0},{5,21},{6,2},{7,23},{8,12},{9,25},... | collective-permute-start | bytes 786440 | tf_op jit(solution)/shard_map/ppermute | solution.py:307
  126.0 30.5 %collective-permute-start.14 = (bf16[2,128,512]{2,1,0:T(8,128)(2,1)}, bf16[2,128,512]{2,1,0:T(8,128)(2,1)}, u32[]{:S(2)}, u32[]{:S(2)}) collective-permute-start(bf16[2,128,512]{2,1,0:T(8,128)(2,1)} %get-tuple-element.49), channel_id=1, source_target_pairs={{0,17},{1,4},{2,19},{3,6},{4,21},{5,0},{6,23},{7,2},{8,25},{9,12},... | collective-permute-start | bytes 786440 | tf_op jit(solution)/shard_map/ppermute | solution.py:307
  141.2 75.4 %collective-permute-start.15 = (bf16[2,128,512]{2,1,0:T(8,128)(2,1)}, bf16[2,128,512]{2,1,0:T(8,128)(2,1)}, u32[]{:S(2)}, u32[]{:S(2)}) collective-permute-start(bf16[2,128,512]{2,1,0:T(8,128)(2,1)} %get-tuple-element.50), channel_id=1, source_target_pairs={{0,1},{1,0},{2,3},{3,2},{4,5},{5,4},{6,7},{7,6},{8,9},{9,8},{10,11... | collective-permute-start | bytes 786440 | tf_op jit(solution)/shard_map/ppermute | solution.py:307
  143.4 73.4 %collective-permute-start.17 = (bf16[2,128,512]{2,1,0:T(8,128)(2,1)}, bf16[2,128,512]{2,1,0:T(8,128)(2,1)}, u32[]{:S(2)}, u32[]{:S(2)}) collective-permute-start(bf16[2,128,512]{2,1,0:T(8,128)(2,1)} %get-tuple-element.51), channel_id=1, source_target_pairs={{0,2},{1,9},{2,4},{3,11},{4,6},{5,13},{6,0},{7,15},{8,10},{9,17},{... | collective-permute-start | bytes 786440 | tf_op jit(solution)/shard_map/ppermute | solution.py:307
  151.6 65.2 %collective-permute-start.18 = (bf16[2,128,512]{2,1,0:T(8,128)(2,1)}, bf16[2,128,512]{2,1,0:T(8,128)(2,1)}, u32[]{:S(2)}, u32[]{:S(2)}) collective-permute-start(bf16[2,128,512]{2,1,0:T(8,128)(2,1)} %get-tuple-element.52), channel_id=1, source_target_pairs={{0,6},{1,25},{2,0},{3,27},{4,2},{5,29},{6,4},{7,31},{8,14},{9,1},{... | collective-permute-start | bytes 786440 | tf_op jit(solution)/shard_map/ppermute | solution.py:307
  156.6 78.9 %collective-permute-start.19 = (bf16[2,128,512]{2,1,0:T(8,128)(2,1)}, bf16[2,128,512]{2,1,0:T(8,128)(2,1)}, u32[]{:S(2)}, u32[]{:S(2)}) collective-permute-start(bf16[2,128,512]{2,1,0:T(8,128)(2,1)} %get-tuple-element.53), channel_id=1, source_target_pairs={{0,9},{1,2},{2,11},{3,4},{4,13},{5,6},{6,15},{7,0},{8,17},{9,10},{... | collective-permute-start | bytes 786440 | tf_op jit(solution)/shard_map/ppermute | solution.py:307
  216.7 25.3 %collective-permute-start.20 = (bf16[2,128,512]{2,1,0:T(8,128)(2,1)}, bf16[2,128,512]{2,1,0:T(8,128)(2,1)S(1)}, u32[]{:S(2)}, u32[]{:S(2)}) collective-permute-start(bf16[2,128,512]{2,1,0:T(8,128)(2,1)} %get-tuple-element.54), channel_id=1, source_target_pairs={{0,25},{1,6},{2,27},{3,0},{4,29},{5,2},{6,31},{7,4},{8,1},{9,14},{... | collective-permute-start | bytes 786440 | tf_op jit(solution)/shard_map/ppermute | solution.py:307
  216.7 65.2 %collective-permute-start.21 = (bf16[2,128,512]{2,1,0:T(8,128)(2,1)}, bf16[2,128,512]{2,1,0:T(8,128)(2,1)S(1)}, u32[]{:S(2)}, u32[]{:S(2)}) collective-permute-start(bf16[2,128,512]{2,1,0:T(8,128)(2,1)} %get-tuple-element.55), channel_id=1, source_target_pairs={{0,4},{1,17},{2,6},{3,19},{4,0},{5,21},{6,2},{7,23},{8,12},{9,25},... | collective-permute-start | bytes 786440 | tf_op jit(solution)/shard_map/ppermute | solution.py:307
  216.8 65.1 %collective-permute-start.22 = (bf16[2,128,512]{2,1,0:T(8,128)(2,1)}, bf16[2,128,512]{2,1,0:T(8,128)(2,1)S(1)}, u32[]{:S(2)}, u32[]{:S(2)}) collective-permute-start(bf16[2,128,512]{2,1,0:T(8,128)(2,1)} %get-tuple-element.56), channel_id=1, source_target_pairs={{0,17},{1,4},{2,19},{3,6},{4,21},{5,0},{6,23},{7,2},{8,25},{9,12},... | collective-permute-start | bytes 786440 | tf_op jit(solution)/shard_map/ppermute | solution.py:307
  217.0 65.0 %collective-permute-start.23 = (bf16[2,128,512]{2,1,0:T(8,128)(2,1)}, bf16[2,128,512]{2,1,0:T(8,128)(2,1)S(1)}, u32[]{:S(2)}, u32[]{:S(2)}) collective-permute-start(bf16[2,128,512]{2,1,0:T(8,128)(2,1)} %get-tuple-element.57), channel_id=1, source_target_pairs={{0,1},{1,0},{2,3},{3,2},{4,5},{5,4},{6,7},{7,6},{8,9},{9,8},{10,11... | collective-permute-start | bytes 786440 | tf_op jit(solution)/shard_map/ppermute | solution.py:307
  235.5 56.7 %collective-permute-start.25 = (bf16[2,128,512]{2,1,0:T(8,128)(2,1)S(1)}, bf16[2,128,512]{2,1,0:T(8,128)(2,1)S(1)}, u32[]{:S(2)}, u32[]{:S(2)}) collective-permute-start(bf16[2,128,512]{2,1,0:T(8,128)(2,1)S(1)} %copy-done.46), channel_id=1, source_target_pairs={{0,2},{1,9},{2,4},{3,11},{4,6},{5,13},{6,0},{7,15},{8,10},{9,17},{... | collective-permute-start | bytes 786440 | tf_op jit(solution)/shard_map/ppermute | solution.py:307
  242.0 123.3 %collective-permute-start.8 = (bf16[4,128,1024]{2,1,0:T(8,128)(2,1)S(1)}, bf16[4,128,1024]{2,1,0:T(8,128)(2,1)}, u32[]{:S(2)}, u32[]{:S(2)}) collective-permute-start(bf16[4,128,1024]{2,1,0:T(8,128)(2,1)S(1)} %project.4), channel_id=1, source_target_pairs={{0,64},{1,65},{2,66},{3,67},{4,68},{5,69},{6,70},{7,71},{8,72},{9,... | collective-permute-start | bytes 3145736 | tf_op jit(solution)/shard_map/ppermute | solution.py:320
  282.0 83.4 %collective-permute-start.16 = (bf16[4,128,1024]{2,1,0:T(8,128)(2,1)}, bf16[4,128,1024]{2,1,0:T(8,128)(2,1)}, u32[]{:S(2)}, u32[]{:S(2)}) collective-permute-start(bf16[4,128,1024]{2,1,0:T(8,128)(2,1)} %project.5), channel_id=1, source_target_pairs={{0,32},{1,33},{2,34},{3,35},{4,36},{5,37},{6,38},{7,39},{8,40},{9,... | collective-permute-start | bytes 3145736 | tf_op jit(solution)/shard_map/ppermute | solution.py:320
  290.0 75.3 %collective-permute-start.24 = (bf16[4,128,1024]{2,1,0:T(8,128)(2,1)}, bf16[4,128,1024]{2,1,0:T(8,128)(2,1)}, u32[]{:S(2)}, u32[]{:S(2)}) collective-permute-start(bf16[4,128,1024]{2,1,0:T(8,128)(2,1)} %project.6), channel_id=1, source_target_pairs={{0,96},{1,97},{2,98},{3,99},{4,100},{5,101},{6,102},{7,103},{8,104... | collective-permute-start | bytes 3145736 | tf_op jit(solution)/shard_map/ppermute | solution.py:320
  293.0 44.2 %collective-permute-start.27 = (bf16[2,128,512]{2,1,0:T(8,128)(2,1)S(1)}, bf16[2,128,512]{2,1,0:T(8,128)(2,1)S(1)}, u32[]{:S(2)}, u32[]{:S(2)}) collective-permute-start(bf16[2,128,512]{2,1,0:T(8,128)(2,1)S(1)} %copy-done.44), channel_id=1, source_target_pairs={{0,9},{1,2},{2,11},{3,4},{4,13},{5,6},{6,15},{7,0},{8,17},{9,10},{... | collective-permute-start | bytes 786440 | tf_op jit(solution)/shard_map/ppermute | solution.py:307
  302.7 43.2 %collective-permute-start.28 = (bf16[2,128,512]{2,1,0:T(8,128)(2,1)S(1)}, bf16[2,128,512]{2,1,0:T(8,128)(2,1)S(1)}, u32[]{:S(2)}, u32[]{:S(2)}) collective-permute-start(bf16[2,128,512]{2,1,0:T(8,128)(2,1)S(1)} %copy-done.43), channel_id=1, source_target_pairs={{0,25},{1,6},{2,27},{3,0},{4,29},{5,2},{6,31},{7,4},{8,1},{9,14},{... | collective-permute-start | bytes 786440 | tf_op jit(solution)/shard_map/ppermute | solution.py:307
  (60 other events, 1550.7 us)

commit v2 on v1

--- a/solution.py
+++ b/solution.py
@@ -69,55 +69,60 @@
     return jnp.where(kind == 0, (z * SIDE + y_end) * SIDE + x, (z * SIDE + y) * SIDE + x_end)
 
 
-def notes_kernel(kind_ref, counts_ref, dests_ref, rels_ref, lists_ref, out_ref):
+def notes_kernel(blocks, counts_ref, dests_ref, rels_ref, lists_ref, out_ref):
     rows = CHIPS * 8
-    blocks = dests_ref.shape[0]
+    x, y, z, _ = coordinates()
     counts = counts_ref[...]
     before = (
         lax.broadcasted_iota(jnp.int32, (CHIPS, CHIPS), 0)
         < lax.broadcasted_iota(jnp.int32, (CHIPS, CHIPS), 1)
     ).astype(F32)
-    used = counts.astype(F32)
-    rank = jnp.dot(jnp.broadcast_to(used, (8, CHIPS)), before, preferred_element_type=F32)[:1]
-    where = jnp.where(counts > 0, rank, -1.0)
+    used = jnp.broadcast_to(counts.astype(F32), (8, CHIPS))
+    rank = jnp.dot(used, before, preferred_element_type=F32)[:1]
+    where = jnp.where(counts > 0, rank, -1.0).astype(jnp.int32)
     row = lax.broadcasted_iota(jnp.int32, (rows, 1), 0)
     slot, place = row // 8, row % 8
     line = place % SIDE
     owner = jnp.where(
-        kind_ref[0] == 0, slot // SIDE * SIDE + line, slot // 16 * 16 + line * SIDE + slot % SIDE
-    )
-    lane = lax.broadcasted_iota(jnp.int32, (rows, CHIPS), 1)
-    position = jnp.sum(jnp.where(lane == owner, where, 0.0), axis=1, keepdims=True)
-    hit = position == lax.broadcasted_iota(jnp.int32, (rows, blocks), 1).astype(F32)
-    hit = hit.astype(BF16)
-    dests = jnp.dot(hit, dests_ref[...].astype(BF16), preferred_element_type=F32)
-    rels = jnp.dot(hit, rels_ref[...].astype(BF16), preferred_element_type=F32)
-    codes = jnp.where(position < 0, -1.0, dests + jnp.where(position >= blocks // 2, float(DST), 0.0))
-    wanted = jnp.where(counts > 0, lists_ref[...], -1).astype(F32)
-    block = jnp.sum(jnp.where(lane == slot, wanted, 0.0), axis=1, keepdims=True)
-    other = jnp.where(lax.broadcasted_iota(jnp.int32, (rows, DST), 1) == 4, block, rels)
-    out_ref[...] = jnp.where(place < SIDE, codes, other).astype(jnp.int32)
-
-
-def make_notes(kind, counts, dests, rels, lists):
-    blocks = dests.shape[0]
-    halves = jnp.concatenate([rels // DST, rels % DST], axis=1)
-    halves = jnp.pad(halves, ((0, 0), (0, DST - halves.shape[1])))
+        (x + y + z) % 2 == 0,
+        slot // SIDE * SIDE + line,
+        slot // 16 * 16 + line * SIDE + slot % SIDE,
+    )
+
+    def lookup(values, index):
+        lane = lax.broadcasted_iota(jnp.int32, (rows, values.shape[1]), 1)
+        return jnp.sum(jnp.where(lane == index, values, 0), axis=1, keepdims=True)
+
+    position = lookup(where, owner)
+    hit = (position == lax.broadcasted_iota(jnp.int32, (rows, blocks), 1)).astype(BF16)
+    dests = jnp.concatenate([dests_ref[:, p * BROWS : (p + 1) * BROWS] for p in range(blocks)], axis=0)
+    dests = jnp.dot(hit, dests.astype(BF16), preferred_element_type=F32).astype(jnp.int32)
+    codes = jnp.where(position < 0, -1, dests + jnp.where(position >= blocks // 2, DST, 0))
+    block = lookup(jnp.where(counts > 0, lists_ref[...], -1), slot)
+    lane = lax.broadcasted_iota(jnp.int32, (rows, DST), 1)
+    other = block
+    for tile in range(BROWS // TILE):
+        rel = lookup(rels_ref[...], position * (BROWS // TILE) + tile)
+        other = jnp.where(lane == tile, rel, other)
+    out_ref[...] = jnp.where(place < SIDE, codes, other)
+
+
+def make_notes(counts, dests, rels, lists):
     vmem = pl.BlockSpec(memory_space=pltpu.VMEM)
     return pl.pallas_call(
-        notes_kernel,
+        functools.partial(notes_kernel, dests.shape[1] // BROWS),
         out_shape=jax.ShapeDtypeStruct((CHIPS * 8, DST), jnp.int32),
-        in_specs=[pl.BlockSpec(memory_space=pltpu.SMEM)] + [vmem] * 4,
+        in_specs=[vmem] * 4,
         out_specs=vmem,
         name="notes",
-    )(kind.reshape(1), counts.reshape(1, CHIPS), dests, halves, lists.reshape(1, CHIPS)).reshape(CHIPS, 8, DST)
+    )(counts, dests, rels, lists).reshape(CHIPS, 8, DST)
 
 
 SENDS = ((1, False), (3, False), (1, True), (3, True), (2, False), (2, True), (0, True))
 
 
 def pick_kernel(step_z, wanted_ref, table_ref, *rest):
-    outs, sems = rest[:-1], rest[-1]
+    outs, (held, sems) = rest[: len(SENDS)], rest[len(SENDS) :]
     x, y, z, core = coordinates()
     copies = []
     for send, (step, crossed) in enumerate(SENDS):
@@ -127,29 +132,34 @@
         for which in range(2):
             block = wanted_ref[group_of(x_to, y_to, (z + step_z) % SIDE, kind, which)]
             start = pl.multiple_of(jnp.maximum(block, 0) * BROWS, BROWS)
-            copies.append(
-                (
-                    block >= 0,
-                    pltpu.make_async_copy(
-                        table_ref.at[pl.ds(start, BROWS)], outs[send].at[which], sems.at[send, which]
-                    ),
-                )
-            )
-    for live, copy in copies:
-        pl.when(live)(copy.start)
-    for live, copy in copies:
-        pl.when(live)(copy.wait)
+            place = held.at[send, which]
+            load = pltpu.make_async_copy(table_ref.at[pl.ds(start, BROWS)], place, sems.at[0, send, which])
+            store = pltpu.make_async_copy(place, outs[send].at[which], sems.at[1, send, which])
+            pl.when(block >= 0)(load.start)
+            copies.append((block >= 0, load, store))
+
+    def hand_on(load, store):
+        load.wait()
+        store.start()
+
+    for live, load, store in copies:
+        pl.when(live)(functools.partial(hand_on, load, store))
+    for live, load, store in copies:
+        pl.when(live)(store.wait)
 
 
 def pick(step_z, wanted, table):
     width = table.shape[1]
-    anywhere = pl.BlockSpec(memory_space=pl.ANY)
+    hbm = pl.BlockSpec(memory_space=pltpu.HBM)
     return pl.pallas_call(
         functools.partial(pick_kernel, step_z),
         out_shape=[jax.ShapeDtypeStruct((2, BROWS, width), BF16)] * len(SENDS),
-        in_specs=[pl.BlockSpec(memory_space=pltpu.SMEM), anywhere],
-        out_specs=[anywhere] * len(SENDS),
-        scratch_shapes=[pltpu.SemaphoreType.DMA((len(SENDS), 2))],
+        in_specs=[pl.BlockSpec(memory_space=pltpu.SMEM), hbm],
+        out_specs=[hbm] * len(SENDS),
+        scratch_shapes=[
+            pltpu.VMEM((len(SENDS), 2, BROWS, width), BF16),
+            pltpu.SemaphoreType.DMA((2, len(SENDS), 2)),
+        ],
         cost_estimate=pl.CostEstimate(
             flops=0, bytes_accessed=4 * len(SENDS) * 2 * BROWS * width, transcendentals=0
         ),
@@ -234,12 +244,12 @@
 def project(step_z, codes, wanted, coef, notes, table, received, own_basis, other_basis):
     width = table.shape[1]
     wide = own_basis.shape[1]
-    anywhere = pl.BlockSpec(memory_space=pl.ANY)
+    hbm = pl.BlockSpec(memory_space=pltpu.HBM)
     smem = pl.BlockSpec(memory_space=pltpu.SMEM)
     return pl.pallas_call(
         functools.partial(project_kernel, step_z),
         out_shape=jax.ShapeDtypeStruct((4, DST, wide), BF16),
-        in_specs=[smem] * 3 + [anywhere] * (4 + len(SENDS)),
+        in_specs=[smem] * 3 + [hbm] * (4 + len(SENDS)),
         out_specs=pl.BlockSpec(memory_space=pltpu.VMEM),
         scratch_shapes=[
             pltpu.VMEM((2, SIDE, 2, BROWS, width), BF16),
@@ -289,13 +299,7 @@
     blocks = tile_rel.shape[1] * TILE // BROWS
     other_basis = lax.ppermute(bases[0], "basis", [(0, 1), (1, 0)])
 
-    sent = make_notes(
-        (x + y + z) % 2,
-        block_counts[0],
-        dest_ids[0].reshape(blocks, BROWS),
-        tile_rel[0].reshape(blocks, BROWS // TILE),
-        block_lists[0, :, 0],
-    )
+    sent = make_notes(block_counts, dest_ids, tile_rel, block_lists.reshape(1, CHIPS))
     notes = lax.all_to_all(sent, "shard", split_axis=0, concat_axis=0, tiled=True)
     wanted = notes[:, SIDE, 4]
     codes = notes[:, :SIDE, 0].reshape(-1)
@@ -308,8 +312,8 @@
 
     groups = jnp.stack([group_of(x, y, (z + s) % SIDE, core, w) for s in HOP2 for w in range(2)])
     lines = (along - jnp.arange(SIDE, dtype=jnp.int32)) % SIDE
-    told = notes[groups[:, None], SIDE + lines[None, :], :4]
-    coef = coeffs[told[..., :2] * DST + told[..., 2:]]
+    told = notes[groups[:, None], SIDE + lines[None, :], : BROWS // TILE]
+    coef = coeffs[told]
     coef = jnp.where(core == 0, coef, coef[..., ::-1]).reshape(len(HOP2), -1)
 
     parts = []

time: 389 us -> 180 us (0.46)
  starting transfers between devices: 193 us -> 63.9 us
  Pallas kernels: 122 us -> 44 us
    ppermute x28, starting transfers between devices: 129 us -> 36.2 us  [body(): lax.ppermute(buf, AXES, hop1_pairs(*send))]
    pallas_call x4, Pallas kernels: 87.7 us -> 11.5 us  [pick(): pl.pallas_call(functools.partial(pick_kernel, step_z), out_shape=[jax.Sha...]
    ppermute x3, starting transfers between devices: 42.2 us -> 7.44 us  [body(): lax.ppermute(part, AXES, hop2_pairs(step_z))]
    unnamed x96 -> x103, local copies, waits for them, and re-layouts: 21.6 us -> 25.3 us
  transfers between devices with their start and end apart: 37 -> 37, of which waited for: 8 -> 8; matrix products, arithmetic and copies ran while one was open for 4% -> 9% of each run, Pallas kernels for 30% -> 23%
where the time goes in v2:
time: 180 us; the launch traced here: 179 us
  starting transfers between devices  63.9 us (36%)
  Pallas kernels  44 us (24%)
  local copies, waits for them, and re-layouts  35.7 us (20%)
  waiting for transfers between devices  33.3 us (18%)
    ppermute x28, starting transfers between devices, body(): lax.ppermute(buf, AXES, hop1_pairs(*send))  36.2 us
    pallas_call x4, Pallas kernels, project(): pl.pallas_call(functools.partial(project_kernel, step_z), out_shape=jax.S...  26.9 us
    unnamed x103, local copies, waits for them, and re-layouts  25.3 us
    ppermute x28, waiting for transfers between devices, body(): lax.ppermute(buf, AXES, hop1_pairs(*send))  13.4 us
    pallas_call x4, Pallas kernels, pick(): pl.pallas_call(functools.partial(pick_kernel, step_z), out_shape=[jax.Sha...  11.5 us
    all_to_all x1, starting transfers between devices, body(): lax.all_to_all(sent, 'shard', split_axis=0, concat_axis=0, tiled=True)  11.3 us
    ppermute x4, waiting for transfers between devices, body(): lax.ppermute(buf, AXES, hop3_pairs(send))  10.2 us
    all_to_all x1, waiting for transfers between devices, body(): lax.all_to_all(sent, 'shard', split_axis=0, concat_axis=0, tiled=True)  9.72 us
  transfers between devices with their start and end apart: 37, of which 8 were waited for; matrix products, arithmetic and copies ran while one was open for 9% of the time, Pallas kernels for 23%

profile of v2, /device:TPU:1, one launch (start us, length us, event | category | flops | bytes accessed | tf_op | source)
XLA Modules:
  0.0 178.9 jit_solution(17453973837232643818)
XLA Ops:
  3.6 11.3 %all-to-all-start = ((s32[64,8,128]{2,1,0:T(8,128)}), s32[64,8,128]{2,1,0:T(8,128)S(1)}, u32[]{:S(2)}, u32[]{:S(2)}) async-start(s32[64,8,128]{2,1,0:T(8,128)} %bitcast.29), calls=%async_computation | async-start | bytes 524288 | tf_op jit(solution)/shard_map/all_to_all | solution.py:303
  15.3 9.7 %all-to-all-done.notes_ref = s32[64,8,128]{2,1,0:T(8,128)S(1)} async-done(((s32[64,8,128]{2,1,0:T(8,128)}), s32[64,8,128]{2,1,0:T(8,128)S(1)}, u32[]{:S(2)}, u32[]{:S(2)}) %all-to-all-start) | async-done | bytes 262176 | tf_op jit(solution)/shard_map/all_to_all | solution.py:303
  26.9 2.8 %pick.4 = (bf16[2,128,512]{2,1,0:T(8,128)(2,1)}, bf16[2,128,512]{2,1,0:T(8,128)(2,1)}, bf16[2,128,512]{2,1,0:T(8,128)(2,1)}, bf16[2,128,512]{2,1,0:T(8,128)(2,1)...) custom-call(s32[64]{0:T(128)} %slice_reduce_fusion.1.wanted_ref, ...), custom_call_target="tpu_custom_call" | custom-call | bytes 3670016 | tf_op jit(solution)/shard_map/pick/pallas_call | solution.py:154
  34.4 4.7 %copy.26 = f32[14824,2]{1,0:T(8,128)} copy(f32[14824,2]{0,1:T(2,128)S(1)} %copy-done.38) | data formatting | bytes 237184 | tf_op args[2]
  40.2 2.9 %pick.5 = (bf16[2,128,512]{2,1,0:T(8,128)(2,1)}, bf16[2,128,512]{2,1,0:T(8,128)(2,1)}, bf16[2,128,512]{2,1,0:T(8,128)(2,1)}, bf16[2,128,512]{2,1,0:T(8,128)(2,1)...) custom-call(s32[64]{0:T(128)} %slice_reduce_fusion.1.wanted_ref, ...), custom_call_target="tpu_custom_call" | custom-call | bytes 3670016 | tf_op jit(solution)/shard_map/pick/pallas_call | solution.py:154
  53.2 3.1 %collective-permute-start.11 = (bf16[2,128,512]{2,1,0:T(8,128)(2,1)}, bf16[2,128,512]{2,1,0:T(8,128)(2,1)S(1)}, u32[]{:S(2)}, u32[]{:S(2)}) collective-permute-start(bf16[2,128,512]{2,1,0:T(8,128)(2,1)} %get-tuple-element.46), channel_id=1, source_target_pairs={{0,9},{1,2},{2,11},{3,4},{4,13},{5,6},{6,15},{7,0},{8,17},{9,10},{... | collective-permute-start | bytes 786440 | tf_op jit(solution)/shard_map/ppermute | solution.py:311
  60.4 3.7 %gather_fusion = f32[64,2]{1,0:T(8,128)S(1)} fusion(f32[14824,2]{1,0:T(8,128)} %copy.26, s32[1024]{0:T(1024)S(1)} %pad_clamp_fusion), kind=kCustom, calls=%fused_computation | custom fusion | bytes 1280 | tf_op jit(solution)/shard_map/gather | solution.py:316
  66.9 2.9 %pick.6 = (bf16[2,128,512]{2,1,0:T(8,128)(2,1)}, bf16[2,128,512]{2,1,0:T(8,128)(2,1)}, bf16[2,128,512]{2,1,0:T(8,128)(2,1)}, bf16[2,128,512]{2,1,0:T(8,128)(2,1)...) custom-call(s32[64]{0:T(128)} %slice_reduce_fusion.1.wanted_ref, ...), custom_call_target="tpu_custom_call" | custom-call | bytes 3670016 | tf_op jit(solution)/shard_map/pick/pallas_call | solution.py:154
  74.7 2.9 %pick.7 = (bf16[2,128,512]{2,1,0:T(8,128)(2,1)}, bf16[2,128,512]{2,1,0:T(8,128)(2,1)}, bf16[2,128,512]{2,1,0:T(8,128)(2,1)}, bf16[2,128,512]{2,1,0:T(8,128)(2,1)...) custom-call(s32[64]{0:T(128)} %slice_reduce_fusion.1.wanted_ref, ...), custom_call_target="tpu_custom_call" | custom-call | bytes 3670016 | tf_op jit(solution)/shard_map/pick/pallas_call | solution.py:154
  90.4 5.6 %project.4 = bf16[4,128,1024]{2,1,0:T(8,128)(2,1)S(1)} custom-call(s32[256]{0:T(256)S(1)} %reshape_squeeze.3.codes_ref, s32[64]{0:T(128)S(1)} %copy-done.37, f32[32]{0:T(128)S(1)} %squeeze.24.coef_ref, s32[64,8,128]{2,1,0:T(8,128)S(1)} %all-to-all-done.notes_ref, bf16[6144,512]{1,0:T(8,128)(2,1)} %table_ref.15, bf16[2,128,512]{2,1,0:T(8,128)(2,1)S(1)} %copy-done.12, ...), custom_call_target="tpu_custom_call" | custom-call | flops 2147483648 | bytes 8388608 | tf_op jit(solution)/shard_map/project/pallas_call | solution.py:249
  96.5 6.1 %project.5 = bf16[4,128,1024]{2,1,0:T(8,128)(2,1)} custom-call(s32[256]{0:T(256)S(1)} %reshape_squeeze.3.codes_ref, s32[64]{0:T(128)S(1)} %copy-done.37, f32[32]{0:T(128)S(1)} %squeeze.26.coef_ref, s32[64,8,128]{2,1,0:T(8,128)S(1)} %all-to-all-done.notes_ref, bf16[6144,512]{1,0:T(8,128)(2,1)} %table_ref.15, bf16[2,128,512]{2,1,0:T(8,128)(2,1)S(1)} %copy-done.24, ...), custom_call_target="tpu_custom_call" | custom-call | flops 2147483648 | bytes 8388608 | tf_op jit(solution)/shard_map/project/pallas_call | solution.py:249
  102.7 4.1 %collective-permute-start.8 = (bf16[4,128,1024]{2,1,0:T(8,128)(2,1)S(1)}, bf16[4,128,1024]{2,1,0:T(8,128)(2,1)}, u32[]{:S(2)}, u32[]{:S(2)}) collective-permute-start(bf16[4,128,1024]{2,1,0:T(8,128)(2,1)S(1)} %project.4), channel_id=1, source_target_pairs={{0,64},{1,65},{2,66},{3,67},{4,68},{5,69},{6,70},{7,71},{8,72},{9,... | collective-permute-start | bytes 3145736 | tf_op jit(solution)/shard_map/ppermute | solution.py:324
  106.8 7.4 %project.6 = bf16[4,128,1024]{2,1,0:T(8,128)(2,1)} custom-call(s32[256]{0:T(256)S(1)} %reshape_squeeze.3.codes_ref, s32[64]{0:T(128)S(1)} %copy-done.37, f32[32]{0:T(128)S(1)} %squeeze.27.coef_ref, s32[64,8,128]{2,1,0:T(8,128)S(1)} %all-to-all-done.notes_ref, bf16[6144,512]{1,0:T(8,128)(2,1)} %table_ref.15, bf16[2,128,512]{2,1,0:T(8,128)(2,1)S(1)} %copy-done.36, ...), custom_call_target="tpu_custom_call" | custom-call | flops 2147483648 | bytes 8388608 | tf_op jit(solution)/shard_map/project/pallas_call | solution.py:249
  114.2 3.4 %collective-permute-start.24 = (bf16[4,128,1024]{2,1,0:T(8,128)(2,1)}, bf16[4,128,1024]{2,1,0:T(8,128)(2,1)}, u32[]{:S(2)}, u32[]{:S(2)}) collective-permute-start(bf16[4,128,1024]{2,1,0:T(8,128)(2,1)} %project.6), channel_id=1, source_target_pairs={{0,96},{1,97},{2,98},{3,99},{4,100},{5,101},{6,102},{7,103},{8,104... | collective-permute-start | bytes 3145736 | tf_op jit(solution)/shard_map/ppermute | solution.py:324
  120.1 3.1 %collective-permute-done.26.rest_1_ = bf16[2,128,512]{2,1,0:T(8,128)(2,1)S(1)} collective-permute-done((bf16[2,128,512]{2,1,0:T(8,128)(2,1)S(1)}, bf16[2,128,512]{2,1,0:T(8,128)(2,1)S(1)}, u32[]{:S(2)}, u32[]{:S(2)}) %collective-permute-start.26) | collective-permute-done | bytes 262176 | tf_op jit(solution)/shard_map/ppermute | solution.py:311
  123.9 5.8 %collective-permute-start.28 = (bf16[2,128,512]{2,1,0:T(8,128)(2,1)S(1)}, bf16[2,128,512]{2,1,0:T(8,128)(2,1)S(1)}, u32[]{:S(2)}, u32[]{:S(2)}) collective-permute-start(bf16[2,128,512]{2,1,0:T(8,128)(2,1)S(1)} %copy-done.43), channel_id=1, source_target_pairs={{0,25},{1,6},{2,27},{3,0},{4,29},{5,2},{6,31},{7,4},{8,1},{9,14},{... | collective-permute-start | bytes 786440 | tf_op jit(solution)/shard_map/ppermute | solution.py:311
  130.4 5.4 %collective-permute-done.28.rest_3_ = bf16[2,128,512]{2,1,0:T(8,128)(2,1)S(1)} collective-permute-done((bf16[2,128,512]{2,1,0:T(8,128)(2,1)S(1)}, bf16[2,128,512]{2,1,0:T(8,128)(2,1)S(1)}, u32[]{:S(2)}, u32[]{:S(2)}) %collective-permute-start.28) | collective-permute-done | bytes 262176 | tf_op jit(solution)/shard_map/ppermute | solution.py:311
  139.5 4.6 %collective-permute-done.30.rest_5_ = bf16[2,128,512]{2,1,0:T(8,128)(2,1)} collective-permute-done((bf16[2,128,512]{2,1,0:T(8,128)(2,1)}, bf16[2,128,512]{2,1,0:T(8,128)(2,1)}, u32[]{:S(2)}, u32[]{:S(2)}) %collective-permute-start.30) | collective-permute-done | bytes 262176 | tf_op jit(solution)/shard_map/ppermute | solution.py:311
  148.9 7.8 %project.7.refs_3_ = bf16[4,128,1024]{2,1,0:T(8,128)(2,1)S(1)} custom-call(s32[256]{0:T(256)S(1)} %reshape_squeeze.3.codes_ref, s32[64]{0:T(128)S(1)} %copy-done.37, f32[32]{0:T(128)S(1)} %squeeze.28.coef_ref, s32[64,8,128]{2,1,0:T(8,128)S(1)} %all-to-all-done.notes_ref, bf16[6144,512]{1,0:T(8,128)(2,1)} %table_ref.15, bf16[2,128,512]{2,1,0:T(8,128)(2,1)S(1)} %copy-done.2, ...), custom_call_target="tpu_custom_call" | custom-call | flops 2147483648 | bytes 8388608 | tf_op jit(solution)/shard_map/project/pallas_call | solution.py:249
  156.8 3.4 %merge.1 = (bf16[128,1024]{1,0:T(8,128)(2,1)S(1)}, bf16[128,1024]{1,0:T(8,128)(2,1)S(1)}, bf16[128,1024]{1,0:T(8,128)(2,1)S(1)}, bf16[128,1024]{1,0:T(8,128)(2,1)S(1)}) custom-call(s32[4]{0:T(128)S(1)} %pad_add_fusion.1.order_ref, bf16[4,128,1024]{2,1,0:T(8,128)(2,1)} %collective-permute-done.8.refs_0_, ...), custom_call_target="tpu_custom_call" | custom-call | tf_op jit(solution)/shard_map/merge/pallas_call | solution.py:283
  160.1 3.7 %collective-permute-start.35 = (bf16[128,1024]{1,0:T(8,128)(2,1)S(1)}, bf16[128,1024]{1,0:T(8,128)(2,1)S(1)}, u32[]{:S(2)}, u32[]{:S(2)}) collective-permute-start(bf16[128,1024]{1,0:T(8,128)(2,1)S(1)} %get-tuple-element.68), channel_id=1, source_target_pairs={{0,1},{1,6},{2,26},{3,3},{4,5},{5,2},{6,30},{7,7},{8,0},{9,9},{10,... | collective-permute-start | bytes 786440 | tf_op jit(solution)/shard_map/ppermute | solution.py:335
  164.0 3.7 %collective-permute-start.32 = (bf16[128,1024]{1,0:T(8,128)(2,1)S(1)}, bf16[128,1024]{1,0:T(8,128)(2,1)S(1)}, u32[]{:S(2)}, u32[]{:S(2)}) collective-permute-start(bf16[128,1024]{1,0:T(8,128)(2,1)S(1)} %get-tuple-element.65), channel_id=1, source_target_pairs={{0,0},{1,3},{2,11},{3,2},{4,4},{5,7},{6,15},{7,6},{8,17},{9,8},{10... | collective-permute-start | bytes 786440 | tf_op jit(solution)/shard_map/ppermute | solution.py:335
  167.9 4.8 %collective-permute-done.35 = bf16[128,1024]{1,0:T(8,128)(2,1)S(1)} collective-permute-done((bf16[128,1024]{1,0:T(8,128)(2,1)S(1)}, bf16[128,1024]{1,0:T(8,128)(2,1)S(1)}, u32[]{:S(2)}, u32[]{:S(2)}) %collective-permute-start.35) | collective-permute-done | bytes 262176 | tf_op jit(solution)/shard_map/ppermute | solution.py:335
  172.7 2.8 %collective-permute-done.34 = bf16[128,1024]{1,0:T(8,128)(2,1)S(1)} collective-permute-done((bf16[128,1024]{1,0:T(8,128)(2,1)S(1)}, bf16[128,1024]{1,0:T(8,128)(2,1)S(1)}, u32[]{:S(2)}, u32[]{:S(2)}) %collective-permute-start.34) | collective-permute-done | bytes 262176 | tf_op jit(solution)/shard_map/ppermute | solution.py:335
  (203 shorter events, 62.4 us)
Async XLA Ops:
  0.0 83.5 %collective-permute-start.7 = (bf16[1024,1024]{1,0:T(8,128)(2,1)}, bf16[1024,1024]{1,0:T(8,128)(2,1)}, u32[]{:S(2)}, u32[]{:S(2)}) collective-permute-start(bf16[1024,1024]{1,0:T(8,128)(2,1)} %bitcast.24), channel_id=1, source_target_pairs={{0,1},{1,0},{2,3},{3,2},{4,5},{5,4},{6,7},{7,6},{8,9},{9,8},{10,11... | collective-permute-start | bytes 6291464 | tf_op jit(solution)/shard_map/ppermute | solution.py:300
  3.6 21.4 %all-to-all-start = ((s32[64,8,128]{2,1,0:T(8,128)}), s32[64,8,128]{2,1,0:T(8,128)S(1)}, u32[]{:S(2)}, u32[]{:S(2)}) async-start(s32[64,8,128]{2,1,0:T(8,128)} %bitcast.29), calls=%async_computation | async-start | bytes 524288 | tf_op jit(solution)/shard_map/all_to_all | solution.py:303
  30.2 14.5 %collective-permute-start.1 = (bf16[2,128,512]{2,1,0:T(8,128)(2,1)}, bf16[2,128,512]{2,1,0:T(8,128)(2,1)S(1)}, u32[]{:S(2)}, u32[]{:S(2)}) collective-permute-start(bf16[2,128,512]{2,1,0:T(8,128)(2,1)} %get-tuple-element.38), channel_id=1, source_target_pairs={{0,6},{1,25},{2,0},{3,27},{4,2},{5,29},{6,4},{7,31},{8,14},{9,1},{... | collective-permute-start | bytes 786440 | tf_op jit(solution)/shard_map/ppermute | solution.py:311
  32.6 14.8 %collective-permute-start.2 = (bf16[2,128,512]{2,1,0:T(8,128)(2,1)}, bf16[2,128,512]{2,1,0:T(8,128)(2,1)S(1)}, u32[]{:S(2)}, u32[]{:S(2)}) collective-permute-start(bf16[2,128,512]{2,1,0:T(8,128)(2,1)} %get-tuple-element.39), channel_id=1, source_target_pairs={{0,9},{1,2},{2,11},{3,4},{4,13},{5,6},{6,15},{7,0},{8,17},{9,10},{... | collective-permute-start | bytes 786440 | tf_op jit(solution)/shard_map/ppermute | solution.py:311
  33.6 14.5 %collective-permute-start.3 = (bf16[2,128,512]{2,1,0:T(8,128)(2,1)}, bf16[2,128,512]{2,1,0:T(8,128)(2,1)S(1)}, u32[]{:S(2)}, u32[]{:S(2)}) collective-permute-start(bf16[2,128,512]{2,1,0:T(8,128)(2,1)} %get-tuple-element.40), channel_id=1, source_target_pairs={{0,25},{1,6},{2,27},{3,0},{4,29},{5,2},{6,31},{7,4},{8,1},{9,14},{... | collective-permute-start | bytes 786440 | tf_op jit(solution)/shard_map/ppermute | solution.py:311
  50.7 13.8 %collective-permute-start.10 = (bf16[2,128,512]{2,1,0:T(8,128)(2,1)}, bf16[2,128,512]{2,1,0:T(8,128)(2,1)S(1)}, u32[]{:S(2)}, u32[]{:S(2)}) collective-permute-start(bf16[2,128,512]{2,1,0:T(8,128)(2,1)} %get-tuple-element.45), channel_id=1, source_target_pairs={{0,6},{1,25},{2,0},{3,27},{4,2},{5,29},{6,4},{7,31},{8,14},{9,1},{... | collective-permute-start | bytes 786440 | tf_op jit(solution)/shard_map/ppermute | solution.py:311
  53.2 16.6 %collective-permute-start.11 = (bf16[2,128,512]{2,1,0:T(8,128)(2,1)}, bf16[2,128,512]{2,1,0:T(8,128)(2,1)S(1)}, u32[]{:S(2)}, u32[]{:S(2)}) collective-permute-start(bf16[2,128,512]{2,1,0:T(8,128)(2,1)} %get-tuple-element.46), channel_id=1, source_target_pairs={{0,9},{1,2},{2,11},{3,4},{4,13},{5,6},{6,15},{7,0},{8,17},{9,10},{... | collective-permute-start | bytes 786440 | tf_op jit(solution)/shard_map/ppermute | solution.py:311
  57.1 12.8 %collective-permute-start.12 = (bf16[2,128,512]{2,1,0:T(8,128)(2,1)S(1)}, bf16[2,128,512]{2,1,0:T(8,128)(2,1)S(1)}, u32[]{:S(2)}, u32[]{:S(2)}) collective-permute-start(bf16[2,128,512]{2,1,0:T(8,128)(2,1)S(1)} %copy-done.48), channel_id=1, source_target_pairs={{0,25},{1,6},{2,27},{3,0},{4,29},{5,2},{6,31},{7,4},{8,1},{9,14},{... | collective-permute-start | bytes 786440 | tf_op jit(solution)/shard_map/ppermute | solution.py:311
  58.1 12.8 %collective-permute-start.13 = (bf16[2,128,512]{2,1,0:T(8,128)(2,1)}, bf16[2,128,512]{2,1,0:T(8,128)(2,1)S(1)}, u32[]{:S(2)}, u32[]{:S(2)}) collective-permute-start(bf16[2,128,512]{2,1,0:T(8,128)(2,1)} %get-tuple-element.48), channel_id=1, source_target_pairs={{0,4},{1,17},{2,6},{3,19},{4,0},{5,21},{6,2},{7,23},{8,12},{9,25},... | collective-permute-start | bytes 786440 | tf_op jit(solution)/shard_map/ppermute | solution.py:311
  72.8 23.2 %collective-permute-start.19 = (bf16[2,128,512]{2,1,0:T(8,128)(2,1)}, bf16[2,128,512]{2,1,0:T(8,128)(2,1)}, u32[]{:S(2)}, u32[]{:S(2)}) collective-permute-start(bf16[2,128,512]{2,1,0:T(8,128)(2,1)} %get-tuple-element.53), channel_id=1, source_target_pairs={{0,9},{1,2},{2,11},{3,4},{4,13},{5,6},{6,15},{7,0},{8,17},{9,10},{... | collective-permute-start | bytes 786440 | tf_op jit(solution)/shard_map/ppermute | solution.py:311
  78.4 24.3 %collective-permute-start.20 = (bf16[2,128,512]{2,1,0:T(8,128)(2,1)}, bf16[2,128,512]{2,1,0:T(8,128)(2,1)S(1)}, u32[]{:S(2)}, u32[]{:S(2)}) collective-permute-start(bf16[2,128,512]{2,1,0:T(8,128)(2,1)} %get-tuple-element.54), channel_id=1, source_target_pairs={{0,25},{1,6},{2,27},{3,0},{4,29},{5,2},{6,31},{7,4},{8,1},{9,14},{... | collective-permute-start | bytes 786440 | tf_op jit(solution)/shard_map/ppermute | solution.py:311
  79.7 27.0 %collective-permute-start.21 = (bf16[2,128,512]{2,1,0:T(8,128)(2,1)}, bf16[2,128,512]{2,1,0:T(8,128)(2,1)S(1)}, u32[]{:S(2)}, u32[]{:S(2)}) collective-permute-start(bf16[2,128,512]{2,1,0:T(8,128)(2,1)} %get-tuple-element.55), channel_id=1, source_target_pairs={{0,4},{1,17},{2,6},{3,19},{4,0},{5,21},{6,2},{7,23},{8,12},{9,25},... | collective-permute-start | bytes 786440 | tf_op jit(solution)/shard_map/ppermute | solution.py:311
  81.6 25.1 %collective-permute-start.22 = (bf16[2,128,512]{2,1,0:T(8,128)(2,1)}, bf16[2,128,512]{2,1,0:T(8,128)(2,1)S(1)}, u32[]{:S(2)}, u32[]{:S(2)}) collective-permute-start(bf16[2,128,512]{2,1,0:T(8,128)(2,1)} %get-tuple-element.56), channel_id=1, source_target_pairs={{0,17},{1,4},{2,19},{3,6},{4,21},{5,0},{6,23},{7,2},{8,25},{9,12},... | collective-permute-start | bytes 786440 | tf_op jit(solution)/shard_map/ppermute | solution.py:311
  83.6 23.2 %collective-permute-start.23 = (bf16[2,128,512]{2,1,0:T(8,128)(2,1)}, bf16[2,128,512]{2,1,0:T(8,128)(2,1)S(1)}, u32[]{:S(2)}, u32[]{:S(2)}) collective-permute-start(bf16[2,128,512]{2,1,0:T(8,128)(2,1)} %get-tuple-element.57), channel_id=1, source_target_pairs={{0,1},{1,0},{2,3},{3,2},{4,5},{5,4},{6,7},{7,6},{8,9},{9,8},{10,11... | collective-permute-start | bytes 786440 | tf_op jit(solution)/shard_map/ppermute | solution.py:311
  96.0 21.6 %collective-permute-start.25 = (bf16[2,128,512]{2,1,0:T(8,128)(2,1)S(1)}, bf16[2,128,512]{2,1,0:T(8,128)(2,1)S(1)}, u32[]{:S(2)}, u32[]{:S(2)}) collective-permute-start(bf16[2,128,512]{2,1,0:T(8,128)(2,1)S(1)} %copy-done.46), channel_id=1, source_target_pairs={{0,2},{1,9},{2,4},{3,11},{4,6},{5,13},{6,0},{7,15},{8,10},{9,17},{... | collective-permute-start | bytes 786440 | tf_op jit(solution)/shard_map/ppermute | solution.py:311
  102.7 54.0 %collective-permute-start.8 = (bf16[4,128,1024]{2,1,0:T(8,128)(2,1)S(1)}, bf16[4,128,1024]{2,1,0:T(8,128)(2,1)}, u32[]{:S(2)}, u32[]{:S(2)}) collective-permute-start(bf16[4,128,1024]{2,1,0:T(8,128)(2,1)S(1)} %project.4), channel_id=1, source_target_pairs={{0,64},{1,65},{2,66},{3,67},{4,68},{5,69},{6,70},{7,71},{8,72},{9,... | collective-permute-start | bytes 3145736 | tf_op jit(solution)/shard_map/ppermute | solution.py:324
  106.8 50.0 %collective-permute-start.16 = (bf16[4,128,1024]{2,1,0:T(8,128)(2,1)}, bf16[4,128,1024]{2,1,0:T(8,128)(2,1)}, u32[]{:S(2)}, u32[]{:S(2)}) collective-permute-start(bf16[4,128,1024]{2,1,0:T(8,128)(2,1)} %project.5), channel_id=1, source_target_pairs={{0,32},{1,33},{2,34},{3,35},{4,36},{5,37},{6,38},{7,39},{8,40},{9,... | collective-permute-start | bytes 3145736 | tf_op jit(solution)/shard_map/ppermute | solution.py:324
  114.2 42.5 %collective-permute-start.24 = (bf16[4,128,1024]{2,1,0:T(8,128)(2,1)}, bf16[4,128,1024]{2,1,0:T(8,128)(2,1)}, u32[]{:S(2)}, u32[]{:S(2)}) collective-permute-start(bf16[4,128,1024]{2,1,0:T(8,128)(2,1)} %project.6), channel_id=1, source_target_pairs={{0,96},{1,97},{2,98},{3,99},{4,100},{5,101},{6,102},{7,103},{8,104... | collective-permute-start | bytes 3145736 | tf_op jit(solution)/shard_map/ppermute | solution.py:324
  118.3 11.4 %collective-permute-start.27 = (bf16[2,128,512]{2,1,0:T(8,128)(2,1)S(1)}, bf16[2,128,512]{2,1,0:T(8,128)(2,1)S(1)}, u32[]{:S(2)}, u32[]{:S(2)}) collective-permute-start(bf16[2,128,512]{2,1,0:T(8,128)(2,1)S(1)} %copy-done.44), channel_id=1, source_target_pairs={{0,9},{1,2},{2,11},{3,4},{4,13},{5,6},{6,15},{7,0},{8,17},{9,10},{... | collective-permute-start | bytes 786440 | tf_op jit(solution)/shard_map/ppermute | solution.py:311
  123.9 11.9 %collective-permute-start.28 = (bf16[2,128,512]{2,1,0:T(8,128)(2,1)S(1)}, bf16[2,128,512]{2,1,0:T(8,128)(2,1)S(1)}, u32[]{:S(2)}, u32[]{:S(2)}) collective-permute-start(bf16[2,128,512]{2,1,0:T(8,128)(2,1)S(1)} %copy-done.43), channel_id=1, source_target_pairs={{0,25},{1,6},{2,27},{3,0},{4,29},{5,2},{6,31},{7,4},{8,1},{9,14},{... | collective-permute-start | bytes 786440 | tf_op jit(solution)/shard_map/ppermute | solution.py:311
  160.1 12.6 %collective-permute-start.35 = (bf16[128,1024]{1,0:T(8,128)(2,1)S(1)}, bf16[128,1024]{1,0:T(8,128)(2,1)S(1)}, u32[]{:S(2)}, u32[]{:S(2)}) collective-permute-start(bf16[128,1024]{1,0:T(8,128)(2,1)S(1)} %get-tuple-element.68), channel_id=1, source_target_pairs={{0,1},{1,6},{2,26},{3,3},{4,5},{5,2},{6,30},{7,7},{8,0},{9,9},{10,... | collective-permute-start | bytes 786440 | tf_op jit(solution)/shard_map/ppermute | solution.py:335
  163.8 11.7 %collective-permute-start.34 = (bf16[128,1024]{1,0:T(8,128)(2,1)S(1)}, bf16[128,1024]{1,0:T(8,128)(2,1)S(1)}, u32[]{:S(2)}, u32[]{:S(2)}) collective-permute-start(bf16[128,1024]{1,0:T(8,128)(2,1)S(1)} %get-tuple-element.67), channel_id=1, source_target_pairs={{0,16},{1,7},{2,27},{3,6},{4,20},{5,3},{6,31},{7,2},{8,1},{9,12},{... | collective-permute-start | bytes 786440 | tf_op jit(solution)/shard_map/ppermute | solution.py:335
  163.9 11.6 %collective-permute-start.33 = (bf16[128,1024]{1,0:T(8,128)(2,1)S(1)}, bf16[128,1024]{1,0:T(8,128)(2,1)S(1)}, u32[]{:S(2)}, u32[]{:S(2)}) collective-permute-start(bf16[128,1024]{1,0:T(8,128)(2,1)S(1)} %get-tuple-element.66), channel_id=1, source_target_pairs={{0,17},{1,2},{2,10},{3,7},{4,21},{5,6},{6,14},{7,3},{8,16},{9,13},... | collective-permute-start | bytes 786440 | tf_op jit(solution)/shard_map/ppermute | solution.py:335
  164.0 14.0 %collective-permute-start.32 = (bf16[128,1024]{1,0:T(8,128)(2,1)S(1)}, bf16[128,1024]{1,0:T(8,128)(2,1)S(1)}, u32[]{:S(2)}, u32[]{:S(2)}) collective-permute-start(bf16[128,1024]{1,0:T(8,128)(2,1)S(1)} %get-tuple-element.65), channel_id=1, source_target_pairs={{0,0},{1,3},{2,11},{3,2},{4,4},{5,7},{6,15},{7,6},{8,17},{9,8},{10... | collective-permute-start | bytes 786440 | tf_op jit(solution)/shard_map/ppermute | solution.py:335
  (64 other events, 531.0 us)

commit v3 on v2

--- a/solution.py
+++ b/solution.py
@@ -13,10 +13,11 @@
 SIDE = 4
 CHIPS = SIDE**3
 AXES = ("shard", "basis")
+CORE_SWAP = [(0, 1), (1, 0)]
 HOP2 = (2, 1, 3, 0)
 BF16 = jnp.bfloat16
 F32 = jnp.float32
-VMEM_LIMIT = 48 * 1024 * 1024
+VMEM_LIMIT = 28 * 1024 * 1024
 
 
 def device_id(x, y, z, core):
@@ -34,12 +35,8 @@
     return found
 
 
-def hop1_pairs(step, crossed):
-    def target(x, y, z, core):
-        kind = 1 - core if crossed else core
-        return (x + step, y, z, 0) if kind == 0 else (x, y + step, z, 1)
-
-    return pairs(target)
+def hop1_pairs(step):
+    return pairs(lambda x, y, z, core: (x + step, y, z, 0) if core == 0 else (x, y + step, z, 1))
 
 
 def hop2_pairs(step):
@@ -100,10 +97,10 @@
     codes = jnp.where(position < 0, -1, dests + jnp.where(position >= blocks // 2, DST, 0))
     block = lookup(jnp.where(counts > 0, lists_ref[...], -1), slot)
     lane = lax.broadcasted_iota(jnp.int32, (rows, DST), 1)
-    other = block
+    other = jnp.where(lane == 0, codes, block)
     for tile in range(BROWS // TILE):
         rel = lookup(rels_ref[...], position * (BROWS // TILE) + tile)
-        other = jnp.where(lane == tile, rel, other)
+        other = jnp.where(lane == 1 + tile, rel, other)
     out_ref[...] = jnp.where(place < SIDE, codes, other)
 
 
@@ -118,109 +115,180 @@
     )(counts, dests, rels, lists).reshape(CHIPS, 8, DST)
 
 
-SENDS = ((1, False), (3, False), (1, True), (3, True), (2, False), (2, True), (0, True))
-
-
-def pick_kernel(step_z, wanted_ref, table_ref, *rest):
-    outs, (held, sems) = rest[: len(SENDS)], rest[len(SENDS) :]
-    x, y, z, core = coordinates()
-    copies = []
-    for send, (step, crossed) in enumerate(SENDS):
-        kind = 1 - core if crossed else core
-        x_to = jnp.where(kind == 0, (x + step) % SIDE, x)
-        y_to = jnp.where(kind == 0, y, (y + step) % SIDE)
+WORDS = 4
+HOP1 = (1, 3, 2)
+
+
+def word(words_ref, group, line, which):
+    return words_ref[(group * SIDE + line) * WORDS + which]
+
+
+def reached(step, step_z, kind, which):
+    x, y, z, _ = coordinates()
+    x_to = jnp.where(kind == 0, (x + step) % SIDE, x)
+    y_to = jnp.where(kind == 0, y, (y + step) % SIDE)
+    return group_of(x_to, y_to, (z + step_z) % SIDE, kind, which)
+
+
+def local_block(words_ref, table_ref, group):
+    block = word(words_ref, group, 0, WORDS - 1)
+    start = pl.multiple_of(jnp.maximum(block, 0) * BROWS, BROWS)
+    return block >= 0, table_ref.at[pl.ds(start, BROWS)]
+
+
+def run_moves(moves):
+    for live, loads, _ in moves:
+
+        @pl.when(live)
+        def _(loads=loads):
+            for load in loads:
+                load.start()
+
+    for live, loads, store in moves:
+
+        @pl.when(live)
+        def _(loads=loads, store=store):
+            for load in loads:
+                load.wait()
+            store.start()
+
+    for live, _, store in moves:
+        pl.when(live)(store.wait)
+
+
+def cross_kernel(steps_z, words_ref, table_ref, out_ref, held, sems):
+    core = lax.axis_index("basis")
+    moves = []
+    for i, step_z in enumerate(steps_z):
+        for step in range(SIDE):
+            for which in range(2):
+                live, source = local_block(words_ref, table_ref, reached(step, step_z, 1 - core, which))
+                at = (i, step, which)
+                load = pltpu.make_async_copy(source, held.at[at], sems.at[(0, *at)])
+                store = pltpu.make_async_copy(held.at[at], out_ref.at[at], sems.at[(1, *at)])
+                moves.append((live, (load,), store))
+    run_moves(moves)
+
+
+def cross(steps_z, words, table):
+    shape = (len(steps_z), SIDE, 2, BROWS, table.shape[1])
+    anywhere = pl.BlockSpec(memory_space=pl.ANY)
+    return pl.pallas_call(
+        functools.partial(cross_kernel, steps_z),
+        out_shape=jax.ShapeDtypeStruct(shape, BF16),
+        in_specs=[pl.BlockSpec(memory_space=pltpu.SMEM), anywhere],
+        out_specs=anywhere,
+        scratch_shapes=[pltpu.VMEM(shape, BF16), pltpu.SemaphoreType.DMA((2, len(steps_z), SIDE, 2))],
+        cost_estimate=pl.CostEstimate(flops=0, bytes_accessed=len(steps_z) * 4 * 2**20, transcendentals=0),
+        name="cross",
+    )(words, table)
+
+
+def pick_kernel(step_z, row, words_ref, table_ref, crossed_ref, *rest):
+    outs, (held, sems) = rest[: len(HOP1)], rest[len(HOP1) :]
+    core = lax.axis_index("basis")
+    moves = []
+    for i, step in enumerate(HOP1):
         for which in range(2):
-            block = wanted_ref[group_of(x_to, y_to, (z + step_z) % SIDE, kind, which)]
-            start = pl.multiple_of(jnp.maximum(block, 0) * BROWS, BROWS)
-            place = held.at[send, which]
-            load = pltpu.make_async_copy(table_ref.at[pl.ds(start, BROWS)], place, sems.at[0, send, which])
-            store = pltpu.make_async_copy(place, outs[send].at[which], sems.at[1, send, which])
-            pl.when(block >= 0)(load.start)
-            copies.append((block >= 0, load, store))
-
-    def hand_on(load, store):
-        load.wait()
-        store.start()
-
-    for live, load, store in copies:
-        pl.when(live)(functools.partial(hand_on, load, store))
-    for live, load, store in copies:
-        pl.when(live)(store.wait)
-
-
-def pick(step_z, wanted, table):
-    width = table.shape[1]
-    hbm = pl.BlockSpec(memory_space=pltpu.HBM)
+            live, source = local_block(words_ref, table_ref, reached(step, step_z, core, which))
+            loads = (
+                pltpu.make_async_copy(source, held.at[i, which, 0], sems.at[0, i, which]),
+                pltpu.make_async_copy(crossed_ref.at[row, step, which], held.at[i, which, 1], sems.at[1, i, which]),
+            )
+            store = pltpu.make_async_copy(held.at[i, which], outs[i].at[which], sems.at[2, i, which])
+            moves.append((live, loads, store))
+    run_moves(moves)
+
+
+def pick(step_z, row, words, table, crossed):
+    shape = (2, 2, BROWS, table.shape[1])
+    anywhere = pl.BlockSpec(memory_space=pl.ANY)
     return pl.pallas_call(
-        functools.partial(pick_kernel, step_z),
-        out_shape=[jax.ShapeDtypeStruct((2, BROWS, width), BF16)] * len(SENDS),
-        in_specs=[pl.BlockSpec(memory_space=pltpu.SMEM), hbm],
-        out_specs=[hbm] * len(SENDS),
+        functools.partial(pick_kernel, step_z, row),
+        out_shape=[jax.ShapeDtypeStruct(shape, BF16)] * len(HOP1),
+        in_specs=[pl.BlockSpec(memory_space=pltpu.SMEM), anywhere, anywhere],
+        out_specs=[anywhere] * len(HOP1),
         scratch_shapes=[
-            pltpu.VMEM((len(SENDS), 2, BROWS, width), BF16),
-            pltpu.SemaphoreType.DMA((2, len(SENDS), 2)),
+            pltpu.VMEM((len(HOP1), *shape), BF16),
+            pltpu.SemaphoreType.DMA((3, len(HOP1), 2)),
         ],
-        cost_estimate=pl.CostEstimate(
-            flops=0, bytes_accessed=4 * len(SENDS) * 2 * BROWS * width, transcendentals=0
-        ),
+        cost_estimate=pl.CostEstimate(flops=0, bytes_accessed=4 * 2**20, transcendentals=0),
         name="pick",
-    )(wanted, table)
-
-
-def project_kernel(step_z, codes_ref, wanted_ref, coef_ref, notes_ref, table_ref, *rest):
-    received = rest[: len(SENDS)]
-    own_basis, other_basis, out_ref, rows, notes, total, basis, sems, more_sems = rest[len(SENDS) :]
+    )(words, table, crossed)
+
+
+def project_kernel(step_z, row, words_ref, notes_ref, coeffs_ref, table_ref, crossed_ref, *rest):
+    received, rest = rest[: len(HOP1)], rest[len(HOP1) :]
+    own_basis, other_basis, out_ref, rows, notes, coeffs, total, basis, sems, coef_sems, more_sems = rest
     x, y, z, core = coordinates()
     width = table_ref.shape[1]
     along = jnp.where(core == 0, x, y)
-    lookup = {sent: received[i] for i, sent in enumerate(SENDS)}
     loads = [
         pltpu.make_async_copy(own_basis, basis.at[0], more_sems.at[0]),
         pltpu.make_async_copy(other_basis, basis.at[1], more_sems.at[1]),
     ]
     pieces, note_loads = [], []
     for which in range(2):
-        group = group_of(x, y, (z + step_z) % SIDE, core, which)
+        group = reached(0, step_z, core, which)
         note_loads.append(pltpu.make_async_copy(notes_ref.at[group], notes.at[which], more_sems.at[2 + which]))
         note_loads[-1].start()
         for step in range(SIDE):
             line = (along - step) % SIDE
-            code = codes_ref[group * SIDE + line]
-            copies = []
-            for part, crossed in enumerate((False, True)):
-                if step == 0 and not crossed:
-                    start = pl.multiple_of(jnp.maximum(wanted_ref[group], 0) * BROWS, BROWS)
-                    source = table_ref.at[pl.ds(start, BROWS)]
-                else:
-                    source = lookup[(step, crossed)].at[which]
-                copies.append(
+            code = word(words_ref, group, line, 0)
+            rels = [word(words_ref, group, line, 1 + tile) for tile in range(2)]
+            copies = [
+                pltpu.make_async_copy(
+                    coeffs_ref.at[rels[tile] // DST], coeffs.at[which, step, tile], coef_sems.at[which, step, tile]
+                )
+                for tile in range(2)
+            ]
+            if step == 0:
+                _, source = local_block(words_ref, table_ref, group)
+                sources = (source, crossed_ref.at[row, 0, which])
+                copies += [
                     pltpu.make_async_copy(source, rows.at[which, step, part], sems.at[which, step, part])
-                )
-            pl.when(code >= 0)(lambda copies=copies: [c.start() for c in copies] and None)
-            pieces.append((which, step, line, code, copies))
+                    for part, source in enumerate(sources)
+                ]
+            else:
+                source = received[HOP1.index(step)].at[which]
+                copies.append(pltpu.make_async_copy(source, rows.at[which, step], sems.at[which, step, 0]))
+
+            @pl.when(code >= 0)
+            def _(copies=copies):
+                for copy in copies:
+                    copy.start()
+
+            pieces.append((which, step, line, code, rels, copies))
     for load in loads:
         load.start()
     total[...] = jnp.zeros_like(total)
     for load in note_loads:
         load.wait()
-    first_tile = lax.broadcasted_iota(jnp.int32, (1, BROWS), 1) < TILE
+    lane = lax.broadcasted_iota(jnp.int32, (2, BROWS), 1)
     dest = lax.broadcasted_iota(jnp.int32, (DST, BROWS), 0)
-    for which, step, line, code, copies in pieces:
+    for which, step, line, code, rels, copies in pieces:
 
         @pl.when(code >= 0)
-        def _(which=which, step=step, line=line, code=code, copies=copies):
+        def _(which=which, step=step, line=line, code=code, rels=rels, copies=copies):
+            for copy in copies:
+                copy.wait()
             half = jnp.where(code >= DST, 1, 0)
             hit = notes[which, pl.ds(line, 1), :] - half * DST == dest
+            coef = [
+                jnp.sum(
+                    jnp.where(lane == rels[tile] % DST, coeffs[which, step, tile], 0.0), axis=1, keepdims=True
+                )
+                for tile in range(2)
+            ]
+            weights = jnp.where(lane < TILE, coef[0], coef[1])
             chosen = []
-            at = ((which * SIDE + step) * (BROWS // TILE)) * 2
             for k in range(2):
-                weight = jnp.where(first_tile, coef_ref[at + k], coef_ref[at + 2 + k])
+                weight = jnp.where(core == 0, weights[k : k + 1], weights[1 - k : 2 - k])
                 high = weight.astype(BF16).astype(F32)
                 high, low = jnp.where(hit, high, 0.0), jnp.where(hit, weight - high, 0.0)
                 chosen.append(jnp.concatenate([high, low], axis=1))
             chosen = jnp.concatenate(chosen, axis=0).astype(BF16)
             for part in range(2):
-                copies[part].wait()
                 block = rows[which, step, part]
                 added = jnp.dot(
                     chosen, jnp.concatenate([block, block], axis=0), preferred_element_type=F32
@@ -241,30 +309,31 @@
         out_ref[:, :, start : start + tile] = result.reshape(4, DST, tile).astype(BF16)
 
 
-def project(step_z, codes, wanted, coef, notes, table, received, own_basis, other_basis):
+def project(step_z, row, words, notes, coeffs, table, crossed, received, own_basis, other_basis):
     width = table.shape[1]
     wide = own_basis.shape[1]
-    hbm = pl.BlockSpec(memory_space=pltpu.HBM)
-    smem = pl.BlockSpec(memory_space=pltpu.SMEM)
+    anywhere = pl.BlockSpec(memory_space=pl.ANY)
     return pl.pallas_call(
-        functools.partial(project_kernel, step_z),
+        functools.partial(project_kernel, step_z, row),
         out_shape=jax.ShapeDtypeStruct((4, DST, wide), BF16),
-        in_specs=[smem] * 3 + [hbm] * (4 + len(SENDS)),
+        in_specs=[pl.BlockSpec(memory_space=pltpu.SMEM)] + [anywhere] * (6 + len(HOP1)),
         out_specs=pl.BlockSpec(memory_space=pltpu.VMEM),
         scratch_shapes=[
             pltpu.VMEM((2, SIDE, 2, BROWS, width), BF16),
             pltpu.VMEM((2, 8, DST), jnp.int32),
+            pltpu.VMEM((2, SIDE, 2, 2, DST), F32),
             pltpu.VMEM((2, 2, 2 * DST, 2 * width), F32),
             pltpu.VMEM((2, 2 * width, wide), BF16),
+            pltpu.SemaphoreType.DMA((2, SIDE, 2)),
             pltpu.SemaphoreType.DMA((2, SIDE, 2)),
             pltpu.SemaphoreType.DMA((4,)),
         ],
         cost_estimate=pl.CostEstimate(
-            flops=2 * 4 * DST * 4 * width * wide, bytes_accessed=8 * 2**20, transcendentals=0
+            flops=2 * 4 * DST * 4 * width * wide, bytes_accessed=16 * 2**20, transcendentals=0
         ),
         compiler_params=pltpu.CompilerParams(vmem_limit_bytes=VMEM_LIMIT),
         name="project",
-    )(codes, wanted, coef, notes, table, *received, own_basis, other_basis)
+    )(words, notes, coeffs, table, crossed, *received, own_basis, other_basis)
 
 
 def merge_kernel(order_ref, *refs):
@@ -297,30 +366,30 @@
 def body(features, bases, coeffs, block_lists, block_counts, tile_rel, dest_ids):
     x, y, z, core = coordinates()
     blocks = tile_rel.shape[1] * TILE // BROWS
-    other_basis = lax.ppermute(bases[0], "basis", [(0, 1), (1, 0)])
+    other_basis = lax.ppermute(bases[0], "basis", CORE_SWAP)
 
     sent = make_notes(block_counts, dest_ids, tile_rel, block_lists.reshape(1, CHIPS))
     notes = lax.all_to_all(sent, "shard", split_axis=0, concat_axis=0, tiled=True)
-    wanted = notes[:, SIDE, 4]
-    codes = notes[:, :SIDE, 0].reshape(-1)
-    along = jnp.where(core == 0, x, y)
-
-    arrived = []
-    for step_z in HOP2:
-        picked = pick(step_z, wanted, features)
-        arrived.append([lax.ppermute(buf, AXES, hop1_pairs(*send)) for buf, send in zip(picked, SENDS)])
-
-    groups = jnp.stack([group_of(x, y, (z + s) % SIDE, core, w) for s in HOP2 for w in range(2)])
-    lines = (along - jnp.arange(SIDE, dtype=jnp.int32)) % SIDE
-    told = notes[groups[:, None], SIDE + lines[None, :], : BROWS // TILE]
-    coef = coeffs[told]
-    coef = jnp.where(core == 0, coef, coef[..., ::-1]).reshape(len(HOP2), -1)
-
+    words = notes[:, SIDE:, :WORDS].reshape(-1)
+    rels = -(-coeffs.shape[0] // DST) * DST
+    table = jnp.pad(coeffs.T, ((0, 0), (0, rels - coeffs.shape[0]))).reshape(2, -1, DST).transpose(1, 0, 2)
+
+    groups = HOP2[:1], HOP2[1:]
+    crossed = [lax.ppermute(cross(steps, words, features), "basis", CORE_SWAP) for steps in groups]
+    crossed = {s: (steps.index(s), buf) for steps, buf in zip(groups, crossed) for s in steps}
+
+    def send(step_z, words):
+        picked = pick(step_z, crossed[step_z][0], words, features, crossed[step_z][1])
+        return [lax.ppermute(buf, AXES, hop1_pairs(step)) for step, buf in zip(HOP1, picked)]
+
+    arrived = [send(step_z, words) for step_z in HOP2[:2]]
     parts = []
     for i, step_z in enumerate(HOP2):
-        part = project(
-            step_z, codes, wanted, coef[i], notes, features, arrived[i], bases[0], other_basis
-        )
+        row, buf = crossed[step_z]
+        part = project(step_z, row, words, notes, table, features, buf, arrived[i], bases[0], other_basis)
+        if i + 2 < len(HOP2):
+            later, part = lax.optimization_barrier((words, part))
+            arrived.append(send(HOP2[i + 2], later))
         parts.append(part if step_z == 0 else lax.ppermute(part, AXES, hop2_pairs(step_z)))
 
     last = jnp.where(core == 0, y, x)

time: 180 us -> 159 us (0.88)
  starting transfers between devices: 63.9 us -> 29.3 us
  blocking collectives: 0 us -> 21.5 us
  local copies, waits for them, and re-layouts: 35.7 us -> 23.7 us
  Pallas kernels: 44 us -> 48.3 us
    ppermute x29 -> x15, starting transfers between devices: 37.6 us -> 15.1 us  [the longest x12 12.3 us: send(): lax.ppermute(buf, AXES, hop1_pairs(step))]
    all_to_all x0 -> x1, blocking collectives: none -> 21.5 us  [body(): lax.all_to_all(sent, 'shard', split_axis=0, concat_axis=0, tiled=True)]
    ppermute x29 -> x15, waiting for transfers between devices: 13.4 us -> 24.7 us  [the longest x12 17.9 us: send(): lax.ppermute(buf, AXES, hop1_pairs(step))]
    all_to_all x1 -> x0, starting transfers between devices: 11.3 us -> none  [body(): lax.all_to_all(sent, 'shard', split_axis=0, concat_axis=0, tiled=True)]
    all_to_all x1 -> x0, waiting for transfers between devices: 9.72 us -> none  [body(): lax.all_to_all(sent, 'shard', split_axis=0, concat_axis=0, tiled=True)]
    gather x10 -> x0, local copies, waits for them, and re-layouts: 5.89 us -> none  [the longest x2 4.06 us: body(): coef = coeffs[told]]
    ppermute x3, starting transfers between devices: 7.44 us -> 2.43 us  [body(): lax.ppermute(part, AXES, hop2_pairs(step_z))]
    pallas_call x8 -> x10, Pallas kernels: 38.4 us -> 42.7 us  [the longest x4 25.1 us: project(): pl.pallas_call(functools.partial(project_kernel, step_z, row), out_shape=...]
  transfers between devices with their start and end apart: 37 -> 22, of which waited for: 8 -> 6; matrix products, arithmetic and copies ran while one was open for 9% -> 1% of each run, Pallas kernels for 23% -> 25%
where the time goes in v3:
time: 159 us
  Pallas kernels  48.3 us (30%)
  waiting for transfers between devices  34.3 us (22%)
  starting transfers between devices  29.3 us (18%)
  local copies, waits for them, and re-layouts  23.7 us (15%)
  blocking collectives  21.5 us (14%)
    pallas_call x4, Pallas kernels, project(): pl.pallas_call(functools.partial(project_kernel, step_z, row), out_shape=...  25.1 us
    unnamed x36, local copies, waits for them, and re-layouts  22 us
    all_to_all x1, blocking collectives, body(): lax.all_to_all(sent, 'shard', split_axis=0, concat_axis=0, tiled=True)  21.5 us
    ppermute x12, waiting for transfers between devices, send(): lax.ppermute(buf, AXES, hop1_pairs(step))  17.9 us
    ppermute x12, starting transfers between devices, send(): lax.ppermute(buf, AXES, hop1_pairs(step))  12.3 us
    ppermute x4, starting transfers between devices, body(): lax.ppermute(buf, AXES, hop3_pairs(send))  11.7 us
    pallas_call x4, Pallas kernels, pick(): pl.pallas_call(functools.partial(pick_kernel, step_z, row), out_shape=[ja...  11.6 us
    ppermute x4, waiting for transfers between devices, body(): lax.ppermute(buf, AXES, hop3_pairs(send))  9.57 us
  transfers between devices with their start and end apart: 22, of which 6 were waited for; matrix products, arithmetic and copies ran while one was open for 1% of the time, Pallas kernels for 25%

profile of v3, /device:TPU:1, one launch (start us, length us, event | category | flops | bytes accessed | tf_op | source)
XLA Modules:
  0.0 158.5 jit_solution(14090316298033912652)
XLA Ops:
  2.2 21.5 %all_to_all.5.notes_ref = s32[64,8,128]{2,1,0:T(8,128)S(1)} all-to-all(s32[64,8,128]{2,1,0:T(8,128)} %bitcast.17), channel_id=1, replica_groups=mesh['shard'=64,'basis'=2] {'shard'}, dimensions={0} | all-to-all | bytes 524288 | tf_op jit(solution)/shard_map/all_to_all | solution.py:372
  24.5 3.4 %cross.3 = bf16[3,4,2,128,512]{4,3,2,1,0:T(8,128)(2,1)} custom-call(s32[1024]{0:T(1024)} %reshape.19.words_ref, bf16[6144,512]{1,0:T(8,128)(2,1)} %table_ref.19), custom_call_target="tpu_custom_call" | custom-call | bytes 12582912 | tf_op jit(solution)/shard_map/cross/pallas_call | solution.py:176
  33.2 6.9 %collective-permute-done.crossed_ref = bf16[1,4,2,128,512]{4,3,2,1,0:T(8,128)(2,1)} collective-permute-done((bf16[1,4,2,128,512]{4,3,2,1,0:T(8,128)(2,1)}, bf16[1,4,2,128,512]{4,3,2,1,0:T(8,128)(2,1)}, u32[]{:S(2)}, u32[]{:S(2)}) %collective-permute-start) | collective-permute-done | bytes 1048608 | tf_op jit(solution)/shard_map/ppermute | solution.py:378
  40.1 2.9 %pick.4 = (bf16[2,2,128,512]{3,2,1,0:T(8,128)(2,1)}, bf16[2,2,128,512]{3,2,1,0:T(8,128)(2,1)}, bf16[2,2,128,512]{3,2,1,0:T(8,128)(2,1)}) custom-call(s32[1024]{0:T(1024)} %reshape.19.words_ref, bf16[6144,512]{1,0:T(8,128)(2,1)} %table_ref.19, bf16[1,4,2,128,512]{4,3,2,1,0:T(8,128)(2,1)} %collective-permute-done.crossed_ref), custom_call_target="tpu_custom_call" | custom-call | bytes 4194304 | tf_op jit(solution)/shard_map/pick/pallas_call | solution.py:206
  43.0 2.7 %collective-permute-start.2 = (bf16[2,2,128,512]{3,2,1,0:T(8,128)(2,1)}, bf16[2,2,128,512]{3,2,1,0:T(8,128)(2,1)}, u32[]{:S(2)}, u32[]{:S(2)}) collective-permute-start(bf16[2,2,128,512]{3,2,1,0:T(8,128)(2,1)} %get-tuple-element.26), channel_id=1, source_target_pairs={{0,6},{1,25},{2,0},{3,27},{4,2},{5,29},{6,4},{7,31},{8,14},{9,1},{... | collective-permute-start | bytes 1572872 | tf_op jit(solution)/shard_map/ppermute | solution.py:383
  47.3 2.7 %pick.5 = (bf16[2,2,128,512]{3,2,1,0:T(8,128)(2,1)}, bf16[2,2,128,512]{3,2,1,0:T(8,128)(2,1)}, bf16[2,2,128,512]{3,2,1,0:T(8,128)(2,1)}) custom-call(s32[1024]{0:T(1024)} %reshape.19.words_ref, bf16[6144,512]{1,0:T(8,128)(2,1)} %table_ref.19, bf16[3,4,2,128,512]{4,3,2,1,0:T(8,128)(2,1)} %copy-done.4), custom_call_target="tpu_custom_call" | custom-call | bytes 4194304 | tf_op jit(solution)/shard_map/pick/pallas_call | solution.py:206
  51.8 6.7 %collective-permute-done.1.rest_0_ = bf16[2,2,128,512]{3,2,1,0:T(8,128)(2,1)} collective-permute-done((bf16[2,2,128,512]{3,2,1,0:T(8,128)(2,1)}, bf16[2,2,128,512]{3,2,1,0:T(8,128)(2,1)}, u32[]{:S(2)}, u32[]{:S(2)}) %collective-permute-start.1) | collective-permute-done | bytes 524320 | tf_op jit(solution)/shard_map/ppermute | solution.py:383
  58.6 2.8 %copy-done = bf16[6144,512]{1,0:T(8,128)(2,1)S(1)} copy-done((bf16[6144,512]{1,0:T(8,128)(2,1)S(1)}, bf16[6144,512]{1,0:T(8,128)(2,1)}, u32[]{:S(2)}) %copy-start) | copy-done | bytes 6291480
  62.9 5.4 %project.4 = bf16[4,128,1024]{2,1,0:T(8,128)(2,1)S(1)} custom-call(s32[1024]{0:T(1024)S(1)} %copy-done.14, s32[64,8,128]{2,1,0:T(8,128)S(1)} %all_to_all.5.notes_ref, f32[116,2,128]{2,1,0:T(2,128)S(1)} %pad_bitcast_fusion.coeffs_ref, bf16[6144,512]{1,0:T(8,128)(2,1)S(1)} %copy-done, bf16[1,4,2,128,512]{4,3,2,1,0:T(8,128)(2,1)} %collective-permute-done.crossed_ref, ...), custom_call_target="tpu_custom_call" | custom-call | flops 2147483648 | bytes 16777216 | tf_op jit(solution)/shard_map/project/pallas_call | solution.py:316
  69.4 2.9 %pick.6 = (bf16[2,2,128,512]{3,2,1,0:T(8,128)(2,1)}, bf16[2,2,128,512]{3,2,1,0:T(8,128)(2,1)}, bf16[2,2,128,512]{3,2,1,0:T(8,128)(2,1)}) custom-call(s32[1024]{0:T(1024)} %reshape.19.words_ref, bf16[6144,512]{1,0:T(8,128)(2,1)} %table_ref.19, bf16[3,4,2,128,512]{4,3,2,1,0:T(8,128)(2,1)} %copy-done.4), custom_call_target="tpu_custom_call" | custom-call | bytes 4194304 | tf_op jit(solution)/shard_map/pick/pallas_call | solution.py:206
  73.8 2.8 %collective-permute-start.12 = (bf16[2,2,128,512]{3,2,1,0:T(8,128)(2,1)}, bf16[2,2,128,512]{3,2,1,0:T(8,128)(2,1)}, u32[]{:S(2)}, u32[]{:S(2)}) collective-permute-start(bf16[2,2,128,512]{3,2,1,0:T(8,128)(2,1)} %get-tuple-element.35), channel_id=1, source_target_pairs={{0,6},{1,25},{2,0},{3,27},{4,2},{5,29},{6,4},{7,31},{8,14},{9,1},{... | collective-permute-start | bytes 1572872 | tf_op jit(solution)/shard_map/ppermute | solution.py:383
  78.4 2.8 %copy-done.1 = bf16[6144,512]{1,0:T(8,128)(2,1)S(1)} copy-done((bf16[6144,512]{1,0:T(8,128)(2,1)S(1)}, bf16[6144,512]{1,0:T(8,128)(2,1)}, u32[]{:S(2)}) %copy-start.1) | copy-done | bytes 6291480
  82.8 7.6 %project.5 = bf16[4,128,1024]{2,1,0:T(8,128)(2,1)} custom-call(s32[1024]{0:T(1024)S(1)} %copy-done.15, s32[64,8,128]{2,1,0:T(8,128)S(1)} %all_to_all.5.notes_ref, f32[116,2,128]{2,1,0:T(2,128)S(1)} %pad_bitcast_fusion.coeffs_ref, bf16[6144,512]{1,0:T(8,128)(2,1)S(1)} %copy-done.1, bf16[3,4,2,128,512]{4,3,2,1,0:T(8,128)(2,1)S(1)} %copy-done.5, ...), custom_call_target="tpu_custom_call" | custom-call | flops 2147483648 | bytes 16777216 | tf_op jit(solution)/shard_map/project/pallas_call | solution.py:316
  90.5 3.1 %pick.7 = (bf16[2,2,128,512]{3,2,1,0:T(8,128)(2,1)}, bf16[2,2,128,512]{3,2,1,0:T(8,128)(2,1)}, bf16[2,2,128,512]{3,2,1,0:T(8,128)(2,1)}) custom-call(s32[1024]{0:T(1024)} %reshape.19.words_ref, bf16[6144,512]{1,0:T(8,128)(2,1)} %table_ref.19, bf16[3,4,2,128,512]{4,3,2,1,0:T(8,128)(2,1)} %copy-done.4), custom_call_target="tpu_custom_call" | custom-call | bytes 4194304 | tf_op jit(solution)/shard_map/pick/pallas_call | solution.py:206
  93.8 2.8 %copy-done.2 = bf16[6144,512]{1,0:T(8,128)(2,1)S(1)} copy-done((bf16[6144,512]{1,0:T(8,128)(2,1)S(1)}, bf16[6144,512]{1,0:T(8,128)(2,1)}, u32[]{:S(2)}) %copy-start.2) | copy-done | bytes 6291480
  98.1 6.5 %project.6 = bf16[4,128,1024]{2,1,0:T(8,128)(2,1)} custom-call(s32[1024]{0:T(1024)S(1)} %copy-done.16, s32[64,8,128]{2,1,0:T(8,128)S(1)} %all_to_all.5.notes_ref, f32[116,2,128]{2,1,0:T(2,128)S(1)} %pad_bitcast_fusion.coeffs_ref, bf16[6144,512]{1,0:T(8,128)(2,1)S(1)} %copy-done.2, bf16[3,4,2,128,512]{4,3,2,1,0:T(8,128)(2,1)S(1)} %copy-done.6, ...), custom_call_target="tpu_custom_call" | custom-call | flops 2147483648 | bytes 16777216 | tf_op jit(solution)/shard_map/project/pallas_call | solution.py:316
  106.5 3.2 %collective-permute-start.16 = (bf16[2,2,128,512]{3,2,1,0:T(8,128)(2,1)}, bf16[2,2,128,512]{3,2,1,0:T(8,128)(2,1)}, u32[]{:S(2)}, u32[]{:S(2)}) collective-permute-start(bf16[2,2,128,512]{3,2,1,0:T(8,128)(2,1)} %get-tuple-element.39), channel_id=1, source_target_pairs={{0,6},{1,25},{2,0},{3,27},{4,2},{5,29},{6,4},{7,31},{8,14},{9,1},{... | collective-permute-start | bytes 1572872 | tf_op jit(solution)/shard_map/ppermute | solution.py:383
  110.6 11.1 %collective-permute-done.16.rest_1_ = bf16[2,2,128,512]{3,2,1,0:T(8,128)(2,1)} collective-permute-done((bf16[2,2,128,512]{3,2,1,0:T(8,128)(2,1)}, bf16[2,2,128,512]{3,2,1,0:T(8,128)(2,1)}, u32[]{:S(2)}, u32[]{:S(2)}) %collective-permute-start.16) | collective-permute-done | bytes 524320 | tf_op jit(solution)/shard_map/ppermute | solution.py:383
  121.7 2.8 %copy-done.3 = bf16[6144,512]{1,0:T(8,128)(2,1)S(1)} copy-done((bf16[6144,512]{1,0:T(8,128)(2,1)S(1)}, bf16[6144,512]{1,0:T(8,128)(2,1)}, u32[]{:S(2)}) %copy-start.3) | copy-done | bytes 6291480
  127.1 5.6 %project.7.refs_3_ = bf16[4,128,1024]{2,1,0:T(8,128)(2,1)S(1)} custom-call(s32[1024]{0:T(1024)S(1)} %copy-done.16, s32[64,8,128]{2,1,0:T(8,128)S(1)} %all_to_all.5.notes_ref, f32[116,2,128]{2,1,0:T(2,128)S(1)} %pad_bitcast_fusion.coeffs_ref, bf16[6144,512]{1,0:T(8,128)(2,1)S(1)} %copy-done.3, bf16[3,4,2,128,512]{4,3,2,1,0:T(8,128)(2,1)S(1)} %copy-done.6, ...), custom_call_target="tpu_custom_call" | custom-call | flops 2147483648 | bytes 16777216 | tf_op jit(solution)/shard_map/project/pallas_call | solution.py:316
  132.7 3.4 %merge.1 = (bf16[128,1024]{1,0:T(8,128)(2,1)S(1)}, bf16[128,1024]{1,0:T(8,128)(2,1)S(1)}, bf16[128,1024]{1,0:T(8,128)(2,1)S(1)}, bf16[128,1024]{1,0:T(8,128)(2,1)S(1)}) custom-call(s32[4]{0:T(128)S(1)} %pad_add_fusion.order_ref, bf16[4,128,1024]{2,1,0:T(8,128)(2,1)} %collective-permute-done.5.refs_0_, bf16[4,128,1024]{2,1,0:T(8,128)(2,1)} %collective-permute-done.10.refs_1_, ...), custom_call_target="tpu_custom_call" | custom-call | tf_op jit(solution)/shard_map/merge/pallas_call | solution.py:352
  138.3 5.1 %collective-permute-start.19 = (bf16[128,1024]{1,0:T(8,128)(2,1)S(1)}, bf16[128,1024]{1,0:T(8,128)(2,1)S(1)}, u32[]{:S(2)}, u32[]{:S(2)}) collective-permute-start(bf16[128,1024]{1,0:T(8,128)(2,1)S(1)} %get-tuple-element.42), channel_id=1, source_target_pairs={{0,17},{1,2},{2,10},{3,7},{4,21},{5,6},{6,14},{7,3},{8,16},{9,13},... | collective-permute-start | bytes 786440 | tf_op jit(solution)/shard_map/ppermute | solution.py:404
  150.6 4.2 %collective-permute-done.20 = bf16[128,1024]{1,0:T(8,128)(2,1)S(1)} collective-permute-done((bf16[128,1024]{1,0:T(8,128)(2,1)S(1)}, bf16[128,1024]{1,0:T(8,128)(2,1)S(1)}, u32[]{:S(2)}, u32[]{:S(2)}) %collective-permute-start.20) | collective-permute-done | bytes 262176 | tf_op jit(solution)/shard_map/ppermute | solution.py:404
  154.8 2.8 %collective-permute-done.21 = bf16[128,1024]{1,0:T(8,128)(2,1)S(1)} collective-permute-done((bf16[128,1024]{1,0:T(8,128)(2,1)S(1)}, bf16[128,1024]{1,0:T(8,128)(2,1)S(1)}, u32[]{:S(2)}, u32[]{:S(2)}) %collective-permute-start.21) | collective-permute-done | bytes 262176 | tf_op jit(solution)/shard_map/ppermute | solution.py:404
  (77 shorter events, 36.6 us)
Async XLA Ops:
  27.8 17.9 %collective-permute-start.6 = (bf16[3,4,2,128,512]{4,3,2,1,0:T(8,128)(2,1)}, bf16[3,4,2,128,512]{4,3,2,1,0:T(8,128)(2,1)S(1)}, u32[]{:S(2)}, u32[]{:S(2)}) collective-permute-start(bf16[3,4,2,128,512]{4,3,2,1,0:T(8,128)(2,1)} %cross.3), channel_id=1, source_target_pairs={{0,1},{1,0},{2,3},{3,2},{4,5},{5,4},{6,7},{7,6},{8,9},{9,8},{10,11... | collective-permute-start | bytes 9437192 | tf_op jit(solution)/shard_map/ppermute | solution.py:378
  30.0 28.6 %collective-permute-start.4 = (bf16[1024,1024]{1,0:T(8,128)(2,1)}, bf16[1024,1024]{1,0:T(8,128)(2,1)}, u32[]{:S(2)}, u32[]{:S(2)}) collective-permute-start(bf16[1024,1024]{1,0:T(8,128)(2,1)} %bitcast.12), channel_id=1, source_target_pairs={{0,1},{1,0},{2,3},{3,2},{4,5},{5,4},{6,7},{7,6},{8,9},{9,8},{10,11... | collective-permute-start | bytes 6291464 | tf_op jit(solution)/shard_map/ppermute | solution.py:369
  32.7 7.4 %collective-permute-start = (bf16[1,4,2,128,512]{4,3,2,1,0:T(8,128)(2,1)}, bf16[1,4,2,128,512]{4,3,2,1,0:T(8,128)(2,1)}, u32[]{:S(2)}, u32[]{:S(2)}) collective-permute-start(bf16[1,4,2,128,512]{4,3,2,1,0:T(8,128)(2,1)} %cross.2), channel_id=1, source_target_pairs={{0,1},{1,0},{2,3},{3,2},{4,5},{5,4},{6,7},{7,6},{8,9},{9,8},{10,11... | collective-permute-start | bytes 3145736 | tf_op jit(solution)/shard_map/ppermute | solution.py:378
  43.0 15.5 %collective-permute-start.1 = (bf16[2,2,128,512]{3,2,1,0:T(8,128)(2,1)}, bf16[2,2,128,512]{3,2,1,0:T(8,128)(2,1)}, u32[]{:S(2)}, u32[]{:S(2)}) collective-permute-start(bf16[2,2,128,512]{3,2,1,0:T(8,128)(2,1)} %get-tuple-element.25), channel_id=1, source_target_pairs={{0,2},{1,9},{2,4},{3,11},{4,6},{5,13},{6,0},{7,15},{8,10},{9,17},{... | collective-permute-start | bytes 1572872 | tf_op jit(solution)/shard_map/ppermute | solution.py:383
  43.0 15.5 %collective-permute-start.2 = (bf16[2,2,128,512]{3,2,1,0:T(8,128)(2,1)}, bf16[2,2,128,512]{3,2,1,0:T(8,128)(2,1)}, u32[]{:S(2)}, u32[]{:S(2)}) collective-permute-start(bf16[2,2,128,512]{3,2,1,0:T(8,128)(2,1)} %get-tuple-element.26), channel_id=1, source_target_pairs={{0,6},{1,25},{2,0},{3,27},{4,2},{5,29},{6,4},{7,31},{8,14},{9,1},{... | collective-permute-start | bytes 1572872 | tf_op jit(solution)/shard_map/ppermute | solution.py:383
  45.7 12.8 %copy-start.14 = (s32[1024]{0:T(1024)S(1)}, s32[1024]{0:T(1024)}, u32[]{:S(2)}) copy-start(s32[1024]{0:T(1024)} %reshape.19.words_ref) | copy-start | bytes 12292
  45.7 12.8 %collective-permute-start.3 = (bf16[2,2,128,512]{3,2,1,0:T(8,128)(2,1)}, bf16[2,2,128,512]{3,2,1,0:T(8,128)(2,1)}, u32[]{:S(2)}, u32[]{:S(2)}) collective-permute-start(bf16[2,2,128,512]{3,2,1,0:T(8,128)(2,1)} %get-tuple-element.27), channel_id=1, source_target_pairs={{0,4},{1,17},{2,6},{3,19},{4,0},{5,21},{6,2},{7,23},{8,12},{9,25},... | collective-permute-start | bytes 1572872 | tf_op jit(solution)/shard_map/ppermute | solution.py:383
  50.1 26.5 %collective-permute-start.7 = (bf16[2,2,128,512]{3,2,1,0:T(8,128)(2,1)}, bf16[2,2,128,512]{3,2,1,0:T(8,128)(2,1)}, u32[]{:S(2)}, u32[]{:S(2)}) collective-permute-start(bf16[2,2,128,512]{3,2,1,0:T(8,128)(2,1)} %get-tuple-element.29), channel_id=1, source_target_pairs={{0,2},{1,9},{2,4},{3,11},{4,6},{5,13},{6,0},{7,15},{8,10},{9,17},{... | collective-permute-start | bytes 1572872 | tf_op jit(solution)/shard_map/ppermute | solution.py:383
  58.5 19.3 %collective-permute-start.8 = (bf16[2,2,128,512]{3,2,1,0:T(8,128)(2,1)}, bf16[2,2,128,512]{3,2,1,0:T(8,128)(2,1)}, u32[]{:S(2)}, u32[]{:S(2)}) collective-permute-start(bf16[2,2,128,512]{3,2,1,0:T(8,128)(2,1)} %get-tuple-element.30), channel_id=1, source_target_pairs={{0,6},{1,25},{2,0},{3,27},{4,2},{5,29},{6,4},{7,31},{8,14},{9,1},{... | collective-permute-start | bytes 1572872 | tf_op jit(solution)/shard_map/ppermute | solution.py:383
  58.5 19.9 %collective-permute-start.9 = (bf16[2,2,128,512]{3,2,1,0:T(8,128)(2,1)}, bf16[2,2,128,512]{3,2,1,0:T(8,128)(2,1)}, u32[]{:S(2)}, u32[]{:S(2)}) collective-permute-start(bf16[2,2,128,512]{3,2,1,0:T(8,128)(2,1)} %get-tuple-element.31), channel_id=1, source_target_pairs={{0,4},{1,17},{2,6},{3,19},{4,0},{5,21},{6,2},{7,23},{8,12},{9,25},... | collective-permute-start | bytes 1572872 | tf_op jit(solution)/shard_map/ppermute | solution.py:383
  72.3 21.4 %collective-permute-start.11 = (bf16[2,2,128,512]{3,2,1,0:T(8,128)(2,1)}, bf16[2,2,128,512]{3,2,1,0:T(8,128)(2,1)}, u32[]{:S(2)}, u32[]{:S(2)}) collective-permute-start(bf16[2,2,128,512]{3,2,1,0:T(8,128)(2,1)} %get-tuple-element.34), channel_id=1, source_target_pairs={{0,2},{1,9},{2,4},{3,11},{4,6},{5,13},{6,0},{7,15},{8,10},{9,17},{... | collective-permute-start | bytes 1572872 | tf_op jit(solution)/shard_map/ppermute | solution.py:383
  73.8 19.9 %collective-permute-start.12 = (bf16[2,2,128,512]{3,2,1,0:T(8,128)(2,1)}, bf16[2,2,128,512]{3,2,1,0:T(8,128)(2,1)}, u32[]{:S(2)}, u32[]{:S(2)}) collective-permute-start(bf16[2,2,128,512]{3,2,1,0:T(8,128)(2,1)} %get-tuple-element.35), channel_id=1, source_target_pairs={{0,6},{1,25},{2,0},{3,27},{4,2},{5,29},{6,4},{7,31},{8,14},{9,1},{... | collective-permute-start | bytes 1572872 | tf_op jit(solution)/shard_map/ppermute | solution.py:383
  76.6 17.1 %collective-permute-start.13 = (bf16[2,2,128,512]{3,2,1,0:T(8,128)(2,1)}, bf16[2,2,128,512]{3,2,1,0:T(8,128)(2,1)}, u32[]{:S(2)}, u32[]{:S(2)}) collective-permute-start(bf16[2,2,128,512]{3,2,1,0:T(8,128)(2,1)} %get-tuple-element.36), channel_id=1, source_target_pairs={{0,4},{1,17},{2,6},{3,19},{4,0},{5,21},{6,2},{7,23},{8,12},{9,25},... | collective-permute-start | bytes 1572872 | tf_op jit(solution)/shard_map/ppermute | solution.py:383
  77.8 54.9 %collective-permute-start.5 = (bf16[4,128,1024]{2,1,0:T(8,128)(2,1)}, bf16[4,128,1024]{2,1,0:T(8,128)(2,1)}, u32[]{:S(2)}, u32[]{:S(2)}) collective-permute-start(bf16[4,128,1024]{2,1,0:T(8,128)(2,1)} %copy-done.11), channel_id=1, source_target_pairs={{0,64},{1,65},{2,66},{3,67},{4,68},{5,69},{6,70},{7,71},{8,72},{9,... | collective-permute-start | bytes 3145736 | tf_op jit(solution)/shard_map/ppermute | solution.py:393
  90.5 20.0 %copy-start.17 = (s32[1,3328]{1,0:T(1,128)S(1)}, s32[1,3328]{1,0:T(1,128)}, u32[]{:S(2)}) copy-start(s32[1,3328]{1,0:T(1,128)} %dests_ref.1) | copy-start | bytes 39940
  93.6 16.1 %collective-permute-start.15 = (bf16[2,2,128,512]{3,2,1,0:T(8,128)(2,1)}, bf16[2,2,128,512]{3,2,1,0:T(8,128)(2,1)S(1)}, u32[]{:S(2)}, u32[]{:S(2)}) collective-permute-start(bf16[2,2,128,512]{3,2,1,0:T(8,128)(2,1)} %get-tuple-element.38), channel_id=1, source_target_pairs={{0,2},{1,9},{2,4},{3,11},{4,6},{5,13},{6,0},{7,15},{8,10},{9,17},{... | collective-permute-start | bytes 1572872 | tf_op jit(solution)/shard_map/ppermute | solution.py:383
  104.7 28.1 %collective-permute-start.14 = (bf16[4,128,1024]{2,1,0:T(8,128)(2,1)}, bf16[4,128,1024]{2,1,0:T(8,128)(2,1)}, u32[]{:S(2)}, u32[]{:S(2)}) collective-permute-start(bf16[4,128,1024]{2,1,0:T(8,128)(2,1)} %project.6), channel_id=1, source_target_pairs={{0,96},{1,97},{2,98},{3,99},{4,100},{5,101},{6,102},{7,103},{8,104... | collective-permute-start | bytes 3145736 | tf_op jit(solution)/shard_map/ppermute | solution.py:393
  106.5 26.3 %collective-permute-start.10 = (bf16[4,128,1024]{2,1,0:T(8,128)(2,1)}, bf16[4,128,1024]{2,1,0:T(8,128)(2,1)}, u32[]{:S(2)}, u32[]{:S(2)}) collective-permute-start(bf16[4,128,1024]{2,1,0:T(8,128)(2,1)} %project.5), channel_id=1, source_target_pairs={{0,32},{1,33},{2,34},{3,35},{4,36},{5,37},{6,38},{7,39},{8,40},{9,... | collective-permute-start | bytes 3145736 | tf_op jit(solution)/shard_map/ppermute | solution.py:393
  106.5 15.2 %collective-permute-start.16 = (bf16[2,2,128,512]{3,2,1,0:T(8,128)(2,1)}, bf16[2,2,128,512]{3,2,1,0:T(8,128)(2,1)}, u32[]{:S(2)}, u32[]{:S(2)}) collective-permute-start(bf16[2,2,128,512]{3,2,1,0:T(8,128)(2,1)} %get-tuple-element.39), channel_id=1, source_target_pairs={{0,6},{1,25},{2,0},{3,27},{4,2},{5,29},{6,4},{7,31},{8,14},{9,1},{... | collective-permute-start | bytes 1572872 | tf_op jit(solution)/shard_map/ppermute | solution.py:383
  110.5 11.3 %collective-permute-start.17 = (bf16[2,2,128,512]{3,2,1,0:T(8,128)(2,1)}, bf16[2,2,128,512]{3,2,1,0:T(8,128)(2,1)}, u32[]{:S(2)}, u32[]{:S(2)}) collective-permute-start(bf16[2,2,128,512]{3,2,1,0:T(8,128)(2,1)} %get-tuple-element.40), channel_id=1, source_target_pairs={{0,4},{1,17},{2,6},{3,19},{4,0},{5,21},{6,2},{7,23},{8,12},{9,25},... | collective-permute-start | bytes 1572872 | tf_op jit(solution)/shard_map/ppermute | solution.py:383
  136.1 14.5 %collective-permute-start.18 = (bf16[128,1024]{1,0:T(8,128)(2,1)S(1)}, bf16[128,1024]{1,0:T(8,128)(2,1)S(1)}, u32[]{:S(2)}, u32[]{:S(2)}) collective-permute-start(bf16[128,1024]{1,0:T(8,128)(2,1)S(1)} %get-tuple-element.41), channel_id=1, source_target_pairs={{0,0},{1,3},{2,11},{3,2},{4,4},{5,7},{6,15},{7,6},{8,17},{9,8},{10... | collective-permute-start | bytes 786440 | tf_op jit(solution)/shard_map/ppermute | solution.py:404
  138.3 12.3 %collective-permute-start.19 = (bf16[128,1024]{1,0:T(8,128)(2,1)S(1)}, bf16[128,1024]{1,0:T(8,128)(2,1)S(1)}, u32[]{:S(2)}, u32[]{:S(2)}) collective-permute-start(bf16[128,1024]{1,0:T(8,128)(2,1)S(1)} %get-tuple-element.42), channel_id=1, source_target_pairs={{0,17},{1,2},{2,10},{3,7},{4,21},{5,6},{6,14},{7,3},{8,16},{9,13},... | collective-permute-start | bytes 786440 | tf_op jit(solution)/shard_map/ppermute | solution.py:404
  143.4 11.4 %collective-permute-start.20 = (bf16[128,1024]{1,0:T(8,128)(2,1)S(1)}, bf16[128,1024]{1,0:T(8,128)(2,1)S(1)}, u32[]{:S(2)}, u32[]{:S(2)}) collective-permute-start(bf16[128,1024]{1,0:T(8,128)(2,1)S(1)} %get-tuple-element.43), channel_id=1, source_target_pairs={{0,16},{1,7},{2,27},{3,6},{4,20},{5,3},{6,31},{7,2},{8,1},{9,12},{... | collective-permute-start | bytes 786440 | tf_op jit(solution)/shard_map/ppermute | solution.py:404
  146.0 11.7 %collective-permute-start.21 = (bf16[128,1024]{1,0:T(8,128)(2,1)S(1)}, bf16[128,1024]{1,0:T(8,128)(2,1)S(1)}, u32[]{:S(2)}, u32[]{:S(2)}) collective-permute-start(bf16[128,1024]{1,0:T(8,128)(2,1)S(1)} %get-tuple-element.44), channel_id=1, source_target_pairs={{0,1},{1,6},{2,26},{3,3},{4,5},{5,2},{6,30},{7,7},{8,0},{9,9},{10,... | collective-permute-start | bytes 786440 | tf_op jit(solution)/shard_map/ppermute | solution.py:404
  (16 other events, 46.7 us)

commit v4 on v3

v4 whole, which is shorter than its diff:
```python
import functools

import jax
import jax.numpy as jnp
from jax import lax
from jax.experimental import pallas as pl
from jax.experimental.pallas import tpu as pltpu
from jax.sharding import PartitionSpec as P

BROWS = 128
TILE = 64
DST = 128
SIDE = 4
CHIPS = SIDE**3
AXES = ("shard", "basis")
CORE_SWAP = [(0, 1), (1, 0)]
HOP2 = (2, 1, 3, 0)
BF16 = jnp.bfloat16
F32 = jnp.float32
SMALL = pl.CostEstimate(flops=1, bytes_accessed=1, transcendentals=0)
VMEM_SMALL = 2 * 1024 * 1024
VMEM_LIMIT = 22 * 1024 * 1024


def device_id(x, y, z, core):
    return ((z % SIDE * SIDE + y % SIDE) * SIDE + x % SIDE) * 2 + core


def pairs(target):
    found = []
    for z in range(SIDE):
        for y in range(SIDE):
            for x in range(SIDE):
                for core in range(2):
                    found.append((device_id(x, y, z, core), device_id(*target(x, y, z, core))))
    assert len({to for _, to in found}) == len(found)
    return found


def hop1_pairs(step):
    return pairs(lambda x, y, z, core: (x + step, y, z, 0) if core == 0 else (x, y + step, z, 1))


def hop2_pairs(step):
    return pairs(lambda x, y, z, core: (x, y, z + step, core))


MATCHED = ((0, 0), (2, 1), (2, 0), (0, 1))
UNMATCHED = ((1, 1), (1, 0), (3, 1), (3, 0))


def hop3_pairs(send):
    def target(x, y, z, core):
        step, half = (MATCHED if (x + y + z) % 2 == core else UNMATCHED)[send]
        return (x, y + step, z, half) if core == 0 else (x + step, y, z, half)

    return pairs(target)


def coordinates():
    chip = lax.axis_index("shard")
    return chip % SIDE, chip // SIDE % SIDE, chip // (SIDE * SIDE), lax.axis_index("basis")


def group_of(x, y, z, kind, which):
    y_end = 2 * which + (x + z) % 2
    x_end = 2 * which + (y + z + 1) % 2
    return jnp.where(kind == 0, (z * SIDE + y_end) * SIDE + x, (z * SIDE + y) * SIDE + x_end)


def notes_kernel(blocks, counts_ref, dests_ref, rels_ref, lists_ref, out_ref):
    rows = CHIPS * 8
    x, y, z, _ = coordinates()
    counts = counts_ref[...]
    before = (
        lax.broadcasted_iota(jnp.int32, (CHIPS, CHIPS), 0)
        < lax.broadcasted_iota(jnp.int32, (CHIPS, CHIPS), 1)
    ).astype(F32)
    used = jnp.broadcast_to(counts.astype(F32), (8, CHIPS))
    rank = jnp.dot(used, before, preferred_element_type=F32)[:1]
    where = jnp.where(counts > 0, rank, -1.0).astype(jnp.int32)
    row = lax.broadcasted_iota(jnp.int32, (rows, 1), 0)
    slot, place = row // 8, row % 8
    line = place % SIDE
    owner = jnp.where(
        (x + y + z) % 2 == 0,
        slot // SIDE * SIDE + line,
        slot // 16 * 16 + line * SIDE + slot % SIDE,
    )

    def lookup(values, index):
        lane = lax.broadcasted_iota(jnp.int32, (rows, values.shape[1]), 1)
        return jnp.sum(jnp.where(lane == index, values, 0), axis=1, keepdims=True)

    position = lookup(where, owner)
    hit = (position == lax.broadcasted_iota(jnp.int32, (rows, blocks), 1)).astype(BF16)
    dests = jnp.concatenate([dests_ref[:, p * BROWS : (p + 1) * BROWS] for p in range(blocks)], axis=0)
    dests = jnp.dot(hit, dests.astype(BF16), preferred_element_type=F32).astype(jnp.int32)
    codes = jnp.where(position < 0, -1, dests + jnp.where(position >= blocks // 2, DST, 0))
    block = lookup(jnp.where(counts > 0, lists_ref[...], -1), slot)
    lane = lax.broadcasted_iota(jnp.int32, (rows, DST), 1)
    other = jnp.where(lane == 0, codes, block)
    for tile in range(BROWS // TILE):
        rel = lookup(rels_ref[...], position * (BROWS // TILE) + tile)
        other = jnp.where(lane == 1 + tile, rel, other)
    out_ref[...] = jnp.where(place < SIDE, codes, other)


def make_notes(counts, dests, rels, lists):
    vmem = pl.BlockSpec(memory_space=pltpu.VMEM)
    return pl.pallas_call(
        functools.partial(notes_kernel, dests.shape[1] // BROWS),
        out_shape=jax.ShapeDtypeStruct((CHIPS * 8, DST), jnp.int32),
        in_specs=[vmem] * 4,
        out_specs=vmem,
        compiler_params=pltpu.CompilerParams(vmem_limit_bytes=VMEM_LIMIT),
        name="notes",
    )(counts, dests, rels, lists).reshape(CHIPS, 8, DST)


WORDS = 4
HOP1 = (1, 3, 2)


def word(words_ref, group, line, which):
    return words_ref[(group * SIDE + line) * WORDS + which]


def reached(step, step_z, kind, which):
    x, y, z, _ = coordinates()
    x_to = jnp.where(kind == 0, (x + step) % SIDE, x)
    y_to = jnp.where(kind == 0, y, (y + step) % SIDE)
    return group_of(x_to, y_to, (z + step_z) % SIDE, kind, which)


def local_block(words_ref, table_ref, group):
    block = word(words_ref, group, 0, WORDS - 1)
    start = pl.multiple_of(jnp.maximum(block, 0) * BROWS, BROWS)
    return block >= 0, table_ref.at[pl.ds(start, BROWS)]


def run_moves(moves):
    for live, copies in moves:

        @pl.when(live)
        def _(copies=copies):
            for copy in copies:
                copy.start()

    for live, copies in moves:

        @pl.when(live)
        def _(copies=copies):
            for copy in copies:
                copy.wait()


def in_hbm(array):
    return pltpu.with_memory_space_constraint(array, pltpu.HBM)


def in_vmem(array):
    return pltpu.with_memory_space_constraint(array, pltpu.VMEM)


SMEM_SPEC = pl.BlockSpec(memory_space=pltpu.SMEM)
HBM_SPEC = pl.BlockSpec(memory_space=pltpu.HBM)
VMEM_SPEC = pl.BlockSpec(memory_space=pltpu.VMEM)


def cross_kernel(steps_z, words_ref, table_ref, out_ref, sems):
    core = lax.axis_index("basis")
    moves = []
    for i, step_z in enumerate(steps_z):
        for step in range(SIDE):
            for which in range(2):
                live, source = local_block(words_ref, table_ref, reached(step, step_z, 1 - core, which))
                at = (i, step, which)
                moves.append((live, (pltpu.make_async_copy(source, out_ref.at[at], sems.at[at]),)))
    run_moves(moves)


def cross(steps_z, words, table):
    shape = (len(steps_z), SIDE, 2, BROWS, table.shape[1])
    return pl.pallas_call(
        functools.partial(cross_kernel, steps_z),
        out_shape=pltpu.VMEM(shape, BF16),
        in_specs=[SMEM_SPEC, HBM_SPEC],
        out_specs=VMEM_SPEC,
        scratch_shapes=[pltpu.SemaphoreType.DMA((len(steps_z), SIDE, 2))],
        compiler_params=pltpu.CompilerParams(vmem_limit_bytes=VMEM_SMALL),
        cost_estimate=SMALL,
        name="cross",
    )(words, in_hbm(table))


def pick_kernel(step_z, row, words_ref, table_ref, crossed_ref, *rest):
    outs, sems = rest[: len(HOP1)], rest[len(HOP1)]
    core = lax.axis_index("basis")
    moves = []
    for i, step in enumerate(HOP1):
        for which in range(2):
            live, source = local_block(words_ref, table_ref, reached(step, step_z, core, which))
            copies = (
                pltpu.make_async_copy(source, outs[i].at[which, 0], sems.at[0, i, which]),
                pltpu.make_async_copy(crossed_ref.at[row, step, which], outs[i].at[which, 1], sems.at[1, i, which]),
            )
            moves.append((live, copies))
    run_moves(moves)


def pick(step_z, row, words, table, crossed):
    return pl.pallas_call(
        functools.partial(pick_kernel, step_z, row),
        out_shape=[pltpu.VMEM((2, 2, BROWS, table.shape[1]), BF16)] * len(HOP1),
        in_specs=[SMEM_SPEC, HBM_SPEC, VMEM_SPEC],
        out_specs=[VMEM_SPEC] * len(HOP1),
        scratch_shapes=[pltpu.SemaphoreType.DMA((2, len(HOP1), 2))],
        compiler_params=pltpu.CompilerParams(vmem_limit_bytes=VMEM_SMALL),
        cost_estimate=SMALL,
        name="pick",
    )(words, in_hbm(table), in_vmem(crossed))


def project_kernel(step_z, row, words_ref, table_ref, notes_ref, coeffs_ref, crossed_ref, *rest):
    received, rest = rest[: len(HOP1)], rest[len(HOP1) :]
    own_basis, other_basis, out_ref, local, total, sems = rest
    x, y, z, core = coordinates()
    width = table_ref.shape[1]
    along = jnp.where(core == 0, x, y)
    pieces = []
    for which in range(2):
        group = reached(0, step_z, core, which)
        for step in HOP1 + (0,):
            line = (along - step) % SIDE
            code = word(words_ref, group, line, 0)
            rels = [word(words_ref, group, line, 1 + tile) for tile in range(2)]
            copy = None
            if step == 0:
                copy = pltpu.make_async_copy(
                    local_block(words_ref, table_ref, group)[1], local.at[which], sems.at[which]
                )
                pl.when(code >= 0)(copy.start)
            pieces.append((which, step, group, line, code, rels, copy))
    total[...] = jnp.zeros_like(total)
    lane = lax.broadcasted_iota(jnp.int32, (2, BROWS), 1)
    dest = lax.broadcasted_iota(jnp.int32, (DST, BROWS), 0)
    for which, step, group, line, code, rels, copy in pieces:

        @pl.when(code >= 0)
        def _(which=which, step=step, group=group, line=line, code=code, rels=rels, copy=copy):
            half = jnp.where(code >= DST, 1, 0)
            hit = notes_ref[group, pl.ds(line, 1), :] - half * DST == dest
            coef = [
                jnp.sum(
                    jnp.where(lane == rels[tile] % DST, coeffs_ref[rels[tile] // DST], 0.0), axis=1, keepdims=True
                )
                for tile in range(2)
            ]
            weights = jnp.where(lane < TILE, coef[0], coef[1])
            chosen = []
            for k in range(2):
                weight = jnp.where(core == 0, weights[k : k + 1], weights[1 - k : 2 - k])
                high = weight.astype(BF16).astype(F32)
                high, low = jnp.where(hit, high, 0.0), jnp.where(hit, weight - high, 0.0)
                chosen.append(jnp.concatenate([high, low], axis=1))
            chosen = jnp.concatenate(chosen, axis=0).astype(BF16)
            for part in range(2):
                if step > 0:
                    block = received[HOP1.index(step)][which, part]
                elif part == 1:
                    block = crossed_ref[row, 0, which]
                else:
                    copy.wait()
                    block = local[which]
                added = jnp.dot(
                    chosen, jnp.concatenate([block, block], axis=0), preferred_element_type=F32
                )
                column = pl.multiple_of(jnp.where(core == part, 0, width), width)
                total[which, half, :, pl.ds(column, width)] += added

    summed = [
        total[:, :, k * DST : (k + 1) * DST, :].reshape(4 * DST, 2 * width).astype(BF16) for k in range(2)
    ]
    wide = own_basis.shape[1]
    tile = 256
    for start in range(0, wide, tile):
        result = jnp.dot(summed[0], own_basis[:, start : start + tile], preferred_element_type=F32)
        result += jnp.dot(summed[1], other_basis[:, start : start + tile], preferred_element_type=F32)
        out_ref[:, :, start : start + tile] = result.reshape(4, DST, tile).astype(BF16)


def project(step_z, row, words, table, *others):
    width = table.shape[1]
    wide = others[-1].shape[1]
    return pl.pallas_call(
        functools.partial(project_kernel, step_z, row),
        out_shape=pltpu.VMEM((4, DST, wide), BF16),
        in_specs=[SMEM_SPEC, HBM_SPEC] + [VMEM_SPEC] * len(others),
        out_specs=VMEM_SPEC,
        scratch_shapes=[
            pltpu.VMEM((2, BROWS, width), BF16),
            pltpu.VMEM((2, 2, 2 * DST, 2 * width), F32),
            pltpu.SemaphoreType.DMA((2,)),
        ],
        cost_estimate=SMALL,
        compiler_params=pltpu.CompilerParams(vmem_limit_bytes=VMEM_LIMIT),
        name="project",
    )(words, in_hbm(table), *map(in_vmem, others))


def merge_kernel(order_ref, *refs):
    ins, outs = refs[:SIDE], refs[SIDE:]
    for send in range(4):
        at = order_ref[send]
        result = ins[0][at].astype(F32)
        for other in ins[1:]:
            result += other[at].astype(F32)
        outs[send][...] = result.astype(BF16)


def merge(order, parts):
    return pl.pallas_call(
        merge_kernel,
        out_shape=[pltpu.VMEM(parts[0].shape[1:], BF16)] * 4,
        in_specs=[SMEM_SPEC] + [VMEM_SPEC] * SIDE,
        out_specs=[VMEM_SPEC] * 4,
        compiler_params=pltpu.CompilerParams(vmem_limit_bytes=VMEM_LIMIT),
        cost_estimate=SMALL,
        name="merge",
    )(order, *map(in_vmem, parts))


def body(features, bases, coeffs, block_lists, block_counts, tile_rel, dest_ids):
    x, y, z, core = coordinates()
    blocks = tile_rel.shape[1] * TILE // BROWS
    other_basis = lax.ppermute(bases[0], "basis", CORE_SWAP)

    sent = make_notes(block_counts, dest_ids, tile_rel, block_lists.reshape(1, CHIPS))
    notes = lax.all_to_all(sent, "shard", split_axis=0, concat_axis=0, tiled=True)
    words = notes[:, SIDE:, :WORDS].reshape(-1)
    rels = -(-coeffs.shape[0] // DST) * DST
    table = jnp.pad(coeffs.T, ((0, 0), (0, rels - coeffs.shape[0]))).reshape(2, -1, DST).transpose(1, 0, 2)

    words, other_basis = lax.optimization_barrier((words, other_basis))
    groups = HOP2[:1], HOP2[1:]
    first = cross(groups[0], words, features)
    first, later = lax.optimization_barrier((first, words))
    second = cross(groups[1], later, features)
    first = lax.ppermute(first, "basis", CORE_SWAP)
    first, second = lax.optimization_barrier((first, second))
    crossed = first, lax.ppermute(second, "basis", CORE_SWAP)
    crossed = {s: (steps.index(s), buf) for steps, buf in zip(groups, crossed) for s in steps}

    arrived, parts, later = [], [], words
    for i, step_z in enumerate(HOP2):
        row, buf = crossed[step_z]
        picked = pick(step_z, row, later, features, buf)
        picked, later = lax.optimization_barrier((picked, later))
        if i > 0:
            picked, arrived[-1] = lax.optimization_barrier((picked, arrived[-1]))
        if i == 3:
            picked, parts[0] = lax.optimization_barrier((picked, parts[0]))
        arrived.append([lax.ppermute(buf, AXES, hop1_pairs(step)) for step, buf in zip(HOP1, picked)])
        part = project(step_z, row, words, features, notes, table, buf, *arrived[i], bases[0], other_basis)
        parts.append(part if step_z == 0 else lax.ppermute(part, AXES, hop2_pairs(step_z)))

    last = jnp.where(core == 0, y, x)
    matched = (x + y + z) % 2 == core
    order = jnp.stack(
        [
            jnp.where(matched, (last + a) % SIDE // 2 * 2 + b, (last + c) % SIDE // 2 * 2 + d)
            for (a, b), (c, d) in zip(MATCHED, UNMATCHED)
        ]
    )
    merged = merge(order, parts)
    ends = [lax.ppermute(buf, AXES, hop3_pairs(send)) for send, buf in enumerate(merged)]
    summed = sum(end.astype(F32) for end in ends)

    rows_dev = blocks // 2 * BROWS
    my_dests = lax.dynamic_slice_in_dim(dest_ids[0], core * rows_dev, rows_dev)
    indegree = jnp.sum(
        (my_dests[None, :] == jnp.arange(DST, dtype=jnp.int32)[:, None]).astype(F32), axis=1
    )
    return (summed / jnp.maximum(indegree, 1.0)[:, None]).astype(BF16)


def solution(mesh):
    placed = (
        P("shard", "basis"),
        P("basis", None, None),
        P(),
        P("shard", None, None),
        P("shard", None),
        P("shard", None),
        P("shard", None),
    )
    return jax.shard_map(
        body, mesh=mesh, in_specs=placed, out_specs=P(("shard", "basis"), None), check_vma=False
    )
```

time: 159 us -> 141 us (0.89)
  local copies, waits for them, and re-layouts: 23.7 us -> 7.05 us
  Pallas kernels: 48.3 us -> 38.1 us
  waiting for transfers between devices: 34.3 us -> 43.7 us
    unnamed x36 -> x26, local copies, waits for them, and re-layouts: 22 us -> 6.83 us
    ppermute x14, waiting for transfers between devices: 24.7 us -> 34.4 us  [the longest x12 33.5 us: body(): lax.ppermute(buf, AXES, hop1_pairs(step))]
    pallas_call x7, Pallas kernels: 21 us -> 14.7 us  [the longest x4 8.6 us: pick(): pl.pallas_call(functools.partial(pick_kernel, step_z, row), out_shape=[pl...]
    pallas_call x4, Pallas kernels: 25.1 us -> 22.6 us  [project(): pl.pallas_call(functools.partial(project_kernel, step_z, row), out_shape=...]
  transfers between devices with their start and end apart: 22 -> 22, of which waited for: 6 -> 12; matrix products, arithmetic and copies ran while one was open for 1% -> 0% of each run, Pallas kernels for 25% -> 24%
where the time goes in v4:
time: 141 us
  waiting for transfers between devices  43.7 us (31%)
  Pallas kernels  38.1 us (27%)
  starting transfers between devices  29.1 us (21%)
  blocking collectives  21.1 us (15%)
  local copies, waits for them, and re-layouts  7.05 us (5%)
    ppermute x12, waiting for transfers between devices, body(): lax.ppermute(buf, AXES, hop1_pairs(step))  33.5 us
    pallas_call x4, Pallas kernels, project(): pl.pallas_call(functools.partial(project_kernel, step_z, row), out_shape=...  22.6 us
    all_to_all x1, blocking collectives, body(): lax.all_to_all(sent, 'shard', split_axis=0, concat_axis=0, tiled=True)  21.1 us
    ppermute x12, starting transfers between devices, body(): lax.ppermute(buf, AXES, hop1_pairs(step))  13.6 us
    ppermute x4, starting transfers between devices, body(): lax.ppermute(buf, AXES, hop3_pairs(send))  11.1 us
    ppermute x4, waiting for transfers between devices, body(): lax.ppermute(buf, AXES, hop3_pairs(send))  9.28 us
    pallas_call x4, Pallas kernels, pick(): pl.pallas_call(functools.partial(pick_kernel, step_z, row), out_shape=[pl...  8.6 us
    unnamed x26, local copies, waits for them, and re-layouts  6.83 us
  transfers between devices with their start and end apart: 22, of which 12 were waited for; matrix products, arithmetic and copies ran while one was open for 0% of the time, Pallas kernels for 24%

profile of v4, /device:TPU:1, one launch (start us, length us, event | category | flops | bytes accessed | tf_op | source)
XLA Modules:
  0.0 140.5 jit_solution(11088357727716583416)
XLA Ops:
  4.9 21.1 %all_to_all.5.notes_ref = s32[64,8,128]{2,1,0:T(8,128)S(1)} all-to-all(s32[64,8,128]{2,1,0:T(8,128)S(1)} %bitcast.17), channel_id=1, replica_groups=mesh['shard'=64,'basis'=2] {'shard'}, dimensions={0} | all-to-all | bytes 524288 | tf_op jit(solution)/shard_map/all_to_all | solution.py:340
  29.5 2.2 %cross.3 = bf16[3,4,2,128,512]{4,3,2,1,0:T(8,128)(2,1)S(1)} custom-call(s32[1024]{0:T(1024)S(1)} %reshape.19.words_ref, bf16[6144,512]{1,0:T(8,128)(2,1)} %table_ref.19), custom_call_target="tpu_custom_call" | custom-call | flops 1 | bytes 1 | tf_op jit(solution)/shard_map/cross/pallas_call | solution.py:185
  34.2 2.4 %collective-permute-start.4 = (bf16[2,2,128,512]{3,2,1,0:T(8,128)(2,1)S(1)}, bf16[2,2,128,512]{3,2,1,0:T(8,128)(2,1)S(1)}, u32[]{:S(2)}, u32[]{:S(2)}) collective-permute-start(bf16[2,2,128,512]{3,2,1,0:T(8,128)(2,1)S(1)} %get-tuple-element.85), channel_id=1, source_target_pairs={{0,6},{1,25},{2,0},{3,27},{4,2},{5,29},{6,4},{7,31},{8,14},{9,1},{... | collective-permute-start | bytes 1572872 | tf_op jit(solution)/shard_map/ppermute | solution.py:364
  39.2 9.9 %collective-permute-done.3.rest_0_ = bf16[2,2,128,512]{3,2,1,0:T(8,128)(2,1)S(1)} collective-permute-done((bf16[2,2,128,512]{3,2,1,0:T(8,128)(2,1)S(1)}, bf16[2,2,128,512]{3,2,1,0:T(8,128)(2,1)S(1)}, u32[]{:S(2)}, u32[]{:S(2)}) %collective-permute-start.3) | collective-permute-done | bytes 524320 | tf_op jit(solution)/shard_map/ppermute | solution.py:364
  49.7 2.1 %collective-permute-start.7 = (bf16[2,2,128,512]{3,2,1,0:T(8,128)(2,1)S(1)}, bf16[2,2,128,512]{3,2,1,0:T(8,128)(2,1)S(1)}, u32[]{:S(2)}, u32[]{:S(2)}) collective-permute-start(bf16[2,2,128,512]{3,2,1,0:T(8,128)(2,1)S(1)} %get-tuple-element.88), channel_id=1, source_target_pairs={{0,6},{1,25},{2,0},{3,27},{4,2},{5,29},{6,4},{7,31},{8,14},{9,1},{... | collective-permute-start | bytes 1572872 | tf_op jit(solution)/shard_map/ppermute | solution.py:364
  52.7 4.6 %project.4 = bf16[4,128,1024]{2,1,0:T(8,128)(2,1)S(1)} custom-call(s32[1024]{0:T(1024)S(1)} %reshape.19.words_ref, bf16[6144,512]{1,0:T(8,128)(2,1)} %table_ref.19, s32[64,8,128]{2,1,0:T(8,128)S(1)} %all_to_all.5.notes_ref, f32[116,2,128]{2,1,0:T(2,128)S(1)} %pad_bitcast_fusion.coeffs_ref, ...), custom_call_target="tpu_custom_call" | custom-call | flops 1 | bytes 1 | tf_op jit(solution)/shard_map/project/pallas_call | solution.py:296
  57.8 2.3 %pick.6 = (bf16[2,2,128,512]{3,2,1,0:T(8,128)(2,1)S(1)}, bf16[2,2,128,512]{3,2,1,0:T(8,128)(2,1)S(1)}, bf16[2,2,128,512]{3,2,1,0:T(8,128)(2,1)S(1)}) custom-call(s32[1024]{0:T(1024)S(1)} %reshape.19.words_ref, bf16[6144,512]{1,0:T(8,128)(2,1)} %table_ref.19, bf16[3,4,2,128,512]{4,3,2,1,0:T(8,128)(2,1)S(1)} %collective-permute-done.2.crossed_ref), custom_call_target="tpu_custom_call" | custom-call | flops 1 | bytes 1 | tf_op jit(solution)/shard_map/pick/pallas_call | solution.py:213
  60.1 3.4 %collective-permute-done.7.rest_1_ = bf16[2,2,128,512]{3,2,1,0:T(8,128)(2,1)S(1)} collective-permute-done((bf16[2,2,128,512]{3,2,1,0:T(8,128)(2,1)S(1)}, bf16[2,2,128,512]{3,2,1,0:T(8,128)(2,1)S(1)}, u32[]{:S(2)}, u32[]{:S(2)}) %collective-permute-start.7) | collective-permute-done | bytes 524320 | tf_op jit(solution)/shard_map/ppermute | solution.py:364
  68.2 6.4 %project.5 = bf16[4,128,1024]{2,1,0:T(8,128)(2,1)} custom-call(s32[1024]{0:T(1024)S(1)} %reshape.19.words_ref, bf16[6144,512]{1,0:T(8,128)(2,1)} %table_ref.19, s32[64,8,128]{2,1,0:T(8,128)S(1)} %all_to_all.5.notes_ref, f32[116,2,128]{2,1,0:T(2,128)S(1)} %pad_bitcast_fusion.coeffs_ref, bf16[3,4,2,128,512]{4,3,2,1,0:T(8,128)(2,1)S(1)} %collective-permute-done.2.crossed_ref, ...), custom_call_target="tpu_custom_call" | custom-call | flops 1 | bytes 1 | tf_op jit(solution)/shard_map/project/pallas_call | solution.py:296
  74.7 4.9 %collective-permute-done.10.rest_1_ = bf16[2,2,128,512]{3,2,1,0:T(8,128)(2,1)S(1)} collective-permute-done((bf16[2,2,128,512]{3,2,1,0:T(8,128)(2,1)S(1)}, bf16[2,2,128,512]{3,2,1,0:T(8,128)(2,1)S(1)}, u32[]{:S(2)}, u32[]{:S(2)}) %collective-permute-start.10) | collective-permute-done | bytes 524320 | tf_op jit(solution)/shard_map/ppermute | solution.py:364
  80.6 6.4 %project.6 = bf16[4,128,1024]{2,1,0:T(8,128)(2,1)} custom-call(s32[1024]{0:T(1024)S(1)} %reshape.19.words_ref, bf16[6144,512]{1,0:T(8,128)(2,1)} %table_ref.19, s32[64,8,128]{2,1,0:T(8,128)S(1)} %all_to_all.5.notes_ref, f32[116,2,128]{2,1,0:T(2,128)S(1)} %pad_bitcast_fusion.coeffs_ref, bf16[3,4,2,128,512]{4,3,2,1,0:T(8,128)(2,1)S(1)} %collective-permute-done.2.crossed_ref, ...), custom_call_target="tpu_custom_call" | custom-call | flops 1 | bytes 1 | tf_op jit(solution)/shard_map/project/pallas_call | solution.py:296
  87.6 2.9 %pick.7 = (bf16[2,2,128,512]{3,2,1,0:T(8,128)(2,1)}, bf16[2,2,128,512]{3,2,1,0:T(8,128)(2,1)}, bf16[2,2,128,512]{3,2,1,0:T(8,128)(2,1)}) custom-call(s32[1024]{0:T(1024)S(1)} %reshape.19.words_ref, bf16[6144,512]{1,0:T(8,128)(2,1)} %table_ref.19, bf16[3,4,2,128,512]{4,3,2,1,0:T(8,128)(2,1)S(1)} %collective-permute-done.2.crossed_ref), custom_call_target="tpu_custom_call" | custom-call | flops 1 | bytes 1 | tf_op jit(solution)/shard_map/pick/pallas_call | solution.py:213
  95.9 5.9 %collective-permute-done.15.rest_0_ = bf16[2,2,128,512]{3,2,1,0:T(8,128)(2,1)} collective-permute-done((bf16[2,2,128,512]{3,2,1,0:T(8,128)(2,1)}, bf16[2,2,128,512]{3,2,1,0:T(8,128)(2,1)}, u32[]{:S(2)}, u32[]{:S(2)}) %collective-permute-start.15) | collective-permute-done | bytes 524320 | tf_op jit(solution)/shard_map/ppermute | solution.py:364
  101.8 4.9 %collective-permute-done.16.rest_1_ = bf16[2,2,128,512]{3,2,1,0:T(8,128)(2,1)} collective-permute-done((bf16[2,2,128,512]{3,2,1,0:T(8,128)(2,1)}, bf16[2,2,128,512]{3,2,1,0:T(8,128)(2,1)}, u32[]{:S(2)}, u32[]{:S(2)}) %collective-permute-start.16) | collective-permute-done | bytes 524320 | tf_op jit(solution)/shard_map/ppermute | solution.py:364
  106.7 1.9 %collective-permute-done.17.rest_2_ = bf16[2,2,128,512]{3,2,1,0:T(8,128)(2,1)} collective-permute-done((bf16[2,2,128,512]{3,2,1,0:T(8,128)(2,1)}, bf16[2,2,128,512]{3,2,1,0:T(8,128)(2,1)}, u32[]{:S(2)}, u32[]{:S(2)}) %collective-permute-start.17) | collective-permute-done | bytes 524320 | tf_op jit(solution)/shard_map/ppermute | solution.py:364
  111.8 5.2 %project.7.refs_3_ = bf16[4,128,1024]{2,1,0:T(8,128)(2,1)S(1)} custom-call(s32[1024]{0:T(1024)S(1)} %reshape.19.words_ref, bf16[6144,512]{1,0:T(8,128)(2,1)} %table_ref.19, s32[64,8,128]{2,1,0:T(8,128)S(1)} %all_to_all.5.notes_ref, f32[116,2,128]{2,1,0:T(2,128)S(1)} %pad_bitcast_fusion.coeffs_ref, ...), custom_call_target="tpu_custom_call" | custom-call | flops 1 | bytes 1 | tf_op jit(solution)/shard_map/project/pallas_call | solution.py:296
  117.0 2.1 %merge.1 = (bf16[128,1024]{1,0:T(8,128)(2,1)S(1)}, bf16[128,1024]{1,0:T(8,128)(2,1)S(1)}, bf16[128,1024]{1,0:T(8,128)(2,1)S(1)}, bf16[128,1024]{1,0:T(8,128)(2,1)S(1)}) custom-call(s32[4]{0:T(128)S(1)} %pad_add_fusion.order_ref, bf16[4,128,1024]{2,1,0:T(8,128)(2,1)S(1)} %copy-done.6, bf16[4,128,1024]{2,1,0:T(8,128)(2,1)} %collective-permute-done.13.refs_1_, ...), custom_call_target="tpu_custom_call" | custom-call | flops 1 | bytes 1 | tf_op jit(solution)/shard_map/merge/pallas_call | solution.py:323
  119.1 1.9 %collective-permute-start.18 = (bf16[128,1024]{1,0:T(8,128)(2,1)S(1)}, bf16[128,1024]{1,0:T(8,128)(2,1)S(1)}, u32[]{:S(2)}, u32[]{:S(2)}) collective-permute-start(bf16[128,1024]{1,0:T(8,128)(2,1)S(1)} %get-tuple-element.101), channel_id=1, source_target_pairs={{0,0},{1,3},{2,11},{3,2},{4,4},{5,7},{6,15},{7,6},{8,17},{9,8},{10... | collective-permute-start | bytes 786440 | tf_op jit(solution)/shard_map/ppermute | solution.py:377
  121.0 4.7 %collective-permute-start.19 = (bf16[128,1024]{1,0:T(8,128)(2,1)S(1)}, bf16[128,1024]{1,0:T(8,128)(2,1)S(1)}, u32[]{:S(2)}, u32[]{:S(2)}) collective-permute-start(bf16[128,1024]{1,0:T(8,128)(2,1)S(1)} %get-tuple-element.102), channel_id=1, source_target_pairs={{0,17},{1,2},{2,10},{3,7},{4,21},{5,6},{6,14},{7,3},{8,16},{9,13},... | collective-permute-start | bytes 786440 | tf_op jit(solution)/shard_map/ppermute | solution.py:377
  125.7 2.5 %collective-permute-start.20 = (bf16[128,1024]{1,0:T(8,128)(2,1)S(1)}, bf16[128,1024]{1,0:T(8,128)(2,1)S(1)}, u32[]{:S(2)}, u32[]{:S(2)}) collective-permute-start(bf16[128,1024]{1,0:T(8,128)(2,1)S(1)} %get-tuple-element.103), channel_id=1, source_target_pairs={{0,16},{1,7},{2,27},{3,6},{4,20},{5,3},{6,31},{7,2},{8,1},{9,12},{... | collective-permute-start | bytes 786440 | tf_op jit(solution)/shard_map/ppermute | solution.py:377
  128.2 1.9 %collective-permute-start.21 = (bf16[128,1024]{1,0:T(8,128)(2,1)S(1)}, bf16[128,1024]{1,0:T(8,128)(2,1)S(1)}, u32[]{:S(2)}, u32[]{:S(2)}) collective-permute-start(bf16[128,1024]{1,0:T(8,128)(2,1)S(1)} %get-tuple-element.104), channel_id=1, source_target_pairs={{0,1},{1,6},{2,26},{3,3},{4,5},{5,2},{6,30},{7,7},{8,0},{9,9},{10,... | collective-permute-start | bytes 786440 | tf_op jit(solution)/shard_map/ppermute | solution.py:377
  130.4 3.7 %collective-permute-done.18 = bf16[128,1024]{1,0:T(8,128)(2,1)S(1)} collective-permute-done((bf16[128,1024]{1,0:T(8,128)(2,1)S(1)}, bf16[128,1024]{1,0:T(8,128)(2,1)S(1)}, u32[]{:S(2)}, u32[]{:S(2)}) %collective-permute-start.18) | collective-permute-done | bytes 262176 | tf_op jit(solution)/shard_map/ppermute | solution.py:377
  134.0 2.8 %collective-permute-done.20 = bf16[128,1024]{1,0:T(8,128)(2,1)S(1)} collective-permute-done((bf16[128,1024]{1,0:T(8,128)(2,1)S(1)}, bf16[128,1024]{1,0:T(8,128)(2,1)S(1)}, u32[]{:S(2)}, u32[]{:S(2)}) %collective-permute-start.20) | collective-permute-done | bytes 262176 | tf_op jit(solution)/shard_map/ppermute | solution.py:377
  136.8 2.8 %collective-permute-done.21 = bf16[128,1024]{1,0:T(8,128)(2,1)S(1)} collective-permute-done((bf16[128,1024]{1,0:T(8,128)(2,1)S(1)}, bf16[128,1024]{1,0:T(8,128)(2,1)S(1)}, u32[]{:S(2)}, u32[]{:S(2)}) %collective-permute-start.21) | collective-permute-done | bytes 262176 | tf_op jit(solution)/shard_map/ppermute | solution.py:377
  (67 shorter events, 31.3 us)
Async XLA Ops:
  0.0 26.2 %collective-permute-start = (bf16[1024,1024]{1,0:T(8,128)(2,1)}, bf16[1024,1024]{1,0:T(8,128)(2,1)S(1)}, u32[]{:S(2)}, u32[]{:S(2)}) collective-permute-start(bf16[1024,1024]{1,0:T(8,128)(2,1)} %bitcast.12), channel_id=1, source_target_pairs={{0,1},{1,0},{2,3},{3,2},{4,5},{5,4},{6,7},{7,6},{8,9},{9,8},{10,11... | collective-permute-start | bytes 6291464 | tf_op jit(solution)/shard_map/ppermute | solution.py:337
  28.1 3.7 %collective-permute-start.1 = (bf16[1,4,2,128,512]{4,3,2,1,0:T(8,128)(2,1)S(1)}, bf16[1,4,2,128,512]{4,3,2,1,0:T(8,128)(2,1)S(1)}, u32[]{:S(2)}, u32[]{:S(2)}) collective-permute-start(bf16[1,4,2,128,512]{4,3,2,1,0:T(8,128)(2,1)S(1)} %cross.2), channel_id=1, source_target_pairs={{0,1},{1,0},{2,3},{3,2},{4,5},{5,4},{6,7},{7,6},{8,9},{9,8},{10,11... | collective-permute-start | bytes 3145736 | tf_op jit(solution)/shard_map/ppermute | solution.py:350
  31.8 5.7 %collective-permute-start.2 = (bf16[3,4,2,128,512]{4,3,2,1,0:T(8,128)(2,1)S(1)}, bf16[3,4,2,128,512]{4,3,2,1,0:T(8,128)(2,1)S(1)}, u32[]{:S(2)}, u32[]{:S(2)}) collective-permute-start(bf16[3,4,2,128,512]{4,3,2,1,0:T(8,128)(2,1)S(1)} %cross.3), channel_id=1, source_target_pairs={{0,1},{1,0},{2,3},{3,2},{4,5},{5,4},{6,7},{7,6},{8,9},{9,8},{10,11... | collective-permute-start | bytes 9437192 | tf_op jit(solution)/shard_map/ppermute | solution.py:352
  33.9 18.8 %copy-start = (bf16[1,1024,1024]{2,1,0:T(8,128)(2,1)S(1)}, bf16[1,1024,1024]{2,1,0:T(8,128)(2,1)}, u32[]{:S(2)}) copy-start(bf16[1,1024,1024]{2,1,0:T(8,128)(2,1)} %param.8) | copy-start | bytes 6291460
  33.9 18.8 %copy-start.3 = (bf16[1024,1024]{1,0:T(8,128)(2,1)S(1)}, bf16[1024,1024]{1,0:T(8,128)(2,1)}, u32[]{:S(2)}) copy-start(bf16[1024,1024]{1,0:T(8,128)(2,1)} %copy-done.2) | copy-start | bytes 6291460
  33.9 15.2 %collective-permute-start.3 = (bf16[2,2,128,512]{3,2,1,0:T(8,128)(2,1)S(1)}, bf16[2,2,128,512]{3,2,1,0:T(8,128)(2,1)S(1)}, u32[]{:S(2)}, u32[]{:S(2)}) collective-permute-start(bf16[2,2,128,512]{3,2,1,0:T(8,128)(2,1)S(1)} %get-tuple-element.84), channel_id=1, source_target_pairs={{0,2},{1,9},{2,4},{3,11},{4,6},{5,13},{6,0},{7,15},{8,10},{9,17},{... | collective-permute-start | bytes 1572872 | tf_op jit(solution)/shard_map/ppermute | solution.py:364
  34.2 14.9 %collective-permute-start.4 = (bf16[2,2,128,512]{3,2,1,0:T(8,128)(2,1)S(1)}, bf16[2,2,128,512]{3,2,1,0:T(8,128)(2,1)S(1)}, u32[]{:S(2)}, u32[]{:S(2)}) collective-permute-start(bf16[2,2,128,512]{3,2,1,0:T(8,128)(2,1)S(1)} %get-tuple-element.85), channel_id=1, source_target_pairs={{0,6},{1,25},{2,0},{3,27},{4,2},{5,29},{6,4},{7,31},{8,14},{9,1},{... | collective-permute-start | bytes 1572872 | tf_op jit(solution)/shard_map/ppermute | solution.py:364
  36.7 12.5 %collective-permute-start.5 = (bf16[2,2,128,512]{3,2,1,0:T(8,128)(2,1)S(1)}, bf16[2,2,128,512]{3,2,1,0:T(8,128)(2,1)S(1)}, u32[]{:S(2)}, u32[]{:S(2)}) collective-permute-start(bf16[2,2,128,512]{3,2,1,0:T(8,128)(2,1)S(1)} %get-tuple-element.86), channel_id=1, source_target_pairs={{0,4},{1,17},{2,6},{3,19},{4,0},{5,21},{6,2},{7,23},{8,12},{9,25},... | collective-permute-start | bytes 1572872 | tf_op jit(solution)/shard_map/ppermute | solution.py:364
  49.1 11.0 %collective-permute-start.6 = (bf16[2,2,128,512]{3,2,1,0:T(8,128)(2,1)S(1)}, bf16[2,2,128,512]{3,2,1,0:T(8,128)(2,1)S(1)}, u32[]{:S(2)}, u32[]{:S(2)}) collective-permute-start(bf16[2,2,128,512]{3,2,1,0:T(8,128)(2,1)S(1)} %get-tuple-element.87), channel_id=1, source_target_pairs={{0,2},{1,9},{2,4},{3,11},{4,6},{5,13},{6,0},{7,15},{8,10},{9,17},{... | collective-permute-start | bytes 1572872 | tf_op jit(solution)/shard_map/ppermute | solution.py:364
  49.7 13.8 %collective-permute-start.7 = (bf16[2,2,128,512]{3,2,1,0:T(8,128)(2,1)S(1)}, bf16[2,2,128,512]{3,2,1,0:T(8,128)(2,1)S(1)}, u32[]{:S(2)}, u32[]{:S(2)}) collective-permute-start(bf16[2,2,128,512]{3,2,1,0:T(8,128)(2,1)S(1)} %get-tuple-element.88), channel_id=1, source_target_pairs={{0,6},{1,25},{2,0},{3,27},{4,2},{5,29},{6,4},{7,31},{8,14},{9,1},{... | collective-permute-start | bytes 1572872 | tf_op jit(solution)/shard_map/ppermute | solution.py:364
  51.8 13.4 %collective-permute-start.8 = (bf16[2,2,128,512]{3,2,1,0:T(8,128)(2,1)S(1)}, bf16[2,2,128,512]{3,2,1,0:T(8,128)(2,1)S(1)}, u32[]{:S(2)}, u32[]{:S(2)}) collective-permute-start(bf16[2,2,128,512]{3,2,1,0:T(8,128)(2,1)S(1)} %get-tuple-element.89), channel_id=1, source_target_pairs={{0,4},{1,17},{2,6},{3,19},{4,0},{5,21},{6,2},{7,23},{8,12},{9,25},... | collective-permute-start | bytes 1572872 | tf_op jit(solution)/shard_map/ppermute | solution.py:364
  57.4 33.1 %collective-permute-start.12 = (bf16[4,128,1024]{2,1,0:T(8,128)(2,1)S(1)}, bf16[4,128,1024]{2,1,0:T(8,128)(2,1)S(1)}, u32[]{:S(2)}, u32[]{:S(2)}) collective-permute-start(bf16[4,128,1024]{2,1,0:T(8,128)(2,1)S(1)} %project.4), channel_id=1, source_target_pairs={{0,64},{1,65},{2,66},{3,67},{4,68},{5,69},{6,70},{7,71},{8,72},{9,... | collective-permute-start | bytes 3145736 | tf_op jit(solution)/shard_map/ppermute | solution.py:366
  65.2 9.6 %collective-permute-start.9 = (bf16[2,2,128,512]{3,2,1,0:T(8,128)(2,1)S(1)}, bf16[2,2,128,512]{3,2,1,0:T(8,128)(2,1)S(1)}, u32[]{:S(2)}, u32[]{:S(2)}) collective-permute-start(bf16[2,2,128,512]{3,2,1,0:T(8,128)(2,1)S(1)} %get-tuple-element.90), channel_id=1, source_target_pairs={{0,2},{1,9},{2,4},{3,11},{4,6},{5,13},{6,0},{7,15},{8,10},{9,17},{... | collective-permute-start | bytes 1572872 | tf_op jit(solution)/shard_map/ppermute | solution.py:364
  66.0 13.6 %collective-permute-start.10 = (bf16[2,2,128,512]{3,2,1,0:T(8,128)(2,1)S(1)}, bf16[2,2,128,512]{3,2,1,0:T(8,128)(2,1)S(1)}, u32[]{:S(2)}, u32[]{:S(2)}) collective-permute-start(bf16[2,2,128,512]{3,2,1,0:T(8,128)(2,1)S(1)} %get-tuple-element.91), channel_id=1, source_target_pairs={{0,6},{1,25},{2,0},{3,27},{4,2},{5,29},{6,4},{7,31},{8,14},{9,1},{... | collective-permute-start | bytes 1572872 | tf_op jit(solution)/shard_map/ppermute | solution.py:364
  67.9 12.8 %collective-permute-start.11 = (bf16[2,2,128,512]{3,2,1,0:T(8,128)(2,1)S(1)}, bf16[2,2,128,512]{3,2,1,0:T(8,128)(2,1)S(1)}, u32[]{:S(2)}, u32[]{:S(2)}) collective-permute-start(bf16[2,2,128,512]{3,2,1,0:T(8,128)(2,1)S(1)} %get-tuple-element.92), channel_id=1, source_target_pairs={{0,4},{1,17},{2,6},{3,19},{4,0},{5,21},{6,2},{7,23},{8,12},{9,25},... | collective-permute-start | bytes 1572872 | tf_op jit(solution)/shard_map/ppermute | solution.py:364
  74.5 42.5 %collective-permute-start.13 = (bf16[4,128,1024]{2,1,0:T(8,128)(2,1)}, bf16[4,128,1024]{2,1,0:T(8,128)(2,1)}, u32[]{:S(2)}, u32[]{:S(2)}) collective-permute-start(bf16[4,128,1024]{2,1,0:T(8,128)(2,1)} %project.5), channel_id=1, source_target_pairs={{0,32},{1,33},{2,34},{3,35},{4,36},{5,37},{6,38},{7,39},{8,40},{9,... | collective-permute-start | bytes 3145736 | tf_op jit(solution)/shard_map/ppermute | solution.py:366
  87.0 30.0 %collective-permute-start.14 = (bf16[4,128,1024]{2,1,0:T(8,128)(2,1)}, bf16[4,128,1024]{2,1,0:T(8,128)(2,1)}, u32[]{:S(2)}, u32[]{:S(2)}) collective-permute-start(bf16[4,128,1024]{2,1,0:T(8,128)(2,1)} %project.6), channel_id=1, source_target_pairs={{0,96},{1,97},{2,98},{3,99},{4,100},{5,101},{6,102},{7,103},{8,104... | collective-permute-start | bytes 3145736 | tf_op jit(solution)/shard_map/ppermute | solution.py:366
  91.5 10.3 %collective-permute-start.15 = (bf16[2,2,128,512]{3,2,1,0:T(8,128)(2,1)}, bf16[2,2,128,512]{3,2,1,0:T(8,128)(2,1)}, u32[]{:S(2)}, u32[]{:S(2)}) collective-permute-start(bf16[2,2,128,512]{3,2,1,0:T(8,128)(2,1)} %get-tuple-element.98), channel_id=1, source_target_pairs={{0,2},{1,9},{2,4},{3,11},{4,6},{5,13},{6,0},{7,15},{8,10},{9,17},{... | collective-permute-start | bytes 1572872 | tf_op jit(solution)/shard_map/ppermute | solution.py:364
  92.9 13.8 %collective-permute-start.16 = (bf16[2,2,128,512]{3,2,1,0:T(8,128)(2,1)}, bf16[2,2,128,512]{3,2,1,0:T(8,128)(2,1)}, u32[]{:S(2)}, u32[]{:S(2)}) collective-permute-start(bf16[2,2,128,512]{3,2,1,0:T(8,128)(2,1)} %get-tuple-element.99), channel_id=1, source_target_pairs={{0,6},{1,25},{2,0},{3,27},{4,2},{5,29},{6,4},{7,31},{8,14},{9,1},{... | collective-permute-start | bytes 1572872 | tf_op jit(solution)/shard_map/ppermute | solution.py:364
  94.6 14.0 %collective-permute-start.17 = (bf16[2,2,128,512]{3,2,1,0:T(8,128)(2,1)}, bf16[2,2,128,512]{3,2,1,0:T(8,128)(2,1)}, u32[]{:S(2)}, u32[]{:S(2)}) collective-permute-start(bf16[2,2,128,512]{3,2,1,0:T(8,128)(2,1)} %get-tuple-element.100), channel_id=1, source_target_pairs={{0,4},{1,17},{2,6},{3,19},{4,0},{5,21},{6,2},{7,23},{8,12},{9,25},... | collective-permute-start | bytes 1572872 | tf_op jit(solution)/shard_map/ppermute | solution.py:364
  119.1 14.9 %collective-permute-start.18 = (bf16[128,1024]{1,0:T(8,128)(2,1)S(1)}, bf16[128,1024]{1,0:T(8,128)(2,1)S(1)}, u32[]{:S(2)}, u32[]{:S(2)}) collective-permute-start(bf16[128,1024]{1,0:T(8,128)(2,1)S(1)} %get-tuple-element.101), channel_id=1, source_target_pairs={{0,0},{1,3},{2,11},{3,2},{4,4},{5,7},{6,15},{7,6},{8,17},{9,8},{10... | collective-permute-start | bytes 786440 | tf_op jit(solution)/shard_map/ppermute | solution.py:377
  121.0 13.0 %collective-permute-start.19 = (bf16[128,1024]{1,0:T(8,128)(2,1)S(1)}, bf16[128,1024]{1,0:T(8,128)(2,1)S(1)}, u32[]{:S(2)}, u32[]{:S(2)}) collective-permute-start(bf16[128,1024]{1,0:T(8,128)(2,1)S(1)} %get-tuple-element.102), channel_id=1, source_target_pairs={{0,17},{1,2},{2,10},{3,7},{4,21},{5,6},{6,14},{7,3},{8,16},{9,13},... | collective-permute-start | bytes 786440 | tf_op jit(solution)/shard_map/ppermute | solution.py:377
  125.7 11.1 %collective-permute-start.20 = (bf16[128,1024]{1,0:T(8,128)(2,1)S(1)}, bf16[128,1024]{1,0:T(8,128)(2,1)S(1)}, u32[]{:S(2)}, u32[]{:S(2)}) collective-permute-start(bf16[128,1024]{1,0:T(8,128)(2,1)S(1)} %get-tuple-element.103), channel_id=1, source_target_pairs={{0,16},{1,7},{2,27},{3,6},{4,20},{5,3},{6,31},{7,2},{8,1},{9,12},{... | collective-permute-start | bytes 786440 | tf_op jit(solution)/shard_map/ppermute | solution.py:377
  128.2 11.4 %collective-permute-start.21 = (bf16[128,1024]{1,0:T(8,128)(2,1)S(1)}, bf16[128,1024]{1,0:T(8,128)(2,1)S(1)}, u32[]{:S(2)}, u32[]{:S(2)}) collective-permute-start(bf16[128,1024]{1,0:T(8,128)(2,1)S(1)} %get-tuple-element.104), channel_id=1, source_target_pairs={{0,1},{1,6},{2,26},{3,3},{4,5},{5,2},{6,30},{7,7},{8,0},{9,9},{10,... | collective-permute-start | bytes 786440 | tf_op jit(solution)/shard_map/ppermute | solution.py:377
  (11 other events, 41.5 us)

commit v5 on v4

--- a/solution.py
+++ b/solution.py
@@ -14,12 +14,13 @@
 CHIPS = SIDE**3
 AXES = ("shard", "basis")
 CORE_SWAP = [(0, 1), (1, 0)]
-HOP2 = (2, 1, 3, 0)
+CHUNKS = (((2, 0), (2, 1)), ((1, 0), (3, 0)), ((1, 1), (3, 1)), ((0, 0), (0, 1)))
+FROM_BELOW, FROM_ABOVE = 1, 2
 BF16 = jnp.bfloat16
 F32 = jnp.float32
 SMALL = pl.CostEstimate(flops=1, bytes_accessed=1, transcendentals=0)
 VMEM_SMALL = 2 * 1024 * 1024
-VMEM_LIMIT = 22 * 1024 * 1024
+VMEM_LIMIT = 16 * 1024 * 1024
 
 
 def device_id(x, y, z, core):
@@ -68,7 +69,27 @@
     return jnp.where(kind == 0, (z * SIDE + y_end) * SIDE + x, (z * SIDE + y) * SIDE + x_end)
 
 
-def notes_kernel(blocks, counts_ref, dests_ref, rels_ref, lists_ref, out_ref):
+def in_hbm(array):
+    return pltpu.with_memory_space_constraint(array, pltpu.HBM)
+
+
+def in_vmem(array):
+    return pltpu.with_memory_space_constraint(array, pltpu.VMEM)
+
+
+SMEM_SPEC = pl.BlockSpec(memory_space=pltpu.SMEM)
+HBM_SPEC = pl.BlockSpec(memory_space=pltpu.HBM)
+VMEM_SPEC = pl.BlockSpec(memory_space=pltpu.VMEM)
+
+
+def notes_kernel(blocks, *refs):
+    given, out_ref, held, sems = refs[:4], refs[4], refs[5:9], refs[9]
+    copies = [pltpu.make_async_copy(a, b, sems.at[i]) for i, (a, b) in enumerate(zip(given, held))]
+    for copy in copies:
+        copy.start()
+    for copy in copies:
+        copy.wait()
+    counts_ref, dests_ref, rels_ref, lists_ref = held
     rows = CHIPS * 8
     x, y, z, _ = coordinates()
     counts = counts_ref[...]
@@ -106,16 +127,16 @@
     out_ref[...] = jnp.where(place < SIDE, codes, other)
 
 
-def make_notes(counts, dests, rels, lists):
-    vmem = pl.BlockSpec(memory_space=pltpu.VMEM)
-    return pl.pallas_call(
-        functools.partial(notes_kernel, dests.shape[1] // BROWS),
+def make_notes(*given):
+    return pl.pallas_call(
+        functools.partial(notes_kernel, given[1].shape[1] // BROWS),
         out_shape=jax.ShapeDtypeStruct((CHIPS * 8, DST), jnp.int32),
-        in_specs=[vmem] * 4,
-        out_specs=vmem,
+        in_specs=[HBM_SPEC] * 4,
+        out_specs=VMEM_SPEC,
+        scratch_shapes=[pltpu.VMEM(array.shape, jnp.int32) for array in given] + [pltpu.SemaphoreType.DMA((4,))],
         compiler_params=pltpu.CompilerParams(vmem_limit_bytes=VMEM_LIMIT),
         name="notes",
-    )(counts, dests, rels, lists).reshape(CHIPS, 8, DST)
+    )(*map(in_hbm, given)).reshape(CHIPS, 8, DST)
 
 
 WORDS = 4
@@ -126,7 +147,7 @@
     return words_ref[(group * SIDE + line) * WORDS + which]
 
 
-def reached(step, step_z, kind, which):
+def reached(step, kind, step_z, which):
     x, y, z, _ = coordinates()
     x_to = jnp.where(kind == 0, (x + step) % SIDE, x)
     y_to = jnp.where(kind == 0, y, (y + step) % SIDE)
@@ -155,63 +176,50 @@
                 copy.wait()
 
 
-def in_hbm(array):
-    return pltpu.with_memory_space_constraint(array, pltpu.HBM)
-
-
-def in_vmem(array):
-    return pltpu.with_memory_space_constraint(array, pltpu.VMEM)
-
-
-SMEM_SPEC = pl.BlockSpec(memory_space=pltpu.SMEM)
-HBM_SPEC = pl.BlockSpec(memory_space=pltpu.HBM)
-VMEM_SPEC = pl.BlockSpec(memory_space=pltpu.VMEM)
-
-
-def cross_kernel(steps_z, words_ref, table_ref, out_ref, sems):
+def cross_kernel(chunks, words_ref, table_ref, out_ref, sems):
     core = lax.axis_index("basis")
     moves = []
-    for i, step_z in enumerate(steps_z):
+    for i, chunk in enumerate(chunks):
         for step in range(SIDE):
-            for which in range(2):
-                live, source = local_block(words_ref, table_ref, reached(step, step_z, 1 - core, which))
-                at = (i, step, which)
+            for pair, place in enumerate(chunk):
+                live, source = local_block(words_ref, table_ref, reached(step, 1 - core, *place))
+                at = (i, step, pair)
                 moves.append((live, (pltpu.make_async_copy(source, out_ref.at[at], sems.at[at]),)))
     run_moves(moves)
 
 
-def cross(steps_z, words, table):
-    shape = (len(steps_z), SIDE, 2, BROWS, table.shape[1])
-    return pl.pallas_call(
-        functools.partial(cross_kernel, steps_z),
+def cross(chunks, words, table):
+    shape = (len(chunks), SIDE, 2, BROWS, table.shape[1])
+    return pl.pallas_call(
+        functools.partial(cross_kernel, chunks),
         out_shape=pltpu.VMEM(shape, BF16),
         in_specs=[SMEM_SPEC, HBM_SPEC],
         out_specs=VMEM_SPEC,
-        scratch_shapes=[pltpu.SemaphoreType.DMA((len(steps_z), SIDE, 2))],
+        scratch_shapes=[pltpu.SemaphoreType.DMA((len(chunks), SIDE, 2))],
         compiler_params=pltpu.CompilerParams(vmem_limit_bytes=VMEM_SMALL),
         cost_estimate=SMALL,
         name="cross",
     )(words, in_hbm(table))
 
 
-def pick_kernel(step_z, row, words_ref, table_ref, crossed_ref, *rest):
+def pick_kernel(chunk, row, words_ref, table_ref, crossed_ref, *rest):
     outs, sems = rest[: len(HOP1)], rest[len(HOP1)]
     core = lax.axis_index("basis")
     moves = []
-    for i, step in enumerate(HOP1):
-        for which in range(2):
-            live, source = local_block(words_ref, table_ref, reached(step, step_z, core, which))
+    for j, step in enumerate(HOP1):
+        for pair, place in enumerate(chunk):
+            live, source = local_block(words_ref, table_ref, reached(step, core, *place))
             copies = (
-                pltpu.make_async_copy(source, outs[i].at[which, 0], sems.at[0, i, which]),
-                pltpu.make_async_copy(crossed_ref.at[row, step, which], outs[i].at[which, 1], sems.at[1, i, which]),
+                pltpu.make_async_copy(source, outs[j].at[pair, 0], sems.at[0, j, pair]),
+                pltpu.make_async_copy(crossed_ref.at[row, step, pair], outs[j].at[pair, 1], sems.at[1, j, pair]),
             )
             moves.append((live, copies))
     run_moves(moves)
 
 
-def pick(step_z, row, words, table, crossed):
-    return pl.pallas_call(
-        functools.partial(pick_kernel, step_z, row),
+def pick(chunk, row, words, table, crossed):
+    return pl.pallas_call(
+        functools.partial(pick_kernel, chunk, row),
         out_shape=[pltpu.VMEM((2, 2, BROWS, table.shape[1]), BF16)] * len(HOP1),
         in_specs=[SMEM_SPEC, HBM_SPEC, VMEM_SPEC],
         out_specs=[VMEM_SPEC] * len(HOP1),
@@ -222,15 +230,16 @@
     )(words, in_hbm(table), in_vmem(crossed))
 
 
-def project_kernel(step_z, row, words_ref, table_ref, notes_ref, coeffs_ref, crossed_ref, *rest):
+def project_kernel(chunk, row, added, words_ref, table_ref, own_basis, other_basis, notes_ref, coeffs_ref, crossed_ref, *rest):
     received, rest = rest[: len(HOP1)], rest[len(HOP1) :]
-    own_basis, other_basis, out_ref, local, total, sems = rest
+    extra, rest = rest[: len(added)], rest[len(added) :]
+    outs, (local, total, sems) = rest[:2], rest[2:]
     x, y, z, core = coordinates()
     width = table_ref.shape[1]
     along = jnp.where(core == 0, x, y)
     pieces = []
-    for which in range(2):
-        group = reached(0, step_z, core, which)
+    for which, place in enumerate(chunk):
+        group = reached(0, core, *place)
         for step in HOP1 + (0,):
             line = (along - step) % SIDE
             code = word(words_ref, group, line, 0)
@@ -273,11 +282,9 @@
                 else:
                     copy.wait()
                     block = local[which]
-                added = jnp.dot(
-                    chosen, jnp.concatenate([block, block], axis=0), preferred_element_type=F32
-                )
+                sums = jnp.dot(chosen, jnp.concatenate([block, block], axis=0), preferred_element_type=F32)
                 column = pl.multiple_of(jnp.where(core == part, 0, width), width)
-                total[which, half, :, pl.ds(column, width)] += added
+                total[which, half, :, pl.ds(column, width)] += sums
 
     summed = [
         total[:, :, k * DST : (k + 1) * DST, :].reshape(4 * DST, 2 * width).astype(BF16) for k in range(2)
@@ -287,102 +294,180 @@
     for start in range(0, wide, tile):
         result = jnp.dot(summed[0], own_basis[:, start : start + tile], preferred_element_type=F32)
         result += jnp.dot(summed[1], other_basis[:, start : start + tile], preferred_element_type=F32)
-        out_ref[:, :, start : start + tile] = result.reshape(4, DST, tile).astype(BF16)
-
-
-def project(step_z, row, words, table, *others):
+        result = result.reshape(2, 2, DST, tile)
+        for which in range(2):
+            here = result[which]
+            if which in added:
+                here += extra[added.index(which)][:, :, start : start + tile].astype(F32)
+            outs[which][:, :, start : start + tile] = here.astype(BF16)
+
+
+def project(chunk, row, added, words, table, *others):
     width = table.shape[1]
-    wide = others[-1].shape[1]
-    return pl.pallas_call(
-        functools.partial(project_kernel, step_z, row),
-        out_shape=pltpu.VMEM((4, DST, wide), BF16),
+    wide = 2 * width
+    return pl.pallas_call(
+        functools.partial(project_kernel, chunk, row, added),
+        out_shape=[pltpu.VMEM((2, DST, wide), BF16)] * 2,
         in_specs=[SMEM_SPEC, HBM_SPEC] + [VMEM_SPEC] * len(others),
-        out_specs=VMEM_SPEC,
+        out_specs=[VMEM_SPEC] * 2,
         scratch_shapes=[
             pltpu.VMEM((2, BROWS, width), BF16),
             pltpu.VMEM((2, 2, 2 * DST, 2 * width), F32),
             pltpu.SemaphoreType.DMA((2,)),
         ],
-        cost_estimate=SMALL,
+        cost_estimate=pl.CostEstimate(flops=6 * 10**9, bytes_accessed=20 * 10**6, transcendentals=0),
         compiler_params=pltpu.CompilerParams(vmem_limit_bytes=VMEM_LIMIT),
         name="project",
     )(words, in_hbm(table), *map(in_vmem, others))
 
 
-def merge_kernel(order_ref, *refs):
-    ins, outs = refs[:SIDE], refs[SIDE:]
-    for send in range(4):
-        at = order_ref[send]
-        result = ins[0][at].astype(F32)
-        for other in ins[1:]:
-            result += other[at].astype(F32)
-        outs[send][...] = result.astype(BF16)
-
-
-def merge(order, parts):
+def merge_kernel(*refs):
+    ins, outs = refs[:6], refs[6:]
+    x, y, z, core = coordinates()
+    last = jnp.where(core == 0, y, x)
+    matched = (x + y + z) % 2 == core
+    for send, ((step, to), (other_step, other_to)) in enumerate(zip(MATCHED, UNMATCHED)):
+        which = (last + jnp.where(matched, step, other_step)) % SIDE // 2
+        half = jnp.where(matched, to, other_to)
+        for group in range(2):
+
+            @pl.when(which == group)
+            def _(group=group, half=half, send=send):
+                result = ins[3 * group][half].astype(F32)
+                for other in ins[3 * group + 1 : 3 * group + 3]:
+                    result += other[half].astype(F32)
+                outs[send][...] = result.astype(BF16)
+
+
+def merge(parts):
     return pl.pallas_call(
         merge_kernel,
         out_shape=[pltpu.VMEM(parts[0].shape[1:], BF16)] * 4,
-        in_specs=[SMEM_SPEC] + [VMEM_SPEC] * SIDE,
+        in_specs=[VMEM_SPEC] * len(parts),
         out_specs=[VMEM_SPEC] * 4,
         compiler_params=pltpu.CompilerParams(vmem_limit_bytes=VMEM_LIMIT),
         cost_estimate=SMALL,
         name="merge",
-    )(order, *map(in_vmem, parts))
+    )(*map(in_vmem, parts))
+
+
+def degree_kernel(dests_ref, out_ref):
+    rows = dests_ref.shape[1] // 2
+    mine = dests_ref[:, pl.ds(pl.multiple_of(lax.axis_index("basis") * rows, BROWS), rows)]
+    hit = mine == lax.broadcasted_iota(jnp.int32, (DST, rows), 0)
+    count = jnp.sum(jnp.where(hit, 1.0, 0.0), axis=1, keepdims=True)
+    out_ref[...] = jnp.broadcast_to(jnp.maximum(count, 1.0), out_ref.shape)
+
+
+def degrees(dests):
+    return pl.pallas_call(
+        degree_kernel,
+        out_shape=pltpu.VMEM((DST, BROWS), F32),
+        in_specs=[VMEM_SPEC],
+        out_specs=VMEM_SPEC,
+        compiler_params=pltpu.CompilerParams(vmem_limit_bytes=2 * VMEM_SMALL),
+        cost_estimate=SMALL,
+        name="degree",
+    )(dests)
+
+
+def table_kernel(coeffs_ref, out_ref):
+    rels = coeffs_ref.shape[1]
+    for i in range(out_ref.shape[0]):
+        here = min(DST, rels - i * DST)
+        out_ref[i, :, :here] = coeffs_ref[:, i * DST : i * DST + here]
+
+
+def make_table(coeffs):
+    rels = coeffs.shape[0]
+    return pl.pallas_call(
+        table_kernel,
+        out_shape=pltpu.VMEM((-(-rels // DST), 2, DST), F32),
+        in_specs=[VMEM_SPEC],
+        out_specs=VMEM_SPEC,
+        compiler_params=pltpu.CompilerParams(vmem_limit_bytes=2 * VMEM_SMALL),
+        cost_estimate=SMALL,
+        name="table",
+    )(coeffs.T)
+
+
+def finish_kernel(degree_ref, *refs):
+    ends, out_ref = refs[:-1], refs[-1]
+    degree = degree_ref[...]
+    for start in range(0, out_ref.shape[1], BROWS):
+        here = slice(start, start + BROWS)
+        summed = ends[0][:, here].astype(F32)
+        for end in ends[1:]:
+            summed += end[:, here].astype(F32)
+        out_ref[:, here] = (summed / degree).astype(BF16)
+
+
+def finish(degree, ends):
+    return pl.pallas_call(
+        finish_kernel,
+        out_shape=jax.ShapeDtypeStruct(ends[0].shape, BF16),
+        in_specs=[VMEM_SPEC] * (1 + len(ends)),
+        out_specs=VMEM_SPEC,
+        compiler_params=pltpu.CompilerParams(vmem_limit_bytes=2 * VMEM_SMALL),
+        cost_estimate=SMALL,
+        name="finish",
+    )(*map(in_vmem, (degree, *ends)))
 
 
 def body(features, bases, coeffs, block_lists, block_counts, tile_rel, dest_ids):
-    x, y, z, core = coordinates()
-    blocks = tile_rel.shape[1] * TILE // BROWS
     other_basis = lax.ppermute(bases[0], "basis", CORE_SWAP)
 
     sent = make_notes(block_counts, dest_ids, tile_rel, block_lists.reshape(1, CHIPS))
     notes = lax.all_to_all(sent, "shard", split_axis=0, concat_axis=0, tiled=True)
     words = notes[:, SIDE:, :WORDS].reshape(-1)
-    rels = -(-coeffs.shape[0] // DST) * DST
-    table = jnp.pad(coeffs.T, ((0, 0), (0, rels - coeffs.shape[0]))).reshape(2, -1, DST).transpose(1, 0, 2)
+    table, degree = make_table(coeffs), degrees(dest_ids)
 
     words, other_basis = lax.optimization_barrier((words, other_basis))
-    groups = HOP2[:1], HOP2[1:]
-    first = cross(groups[0], words, features)
+    both = bases[0], other_basis
+
+    first = cross(CHUNKS[:1], words, features)
     first, later = lax.optimization_barrier((first, words))
-    second = cross(groups[1], later, features)
+    second = cross(CHUNKS[1:], later, features)
     first = lax.ppermute(first, "basis", CORE_SWAP)
     first, second = lax.optimization_barrier((first, second))
-    crossed = first, lax.ppermute(second, "basis", CORE_SWAP)
-    crossed = {s: (steps.index(s), buf) for steps, buf in zip(groups, crossed) for s in steps}
-
-    arrived, parts, later = [], [], words
-    for i, step_z in enumerate(HOP2):
-        row, buf = crossed[step_z]
-        picked = pick(step_z, row, later, features, buf)
-        picked, later = lax.optimization_barrier((picked, later))
-        if i > 0:
-            picked, arrived[-1] = lax.optimization_barrier((picked, arrived[-1]))
-        if i == 3:
-            picked, parts[0] = lax.optimization_barrier((picked, parts[0]))
-        arrived.append([lax.ppermute(buf, AXES, hop1_pairs(step)) for step, buf in zip(HOP1, picked)])
-        part = project(step_z, row, words, features, notes, table, buf, *arrived[i], bases[0], other_basis)
-        parts.append(part if step_z == 0 else lax.ppermute(part, AXES, hop2_pairs(step_z)))
-
-    last = jnp.where(core == 0, y, x)
-    matched = (x + y + z) % 2 == core
-    order = jnp.stack(
-        [
-            jnp.where(matched, (last + a) % SIDE // 2 * 2 + b, (last + c) % SIDE // 2 * 2 + d)
-            for (a, b), (c, d) in zip(MATCHED, UNMATCHED)
-        ]
-    )
-    merged = merge(order, parts)
+    second = lax.ppermute(second, "basis", CORE_SWAP)
+    crossed = [(0, first)] + [(i, second) for i in range(len(CHUNKS) - 1)]
+
+    def pick_chunk(i, after):
+        (row, buf), (ready, _) = crossed[i], lax.optimization_barrier((words, after))
+        bufs = pick(CHUNKS[i], row, ready, features, buf)
+        return lax.optimization_barrier((bufs, words))
+
+    picked, ready = [pick_chunk(0, words)[0]], words
+    bufs, _ = pick_chunk(1, picked[0])
+    picked.append(bufs)
+    arrived, parts = [], []
+    for i, (chunk, (row, buf)) in enumerate(zip(CHUNKS, crossed)):
+        came = []
+        for j, step in enumerate(HOP1):
+            sent = picked[i][j]
+            if i > 0:
+                sent, arrived[-1][j] = lax.optimization_barrier((sent, arrived[-1][j]))
+            came.append(lax.ppermute(sent, AXES, hop1_pairs(step)))
+        arrived.append(came)
+        given = [ready, features, *both, notes, table, buf, *came]
+        added = ()
+        if i == FROM_BELOW:
+            added, given = (0,), given + [parts[0][0]]
+        if i == FROM_ABOVE:
+            added, given = (1,), given + [parts[0][1]]
+        part = project(chunk, row, added, *given)
+        if i + 2 < len(CHUNKS):
+            bufs, ready = pick_chunk(i + 2, part)
+            picked.append(bufs)
+        if i < len(CHUNKS) - 1:
+            part = [lax.ppermute(p, AXES, hop2_pairs(step)) for p, step in zip(part, (1, 3))]
+        parts.append(part)
+    parts = [parts[3][0], *parts[1], parts[3][1], *parts[2]]
+
+    merged = merge(parts)
     ends = [lax.ppermute(buf, AXES, hop3_pairs(send)) for send, buf in enumerate(merged)]
-    summed = sum(end.astype(F32) for end in ends)
-
-    rows_dev = blocks // 2 * BROWS
-    my_dests = lax.dynamic_slice_in_dim(dest_ids[0], core * rows_dev, rows_dev)
-    indegree = jnp.sum(
-        (my_dests[None, :] == jnp.arange(DST, dtype=jnp.int32)[:, None]).astype(F32), axis=1
-    )
-    return (summed / jnp.maximum(indegree, 1.0)[:, None]).astype(BF16)
+    return finish(degree, ends)
 
 
 def solution(mesh):

time: 141 us -> 126 us (0.89); the launches traced: 141 us -> 124 us
  waiting for transfers between devices: 43.7 us -> 34.4 us
  local copies, waits for them, and re-layouts: 7.05 us -> 0.2 us
  starting transfers between devices: 29.1 us -> 34.3 us
  Pallas kernels: 38.1 us -> 33.6 us
    unnamed x26 -> x6, local copies, waits for them, and re-layouts: 6.83 us -> 0.02 us
    ppermute x16 -> x19, starting transfers between devices: 15.2 us -> 20.8 us  [the longest x12 14.5 us: body(): came.append(lax.ppermute(sent, AXES, hop1_pairs(step)))]
    ppermute x4, waiting for transfers between devices: 9.28 us -> 4.27 us  [body(): lax.ppermute(buf, AXES, hop3_pairs(send))]
    ppermute x16 -> x19, waiting for transfers between devices: 34.4 us -> 30.1 us  [the longest x12 16.3 us: body(): came.append(lax.ppermute(sent, AXES, hop1_pairs(step)))]
    pallas_call x11 -> x14, Pallas kernels: 36.1 us -> 33.1 us  [the longest x4 18.6 us: project(): pl.pallas_call(functools.partial(project_kernel, chunk, row, added), out_...]
    pallas_call x1, Pallas kernels: 2.07 us -> 0.44 us  [merge(): pl.pallas_call(merge_kernel, out_shape=[pltpu.VMEM(parts[0].shape[1:], BF...]
  transfers between devices with their start and end apart: 22 -> 25, of which waited for: 12 -> 7; matrix products, arithmetic and copies ran while one was open for 0% -> 0% of each run, Pallas kernels for 24% -> 25%
where the time goes in v5:
time: 126 us; the launch traced here: 124 us
  waiting for transfers between devices  34.4 us (27%)
  starting transfers between devices  34.3 us (27%)
  Pallas kernels  33.6 us (27%)
  blocking collectives  21.1 us (17%)
    all_to_all x1, blocking collectives, body(): lax.all_to_all(sent, 'shard', split_axis=0, concat_axis=0, tiled=True)  21.1 us
    pallas_call x4, Pallas kernels, project(): pl.pallas_call(functools.partial(project_kernel, chunk, row, added), out_...  18.6 us
    ppermute x12, waiting for transfers between devices, body(): came.append(lax.ppermute(sent, AXES, hop1_pairs(step)))  16.3 us
    ppermute x12, starting transfers between devices, body(): came.append(lax.ppermute(sent, AXES, hop1_pairs(step)))  14.5 us
    ppermute x6, waiting for transfers between devices, body(): lax.ppermute(p, AXES, hop2_pairs(step))  13.2 us
    ppermute x4, starting transfers between devices, body(): lax.ppermute(buf, AXES, hop3_pairs(send))  10.5 us
    pallas_call x4, Pallas kernels, pick(): pl.pallas_call(functools.partial(pick_kernel, chunk, row), out_shape=[plt...  7.92 us
    ppermute x6, starting transfers between devices, body(): lax.ppermute(p, AXES, hop2_pairs(step))  5.89 us
  transfers between devices with their start and end apart: 25, of which 7 were waited for; matrix products, arithmetic and copies ran while one was open for 0% of the time, Pallas kernels for 25%

profile of v5, /device:TPU:1, one launch (start us, length us, event | category | flops | bytes accessed | tf_op | source)
XLA Modules:
  0.0 123.8 jit_solution(817870968160948187)
XLA Ops:
  3.0 21.1 %all_to_all.5.notes_ref = s32[64,8,128]{2,1,0:T(8,128)S(1)} all-to-all(s32[64,8,128]{2,1,0:T(8,128)S(1)} %bitcast.4), channel_id=1, replica_groups=mesh['shard'=64,'basis'=2] {'shard'}, dimensions={0} | all-to-all | bytes 524288 | tf_op jit(solution)/shard_map/all_to_all | solution.py:421
  27.7 2.2 %cross.3 = bf16[3,4,2,128,512]{4,3,2,1,0:T(8,128)(2,1)S(1)} custom-call(s32[1024]{0:T(1024)S(1)} %reshape.11.words_ref, bf16[6144,512]{1,0:T(8,128)(2,1)} %table_ref.19), custom_call_target="tpu_custom_call" | custom-call | flops 1 | bytes 1 | tf_op jit(solution)/shard_map/cross/pallas_call | solution.py:193
  30.3 2.1 %pick.4 = (bf16[2,2,128,512]{3,2,1,0:T(8,128)(2,1)S(1)}, bf16[2,2,128,512]{3,2,1,0:T(8,128)(2,1)S(1)}, bf16[2,2,128,512]{3,2,1,0:T(8,128)(2,1)S(1)}) custom-call(s32[1024]{0:T(1024)S(1)} %reshape.11.words_ref, bf16[6144,512]{1,0:T(8,128)(2,1)} %table_ref.19, bf16[1,4,2,128,512]{4,3,2,1,0:T(8,128)(2,1)S(1)} %collective-permute-done.1.crossed_ref), custom_call_target="tpu_custom_call" | custom-call | flops 1 | bytes 1 | tf_op jit(solution)/shard_map/pick/pallas_call | solution.py:221
  33.1 1.9 %collective-permute-start.3 = (bf16[2,2,128,512]{3,2,1,0:T(8,128)(2,1)S(1)}, bf16[2,2,128,512]{3,2,1,0:T(8,128)(2,1)S(1)}, u32[]{:S(2)}, u32[]{:S(2)}) collective-permute-start(bf16[2,2,128,512]{3,2,1,0:T(8,128)(2,1)S(1)} %get-tuple-element.72), channel_id=1, source_target_pairs={{0,6},{1,25},{2,0},{3,27},{4,2},{5,29},{6,4},{7,31},{8,14},{9,1},{... | collective-permute-start | bytes 1572872 | tf_op jit(solution)/shard_map/ppermute | solution.py:451
  35.7 2.0 %pick.6 = (bf16[2,2,128,512]{3,2,1,0:T(8,128)(2,1)S(1)}, bf16[2,2,128,512]{3,2,1,0:T(8,128)(2,1)S(1)}, bf16[2,2,128,512]{3,2,1,0:T(8,128)(2,1)S(1)}) custom-call(s32[1024]{0:T(1024)S(1)} %reshape.11.words_ref, bf16[6144,512]{1,0:T(8,128)(2,1)} %table_ref.19, bf16[3,4,2,128,512]{4,3,2,1,0:T(8,128)(2,1)S(1)} %collective-permute-done.5.crossed_ref), custom_call_target="tpu_custom_call" | custom-call | flops 1 | bytes 1 | tf_op jit(solution)/shard_map/pick/pallas_call | solution.py:221
  37.6 4.8 %collective-permute-done.4.rest_2_ = bf16[2,2,128,512]{3,2,1,0:T(8,128)(2,1)S(1)} collective-permute-done((bf16[2,2,128,512]{3,2,1,0:T(8,128)(2,1)S(1)}, bf16[2,2,128,512]{3,2,1,0:T(8,128)(2,1)S(1)}, u32[]{:S(2)}, u32[]{:S(2)}) %collective-permute-start.4) | collective-permute-done | bytes 524320 | tf_op jit(solution)/shard_map/ppermute | solution.py:451
  42.9 3.4 %collective-permute-done.3.rest_1_ = bf16[2,2,128,512]{3,2,1,0:T(8,128)(2,1)S(1)} collective-permute-done((bf16[2,2,128,512]{3,2,1,0:T(8,128)(2,1)S(1)}, bf16[2,2,128,512]{3,2,1,0:T(8,128)(2,1)S(1)}, u32[]{:S(2)}, u32[]{:S(2)}) %collective-permute-start.3) | collective-permute-done | bytes 524320 | tf_op jit(solution)/shard_map/ppermute | solution.py:451
  46.3 2.3 %collective-permute-start.7 = (bf16[2,2,128,512]{3,2,1,0:T(8,128)(2,1)S(1)}, bf16[2,2,128,512]{3,2,1,0:T(8,128)(2,1)S(1)}, u32[]{:S(2)}, u32[]{:S(2)}) collective-permute-start(bf16[2,2,128,512]{3,2,1,0:T(8,128)(2,1)S(1)} %get-tuple-element.89), channel_id=1, source_target_pairs={{0,6},{1,25},{2,0},{3,27},{4,2},{5,29},{6,4},{7,31},{8,14},{9,1},{... | collective-permute-start | bytes 1572872 | tf_op jit(solution)/shard_map/ppermute | solution.py:451
  48.7 4.8 %project.4 = (bf16[2,128,1024]{2,1,0:T(8,128)(2,1)S(1)}, bf16[2,128,1024]{2,1,0:T(8,128)(2,1)S(1)}) custom-call(s32[1024]{0:T(1024)S(1)} %reshape.11.words_ref, bf16[6144,512]{1,0:T(8,128)(2,1)} %table_ref.19, bf16[1024,1024]{1,0:T(8,128)(2,1)S(1)} %bitcast.7, bf16[1024,1024]{1,0:T(8,128)(2,1)S(1)} %collective-permute-done.other_basis, ...), custom_call_target="tpu_custom_call" | custom-call | flops 6000000000 | bytes 20000000 | tf_op jit(solution)/shard_map/project/pallas_call | solution.py:308
  53.7 2.5 %collective-permute-start.18 = (bf16[2,128,1024]{2,1,0:T(8,128)(2,1)S(1)}, bf16[2,128,1024]{2,1,0:T(8,128)(2,1)S(1)}, u32[]{:S(2)}, u32[]{:S(2)}) collective-permute-start(bf16[2,128,1024]{2,1,0:T(8,128)(2,1)S(1)} %get-tuple-element.75), channel_id=1, source_target_pairs={{0,96},{1,97},{2,98},{3,99},{4,100},{5,101},{6,102},{7,103},{8,104... | collective-permute-start | bytes 1572872 | tf_op jit(solution)/shard_map/ppermute | solution.py:464
  56.2 1.9 %pick.5 = (bf16[2,2,128,512]{3,2,1,0:T(8,128)(2,1)S(1)}, bf16[2,2,128,512]{3,2,1,0:T(8,128)(2,1)S(1)}, bf16[2,2,128,512]{3,2,1,0:T(8,128)(2,1)S(1)}) custom-call(s32[1024]{0:T(1024)S(1)} %reshape.11.words_ref, bf16[6144,512]{1,0:T(8,128)(2,1)} %table_ref.19, bf16[3,4,2,128,512]{4,3,2,1,0:T(8,128)(2,1)S(1)} %collective-permute-done.5.crossed_ref), custom_call_target="tpu_custom_call" | custom-call | flops 1 | bytes 1 | tf_op jit(solution)/shard_map/pick/pallas_call | solution.py:221
  59.8 2.0 %collective-permute-start.12 = (bf16[2,2,128,512]{3,2,1,0:T(8,128)(2,1)S(1)}, bf16[2,2,128,512]{3,2,1,0:T(8,128)(2,1)S(1)}, u32[]{:S(2)}, u32[]{:S(2)}) collective-permute-start(bf16[2,2,128,512]{3,2,1,0:T(8,128)(2,1)S(1)} %get-tuple-element.105), channel_id=1, source_target_pairs={{0,6},{1,25},{2,0},{3,27},{4,2},{5,29},{6,4},{7,31},{8,14},{9,1},{... | collective-permute-start | bytes 1572872 | tf_op jit(solution)/shard_map/ppermute | solution.py:451
  61.7 5.6 %collective-permute-done.9.rest_3_ = bf16[2,128,1024]{2,1,0:T(8,128)(2,1)S(1)} collective-permute-done((bf16[2,128,1024]{2,1,0:T(8,128)(2,1)S(1)}, bf16[2,128,1024]{2,1,0:T(8,128)(2,1)S(1)}, u32[]{:S(2)}, u32[]{:S(2)}) %collective-permute-start.9) | collective-permute-done | bytes 524320 | tf_op jit(solution)/shard_map/ppermute | solution.py:464
  67.3 4.6 %project.5 = (bf16[2,128,1024]{2,1,0:T(8,128)(2,1)S(1)}, bf16[2,128,1024]{2,1,0:T(8,128)(2,1)S(1)}) custom-call(s32[1024]{0:T(1024)S(1)} %reshape.11.words_ref, bf16[6144,512]{1,0:T(8,128)(2,1)} %table_ref.19, bf16[1024,1024]{1,0:T(8,128)(2,1)S(1)} %bitcast.8, bf16[1024,1024]{1,0:T(8,128)(2,1)S(1)} %collective-permute-done.other_basis, ...), custom_call_target="tpu_custom_call" | custom-call | flops 6000000000 | bytes 20000000 | tf_op jit(solution)/shard_map/project/pallas_call | solution.py:308
  74.5 2.4 %collective-permute-start.17 = (bf16[2,128,1024]{2,1,0:T(8,128)(2,1)S(1)}, bf16[2,128,1024]{2,1,0:T(8,128)(2,1)S(1)}, u32[]{:S(2)}, u32[]{:S(2)}) collective-permute-start(bf16[2,128,1024]{2,1,0:T(8,128)(2,1)S(1)} %get-tuple-element.93), channel_id=1, source_target_pairs={{0,96},{1,97},{2,98},{3,99},{4,100},{5,101},{6,102},{7,103},{8,104... | collective-permute-start | bytes 1572872 | tf_op jit(solution)/shard_map/ppermute | solution.py:464
  76.8 2.8 %collective-permute-start.15 = (bf16[2,2,128,512]{3,2,1,0:T(8,128)(2,1)S(1)}, bf16[2,2,128,512]{3,2,1,0:T(8,128)(2,1)S(1)}, u32[]{:S(2)}, u32[]{:S(2)}) collective-permute-start(bf16[2,2,128,512]{3,2,1,0:T(8,128)(2,1)S(1)} %get-tuple-element.110), channel_id=1, source_target_pairs={{0,4},{1,17},{2,6},{3,19},{4,0},{5,21},{6,2},{7,23},{8,12},{9,25},... | collective-permute-start | bytes 1572872 | tf_op jit(solution)/shard_map/ppermute | solution.py:451
  79.7 2.1 %collective-permute-start.13 = (bf16[2,2,128,512]{3,2,1,0:T(8,128)(2,1)S(1)}, bf16[2,2,128,512]{3,2,1,0:T(8,128)(2,1)S(1)}, u32[]{:S(2)}, u32[]{:S(2)}) collective-permute-start(bf16[2,2,128,512]{3,2,1,0:T(8,128)(2,1)S(1)} %get-tuple-element.106), channel_id=1, source_target_pairs={{0,6},{1,25},{2,0},{3,27},{4,2},{5,29},{6,4},{7,31},{8,14},{9,1},{... | collective-permute-start | bytes 1572872 | tf_op jit(solution)/shard_map/ppermute | solution.py:451
  82.4 4.3 %project.7 = (bf16[2,128,1024]{2,1,0:T(8,128)(2,1)S(1)}, bf16[2,128,1024]{2,1,0:T(8,128)(2,1)S(1)}) custom-call(s32[1024]{0:T(1024)S(1)} %reshape.11.words_ref, bf16[6144,512]{1,0:T(8,128)(2,1)} %table_ref.19, bf16[1024,1024]{1,0:T(8,128)(2,1)S(1)} %bitcast.9, bf16[1024,1024]{1,0:T(8,128)(2,1)S(1)} %collective-permute-done.other_basis, ...), custom_call_target="tpu_custom_call" | custom-call | flops 6000000000 | bytes 20000000 | tf_op jit(solution)/shard_map/project/pallas_call | solution.py:308
  86.7 8.1 %collective-permute-done.13.rest_1_ = bf16[2,2,128,512]{3,2,1,0:T(8,128)(2,1)S(1)} collective-permute-done((bf16[2,2,128,512]{3,2,1,0:T(8,128)(2,1)S(1)}, bf16[2,2,128,512]{3,2,1,0:T(8,128)(2,1)S(1)}, u32[]{:S(2)}, u32[]{:S(2)}) %collective-permute-start.13) | collective-permute-done | bytes 524320 | tf_op jit(solution)/shard_map/ppermute | solution.py:451
  94.9 5.0 %project.6 = (bf16[2,128,1024]{2,1,0:T(8,128)(2,1)S(1)}, bf16[2,128,1024]{2,1,0:T(8,128)(2,1)S(1)}) custom-call(s32[1024]{0:T(1024)S(1)} %reshape.11.words_ref, bf16[6144,512]{1,0:T(8,128)(2,1)} %table_ref.19, bf16[1024,1024]{1,0:T(8,128)(2,1)S(1)} %bitcast.10, bf16[1024,1024]{1,0:T(8,128)(2,1)S(1)} %collective-permute-done.other_basis, ...), custom_call_target="tpu_custom_call" | custom-call | flops 6000000000 | bytes 20000000 | tf_op jit(solution)/shard_map/project/pallas_call | solution.py:308
  99.9 7.6 %collective-permute-done.20.refs_5_ = bf16[2,128,1024]{2,1,0:T(8,128)(2,1)S(1)} collective-permute-done((bf16[2,128,1024]{2,1,0:T(8,128)(2,1)S(1)}, bf16[2,128,1024]{2,1,0:T(8,128)(2,1)S(1)}, u32[]{:S(2)}, u32[]{:S(2)}) %collective-permute-start.20) | collective-permute-done | bytes 524320 | tf_op jit(solution)/shard_map/ppermute | solution.py:464
  108.0 1.9 %collective-permute-start.21 = (bf16[128,1024]{1,0:T(8,128)(2,1)S(1)}, bf16[128,1024]{1,0:T(8,128)(2,1)S(1)}, u32[]{:S(2)}, u32[]{:S(2)}) collective-permute-start(bf16[128,1024]{1,0:T(8,128)(2,1)S(1)} %get-tuple-element.115), channel_id=1, source_target_pairs={{0,0},{1,3},{2,11},{3,2},{4,4},{5,7},{6,15},{7,6},{8,17},{9,8},{10... | collective-permute-start | bytes 786440 | tf_op jit(solution)/shard_map/ppermute | solution.py:469
  110.9 7.6 %collective-permute-start.24 = (bf16[128,1024]{1,0:T(8,128)(2,1)S(1)}, bf16[128,1024]{1,0:T(8,128)(2,1)S(1)}, u32[]{:S(2)}, u32[]{:S(2)}) collective-permute-start(bf16[128,1024]{1,0:T(8,128)(2,1)S(1)} %get-tuple-element.118), channel_id=1, source_target_pairs={{0,1},{1,6},{2,26},{3,3},{4,5},{5,2},{6,30},{7,7},{8,0},{9,9},{10,... | collective-permute-start | bytes 786440 | tf_op jit(solution)/shard_map/ppermute | solution.py:469
  118.7 4.3 %collective-permute-done.21.refs_0_ = bf16[128,1024]{1,0:T(8,128)(2,1)S(1)} collective-permute-done((bf16[128,1024]{1,0:T(8,128)(2,1)S(1)}, bf16[128,1024]{1,0:T(8,128)(2,1)S(1)}, u32[]{:S(2)}, u32[]{:S(2)}) %collective-permute-start.21) | collective-permute-done | bytes 262176 | tf_op jit(solution)/shard_map/ppermute | solution.py:469
  (50 shorter events, 16.4 us)
Async XLA Ops:
  0.0 24.3 %collective-permute-start = (bf16[1024,1024]{1,0:T(8,128)(2,1)}, bf16[1024,1024]{1,0:T(8,128)(2,1)S(1)}, u32[]{:S(2)}, u32[]{:S(2)}) collective-permute-start(bf16[1024,1024]{1,0:T(8,128)(2,1)} %bitcast.6), channel_id=1, source_target_pairs={{0,1},{1,0},{2,3},{3,2},{4,5},{5,4},{6,7},{7,6},{8,9},{9,8},{10,11... | collective-permute-start | bytes 6291464 | tf_op jit(solution)/shard_map/ppermute | solution.py:418
  30.0 5.7 %collective-permute-start.5 = (bf16[3,4,2,128,512]{4,3,2,1,0:T(8,128)(2,1)S(1)}, bf16[3,4,2,128,512]{4,3,2,1,0:T(8,128)(2,1)S(1)}, u32[]{:S(2)}, u32[]{:S(2)}) collective-permute-start(bf16[3,4,2,128,512]{4,3,2,1,0:T(8,128)(2,1)S(1)} %cross.3), channel_id=1, source_target_pairs={{0,1},{1,0},{2,3},{3,2},{4,5},{5,4},{6,7},{7,6},{8,9},{9,8},{10,11... | collective-permute-start | bytes 9437192 | tf_op jit(solution)/shard_map/ppermute | solution.py:433
  32.5 10.0 %collective-permute-start.4 = (bf16[2,2,128,512]{3,2,1,0:T(8,128)(2,1)S(1)}, bf16[2,2,128,512]{3,2,1,0:T(8,128)(2,1)S(1)}, u32[]{:S(2)}, u32[]{:S(2)}) collective-permute-start(bf16[2,2,128,512]{3,2,1,0:T(8,128)(2,1)S(1)} %get-tuple-element.73), channel_id=1, source_target_pairs={{0,4},{1,17},{2,6},{3,19},{4,0},{5,21},{6,2},{7,23},{8,12},{9,25},... | collective-permute-start | bytes 1572872 | tf_op jit(solution)/shard_map/ppermute | solution.py:451
  33.1 13.2 %collective-permute-start.3 = (bf16[2,2,128,512]{3,2,1,0:T(8,128)(2,1)S(1)}, bf16[2,2,128,512]{3,2,1,0:T(8,128)(2,1)S(1)}, u32[]{:S(2)}, u32[]{:S(2)}) collective-permute-start(bf16[2,2,128,512]{3,2,1,0:T(8,128)(2,1)S(1)} %get-tuple-element.72), channel_id=1, source_target_pairs={{0,6},{1,25},{2,0},{3,27},{4,2},{5,29},{6,4},{7,31},{8,14},{9,1},{... | collective-permute-start | bytes 1572872 | tf_op jit(solution)/shard_map/ppermute | solution.py:451
  35.0 13.6 %collective-permute-start.2 = (bf16[2,2,128,512]{3,2,1,0:T(8,128)(2,1)S(1)}, bf16[2,2,128,512]{3,2,1,0:T(8,128)(2,1)S(1)}, u32[]{:S(2)}, u32[]{:S(2)}) collective-permute-start(bf16[2,2,128,512]{3,2,1,0:T(8,128)(2,1)S(1)} %get-tuple-element.71), channel_id=1, source_target_pairs={{0,2},{1,9},{2,4},{3,11},{4,6},{5,13},{6,0},{7,15},{8,10},{9,17},{... | collective-permute-start | bytes 1572872 | tf_op jit(solution)/shard_map/ppermute | solution.py:451
  42.4 15.7 %collective-permute-start.8 = (bf16[2,2,128,512]{3,2,1,0:T(8,128)(2,1)S(1)}, bf16[2,2,128,512]{3,2,1,0:T(8,128)(2,1)S(1)}, u32[]{:S(2)}, u32[]{:S(2)}) collective-permute-start(bf16[2,2,128,512]{3,2,1,0:T(8,128)(2,1)S(1)} %get-tuple-element.91), channel_id=1, source_target_pairs={{0,4},{1,17},{2,6},{3,19},{4,0},{5,21},{6,2},{7,23},{8,12},{9,25},... | collective-permute-start | bytes 1572872 | tf_op jit(solution)/shard_map/ppermute | solution.py:451
  46.3 13.5 %collective-permute-start.7 = (bf16[2,2,128,512]{3,2,1,0:T(8,128)(2,1)S(1)}, bf16[2,2,128,512]{3,2,1,0:T(8,128)(2,1)S(1)}, u32[]{:S(2)}, u32[]{:S(2)}) collective-permute-start(bf16[2,2,128,512]{3,2,1,0:T(8,128)(2,1)S(1)} %get-tuple-element.89), channel_id=1, source_target_pairs={{0,6},{1,25},{2,0},{3,27},{4,2},{5,29},{6,4},{7,31},{8,14},{9,1},{... | collective-permute-start | bytes 1572872 | tf_op jit(solution)/shard_map/ppermute | solution.py:451
  48.7 13.1 %collective-permute-start.6 = (bf16[2,2,128,512]{3,2,1,0:T(8,128)(2,1)S(1)}, bf16[2,2,128,512]{3,2,1,0:T(8,128)(2,1)S(1)}, u32[]{:S(2)}, u32[]{:S(2)}) collective-permute-start(bf16[2,2,128,512]{3,2,1,0:T(8,128)(2,1)S(1)} %get-tuple-element.87), channel_id=1, source_target_pairs={{0,2},{1,9},{2,4},{3,11},{4,6},{5,13},{6,0},{7,15},{8,10},{9,17},{... | collective-permute-start | bytes 1572872 | tf_op jit(solution)/shard_map/ppermute | solution.py:451
  53.4 13.9 %collective-permute-start.9 = (bf16[2,128,1024]{2,1,0:T(8,128)(2,1)S(1)}, bf16[2,128,1024]{2,1,0:T(8,128)(2,1)S(1)}, u32[]{:S(2)}, u32[]{:S(2)}) collective-permute-start(bf16[2,128,1024]{2,1,0:T(8,128)(2,1)S(1)} %get-tuple-element.74), channel_id=1, source_target_pairs={{0,32},{1,33},{2,34},{3,35},{4,36},{5,37},{6,38},{7,39},{8,40},{9,... | collective-permute-start | bytes 1572872 | tf_op jit(solution)/shard_map/ppermute | solution.py:464
  53.7 28.1 %collective-permute-start.18 = (bf16[2,128,1024]{2,1,0:T(8,128)(2,1)S(1)}, bf16[2,128,1024]{2,1,0:T(8,128)(2,1)S(1)}, u32[]{:S(2)}, u32[]{:S(2)}) collective-permute-start(bf16[2,128,1024]{2,1,0:T(8,128)(2,1)S(1)} %get-tuple-element.75), channel_id=1, source_target_pairs={{0,96},{1,97},{2,98},{3,99},{4,100},{5,101},{6,102},{7,103},{8,104... | collective-permute-start | bytes 1572872 | tf_op jit(solution)/shard_map/ppermute | solution.py:464
  58.2 16.3 %collective-permute-start.14 = (bf16[2,2,128,512]{3,2,1,0:T(8,128)(2,1)S(1)}, bf16[2,2,128,512]{3,2,1,0:T(8,128)(2,1)S(1)}, u32[]{:S(2)}, u32[]{:S(2)}) collective-permute-start(bf16[2,2,128,512]{3,2,1,0:T(8,128)(2,1)S(1)} %get-tuple-element.109), channel_id=1, source_target_pairs={{0,4},{1,17},{2,6},{3,19},{4,0},{5,21},{6,2},{7,23},{8,12},{9,25},... | collective-permute-start | bytes 1572872 | tf_op jit(solution)/shard_map/ppermute | solution.py:451
  59.8 17.1 %collective-permute-start.12 = (bf16[2,2,128,512]{3,2,1,0:T(8,128)(2,1)S(1)}, bf16[2,2,128,512]{3,2,1,0:T(8,128)(2,1)S(1)}, u32[]{:S(2)}, u32[]{:S(2)}) collective-permute-start(bf16[2,2,128,512]{3,2,1,0:T(8,128)(2,1)S(1)} %get-tuple-element.105), channel_id=1, source_target_pairs={{0,6},{1,25},{2,0},{3,27},{4,2},{5,29},{6,4},{7,31},{8,14},{9,1},{... | collective-permute-start | bytes 1572872 | tf_op jit(solution)/shard_map/ppermute | solution.py:451
  61.7 17.9 %collective-permute-start.10 = (bf16[2,2,128,512]{3,2,1,0:T(8,128)(2,1)S(1)}, bf16[2,2,128,512]{3,2,1,0:T(8,128)(2,1)S(1)}, u32[]{:S(2)}, u32[]{:S(2)}) collective-permute-start(bf16[2,2,128,512]{3,2,1,0:T(8,128)(2,1)S(1)} %get-tuple-element.101), channel_id=1, source_target_pairs={{0,2},{1,9},{2,4},{3,11},{4,6},{5,13},{6,0},{7,15},{8,10},{9,17},{... | collective-permute-start | bytes 1572872 | tf_op jit(solution)/shard_map/ppermute | solution.py:451
  71.9 28.0 %collective-permute-start.16 = (bf16[2,128,1024]{2,1,0:T(8,128)(2,1)S(1)}, bf16[2,128,1024]{2,1,0:T(8,128)(2,1)S(1)}, u32[]{:S(2)}, u32[]{:S(2)}) collective-permute-start(bf16[2,128,1024]{2,1,0:T(8,128)(2,1)S(1)} %get-tuple-element.92), channel_id=1, source_target_pairs={{0,32},{1,33},{2,34},{3,35},{4,36},{5,37},{6,38},{7,39},{8,40},{9,... | collective-permute-start | bytes 1572872 | tf_op jit(solution)/shard_map/ppermute | solution.py:464
  74.5 25.5 %collective-permute-start.17 = (bf16[2,128,1024]{2,1,0:T(8,128)(2,1)S(1)}, bf16[2,128,1024]{2,1,0:T(8,128)(2,1)S(1)}, u32[]{:S(2)}, u32[]{:S(2)}) collective-permute-start(bf16[2,128,1024]{2,1,0:T(8,128)(2,1)S(1)} %get-tuple-element.93), channel_id=1, source_target_pairs={{0,96},{1,97},{2,98},{3,99},{4,100},{5,101},{6,102},{7,103},{8,104... | collective-permute-start | bytes 1572872 | tf_op jit(solution)/shard_map/ppermute | solution.py:464
  76.8 9.8 %collective-permute-start.15 = (bf16[2,2,128,512]{3,2,1,0:T(8,128)(2,1)S(1)}, bf16[2,2,128,512]{3,2,1,0:T(8,128)(2,1)S(1)}, u32[]{:S(2)}, u32[]{:S(2)}) collective-permute-start(bf16[2,2,128,512]{3,2,1,0:T(8,128)(2,1)S(1)} %get-tuple-element.110), channel_id=1, source_target_pairs={{0,4},{1,17},{2,6},{3,19},{4,0},{5,21},{6,2},{7,23},{8,12},{9,25},... | collective-permute-start | bytes 1572872 | tf_op jit(solution)/shard_map/ppermute | solution.py:451
  79.7 15.1 %collective-permute-start.13 = (bf16[2,2,128,512]{3,2,1,0:T(8,128)(2,1)S(1)}, bf16[2,2,128,512]{3,2,1,0:T(8,128)(2,1)S(1)}, u32[]{:S(2)}, u32[]{:S(2)}) collective-permute-start(bf16[2,2,128,512]{3,2,1,0:T(8,128)(2,1)S(1)} %get-tuple-element.106), channel_id=1, source_target_pairs={{0,6},{1,25},{2,0},{3,27},{4,2},{5,29},{6,4},{7,31},{8,14},{9,1},{... | collective-permute-start | bytes 1572872 | tf_op jit(solution)/shard_map/ppermute | solution.py:451
  81.8 13.1 %collective-permute-start.11 = (bf16[2,2,128,512]{3,2,1,0:T(8,128)(2,1)S(1)}, bf16[2,2,128,512]{3,2,1,0:T(8,128)(2,1)S(1)}, u32[]{:S(2)}, u32[]{:S(2)}) collective-permute-start(bf16[2,2,128,512]{3,2,1,0:T(8,128)(2,1)S(1)} %get-tuple-element.102), channel_id=1, source_target_pairs={{0,2},{1,9},{2,4},{3,11},{4,6},{5,13},{6,0},{7,15},{8,10},{9,17},{... | collective-permute-start | bytes 1572872 | tf_op jit(solution)/shard_map/ppermute | solution.py:451
  86.7 13.3 %collective-permute-start.19 = (bf16[2,128,1024]{2,1,0:T(8,128)(2,1)S(1)}, bf16[2,128,1024]{2,1,0:T(8,128)(2,1)S(1)}, u32[]{:S(2)}, u32[]{:S(2)}) collective-permute-start(bf16[2,128,1024]{2,1,0:T(8,128)(2,1)S(1)} %get-tuple-element.113), channel_id=1, source_target_pairs={{0,32},{1,33},{2,34},{3,35},{4,36},{5,37},{6,38},{7,39},{8,40},{9,... | collective-permute-start | bytes 1572872 | tf_op jit(solution)/shard_map/ppermute | solution.py:464
  94.8 12.7 %collective-permute-start.20 = (bf16[2,128,1024]{2,1,0:T(8,128)(2,1)S(1)}, bf16[2,128,1024]{2,1,0:T(8,128)(2,1)S(1)}, u32[]{:S(2)}, u32[]{:S(2)}) collective-permute-start(bf16[2,128,1024]{2,1,0:T(8,128)(2,1)S(1)} %get-tuple-element.114), channel_id=1, source_target_pairs={{0,96},{1,97},{2,98},{3,99},{4,100},{5,101},{6,102},{7,103},{8,104... | collective-permute-start | bytes 1572872 | tf_op jit(solution)/shard_map/ppermute | solution.py:464
  108.0 14.9 %collective-permute-start.21 = (bf16[128,1024]{1,0:T(8,128)(2,1)S(1)}, bf16[128,1024]{1,0:T(8,128)(2,1)S(1)}, u32[]{:S(2)}, u32[]{:S(2)}) collective-permute-start(bf16[128,1024]{1,0:T(8,128)(2,1)S(1)} %get-tuple-element.115), channel_id=1, source_target_pairs={{0,0},{1,3},{2,11},{3,2},{4,4},{5,7},{6,15},{7,6},{8,17},{9,8},{10... | collective-permute-start | bytes 786440 | tf_op jit(solution)/shard_map/ppermute | solution.py:469
  109.9 13.0 %collective-permute-start.22 = (bf16[128,1024]{1,0:T(8,128)(2,1)S(1)}, bf16[128,1024]{1,0:T(8,128)(2,1)S(1)}, u32[]{:S(2)}, u32[]{:S(2)}) collective-permute-start(bf16[128,1024]{1,0:T(8,128)(2,1)S(1)} %get-tuple-element.116), channel_id=1, source_target_pairs={{0,17},{1,2},{2,10},{3,7},{4,21},{5,6},{6,14},{7,3},{8,16},{9,13},... | collective-permute-start | bytes 786440 | tf_op jit(solution)/shard_map/ppermute | solution.py:469
  110.0 12.9 %collective-permute-start.23 = (bf16[128,1024]{1,0:T(8,128)(2,1)S(1)}, bf16[128,1024]{1,0:T(8,128)(2,1)S(1)}, u32[]{:S(2)}, u32[]{:S(2)}) collective-permute-start(bf16[128,1024]{1,0:T(8,128)(2,1)S(1)} %get-tuple-element.117), channel_id=1, source_target_pairs={{0,16},{1,7},{2,27},{3,6},{4,20},{5,3},{6,31},{7,2},{8,1},{9,12},{... | collective-permute-start | bytes 786440 | tf_op jit(solution)/shard_map/ppermute | solution.py:469
  110.9 12.0 %collective-permute-start.24 = (bf16[128,1024]{1,0:T(8,128)(2,1)S(1)}, bf16[128,1024]{1,0:T(8,128)(2,1)S(1)}, u32[]{:S(2)}, u32[]{:S(2)}) collective-permute-start(bf16[128,1024]{1,0:T(8,128)(2,1)S(1)} %get-tuple-element.118), channel_id=1, source_target_pairs={{0,1},{1,6},{2,26},{3,3},{4,5},{5,2},{6,30},{7,7},{8,0},{9,9},{10,... | collective-permute-start | bytes 786440 | tf_op jit(solution)/shard_map/ppermute | solution.py:469
  (4 other events, 41.2 us)

commit v6 on v5

--- a/solution.py
+++ b/solution.py
@@ -299,15 +299,15 @@
             here = result[which]
             if which in added:
                 here += extra[added.index(which)][:, :, start : start + tile].astype(F32)
-            outs[which][:, :, start : start + tile] = here.astype(BF16)
-
-
-def project(chunk, row, added, words, table, *others):
+            outs[which][:, :, start : start + tile] = here.astype(outs[which].dtype)
+
+
+def project(chunk, row, added, kept, words, table, *others):
     width = table.shape[1]
     wide = 2 * width
     return pl.pallas_call(
         functools.partial(project_kernel, chunk, row, added),
-        out_shape=[pltpu.VMEM((2, DST, wide), BF16)] * 2,
+        out_shape=[pltpu.VMEM((2, DST, wide), F32 if which in kept else BF16) for which in range(2)],
         in_specs=[SMEM_SPEC, HBM_SPEC] + [VMEM_SPEC] * len(others),
         out_specs=[VMEM_SPEC] * 2,
         scratch_shapes=[
@@ -321,6 +321,22 @@
     )(words, in_hbm(table), *map(in_vmem, others))
 
 
+def join_kernel(part_ref, relayed_ref, out_ref):
+    out_ref[...] = (part_ref[...] + relayed_ref[...].astype(F32)).astype(BF16)
+
+
+def join(part, relayed):
+    return pl.pallas_call(
+        join_kernel,
+        out_shape=pltpu.VMEM(part.shape, BF16),
+        in_specs=[VMEM_SPEC] * 2,
+        out_specs=VMEM_SPEC,
+        compiler_params=pltpu.CompilerParams(vmem_limit_bytes=VMEM_SMALL),
+        cost_estimate=SMALL,
+        name="join",
+    )(in_vmem(part), in_vmem(relayed))
+
+
 def merge_kernel(*refs):
     ins, outs = refs[:6], refs[6:]
     x, y, z, core = coordinates()
@@ -439,27 +455,30 @@
         return lax.optimization_barrier((bufs, words))
 
     picked, ready = [pick_chunk(0, words)[0]], words
-    bufs, _ = pick_chunk(1, picked[0])
+    bufs, ready = pick_chunk(1, picked[0])
     picked.append(bufs)
     arrived, parts = [], []
     for i, (chunk, (row, buf)) in enumerate(zip(CHUNKS, crossed)):
         came = []
         for j, step in enumerate(HOP1):
             sent = picked[i][j]
-            if i > 0:
-                sent, arrived[-1][j] = lax.optimization_barrier((sent, arrived[-1][j]))
+            if i > 1:
+                sent, arrived[-2][j] = lax.optimization_barrier((sent, arrived[-2][j]))
             came.append(lax.ppermute(sent, AXES, hop1_pairs(step)))
         arrived.append(came)
         given = [ready, features, *both, notes, table, buf, *came]
         added = ()
-        if i == FROM_BELOW:
-            added, given = (0,), given + [parts[0][0]]
         if i == FROM_ABOVE:
             added, given = (1,), given + [parts[0][1]]
-        part = project(chunk, row, added, *given)
+        part = project(chunk, row, added, (0,) if i == FROM_BELOW else (), *given)
         if i + 2 < len(CHUNKS):
             bufs, ready = pick_chunk(i + 2, part)
             picked.append(bufs)
+        if i == FROM_BELOW:
+            part = [join(part[0], parts[0][0]), part[1]]
+            part[0], parts[0][1] = lax.optimization_barrier((part[0], parts[0][1]))
+        if i == FROM_ABOVE:
+            part, parts[-1] = lax.optimization_barrier((part, parts[-1]))
         if i < len(CHUNKS) - 1:
             part = [lax.ppermute(p, AXES, hop2_pairs(step)) for p, step in zip(part, (1, 3))]
         parts.append(part)

time: 126 us -> 115 us (0.913)
  waiting for transfers between devices: 34.4 us -> 14.3 us
  starting transfers between devices: 34.3 us -> 44.8 us
    ppermute x12, waiting for transfers between devices: 16.3 us -> 2.03 us  [body(): came.append(lax.ppermute(sent, AXES, hop1_pairs(step)))]
    ppermute x12, starting transfers between devices: 14.5 us -> 22.1 us  [body(): came.append(lax.ppermute(sent, AXES, hop1_pairs(step)))]
    ppermute x6, waiting for transfers between devices: 13.2 us -> 6.99 us  [body(): lax.ppermute(p, AXES, hop2_pairs(step))]
    ppermute x6, starting transfers between devices: 5.89 us -> 8.12 us  [body(): lax.ppermute(p, AXES, hop2_pairs(step))]
    ppermute x4, starting transfers between devices: 10.5 us -> 12.4 us  [body(): lax.ppermute(buf, AXES, hop3_pairs(send))]
    pallas_call x4, Pallas kernels: 7.92 us -> 6.59 us  [pick(): pl.pallas_call(functools.partial(pick_kernel, chunk, row), out_shape=[plt...]
  transfers between devices with their start and end apart: 25 -> 25, of which waited for: 7 -> 9; matrix products, arithmetic and copies ran while one was open for 0% -> 0% of each run, Pallas kernels for 25% -> 26%
where the time goes in v6:
time: 115 us; the launch traced here: 113 us
  starting transfers between devices  44.8 us (39%)
  Pallas kernels  32.6 us (28%)
  blocking collectives  21.1 us (18%)
  waiting for transfers between devices  14.3 us (12%)
    ppermute x12, starting transfers between devices, body(): came.append(lax.ppermute(sent, AXES, hop1_pairs(step)))  22.1 us
    all_to_all x1, blocking collectives, body(): lax.all_to_all(sent, 'shard', split_axis=0, concat_axis=0, tiled=True)  21.1 us
    pallas_call x4, Pallas kernels, project(): pl.pallas_call(functools.partial(project_kernel, chunk, row, added), out_...  18.8 us
    ppermute x4, starting transfers between devices, body(): lax.ppermute(buf, AXES, hop3_pairs(send))  12.4 us
    ppermute x6, starting transfers between devices, body(): lax.ppermute(p, AXES, hop2_pairs(step))  8.12 us
    ppermute x6, waiting for transfers between devices, body(): lax.ppermute(p, AXES, hop2_pairs(step))  6.99 us
    pallas_call x4, Pallas kernels, pick(): pl.pallas_call(functools.partial(pick_kernel, chunk, row), out_shape=[plt...  6.59 us
    ppermute x4, waiting for transfers between devices, body(): lax.ppermute(buf, AXES, hop3_pairs(send))  5.13 us
  transfers between devices with their start and end apart: 25, of which 9 were waited for; matrix products, arithmetic and copies ran while one was open for 0% of the time, Pallas kernels for 26%

profile of v6, /device:TPU:1, one launch (start us, length us, event | category | flops | bytes accessed | tf_op | source)
XLA Modules:
  0.0 113.2 jit_solution(378133219060767811)
XLA Ops:
  3.0 21.1 %all_to_all.5.notes_ref = s32[64,8,128]{2,1,0:T(8,128)S(1)} all-to-all(s32[64,8,128]{2,1,0:T(8,128)S(1)} %bitcast.4), channel_id=1, replica_groups=mesh['shard'=64,'basis'=2] {'shard'}, dimensions={0} | all-to-all | bytes 524288 | tf_op jit(solution)/shard_map/all_to_all | solution.py:437
  24.3 1.9 %cross.2 = bf16[1,4,2,128,512]{4,3,2,1,0:T(8,128)(2,1)S(1)} custom-call(s32[1024]{0:T(1024)S(1)} %reshape.11.words_ref, bf16[6144,512]{1,0:T(8,128)(2,1)} %table_ref.19), custom_call_target="tpu_custom_call" | custom-call | flops 1 | bytes 1 | tf_op jit(solution)/shard_map/cross/pallas_call | solution.py:193
  26.6 2.2 %cross.3 = bf16[3,4,2,128,512]{4,3,2,1,0:T(8,128)(2,1)S(1)} custom-call(s32[1024]{0:T(1024)S(1)} %reshape.11.words_ref, bf16[6144,512]{1,0:T(8,128)(2,1)} %table_ref.19), custom_call_target="tpu_custom_call" | custom-call | flops 1 | bytes 1 | tf_op jit(solution)/shard_map/cross/pallas_call | solution.py:193
  30.5 2.4 %collective-permute-start.4 = (bf16[2,2,128,512]{3,2,1,0:T(8,128)(2,1)S(1)}, bf16[2,2,128,512]{3,2,1,0:T(8,128)(2,1)S(1)}, u32[]{:S(2)}, u32[]{:S(2)}) collective-permute-start(bf16[2,2,128,512]{3,2,1,0:T(8,128)(2,1)S(1)} %get-tuple-element.75), channel_id=1, source_target_pairs={{0,6},{1,25},{2,0},{3,27},{4,2},{5,29},{6,4},{7,31},{8,14},{9,1},{... | collective-permute-start | bytes 1572872 | tf_op jit(solution)/shard_map/ppermute | solution.py:467
  33.0 1.8 %collective-permute-start.5 = (bf16[2,2,128,512]{3,2,1,0:T(8,128)(2,1)S(1)}, bf16[2,2,128,512]{3,2,1,0:T(8,128)(2,1)S(1)}, u32[]{:S(2)}, u32[]{:S(2)}) collective-permute-start(bf16[2,2,128,512]{3,2,1,0:T(8,128)(2,1)S(1)} %get-tuple-element.76), channel_id=1, source_target_pairs={{0,4},{1,17},{2,6},{3,19},{4,0},{5,21},{6,2},{7,23},{8,12},{9,25},... | collective-permute-start | bytes 1572872 | tf_op jit(solution)/shard_map/ppermute | solution.py:467
  37.3 2.0 %collective-permute-start.7 = (bf16[2,2,128,512]{3,2,1,0:T(8,128)(2,1)S(1)}, bf16[2,2,128,512]{3,2,1,0:T(8,128)(2,1)S(1)}, u32[]{:S(2)}, u32[]{:S(2)}) collective-permute-start(bf16[2,2,128,512]{3,2,1,0:T(8,128)(2,1)S(1)} %get-tuple-element.92), channel_id=1, source_target_pairs={{0,6},{1,25},{2,0},{3,27},{4,2},{5,29},{6,4},{7,31},{8,14},{9,1},{... | collective-permute-start | bytes 1572872 | tf_op jit(solution)/shard_map/ppermute | solution.py:467
  39.7 7.5 %collective-permute-start.8 = (bf16[2,2,128,512]{3,2,1,0:T(8,128)(2,1)S(1)}, bf16[2,2,128,512]{3,2,1,0:T(8,128)(2,1)S(1)}, u32[]{:S(2)}, u32[]{:S(2)}) collective-permute-start(bf16[2,2,128,512]{3,2,1,0:T(8,128)(2,1)S(1)} %get-tuple-element.93), channel_id=1, source_target_pairs={{0,4},{1,17},{2,6},{3,19},{4,0},{5,21},{6,2},{7,23},{8,12},{9,25},... | collective-permute-start | bytes 1572872 | tf_op jit(solution)/shard_map/ppermute | solution.py:467
  47.2 4.4 %project.4 = (bf16[2,128,1024]{2,1,0:T(8,128)(2,1)S(1)}, bf16[2,128,1024]{2,1,0:T(8,128)(2,1)S(1)}) custom-call(s32[1024]{0:T(1024)S(1)} %reshape.11.words_ref, bf16[6144,512]{1,0:T(8,128)(2,1)} %table_ref.19, bf16[1024,1024]{1,0:T(8,128)(2,1)S(1)} %bitcast.7, bf16[1024,1024]{1,0:T(8,128)(2,1)S(1)} %collective-permute-done.other_basis, ...), custom_call_target="tpu_custom_call" | custom-call | flops 6000000000 | bytes 20000000 | tf_op jit(solution)/shard_map/project/pallas_call | solution.py:308
  51.8 2.6 %collective-permute-start.16 = (bf16[2,128,1024]{2,1,0:T(8,128)(2,1)S(1)}, bf16[2,128,1024]{2,1,0:T(8,128)(2,1)S(1)}, u32[]{:S(2)}, u32[]{:S(2)}) collective-permute-start(bf16[2,128,1024]{2,1,0:T(8,128)(2,1)S(1)} %get-tuple-element.85), channel_id=1, source_target_pairs={{0,96},{1,97},{2,98},{3,99},{4,100},{5,101},{6,102},{7,103},{8,104... | collective-permute-start | bytes 1572872 | tf_op jit(solution)/shard_map/ppermute | solution.py:483
  56.1 2.3 %collective-permute-start.14 = (bf16[2,2,128,512]{3,2,1,0:T(8,128)(2,1)S(1)}, bf16[2,2,128,512]{3,2,1,0:T(8,128)(2,1)S(1)}, u32[]{:S(2)}, u32[]{:S(2)}) collective-permute-start(bf16[2,2,128,512]{3,2,1,0:T(8,128)(2,1)S(1)} %get-tuple-element.113), channel_id=1, source_target_pairs={{0,4},{1,17},{2,6},{3,19},{4,0},{5,21},{6,2},{7,23},{8,12},{9,25},... | collective-permute-start | bytes 1572872 | tf_op jit(solution)/shard_map/ppermute | solution.py:467
  59.9 4.6 %project.5 = (f32[2,128,1024]{2,1,0:T(8,128)S(1)}, bf16[2,128,1024]{2,1,0:T(8,128)(2,1)S(1)}) custom-call(s32[1024]{0:T(1024)S(1)} %reshape.11.words_ref, bf16[6144,512]{1,0:T(8,128)(2,1)} %table_ref.19, bf16[1024,1024]{1,0:T(8,128)(2,1)S(1)} %bitcast.8, bf16[1024,1024]{1,0:T(8,128)(2,1)S(1)} %collective-permute-done.other_basis, ...), custom_call_target="tpu_custom_call" | custom-call | flops 6000000000 | bytes 20000000 | tf_op jit(solution)/shard_map/project/pallas_call | solution.py:308
  65.0 2.6 %collective-permute-start.18 = (bf16[2,128,1024]{2,1,0:T(8,128)(2,1)S(1)}, bf16[2,128,1024]{2,1,0:T(8,128)(2,1)S(1)}, u32[]{:S(2)}, u32[]{:S(2)}) collective-permute-start(bf16[2,128,1024]{2,1,0:T(8,128)(2,1)S(1)} %get-tuple-element.95), channel_id=1, source_target_pairs={{0,96},{1,97},{2,98},{3,99},{4,100},{5,101},{6,102},{7,103},{8,104... | collective-permute-start | bytes 1572872 | tf_op jit(solution)/shard_map/ppermute | solution.py:483
  67.8 2.3 %pick.7 = (bf16[2,2,128,512]{3,2,1,0:T(8,128)(2,1)S(1)}, bf16[2,2,128,512]{3,2,1,0:T(8,128)(2,1)S(1)}, bf16[2,2,128,512]{3,2,1,0:T(8,128)(2,1)S(1)}) custom-call(s32[1024]{0:T(1024)S(1)} %reshape.11.words_ref, bf16[6144,512]{1,0:T(8,128)(2,1)} %table_ref.19, bf16[3,4,2,128,512]{4,3,2,1,0:T(8,128)(2,1)S(1)} %collective-permute-done.2.crossed_ref), custom_call_target="tpu_custom_call" | custom-call | flops 1 | bytes 1 | tf_op jit(solution)/shard_map/pick/pallas_call | solution.py:221
  70.1 1.9 %collective-permute-start.11 = (bf16[2,2,128,512]{3,2,1,0:T(8,128)(2,1)S(1)}, bf16[2,2,128,512]{3,2,1,0:T(8,128)(2,1)S(1)}, u32[]{:S(2)}, u32[]{:S(2)}) collective-permute-start(bf16[2,2,128,512]{3,2,1,0:T(8,128)(2,1)S(1)} %get-tuple-element.106), channel_id=1, source_target_pairs={{0,4},{1,17},{2,6},{3,19},{4,0},{5,21},{6,2},{7,23},{8,12},{9,25},... | collective-permute-start | bytes 1572872 | tf_op jit(solution)/shard_map/ppermute | solution.py:467
  73.5 5.2 %project.7 = (bf16[2,128,1024]{2,1,0:T(8,128)(2,1)S(1)}, bf16[2,128,1024]{2,1,0:T(8,128)(2,1)S(1)}) custom-call(s32[1024]{0:T(1024)S(1)} %reshape.11.words_ref, bf16[6144,512]{1,0:T(8,128)(2,1)} %table_ref.19, bf16[1024,1024]{1,0:T(8,128)(2,1)S(1)} %bitcast.9, bf16[1024,1024]{1,0:T(8,128)(2,1)S(1)} %collective-permute-done.other_basis, ...), custom_call_target="tpu_custom_call" | custom-call | flops 6000000000 | bytes 20000000 | tf_op jit(solution)/shard_map/project/pallas_call | solution.py:308
  78.7 2.7 %collective-permute-done.17.refs_1_ = bf16[2,128,1024]{2,1,0:T(8,128)(2,1)S(1)} collective-permute-done((bf16[2,128,1024]{2,1,0:T(8,128)(2,1)S(1)}, bf16[2,128,1024]{2,1,0:T(8,128)(2,1)S(1)}, u32[]{:S(2)}, u32[]{:S(2)}) %collective-permute-start.17) | collective-permute-done | bytes 524320 | tf_op jit(solution)/shard_map/ppermute | solution.py:483
  81.4 2.7 %collective-permute-start.20 = (bf16[2,128,1024]{2,1,0:T(8,128)(2,1)S(1)}, bf16[2,128,1024]{2,1,0:T(8,128)(2,1)S(1)}, u32[]{:S(2)}, u32[]{:S(2)}) collective-permute-start(bf16[2,128,1024]{2,1,0:T(8,128)(2,1)S(1)} %get-tuple-element.122), channel_id=1, source_target_pairs={{0,96},{1,97},{2,98},{3,99},{4,100},{5,101},{6,102},{7,103},{8,104... | collective-permute-start | bytes 1572872 | tf_op jit(solution)/shard_map/ppermute | solution.py:483
  85.6 4.6 %project.6 = (bf16[2,128,1024]{2,1,0:T(8,128)(2,1)S(1)}, bf16[2,128,1024]{2,1,0:T(8,128)(2,1)S(1)}) custom-call(s32[1024]{0:T(1024)S(1)} %reshape.11.words_ref, bf16[6144,512]{1,0:T(8,128)(2,1)} %table_ref.19, bf16[1024,1024]{1,0:T(8,128)(2,1)S(1)} %bitcast.10, bf16[1024,1024]{1,0:T(8,128)(2,1)S(1)} %collective-permute-done.other_basis, ...), custom_call_target="tpu_custom_call" | custom-call | flops 6000000000 | bytes 20000000 | tf_op jit(solution)/shard_map/project/pallas_call | solution.py:308
  90.3 3.8 %collective-permute-done.19.refs_4_ = bf16[2,128,1024]{2,1,0:T(8,128)(2,1)S(1)} collective-permute-done((bf16[2,128,1024]{2,1,0:T(8,128)(2,1)S(1)}, bf16[2,128,1024]{2,1,0:T(8,128)(2,1)S(1)}, u32[]{:S(2)}, u32[]{:S(2)}) %collective-permute-start.19) | collective-permute-done | bytes 524320 | tf_op jit(solution)/shard_map/ppermute | solution.py:483
  94.6 3.4 %collective-permute-start.21 = (bf16[128,1024]{1,0:T(8,128)(2,1)S(1)}, bf16[128,1024]{1,0:T(8,128)(2,1)S(1)}, u32[]{:S(2)}, u32[]{:S(2)}) collective-permute-start(bf16[128,1024]{1,0:T(8,128)(2,1)S(1)} %get-tuple-element.123), channel_id=1, source_target_pairs={{0,0},{1,3},{2,11},{3,2},{4,4},{5,7},{6,15},{7,6},{8,17},{9,8},{10... | collective-permute-start | bytes 786440 | tf_op jit(solution)/shard_map/ppermute | solution.py:488
  98.0 2.8 %collective-permute-start.22 = (bf16[128,1024]{1,0:T(8,128)(2,1)S(1)}, bf16[128,1024]{1,0:T(8,128)(2,1)S(1)}, u32[]{:S(2)}, u32[]{:S(2)}) collective-permute-start(bf16[128,1024]{1,0:T(8,128)(2,1)S(1)} %get-tuple-element.124), channel_id=1, source_target_pairs={{0,17},{1,2},{2,10},{3,7},{4,21},{5,6},{6,14},{7,3},{8,16},{9,13},... | collective-permute-start | bytes 786440 | tf_op jit(solution)/shard_map/ppermute | solution.py:488
  100.8 2.5 %collective-permute-start.23 = (bf16[128,1024]{1,0:T(8,128)(2,1)S(1)}, bf16[128,1024]{1,0:T(8,128)(2,1)S(1)}, u32[]{:S(2)}, u32[]{:S(2)}) collective-permute-start(bf16[128,1024]{1,0:T(8,128)(2,1)S(1)} %get-tuple-element.125), channel_id=1, source_target_pairs={{0,16},{1,7},{2,27},{3,6},{4,20},{5,3},{6,31},{7,2},{8,1},{9,12},{... | collective-permute-start | bytes 786440 | tf_op jit(solution)/shard_map/ppermute | solution.py:488
  103.3 3.7 %collective-permute-start.24 = (bf16[128,1024]{1,0:T(8,128)(2,1)S(1)}, bf16[128,1024]{1,0:T(8,128)(2,1)S(1)}, u32[]{:S(2)}, u32[]{:S(2)}) collective-permute-start(bf16[128,1024]{1,0:T(8,128)(2,1)S(1)} %get-tuple-element.126), channel_id=1, source_target_pairs={{0,1},{1,6},{2,26},{3,3},{4,5},{5,2},{6,30},{7,7},{8,0},{9,9},{10,... | collective-permute-start | bytes 786440 | tf_op jit(solution)/shard_map/ppermute | solution.py:488
  107.2 3.8 %collective-permute-done.21.refs_0_ = bf16[128,1024]{1,0:T(8,128)(2,1)S(1)} collective-permute-done((bf16[128,1024]{1,0:T(8,128)(2,1)S(1)}, bf16[128,1024]{1,0:T(8,128)(2,1)S(1)}, u32[]{:S(2)}, u32[]{:S(2)}) %collective-permute-start.21) | collective-permute-done | bytes 262176 | tf_op jit(solution)/shard_map/ppermute | solution.py:488
  (51 shorter events, 18.1 us)
Async XLA Ops:
  0.0 24.3 %collective-permute-start = (bf16[1024,1024]{1,0:T(8,128)(2,1)}, bf16[1024,1024]{1,0:T(8,128)(2,1)S(1)}, u32[]{:S(2)}, u32[]{:S(2)}) collective-permute-start(bf16[1024,1024]{1,0:T(8,128)(2,1)} %bitcast.6), channel_id=1, source_target_pairs={{0,1},{1,0},{2,3},{3,2},{4,5},{5,4},{6,7},{7,6},{8,9},{9,8},{10,11... | collective-permute-start | bytes 6291464 | tf_op jit(solution)/shard_map/ppermute | solution.py:434
  29.0 5.8 %collective-permute-start.2 = (bf16[3,4,2,128,512]{4,3,2,1,0:T(8,128)(2,1)S(1)}, bf16[3,4,2,128,512]{4,3,2,1,0:T(8,128)(2,1)S(1)}, u32[]{:S(2)}, u32[]{:S(2)}) collective-permute-start(bf16[3,4,2,128,512]{4,3,2,1,0:T(8,128)(2,1)S(1)} %cross.3), channel_id=1, source_target_pairs={{0,1},{1,0},{2,3},{3,2},{4,5},{5,4},{6,7},{7,6},{8,9},{9,8},{10,11... | collective-permute-start | bytes 9437192 | tf_op jit(solution)/shard_map/ppermute | solution.py:449
  30.1 9.6 %collective-permute-start.3 = (bf16[2,2,128,512]{3,2,1,0:T(8,128)(2,1)S(1)}, bf16[2,2,128,512]{3,2,1,0:T(8,128)(2,1)S(1)}, u32[]{:S(2)}, u32[]{:S(2)}) collective-permute-start(bf16[2,2,128,512]{3,2,1,0:T(8,128)(2,1)S(1)} %get-tuple-element.74), channel_id=1, source_target_pairs={{0,2},{1,9},{2,4},{3,11},{4,6},{5,13},{6,0},{7,15},{8,10},{9,17},{... | collective-permute-start | bytes 1572872 | tf_op jit(solution)/shard_map/ppermute | solution.py:467
  30.5 16.7 %collective-permute-start.4 = (bf16[2,2,128,512]{3,2,1,0:T(8,128)(2,1)S(1)}, bf16[2,2,128,512]{3,2,1,0:T(8,128)(2,1)S(1)}, u32[]{:S(2)}, u32[]{:S(2)}) collective-permute-start(bf16[2,2,128,512]{3,2,1,0:T(8,128)(2,1)S(1)} %get-tuple-element.75), channel_id=1, source_target_pairs={{0,6},{1,25},{2,0},{3,27},{4,2},{5,29},{6,4},{7,31},{8,14},{9,1},{... | collective-permute-start | bytes 1572872 | tf_op jit(solution)/shard_map/ppermute | solution.py:467
  33.0 14.3 %collective-permute-start.5 = (bf16[2,2,128,512]{3,2,1,0:T(8,128)(2,1)S(1)}, bf16[2,2,128,512]{3,2,1,0:T(8,128)(2,1)S(1)}, u32[]{:S(2)}, u32[]{:S(2)}) collective-permute-start(bf16[2,2,128,512]{3,2,1,0:T(8,128)(2,1)S(1)} %get-tuple-element.76), channel_id=1, source_target_pairs={{0,4},{1,17},{2,6},{3,19},{4,0},{5,21},{6,2},{7,23},{8,12},{9,25},... | collective-permute-start | bytes 1572872 | tf_op jit(solution)/shard_map/ppermute | solution.py:467
  36.5 19.6 %collective-permute-start.6 = (bf16[2,2,128,512]{3,2,1,0:T(8,128)(2,1)S(1)}, bf16[2,2,128,512]{3,2,1,0:T(8,128)(2,1)S(1)}, u32[]{:S(2)}, u32[]{:S(2)}) collective-permute-start(bf16[2,2,128,512]{3,2,1,0:T(8,128)(2,1)S(1)} %get-tuple-element.91), channel_id=1, source_target_pairs={{0,2},{1,9},{2,4},{3,11},{4,6},{5,13},{6,0},{7,15},{8,10},{9,17},{... | collective-permute-start | bytes 1572872 | tf_op jit(solution)/shard_map/ppermute | solution.py:467
  37.3 21.2 %collective-permute-start.7 = (bf16[2,2,128,512]{3,2,1,0:T(8,128)(2,1)S(1)}, bf16[2,2,128,512]{3,2,1,0:T(8,128)(2,1)S(1)}, u32[]{:S(2)}, u32[]{:S(2)}) collective-permute-start(bf16[2,2,128,512]{3,2,1,0:T(8,128)(2,1)S(1)} %get-tuple-element.92), channel_id=1, source_target_pairs={{0,6},{1,25},{2,0},{3,27},{4,2},{5,29},{6,4},{7,31},{8,14},{9,1},{... | collective-permute-start | bytes 1572872 | tf_op jit(solution)/shard_map/ppermute | solution.py:467
  39.7 19.6 %collective-permute-start.8 = (bf16[2,2,128,512]{3,2,1,0:T(8,128)(2,1)S(1)}, bf16[2,2,128,512]{3,2,1,0:T(8,128)(2,1)S(1)}, u32[]{:S(2)}, u32[]{:S(2)}) collective-permute-start(bf16[2,2,128,512]{3,2,1,0:T(8,128)(2,1)S(1)} %get-tuple-element.93), channel_id=1, source_target_pairs={{0,4},{1,17},{2,6},{3,19},{4,0},{5,21},{6,2},{7,23},{8,12},{9,25},... | collective-permute-start | bytes 1572872 | tf_op jit(solution)/shard_map/ppermute | solution.py:467
  51.6 13.3 %collective-permute-start.15 = (bf16[2,128,1024]{2,1,0:T(8,128)(2,1)S(1)}, bf16[2,128,1024]{2,1,0:T(8,128)(2,1)S(1)}, u32[]{:S(2)}, u32[]{:S(2)}) collective-permute-start(bf16[2,128,1024]{2,1,0:T(8,128)(2,1)S(1)} %get-tuple-element.84), channel_id=1, source_target_pairs={{0,32},{1,33},{2,34},{3,35},{4,36},{5,37},{6,38},{7,39},{8,40},{9,... | collective-permute-start | bytes 1572872 | tf_op jit(solution)/shard_map/ppermute | solution.py:483
  51.8 15.9 %collective-permute-start.16 = (bf16[2,128,1024]{2,1,0:T(8,128)(2,1)S(1)}, bf16[2,128,1024]{2,1,0:T(8,128)(2,1)S(1)}, u32[]{:S(2)}, u32[]{:S(2)}) collective-permute-start(bf16[2,128,1024]{2,1,0:T(8,128)(2,1)S(1)} %get-tuple-element.85), channel_id=1, source_target_pairs={{0,96},{1,97},{2,98},{3,99},{4,100},{5,101},{6,102},{7,103},{8,104... | collective-permute-start | bytes 1572872 | tf_op jit(solution)/shard_map/ppermute | solution.py:483
  56.1 14.0 %collective-permute-start.14 = (bf16[2,2,128,512]{3,2,1,0:T(8,128)(2,1)S(1)}, bf16[2,2,128,512]{3,2,1,0:T(8,128)(2,1)S(1)}, u32[]{:S(2)}, u32[]{:S(2)}) collective-permute-start(bf16[2,2,128,512]{3,2,1,0:T(8,128)(2,1)S(1)} %get-tuple-element.113), channel_id=1, source_target_pairs={{0,4},{1,17},{2,6},{3,19},{4,0},{5,21},{6,2},{7,23},{8,12},{9,25},... | collective-permute-start | bytes 1572872 | tf_op jit(solution)/shard_map/ppermute | solution.py:467
  58.5 13.6 %collective-permute-start.13 = (bf16[2,2,128,512]{3,2,1,0:T(8,128)(2,1)S(1)}, bf16[2,2,128,512]{3,2,1,0:T(8,128)(2,1)S(1)}, u32[]{:S(2)}, u32[]{:S(2)}) collective-permute-start(bf16[2,2,128,512]{3,2,1,0:T(8,128)(2,1)S(1)} %get-tuple-element.111), channel_id=1, source_target_pairs={{0,6},{1,25},{2,0},{3,27},{4,2},{5,29},{6,4},{7,31},{8,14},{9,1},{... | collective-permute-start | bytes 1572872 | tf_op jit(solution)/shard_map/ppermute | solution.py:467
  59.4 13.3 %collective-permute-start.12 = (bf16[2,2,128,512]{3,2,1,0:T(8,128)(2,1)S(1)}, bf16[2,2,128,512]{3,2,1,0:T(8,128)(2,1)S(1)}, u32[]{:S(2)}, u32[]{:S(2)}) collective-permute-start(bf16[2,2,128,512]{3,2,1,0:T(8,128)(2,1)S(1)} %get-tuple-element.109), channel_id=1, source_target_pairs={{0,2},{1,9},{2,4},{3,11},{4,6},{5,13},{6,0},{7,15},{8,10},{9,17},{... | collective-permute-start | bytes 1572872 | tf_op jit(solution)/shard_map/ppermute | solution.py:467
  65.0 16.4 %collective-permute-start.18 = (bf16[2,128,1024]{2,1,0:T(8,128)(2,1)S(1)}, bf16[2,128,1024]{2,1,0:T(8,128)(2,1)S(1)}, u32[]{:S(2)}, u32[]{:S(2)}) collective-permute-start(bf16[2,128,1024]{2,1,0:T(8,128)(2,1)S(1)} %get-tuple-element.95), channel_id=1, source_target_pairs={{0,96},{1,97},{2,98},{3,99},{4,100},{5,101},{6,102},{7,103},{8,104... | collective-permute-start | bytes 1572872 | tf_op jit(solution)/shard_map/ppermute | solution.py:483
  67.7 13.7 %collective-permute-start.17 = (bf16[2,128,1024]{2,1,0:T(8,128)(2,1)S(1)}, bf16[2,128,1024]{2,1,0:T(8,128)(2,1)S(1)}, u32[]{:S(2)}, u32[]{:S(2)}) collective-permute-start(bf16[2,128,1024]{2,1,0:T(8,128)(2,1)S(1)} %join.1), channel_id=1, source_target_pairs={{0,32},{1,33},{2,34},{3,35},{4,36},{5,37},{6,38},{7,39},{8,40},{9,... | collective-permute-start | bytes 1572872 | tf_op jit(solution)/shard_map/ppermute | solution.py:483
  70.1 14.0 %collective-permute-start.11 = (bf16[2,2,128,512]{3,2,1,0:T(8,128)(2,1)S(1)}, bf16[2,2,128,512]{3,2,1,0:T(8,128)(2,1)S(1)}, u32[]{:S(2)}, u32[]{:S(2)}) collective-permute-start(bf16[2,2,128,512]{3,2,1,0:T(8,128)(2,1)S(1)} %get-tuple-element.106), channel_id=1, source_target_pairs={{0,4},{1,17},{2,6},{3,19},{4,0},{5,21},{6,2},{7,23},{8,12},{9,25},... | collective-permute-start | bytes 1572872 | tf_op jit(solution)/shard_map/ppermute | solution.py:467
  72.0 13.2 %collective-permute-start.10 = (bf16[2,2,128,512]{3,2,1,0:T(8,128)(2,1)S(1)}, bf16[2,2,128,512]{3,2,1,0:T(8,128)(2,1)S(1)}, u32[]{:S(2)}, u32[]{:S(2)}) collective-permute-start(bf16[2,2,128,512]{3,2,1,0:T(8,128)(2,1)S(1)} %get-tuple-element.104), channel_id=1, source_target_pairs={{0,6},{1,25},{2,0},{3,27},{4,2},{5,29},{6,4},{7,31},{8,14},{9,1},{... | collective-permute-start | bytes 1572872 | tf_op jit(solution)/shard_map/ppermute | solution.py:467
  72.7 12.9 %collective-permute-start.9 = (bf16[2,2,128,512]{3,2,1,0:T(8,128)(2,1)S(1)}, bf16[2,2,128,512]{3,2,1,0:T(8,128)(2,1)S(1)}, u32[]{:S(2)}, u32[]{:S(2)}) collective-permute-start(bf16[2,2,128,512]{3,2,1,0:T(8,128)(2,1)S(1)} %get-tuple-element.102), channel_id=1, source_target_pairs={{0,2},{1,9},{2,4},{3,11},{4,6},{5,13},{6,0},{7,15},{8,10},{9,17},{... | collective-permute-start | bytes 1572872 | tf_op jit(solution)/shard_map/ppermute | solution.py:467
  81.4 12.7 %collective-permute-start.19 = (bf16[2,128,1024]{2,1,0:T(8,128)(2,1)S(1)}, bf16[2,128,1024]{2,1,0:T(8,128)(2,1)S(1)}, u32[]{:S(2)}, u32[]{:S(2)}) collective-permute-start(bf16[2,128,1024]{2,1,0:T(8,128)(2,1)S(1)} %get-tuple-element.121), channel_id=1, source_target_pairs={{0,32},{1,33},{2,34},{3,35},{4,36},{5,37},{6,38},{7,39},{8,40},{9,... | collective-permute-start | bytes 1572872 | tf_op jit(solution)/shard_map/ppermute | solution.py:483
  81.4 12.7 %collective-permute-start.20 = (bf16[2,128,1024]{2,1,0:T(8,128)(2,1)S(1)}, bf16[2,128,1024]{2,1,0:T(8,128)(2,1)S(1)}, u32[]{:S(2)}, u32[]{:S(2)}) collective-permute-start(bf16[2,128,1024]{2,1,0:T(8,128)(2,1)S(1)} %get-tuple-element.122), channel_id=1, source_target_pairs={{0,96},{1,97},{2,98},{3,99},{4,100},{5,101},{6,102},{7,103},{8,104... | collective-permute-start | bytes 1572872 | tf_op jit(solution)/shard_map/ppermute | solution.py:483
  94.6 16.4 %collective-permute-start.21 = (bf16[128,1024]{1,0:T(8,128)(2,1)S(1)}, bf16[128,1024]{1,0:T(8,128)(2,1)S(1)}, u32[]{:S(2)}, u32[]{:S(2)}) collective-permute-start(bf16[128,1024]{1,0:T(8,128)(2,1)S(1)} %get-tuple-element.123), channel_id=1, source_target_pairs={{0,0},{1,3},{2,11},{3,2},{4,4},{5,7},{6,15},{7,6},{8,17},{9,8},{10... | collective-permute-start | bytes 786440 | tf_op jit(solution)/shard_map/ppermute | solution.py:488
  98.0 13.0 %collective-permute-start.22 = (bf16[128,1024]{1,0:T(8,128)(2,1)S(1)}, bf16[128,1024]{1,0:T(8,128)(2,1)S(1)}, u32[]{:S(2)}, u32[]{:S(2)}) collective-permute-start(bf16[128,1024]{1,0:T(8,128)(2,1)S(1)} %get-tuple-element.124), channel_id=1, source_target_pairs={{0,17},{1,2},{2,10},{3,7},{4,21},{5,6},{6,14},{7,3},{8,16},{9,13},... | collective-permute-start | bytes 786440 | tf_op jit(solution)/shard_map/ppermute | solution.py:488
  100.8 10.2 %collective-permute-start.23 = (bf16[128,1024]{1,0:T(8,128)(2,1)S(1)}, bf16[128,1024]{1,0:T(8,128)(2,1)S(1)}, u32[]{:S(2)}, u32[]{:S(2)}) collective-permute-start(bf16[128,1024]{1,0:T(8,128)(2,1)S(1)} %get-tuple-element.125), channel_id=1, source_target_pairs={{0,16},{1,7},{2,27},{3,6},{4,20},{5,3},{6,31},{7,2},{8,1},{9,12},{... | collective-permute-start | bytes 786440 | tf_op jit(solution)/shard_map/ppermute | solution.py:488
  103.3 9.1 %collective-permute-start.24 = (bf16[128,1024]{1,0:T(8,128)(2,1)S(1)}, bf16[128,1024]{1,0:T(8,128)(2,1)S(1)}, u32[]{:S(2)}, u32[]{:S(2)}) collective-permute-start(bf16[128,1024]{1,0:T(8,128)(2,1)S(1)} %get-tuple-element.126), channel_id=1, source_target_pairs={{0,1},{1,6},{2,26},{3,3},{4,5},{5,2},{6,30},{7,7},{8,0},{9,9},{10,... | collective-permute-start | bytes 786440 | tf_op jit(solution)/shard_map/ppermute | solution.py:488
  (4 other events, 37.9 us)

commit v7 on v6

--- a/solution.py
+++ b/solution.py
@@ -46,8 +46,8 @@
     return pairs(lambda x, y, z, core: (x, y, z + step, core))
 
 
-MATCHED = ((0, 0), (2, 1), (2, 0), (0, 1))
-UNMATCHED = ((1, 1), (1, 0), (3, 1), (3, 0))
+MATCHED = ((2, 1), (2, 0), (0, 0), (0, 1))
+UNMATCHED = ((1, 0), (3, 1), (1, 1), (3, 0))
 
 
 def hop3_pairs(send):

time: 115 us -> 113 us (0.983)
  starting transfers between devices: 44.8 us -> 40.6 us
  waiting for transfers between devices: 14.3 us -> 16.5 us
    ppermute x12, waiting for transfers between devices: 2.03 us -> 8.87 us  [body(): came.append(lax.ppermute(sent, AXES, hop1_pairs(step)))]
    ppermute x12, starting transfers between devices: 22.1 us -> 15.5 us  [body(): came.append(lax.ppermute(sent, AXES, hop1_pairs(step)))]
    ppermute x6, waiting for transfers between devices: 6.99 us -> 1.4 us  [body(): lax.ppermute(p, AXES, hop2_pairs(step))]
    ppermute x4, starting transfers between devices: 12.4 us -> 14.6 us  [body(): lax.ppermute(buf, AXES, hop3_pairs(send))]
  transfers between devices with their start and end apart: 25 -> 25, of which waited for: 9 -> 7; matrix products, arithmetic and copies ran while one was open for 0% -> 0% of each run, Pallas kernels for 26% -> 27%
where the time goes in v7:
time: 113 us; the launch traced here: 112 us
  starting transfers between devices  40.6 us (36%)
  Pallas kernels  33.2 us (29%)
  blocking collectives  21.1 us (19%)
  waiting for transfers between devices  16.5 us (15%)
    all_to_all x1, blocking collectives, body(): lax.all_to_all(sent, 'shard', split_axis=0, concat_axis=0, tiled=True)  21.1 us
    pallas_call x4, Pallas kernels, project(): pl.pallas_call(functools.partial(project_kernel, chunk, row, added), out_...  18.9 us
    ppermute x12, starting transfers between devices, body(): came.append(lax.ppermute(sent, AXES, hop1_pairs(step)))  15.5 us
    ppermute x4, starting transfers between devices, body(): lax.ppermute(buf, AXES, hop3_pairs(send))  14.6 us
    ppermute x12, waiting for transfers between devices, body(): came.append(lax.ppermute(sent, AXES, hop1_pairs(step)))  8.87 us
    ppermute x6, starting transfers between devices, body(): lax.ppermute(p, AXES, hop2_pairs(step))  7.34 us
    pallas_call x4, Pallas kernels, pick(): pl.pallas_call(functools.partial(pick_kernel, chunk, row), out_shape=[plt...  6.84 us
    ppermute x4, waiting for transfers between devices, body(): lax.ppermute(buf, AXES, hop3_pairs(send))  5.51 us
  transfers between devices with their start and end apart: 25, of which 7 were waited for; matrix products, arithmetic and copies ran while one was open for 0% of the time, Pallas kernels for 27%

profile of v7, /device:TPU:1, one launch (start us, length us, event | category | flops | bytes accessed | tf_op | source)
XLA Modules:
  0.0 111.9 jit_solution(1851983539719588485)
XLA Ops:
  1.4 1.6 %notes.1 = s32[512,128]{1,0:T(8,128)S(1)} custom-call(s32[1,64]{1,0:T(1,128)} %refs_0_.1, s32[1,3328]{1,0:T(1,128)} %refs_1_.1, s32[1,52]{1,0:T(1,128)} %refs_2_.1, s32[1,64]{1,0:T(1,128)} %bitcast.11), custom_call_target="tpu_custom_call" | custom-call | tf_op jit(solution)/shard_map/notes/pallas_call | solution.py:131
  3.0 21.1 %all_to_all.5.notes_ref = s32[64,8,128]{2,1,0:T(8,128)S(1)} all-to-all(s32[64,8,128]{2,1,0:T(8,128)S(1)} %bitcast.4), channel_id=1, replica_groups=mesh['shard'=64,'basis'=2] {'shard'}, dimensions={0} | all-to-all | bytes 524288 | tf_op jit(solution)/shard_map/all_to_all | solution.py:437
  24.3 1.8 %cross.2 = bf16[1,4,2,128,512]{4,3,2,1,0:T(8,128)(2,1)S(1)} custom-call(s32[1024]{0:T(1024)S(1)} %reshape.11.words_ref, bf16[6144,512]{1,0:T(8,128)(2,1)} %table_ref.19), custom_call_target="tpu_custom_call" | custom-call | flops 1 | bytes 1 | tf_op jit(solution)/shard_map/cross/pallas_call | solution.py:193
  27.5 2.4 %cross.3 = bf16[3,4,2,128,512]{4,3,2,1,0:T(8,128)(2,1)S(1)} custom-call(s32[1024]{0:T(1024)S(1)} %reshape.11.words_ref, bf16[6144,512]{1,0:T(8,128)(2,1)} %table_ref.19), custom_call_target="tpu_custom_call" | custom-call | flops 1 | bytes 1 | tf_op jit(solution)/shard_map/cross/pallas_call | solution.py:193
  31.0 2.1 %collective-permute-start.3 = (bf16[2,2,128,512]{3,2,1,0:T(8,128)(2,1)S(1)}, bf16[2,2,128,512]{3,2,1,0:T(8,128)(2,1)S(1)}, u32[]{:S(2)}, u32[]{:S(2)}) collective-permute-start(bf16[2,2,128,512]{3,2,1,0:T(8,128)(2,1)S(1)} %get-tuple-element.74), channel_id=1, source_target_pairs={{0,2},{1,9},{2,4},{3,11},{4,6},{5,13},{6,0},{7,15},{8,10},{9,17},{... | collective-permute-start | bytes 1572872 | tf_op jit(solution)/shard_map/ppermute | solution.py:467
  35.7 2.4 %pick.5 = (bf16[2,2,128,512]{3,2,1,0:T(8,128)(2,1)S(1)}, bf16[2,2,128,512]{3,2,1,0:T(8,128)(2,1)S(1)}, bf16[2,2,128,512]{3,2,1,0:T(8,128)(2,1)S(1)}) custom-call(s32[1024]{0:T(1024)S(1)} %reshape.11.words_ref, bf16[6144,512]{1,0:T(8,128)(2,1)} %table_ref.19, bf16[3,4,2,128,512]{4,3,2,1,0:T(8,128)(2,1)S(1)} %collective-permute-done.2.crossed_ref), custom_call_target="tpu_custom_call" | custom-call | flops 1 | bytes 1 | tf_op jit(solution)/shard_map/pick/pallas_call | solution.py:221
  38.2 2.7 %collective-permute-start.7 = (bf16[2,2,128,512]{3,2,1,0:T(8,128)(2,1)S(1)}, bf16[2,2,128,512]{3,2,1,0:T(8,128)(2,1)S(1)}, u32[]{:S(2)}, u32[]{:S(2)}) collective-permute-start(bf16[2,2,128,512]{3,2,1,0:T(8,128)(2,1)S(1)} %get-tuple-element.92), channel_id=1, source_target_pairs={{0,6},{1,25},{2,0},{3,27},{4,2},{5,29},{6,4},{7,31},{8,14},{9,1},{... | collective-permute-start | bytes 1572872 | tf_op jit(solution)/shard_map/ppermute | solution.py:467
  41.8 4.8 %collective-permute-done.5.rest_2_ = bf16[2,2,128,512]{3,2,1,0:T(8,128)(2,1)S(1)} collective-permute-done((bf16[2,2,128,512]{3,2,1,0:T(8,128)(2,1)S(1)}, bf16[2,2,128,512]{3,2,1,0:T(8,128)(2,1)S(1)}, u32[]{:S(2)}, u32[]{:S(2)}) %collective-permute-start.5) | collective-permute-done | bytes 524320 | tf_op jit(solution)/shard_map/ppermute | solution.py:467
  46.6 5.0 %project.4 = (bf16[2,128,1024]{2,1,0:T(8,128)(2,1)S(1)}, bf16[2,128,1024]{2,1,0:T(8,128)(2,1)S(1)}) custom-call(s32[1024]{0:T(1024)S(1)} %reshape.11.words_ref, bf16[6144,512]{1,0:T(8,128)(2,1)} %table_ref.19, bf16[1024,1024]{1,0:T(8,128)(2,1)S(1)} %bitcast.7, bf16[1024,1024]{1,0:T(8,128)(2,1)S(1)} %collective-permute-done.other_basis, ...), custom_call_target="tpu_custom_call" | custom-call | flops 6000000000 | bytes 20000000 | tf_op jit(solution)/shard_map/project/pallas_call | solution.py:308
  51.7 2.2 %collective-permute-start.15 = (bf16[2,128,1024]{2,1,0:T(8,128)(2,1)S(1)}, bf16[2,128,1024]{2,1,0:T(8,128)(2,1)S(1)}, u32[]{:S(2)}, u32[]{:S(2)}) collective-permute-start(bf16[2,128,1024]{2,1,0:T(8,128)(2,1)S(1)} %get-tuple-element.84), channel_id=1, source_target_pairs={{0,32},{1,33},{2,34},{3,35},{4,36},{5,37},{6,38},{7,39},{8,40},{9,... | collective-permute-start | bytes 1572872 | tf_op jit(solution)/shard_map/ppermute | solution.py:483
  54.4 1.7 %pick.6 = (bf16[2,2,128,512]{3,2,1,0:T(8,128)(2,1)S(1)}, bf16[2,2,128,512]{3,2,1,0:T(8,128)(2,1)S(1)}, bf16[2,2,128,512]{3,2,1,0:T(8,128)(2,1)S(1)}) custom-call(s32[1024]{0:T(1024)S(1)} %reshape.11.words_ref, bf16[6144,512]{1,0:T(8,128)(2,1)} %table_ref.19, bf16[3,4,2,128,512]{4,3,2,1,0:T(8,128)(2,1)S(1)} %collective-permute-done.2.crossed_ref), custom_call_target="tpu_custom_call" | custom-call | flops 1 | bytes 1 | tf_op jit(solution)/shard_map/pick/pallas_call | solution.py:221
  56.2 1.8 %collective-permute-start.14 = (bf16[2,2,128,512]{3,2,1,0:T(8,128)(2,1)S(1)}, bf16[2,2,128,512]{3,2,1,0:T(8,128)(2,1)S(1)}, u32[]{:S(2)}, u32[]{:S(2)}) collective-permute-start(bf16[2,2,128,512]{3,2,1,0:T(8,128)(2,1)S(1)} %get-tuple-element.113), channel_id=1, source_target_pairs={{0,4},{1,17},{2,6},{3,19},{4,0},{5,21},{6,2},{7,23},{8,12},{9,25},... | collective-permute-start | bytes 1572872 | tf_op jit(solution)/shard_map/ppermute | solution.py:467
  59.4 4.5 %project.5 = (f32[2,128,1024]{2,1,0:T(8,128)S(1)}, bf16[2,128,1024]{2,1,0:T(8,128)(2,1)S(1)}) custom-call(s32[1024]{0:T(1024)S(1)} %reshape.11.words_ref, bf16[6144,512]{1,0:T(8,128)(2,1)} %table_ref.19, bf16[1024,1024]{1,0:T(8,128)(2,1)S(1)} %bitcast.8, bf16[1024,1024]{1,0:T(8,128)(2,1)S(1)} %collective-permute-done.other_basis, ...), custom_call_target="tpu_custom_call" | custom-call | flops 6000000000 | bytes 20000000 | tf_op jit(solution)/shard_map/project/pallas_call | solution.py:308
  66.9 1.9 %pick.7 = (bf16[2,2,128,512]{3,2,1,0:T(8,128)(2,1)S(1)}, bf16[2,2,128,512]{3,2,1,0:T(8,128)(2,1)S(1)}, bf16[2,2,128,512]{3,2,1,0:T(8,128)(2,1)S(1)}) custom-call(s32[1024]{0:T(1024)S(1)} %reshape.11.words_ref, bf16[6144,512]{1,0:T(8,128)(2,1)} %table_ref.19, bf16[3,4,2,128,512]{4,3,2,1,0:T(8,128)(2,1)S(1)} %collective-permute-done.2.crossed_ref), custom_call_target="tpu_custom_call" | custom-call | flops 1 | bytes 1 | tf_op jit(solution)/shard_map/pick/pallas_call | solution.py:221
  68.9 3.1 %collective-permute-start.11 = (bf16[2,2,128,512]{3,2,1,0:T(8,128)(2,1)S(1)}, bf16[2,2,128,512]{3,2,1,0:T(8,128)(2,1)S(1)}, u32[]{:S(2)}, u32[]{:S(2)}) collective-permute-start(bf16[2,2,128,512]{3,2,1,0:T(8,128)(2,1)S(1)} %get-tuple-element.106), channel_id=1, source_target_pairs={{0,4},{1,17},{2,6},{3,19},{4,0},{5,21},{6,2},{7,23},{8,12},{9,25},... | collective-permute-start | bytes 1572872 | tf_op jit(solution)/shard_map/ppermute | solution.py:467
  71.9 1.6 %collective-permute-start.10 = (bf16[2,2,128,512]{3,2,1,0:T(8,128)(2,1)S(1)}, bf16[2,2,128,512]{3,2,1,0:T(8,128)(2,1)S(1)}, u32[]{:S(2)}, u32[]{:S(2)}) collective-permute-start(bf16[2,2,128,512]{3,2,1,0:T(8,128)(2,1)S(1)} %get-tuple-element.104), channel_id=1, source_target_pairs={{0,6},{1,25},{2,0},{3,27},{4,2},{5,29},{6,4},{7,31},{8,14},{9,1},{... | collective-permute-start | bytes 1572872 | tf_op jit(solution)/shard_map/ppermute | solution.py:467
  73.6 4.4 %project.7 = (bf16[2,128,1024]{2,1,0:T(8,128)(2,1)S(1)}, bf16[2,128,1024]{2,1,0:T(8,128)(2,1)S(1)}) custom-call(s32[1024]{0:T(1024)S(1)} %reshape.11.words_ref, bf16[6144,512]{1,0:T(8,128)(2,1)} %table_ref.19, bf16[1024,1024]{1,0:T(8,128)(2,1)S(1)} %bitcast.9, bf16[1024,1024]{1,0:T(8,128)(2,1)S(1)} %collective-permute-done.other_basis, ...), custom_call_target="tpu_custom_call" | custom-call | flops 6000000000 | bytes 20000000 | tf_op jit(solution)/shard_map/project/pallas_call | solution.py:308
  78.2 1.9 %collective-permute-start.19 = (bf16[2,128,1024]{2,1,0:T(8,128)(2,1)S(1)}, bf16[2,128,1024]{2,1,0:T(8,128)(2,1)S(1)}, u32[]{:S(2)}, u32[]{:S(2)}) collective-permute-start(bf16[2,128,1024]{2,1,0:T(8,128)(2,1)S(1)} %get-tuple-element.121), channel_id=1, source_target_pairs={{0,32},{1,33},{2,34},{3,35},{4,36},{5,37},{6,38},{7,39},{8,40},{9,... | collective-permute-start | bytes 1572872 | tf_op jit(solution)/shard_map/ppermute | solution.py:483
  81.1 4.0 %collective-permute-done.10.rest_1_ = bf16[2,2,128,512]{3,2,1,0:T(8,128)(2,1)S(1)} collective-permute-done((bf16[2,2,128,512]{3,2,1,0:T(8,128)(2,1)S(1)}, bf16[2,2,128,512]{3,2,1,0:T(8,128)(2,1)S(1)}, u32[]{:S(2)}, u32[]{:S(2)}) %collective-permute-start.10) | collective-permute-done | bytes 524320 | tf_op jit(solution)/shard_map/ppermute | solution.py:467
  85.1 5.0 %project.6 = (bf16[2,128,1024]{2,1,0:T(8,128)(2,1)S(1)}, bf16[2,128,1024]{2,1,0:T(8,128)(2,1)S(1)}) custom-call(s32[1024]{0:T(1024)S(1)} %reshape.11.words_ref, bf16[6144,512]{1,0:T(8,128)(2,1)} %table_ref.19, bf16[1024,1024]{1,0:T(8,128)(2,1)S(1)} %bitcast.10, bf16[1024,1024]{1,0:T(8,128)(2,1)S(1)} %collective-permute-done.other_basis, ...), custom_call_target="tpu_custom_call" | custom-call | flops 6000000000 | bytes 20000000 | tf_op jit(solution)/shard_map/project/pallas_call | solution.py:308
  90.6 6.7 %collective-permute-start.21 = (bf16[128,1024]{1,0:T(8,128)(2,1)S(1)}, bf16[128,1024]{1,0:T(8,128)(2,1)S(1)}, u32[]{:S(2)}, u32[]{:S(2)}) collective-permute-start(bf16[128,1024]{1,0:T(8,128)(2,1)S(1)} %get-tuple-element.123), channel_id=1, source_target_pairs={{0,17},{1,2},{2,10},{3,7},{4,21},{5,6},{6,14},{7,3},{8,16},{9,13},... | collective-permute-start | bytes 786440 | tf_op jit(solution)/shard_map/ppermute | solution.py:488
  97.3 3.9 %collective-permute-start.23 = (bf16[128,1024]{1,0:T(8,128)(2,1)S(1)}, bf16[128,1024]{1,0:T(8,128)(2,1)S(1)}, u32[]{:S(2)}, u32[]{:S(2)}) collective-permute-start(bf16[128,1024]{1,0:T(8,128)(2,1)S(1)} %get-tuple-element.125), channel_id=1, source_target_pairs={{0,0},{1,3},{2,11},{3,2},{4,4},{5,7},{6,15},{7,6},{8,17},{9,8},{10... | collective-permute-start | bytes 786440 | tf_op jit(solution)/shard_map/ppermute | solution.py:488
  101.2 4.0 %collective-permute-start.24 = (bf16[128,1024]{1,0:T(8,128)(2,1)S(1)}, bf16[128,1024]{1,0:T(8,128)(2,1)S(1)}, u32[]{:S(2)}, u32[]{:S(2)}) collective-permute-start(bf16[128,1024]{1,0:T(8,128)(2,1)S(1)} %get-tuple-element.126), channel_id=1, source_target_pairs={{0,1},{1,6},{2,26},{3,3},{4,5},{5,2},{6,30},{7,7},{8,0},{9,9},{10,... | collective-permute-start | bytes 786440 | tf_op jit(solution)/shard_map/ppermute | solution.py:488
  105.4 5.5 %collective-permute-done.23.refs_2_ = bf16[128,1024]{1,0:T(8,128)(2,1)S(1)} collective-permute-done((bf16[128,1024]{1,0:T(8,128)(2,1)S(1)}, bf16[128,1024]{1,0:T(8,128)(2,1)S(1)}, u32[]{:S(2)}, u32[]{:S(2)}) %collective-permute-start.23) | collective-permute-done | bytes 262176 | tf_op jit(solution)/shard_map/ppermute | solution.py:488
  (51 shorter events, 15.5 us)
Async XLA Ops:
  0.0 24.3 %collective-permute-start = (bf16[1024,1024]{1,0:T(8,128)(2,1)}, bf16[1024,1024]{1,0:T(8,128)(2,1)S(1)}, u32[]{:S(2)}, u32[]{:S(2)}) collective-permute-start(bf16[1024,1024]{1,0:T(8,128)(2,1)} %bitcast.6), channel_id=1, source_target_pairs={{0,1},{1,0},{2,3},{3,2},{4,5},{5,4},{6,7},{7,6},{8,9},{9,8},{10,11... | collective-permute-start | bytes 6291464 | tf_op jit(solution)/shard_map/ppermute | solution.py:434
  30.0 5.7 %collective-permute-start.2 = (bf16[3,4,2,128,512]{4,3,2,1,0:T(8,128)(2,1)S(1)}, bf16[3,4,2,128,512]{4,3,2,1,0:T(8,128)(2,1)S(1)}, u32[]{:S(2)}, u32[]{:S(2)}) collective-permute-start(bf16[3,4,2,128,512]{4,3,2,1,0:T(8,128)(2,1)S(1)} %cross.3), channel_id=1, source_target_pairs={{0,1},{1,0},{2,3},{3,2},{4,5},{5,4},{6,7},{7,6},{8,9},{9,8},{10,11... | collective-permute-start | bytes 9437192 | tf_op jit(solution)/shard_map/ppermute | solution.py:449
  31.0 9.9 %collective-permute-start.3 = (bf16[2,2,128,512]{3,2,1,0:T(8,128)(2,1)S(1)}, bf16[2,2,128,512]{3,2,1,0:T(8,128)(2,1)S(1)}, u32[]{:S(2)}, u32[]{:S(2)}) collective-permute-start(bf16[2,2,128,512]{3,2,1,0:T(8,128)(2,1)S(1)} %get-tuple-element.74), channel_id=1, source_target_pairs={{0,2},{1,9},{2,4},{3,11},{4,6},{5,13},{6,0},{7,15},{8,10},{9,17},{... | collective-permute-start | bytes 1572872 | tf_op jit(solution)/shard_map/ppermute | solution.py:467
  33.1 8.7 %collective-permute-start.4 = (bf16[2,2,128,512]{3,2,1,0:T(8,128)(2,1)S(1)}, bf16[2,2,128,512]{3,2,1,0:T(8,128)(2,1)S(1)}, u32[]{:S(2)}, u32[]{:S(2)}) collective-permute-start(bf16[2,2,128,512]{3,2,1,0:T(8,128)(2,1)S(1)} %get-tuple-element.75), channel_id=1, source_target_pairs={{0,6},{1,25},{2,0},{3,27},{4,2},{5,29},{6,4},{7,31},{8,14},{9,1},{... | collective-permute-start | bytes 1572872 | tf_op jit(solution)/shard_map/ppermute | solution.py:467
  33.8 12.9 %collective-permute-start.5 = (bf16[2,2,128,512]{3,2,1,0:T(8,128)(2,1)S(1)}, bf16[2,2,128,512]{3,2,1,0:T(8,128)(2,1)S(1)}, u32[]{:S(2)}, u32[]{:S(2)}) collective-permute-start(bf16[2,2,128,512]{3,2,1,0:T(8,128)(2,1)S(1)} %get-tuple-element.76), channel_id=1, source_target_pairs={{0,4},{1,17},{2,6},{3,19},{4,0},{5,21},{6,2},{7,23},{8,12},{9,25},... | collective-permute-start | bytes 1572872 | tf_op jit(solution)/shard_map/ppermute | solution.py:467
  38.1 18.0 %collective-permute-start.6 = (bf16[2,2,128,512]{3,2,1,0:T(8,128)(2,1)S(1)}, bf16[2,2,128,512]{3,2,1,0:T(8,128)(2,1)S(1)}, u32[]{:S(2)}, u32[]{:S(2)}) collective-permute-start(bf16[2,2,128,512]{3,2,1,0:T(8,128)(2,1)S(1)} %get-tuple-element.91), channel_id=1, source_target_pairs={{0,2},{1,9},{2,4},{3,11},{4,6},{5,13},{6,0},{7,15},{8,10},{9,17},{... | collective-permute-start | bytes 1572872 | tf_op jit(solution)/shard_map/ppermute | solution.py:467
  38.2 19.7 %collective-permute-start.7 = (bf16[2,2,128,512]{3,2,1,0:T(8,128)(2,1)S(1)}, bf16[2,2,128,512]{3,2,1,0:T(8,128)(2,1)S(1)}, u32[]{:S(2)}, u32[]{:S(2)}) collective-permute-start(bf16[2,2,128,512]{3,2,1,0:T(8,128)(2,1)S(1)} %get-tuple-element.92), channel_id=1, source_target_pairs={{0,6},{1,25},{2,0},{3,27},{4,2},{5,29},{6,4},{7,31},{8,14},{9,1},{... | collective-permute-start | bytes 1572872 | tf_op jit(solution)/shard_map/ppermute | solution.py:467
  40.9 18.5 %collective-permute-start.8 = (bf16[2,2,128,512]{3,2,1,0:T(8,128)(2,1)S(1)}, bf16[2,2,128,512]{3,2,1,0:T(8,128)(2,1)S(1)}, u32[]{:S(2)}, u32[]{:S(2)}) collective-permute-start(bf16[2,2,128,512]{3,2,1,0:T(8,128)(2,1)S(1)} %get-tuple-element.93), channel_id=1, source_target_pairs={{0,4},{1,17},{2,6},{3,19},{4,0},{5,21},{6,2},{7,23},{8,12},{9,25},... | collective-permute-start | bytes 1572872 | tf_op jit(solution)/shard_map/ppermute | solution.py:467
  51.7 12.9 %collective-permute-start.15 = (bf16[2,128,1024]{2,1,0:T(8,128)(2,1)S(1)}, bf16[2,128,1024]{2,1,0:T(8,128)(2,1)S(1)}, u32[]{:S(2)}, u32[]{:S(2)}) collective-permute-start(bf16[2,128,1024]{2,1,0:T(8,128)(2,1)S(1)} %get-tuple-element.84), channel_id=1, source_target_pairs={{0,32},{1,33},{2,34},{3,35},{4,36},{5,37},{6,38},{7,39},{8,40},{9,... | collective-permute-start | bytes 1572872 | tf_op jit(solution)/shard_map/ppermute | solution.py:483
  53.9 12.6 %collective-permute-start.16 = (bf16[2,128,1024]{2,1,0:T(8,128)(2,1)S(1)}, bf16[2,128,1024]{2,1,0:T(8,128)(2,1)S(1)}, u32[]{:S(2)}, u32[]{:S(2)}) collective-permute-start(bf16[2,128,1024]{2,1,0:T(8,128)(2,1)S(1)} %get-tuple-element.85), channel_id=1, source_target_pairs={{0,96},{1,97},{2,98},{3,99},{4,100},{5,101},{6,102},{7,103},{8,104... | collective-permute-start | bytes 1572872 | tf_op jit(solution)/shard_map/ppermute | solution.py:483
  56.2 12.7 %collective-permute-start.14 = (bf16[2,2,128,512]{3,2,1,0:T(8,128)(2,1)S(1)}, bf16[2,2,128,512]{3,2,1,0:T(8,128)(2,1)S(1)}, u32[]{:S(2)}, u32[]{:S(2)}) collective-permute-start(bf16[2,2,128,512]{3,2,1,0:T(8,128)(2,1)S(1)} %get-tuple-element.113), channel_id=1, source_target_pairs={{0,4},{1,17},{2,6},{3,19},{4,0},{5,21},{6,2},{7,23},{8,12},{9,25},... | collective-permute-start | bytes 1572872 | tf_op jit(solution)/shard_map/ppermute | solution.py:467
  57.9 14.0 %collective-permute-start.13 = (bf16[2,2,128,512]{3,2,1,0:T(8,128)(2,1)S(1)}, bf16[2,2,128,512]{3,2,1,0:T(8,128)(2,1)S(1)}, u32[]{:S(2)}, u32[]{:S(2)}) collective-permute-start(bf16[2,2,128,512]{3,2,1,0:T(8,128)(2,1)S(1)} %get-tuple-element.111), channel_id=1, source_target_pairs={{0,6},{1,25},{2,0},{3,27},{4,2},{5,29},{6,4},{7,31},{8,14},{9,1},{... | collective-permute-start | bytes 1572872 | tf_op jit(solution)/shard_map/ppermute | solution.py:467
  59.3 14.2 %collective-permute-start.12 = (bf16[2,2,128,512]{3,2,1,0:T(8,128)(2,1)S(1)}, bf16[2,2,128,512]{3,2,1,0:T(8,128)(2,1)S(1)}, u32[]{:S(2)}, u32[]{:S(2)}) collective-permute-start(bf16[2,2,128,512]{3,2,1,0:T(8,128)(2,1)S(1)} %get-tuple-element.109), channel_id=1, source_target_pairs={{0,2},{1,9},{2,4},{3,11},{4,6},{5,13},{6,0},{7,15},{8,10},{9,17},{... | collective-permute-start | bytes 1572872 | tf_op jit(solution)/shard_map/ppermute | solution.py:467
  64.6 13.6 %collective-permute-start.18 = (bf16[2,128,1024]{2,1,0:T(8,128)(2,1)S(1)}, bf16[2,128,1024]{2,1,0:T(8,128)(2,1)S(1)}, u32[]{:S(2)}, u32[]{:S(2)}) collective-permute-start(bf16[2,128,1024]{2,1,0:T(8,128)(2,1)S(1)} %get-tuple-element.95), channel_id=1, source_target_pairs={{0,96},{1,97},{2,98},{3,99},{4,100},{5,101},{6,102},{7,103},{8,104... | collective-permute-start | bytes 1572872 | tf_op jit(solution)/shard_map/ppermute | solution.py:483
  66.5 11.7 %collective-permute-start.17 = (bf16[2,128,1024]{2,1,0:T(8,128)(2,1)S(1)}, bf16[2,128,1024]{2,1,0:T(8,128)(2,1)S(1)}, u32[]{:S(2)}, u32[]{:S(2)}) collective-permute-start(bf16[2,128,1024]{2,1,0:T(8,128)(2,1)S(1)} %join.1), channel_id=1, source_target_pairs={{0,32},{1,33},{2,34},{3,35},{4,36},{5,37},{6,38},{7,39},{8,40},{9,... | collective-permute-start | bytes 1572872 | tf_op jit(solution)/shard_map/ppermute | solution.py:483
  68.9 12.2 %collective-permute-start.11 = (bf16[2,2,128,512]{3,2,1,0:T(8,128)(2,1)S(1)}, bf16[2,2,128,512]{3,2,1,0:T(8,128)(2,1)S(1)}, u32[]{:S(2)}, u32[]{:S(2)}) collective-permute-start(bf16[2,2,128,512]{3,2,1,0:T(8,128)(2,1)S(1)} %get-tuple-element.106), channel_id=1, source_target_pairs={{0,4},{1,17},{2,6},{3,19},{4,0},{5,21},{6,2},{7,23},{8,12},{9,25},... | collective-permute-start | bytes 1572872 | tf_op jit(solution)/shard_map/ppermute | solution.py:467
  71.9 13.2 %collective-permute-start.10 = (bf16[2,2,128,512]{3,2,1,0:T(8,128)(2,1)S(1)}, bf16[2,2,128,512]{3,2,1,0:T(8,128)(2,1)S(1)}, u32[]{:S(2)}, u32[]{:S(2)}) collective-permute-start(bf16[2,2,128,512]{3,2,1,0:T(8,128)(2,1)S(1)} %get-tuple-element.104), channel_id=1, source_target_pairs={{0,6},{1,25},{2,0},{3,27},{4,2},{5,29},{6,4},{7,31},{8,14},{9,1},{... | collective-permute-start | bytes 1572872 | tf_op jit(solution)/shard_map/ppermute | solution.py:467
  73.6 11.5 %collective-permute-start.9 = (bf16[2,2,128,512]{3,2,1,0:T(8,128)(2,1)S(1)}, bf16[2,2,128,512]{3,2,1,0:T(8,128)(2,1)S(1)}, u32[]{:S(2)}, u32[]{:S(2)}) collective-permute-start(bf16[2,2,128,512]{3,2,1,0:T(8,128)(2,1)S(1)} %get-tuple-element.102), channel_id=1, source_target_pairs={{0,2},{1,9},{2,4},{3,11},{4,6},{5,13},{6,0},{7,15},{8,10},{9,17},{... | collective-permute-start | bytes 1572872 | tf_op jit(solution)/shard_map/ppermute | solution.py:467
  78.2 11.9 %collective-permute-start.19 = (bf16[2,128,1024]{2,1,0:T(8,128)(2,1)S(1)}, bf16[2,128,1024]{2,1,0:T(8,128)(2,1)S(1)}, u32[]{:S(2)}, u32[]{:S(2)}) collective-permute-start(bf16[2,128,1024]{2,1,0:T(8,128)(2,1)S(1)} %get-tuple-element.121), channel_id=1, source_target_pairs={{0,32},{1,33},{2,34},{3,35},{4,36},{5,37},{6,38},{7,39},{8,40},{9,... | collective-permute-start | bytes 1572872 | tf_op jit(solution)/shard_map/ppermute | solution.py:483
  80.0 10.0 %collective-permute-start.20 = (bf16[2,128,1024]{2,1,0:T(8,128)(2,1)S(1)}, bf16[2,128,1024]{2,1,0:T(8,128)(2,1)S(1)}, u32[]{:S(2)}, u32[]{:S(2)}) collective-permute-start(bf16[2,128,1024]{2,1,0:T(8,128)(2,1)S(1)} %get-tuple-element.122), channel_id=1, source_target_pairs={{0,96},{1,97},{2,98},{3,99},{4,100},{5,101},{6,102},{7,103},{8,104... | collective-permute-start | bytes 1572872 | tf_op jit(solution)/shard_map/ppermute | solution.py:483
  90.6 14.8 %collective-permute-start.21 = (bf16[128,1024]{1,0:T(8,128)(2,1)S(1)}, bf16[128,1024]{1,0:T(8,128)(2,1)S(1)}, u32[]{:S(2)}, u32[]{:S(2)}) collective-permute-start(bf16[128,1024]{1,0:T(8,128)(2,1)S(1)} %get-tuple-element.123), channel_id=1, source_target_pairs={{0,17},{1,2},{2,10},{3,7},{4,21},{5,6},{6,14},{7,3},{8,16},{9,13},... | collective-permute-start | bytes 786440 | tf_op jit(solution)/shard_map/ppermute | solution.py:488
  97.3 8.2 %collective-permute-start.22 = (bf16[128,1024]{1,0:T(8,128)(2,1)S(1)}, bf16[128,1024]{1,0:T(8,128)(2,1)S(1)}, u32[]{:S(2)}, u32[]{:S(2)}) collective-permute-start(bf16[128,1024]{1,0:T(8,128)(2,1)S(1)} %get-tuple-element.124), channel_id=1, source_target_pairs={{0,16},{1,7},{2,27},{3,6},{4,20},{5,3},{6,31},{7,2},{8,1},{9,12},{... | collective-permute-start | bytes 786440 | tf_op jit(solution)/shard_map/ppermute | solution.py:488
  97.3 13.7 %collective-permute-start.23 = (bf16[128,1024]{1,0:T(8,128)(2,1)S(1)}, bf16[128,1024]{1,0:T(8,128)(2,1)S(1)}, u32[]{:S(2)}, u32[]{:S(2)}) collective-permute-start(bf16[128,1024]{1,0:T(8,128)(2,1)S(1)} %get-tuple-element.125), channel_id=1, source_target_pairs={{0,0},{1,3},{2,11},{3,2},{4,4},{5,7},{6,15},{7,6},{8,17},{9,8},{10... | collective-permute-start | bytes 786440 | tf_op jit(solution)/shard_map/ppermute | solution.py:488
  101.2 9.8 %collective-permute-start.24 = (bf16[128,1024]{1,0:T(8,128)(2,1)S(1)}, bf16[128,1024]{1,0:T(8,128)(2,1)S(1)}, u32[]{:S(2)}, u32[]{:S(2)}) collective-permute-start(bf16[128,1024]{1,0:T(8,128)(2,1)S(1)} %get-tuple-element.126), channel_id=1, source_target_pairs={{0,1},{1,6},{2,26},{3,3},{4,5},{5,2},{6,30},{7,7},{8,0},{9,9},{10,... | collective-permute-start | bytes 786440 | tf_op jit(solution)/shard_map/ppermute | solution.py:488
  (4 other events, 35.7 us)

commit v8 on v7

--- a/solution.py
+++ b/solution.py
@@ -251,7 +251,19 @@
                 )
                 pl.when(code >= 0)(copy.start)
             pieces.append((which, step, group, line, code, rels, copy))
-    total[...] = jnp.zeros_like(total)
+    codes = [[code for which_, *_, code, _, _ in pieces if which_ == which] for which in range(2)]
+    low = [functools.reduce(jnp.logical_or, [(code >= 0) & (code < DST) for code in some]) for some in codes]
+    high = [functools.reduce(jnp.logical_or, [code >= DST for code in some]) for some in codes]
+    main = [jnp.where(has, 0, 1) for has in low]
+    both = (low[0] & high[0]) | (low[1] & high[1])
+
+    def clear(halves):
+        for which in range(2):
+            total[which, halves[which]] = jnp.zeros(total.shape[2:], F32)
+
+    other = [1 - half for half in main]
+    clear(main)
+    pl.when(both)(lambda: clear(other))
     lane = lax.broadcasted_iota(jnp.int32, (2, BROWS), 1)
     dest = lax.broadcasted_iota(jnp.int32, (DST, BROWS), 0)
     for which, step, group, line, code, rels, copy in pieces:
@@ -270,9 +282,9 @@
             chosen = []
             for k in range(2):
                 weight = jnp.where(core == 0, weights[k : k + 1], weights[1 - k : 2 - k])
-                high = weight.astype(BF16).astype(F32)
-                high, low = jnp.where(hit, high, 0.0), jnp.where(hit, weight - high, 0.0)
-                chosen.append(jnp.concatenate([high, low], axis=1))
+                round_ = weight.astype(BF16).astype(F32)
+                rest_ = jnp.where(hit, weight - round_, 0.0)
+                chosen.append(jnp.concatenate([jnp.where(hit, round_, 0.0), rest_], axis=1))
             chosen = jnp.concatenate(chosen, axis=0).astype(BF16)
             for part in range(2):
                 if step > 0:
@@ -286,20 +298,39 @@
                 column = pl.multiple_of(jnp.where(core == part, 0, width), width)
                 total[which, half, :, pl.ds(column, width)] += sums
 
-    summed = [
-        total[:, :, k * DST : (k + 1) * DST, :].reshape(4 * DST, 2 * width).astype(BF16) for k in range(2)
-    ]
     wide = own_basis.shape[1]
     tile = 256
-    for start in range(0, wide, tile):
-        result = jnp.dot(summed[0], own_basis[:, start : start + tile], preferred_element_type=F32)
-        result += jnp.dot(summed[1], other_basis[:, start : start + tile], preferred_element_type=F32)
-        result = result.reshape(2, 2, DST, tile)
+
+    def store(halves, which, here, columns):
+        if which in added:
+            here += extra[added.index(which)][halves[which], :, columns].astype(F32)
+        outs[which][halves[which], :, columns] = here.astype(outs[which].dtype)
+
+    def project_half(halves):
+        summed = [
+            jnp.concatenate(
+                [total[which, halves[which], k * DST : (k + 1) * DST, :].astype(BF16) for which in range(2)], axis=0
+            )
+            for k in range(2)
+        ]
+        for start in range(0, wide, tile):
+            columns = slice(start, start + tile)
+            result = jnp.dot(summed[0], own_basis[:, columns], preferred_element_type=F32)
+            result += jnp.dot(summed[1], other_basis[:, columns], preferred_element_type=F32)
+            for which in range(2):
+                store(halves, which, result[which * DST : (which + 1) * DST], columns)
+
+    project_half(main)
+
+    @pl.when(both)
+    def _():
+        project_half(other)
+
+    @pl.when(jnp.logical_not(both))
+    def _():
         for which in range(2):
-            here = result[which]
-            if which in added:
-                here += extra[added.index(which)][:, :, start : start + tile].astype(F32)
-            outs[which][:, :, start : start + tile] = here.astype(outs[which].dtype)
+            for start in range(0, wide, tile):
+                store(other, which, jnp.zeros((DST, tile), F32), slice(start, start + tile))
 
 
 def project(chunk, row, added, kept, words, table, *others):

time: 113 us -> 114 us (level)
  waiting for transfers between devices: 16.5 us -> 22.5 us
  Pallas kernels: 33.2 us -> 30 us
  starting transfers between devices: 40.6 us -> 38.3 us
    ppermute x12, waiting for transfers between devices: 8.87 us -> 14.6 us  [body(): came.append(lax.ppermute(sent, AXES, hop1_pairs(step)))]
    pallas_call x4, Pallas kernels: 18.9 us -> 14.4 us  [project(): pl.pallas_call(functools.partial(project_kernel, chunk, row, added), out_...]
    ppermute x12, starting transfers between devices: 15.5 us -> 13.9 us  [body(): came.append(lax.ppermute(sent, AXES, hop1_pairs(step)))]
    pallas_call x4, Pallas kernels: 6.84 us -> 8.36 us  [pick(): pl.pallas_call(functools.partial(pick_kernel, chunk, row), out_shape=[plt...]
  transfers between devices with their start and end apart: 25 -> 25, of which waited for: 7 -> 8; matrix products, arithmetic and copies ran while one was open for 0% -> 0% of each run, Pallas kernels for 27% -> 24%
where the time goes in v8:
time: 114 us; the launch traced here: 112 us
  starting transfers between devices  38.3 us (34%)
  Pallas kernels  30 us (26%)
  waiting for transfers between devices  22.5 us (20%)
  blocking collectives  21.1 us (19%)
    all_to_all x1, blocking collectives, body(): lax.all_to_all(sent, 'shard', split_axis=0, concat_axis=0, tiled=True)  21.1 us
    ppermute x12, waiting for transfers between devices, body(): came.append(lax.ppermute(sent, AXES, hop1_pairs(step)))  14.6 us
    pallas_call x4, Pallas kernels, project(): pl.pallas_call(functools.partial(project_kernel, chunk, row, added), out_...  14.4 us
    ppermute x12, starting transfers between devices, body(): came.append(lax.ppermute(sent, AXES, hop1_pairs(step)))  13.9 us
    ppermute x4, starting transfers between devices, body(): lax.ppermute(buf, AXES, hop3_pairs(send))  13.9 us
    pallas_call x4, Pallas kernels, pick(): pl.pallas_call(functools.partial(pick_kernel, chunk, row), out_shape=[plt...  8.36 us
    ppermute x6, starting transfers between devices, body(): lax.ppermute(p, AXES, hop2_pairs(step))  7.08 us
    ppermute x4, waiting for transfers between devices, body(): lax.ppermute(buf, AXES, hop3_pairs(send))  5.51 us
  transfers between devices with their start and end apart: 25, of which 8 were waited for; matrix products, arithmetic and copies ran while one was open for 0% of the time, Pallas kernels for 24%

profile of v8, /device:TPU:1, one launch (start us, length us, event | category | flops | bytes accessed | tf_op | source)
XLA Modules:
  0.0 112.3 jit_solution(15625507859699959551)
XLA Ops:
  3.0 21.1 %all_to_all.5.notes_ref = s32[64,8,128]{2,1,0:T(8,128)S(1)} all-to-all(s32[64,8,128]{2,1,0:T(8,128)S(1)} %bitcast.4), channel_id=1, replica_groups=mesh['shard'=64,'basis'=2] {'shard'}, dimensions={0} | all-to-all | bytes 524288 | tf_op jit(solution)/shard_map/all_to_all | solution.py:468
  27.6 2.3 %cross.3 = bf16[3,4,2,128,512]{4,3,2,1,0:T(8,128)(2,1)S(1)} custom-call(s32[1024]{0:T(1024)S(1)} %reshape.11.words_ref, bf16[6144,512]{1,0:T(8,128)(2,1)} %table_ref.19), custom_call_target="tpu_custom_call" | custom-call | flops 1 | bytes 1 | tf_op jit(solution)/shard_map/cross/pallas_call | solution.py:193
  30.3 2.1 %pick.4 = (bf16[2,2,128,512]{3,2,1,0:T(8,128)(2,1)S(1)}, bf16[2,2,128,512]{3,2,1,0:T(8,128)(2,1)S(1)}, bf16[2,2,128,512]{3,2,1,0:T(8,128)(2,1)S(1)}) custom-call(s32[1024]{0:T(1024)S(1)} %reshape.11.words_ref, bf16[6144,512]{1,0:T(8,128)(2,1)} %table_ref.19, bf16[1,4,2,128,512]{4,3,2,1,0:T(8,128)(2,1)S(1)} %collective-permute-done.1.crossed_ref), custom_call_target="tpu_custom_call" | custom-call | flops 1 | bytes 1 | tf_op jit(solution)/shard_map/pick/pallas_call | solution.py:221
  32.5 2.6 %collective-permute-start.4 = (bf16[2,2,128,512]{3,2,1,0:T(8,128)(2,1)S(1)}, bf16[2,2,128,512]{3,2,1,0:T(8,128)(2,1)S(1)}, u32[]{:S(2)}, u32[]{:S(2)}) collective-permute-start(bf16[2,2,128,512]{3,2,1,0:T(8,128)(2,1)S(1)} %get-tuple-element.75), channel_id=1, source_target_pairs={{0,6},{1,25},{2,0},{3,27},{4,2},{5,29},{6,4},{7,31},{8,14},{9,1},{... | collective-permute-start | bytes 1572872 | tf_op jit(solution)/shard_map/ppermute | solution.py:498
  35.7 2.0 %pick.5 = (bf16[2,2,128,512]{3,2,1,0:T(8,128)(2,1)S(1)}, bf16[2,2,128,512]{3,2,1,0:T(8,128)(2,1)S(1)}, bf16[2,2,128,512]{3,2,1,0:T(8,128)(2,1)S(1)}) custom-call(s32[1024]{0:T(1024)S(1)} %reshape.11.words_ref, bf16[6144,512]{1,0:T(8,128)(2,1)} %table_ref.19, bf16[3,4,2,128,512]{4,3,2,1,0:T(8,128)(2,1)S(1)} %collective-permute-done.2.crossed_ref), custom_call_target="tpu_custom_call" | custom-call | flops 1 | bytes 1 | tf_op jit(solution)/shard_map/pick/pallas_call | solution.py:221
  37.9 2.6 %collective-permute-start.7 = (bf16[2,2,128,512]{3,2,1,0:T(8,128)(2,1)S(1)}, bf16[2,2,128,512]{3,2,1,0:T(8,128)(2,1)S(1)}, u32[]{:S(2)}, u32[]{:S(2)}) collective-permute-start(bf16[2,2,128,512]{3,2,1,0:T(8,128)(2,1)S(1)} %get-tuple-element.92), channel_id=1, source_target_pairs={{0,6},{1,25},{2,0},{3,27},{4,2},{5,29},{6,4},{7,31},{8,14},{9,1},{... | collective-permute-start | bytes 1572872 | tf_op jit(solution)/shard_map/ppermute | solution.py:498
  40.4 7.2 %collective-permute-done.3.rest_0_ = bf16[2,2,128,512]{3,2,1,0:T(8,128)(2,1)S(1)} collective-permute-done((bf16[2,2,128,512]{3,2,1,0:T(8,128)(2,1)S(1)}, bf16[2,2,128,512]{3,2,1,0:T(8,128)(2,1)S(1)}, u32[]{:S(2)}, u32[]{:S(2)}) %collective-permute-start.3) | collective-permute-done | bytes 524320 | tf_op jit(solution)/shard_map/ppermute | solution.py:498
  47.6 2.9 %project.4 = (bf16[2,128,1024]{2,1,0:T(8,128)(2,1)S(1)}, bf16[2,128,1024]{2,1,0:T(8,128)(2,1)S(1)}) custom-call(s32[1024]{0:T(1024)S(1)} %reshape.11.words_ref, bf16[6144,512]{1,0:T(8,128)(2,1)} %table_ref.19, bf16[1024,1024]{1,0:T(8,128)(2,1)S(1)} %bitcast.7, bf16[1024,1024]{1,0:T(8,128)(2,1)S(1)} %collective-permute-done.other_basis, ...), custom_call_target="tpu_custom_call" | custom-call | flops 6000000000 | bytes 20000000 | tf_op jit(solution)/shard_map/project/pallas_call | solution.py:339
  50.7 2.7 %collective-permute-start.16 = (bf16[2,128,1024]{2,1,0:T(8,128)(2,1)S(1)}, bf16[2,128,1024]{2,1,0:T(8,128)(2,1)S(1)}, u32[]{:S(2)}, u32[]{:S(2)}) collective-permute-start(bf16[2,128,1024]{2,1,0:T(8,128)(2,1)S(1)} %get-tuple-element.85), channel_id=1, source_target_pairs={{0,96},{1,97},{2,98},{3,99},{4,100},{5,101},{6,102},{7,103},{8,104... | collective-permute-start | bytes 1572872 | tf_op jit(solution)/shard_map/ppermute | solution.py:514
  53.4 2.2 %pick.6 = (bf16[2,2,128,512]{3,2,1,0:T(8,128)(2,1)S(1)}, bf16[2,2,128,512]{3,2,1,0:T(8,128)(2,1)S(1)}, bf16[2,2,128,512]{3,2,1,0:T(8,128)(2,1)S(1)}) custom-call(s32[1024]{0:T(1024)S(1)} %reshape.11.words_ref, bf16[6144,512]{1,0:T(8,128)(2,1)} %table_ref.19, bf16[3,4,2,128,512]{4,3,2,1,0:T(8,128)(2,1)S(1)} %collective-permute-done.2.crossed_ref), custom_call_target="tpu_custom_call" | custom-call | flops 1 | bytes 1 | tf_op jit(solution)/shard_map/pick/pallas_call | solution.py:221
  55.5 3.3 %collective-permute-done.6.rest_0_ = bf16[2,2,128,512]{3,2,1,0:T(8,128)(2,1)S(1)} collective-permute-done((bf16[2,2,128,512]{3,2,1,0:T(8,128)(2,1)S(1)}, bf16[2,2,128,512]{3,2,1,0:T(8,128)(2,1)S(1)}, u32[]{:S(2)}, u32[]{:S(2)}) %collective-permute-start.6) | collective-permute-done | bytes 524320 | tf_op jit(solution)/shard_map/ppermute | solution.py:498
  58.9 2.7 %collective-permute-start.13 = (bf16[2,2,128,512]{3,2,1,0:T(8,128)(2,1)S(1)}, bf16[2,2,128,512]{3,2,1,0:T(8,128)(2,1)S(1)}, u32[]{:S(2)}, u32[]{:S(2)}) collective-permute-start(bf16[2,2,128,512]{3,2,1,0:T(8,128)(2,1)S(1)} %get-tuple-element.111), channel_id=1, source_target_pairs={{0,6},{1,25},{2,0},{3,27},{4,2},{5,29},{6,4},{7,31},{8,14},{9,1},{... | collective-permute-start | bytes 1572872 | tf_op jit(solution)/shard_map/ppermute | solution.py:498
  61.5 3.5 %project.5 = (f32[2,128,1024]{2,1,0:T(8,128)S(1)}, bf16[2,128,1024]{2,1,0:T(8,128)(2,1)S(1)}) custom-call(s32[1024]{0:T(1024)S(1)} %reshape.11.words_ref, bf16[6144,512]{1,0:T(8,128)(2,1)} %table_ref.19, bf16[1024,1024]{1,0:T(8,128)(2,1)S(1)} %bitcast.8, bf16[1024,1024]{1,0:T(8,128)(2,1)S(1)} %collective-permute-done.other_basis, ...), custom_call_target="tpu_custom_call" | custom-call | flops 6000000000 | bytes 20000000 | tf_op jit(solution)/shard_map/project/pallas_call | solution.py:339
  66.8 2.1 %pick.7 = (bf16[2,2,128,512]{3,2,1,0:T(8,128)(2,1)S(1)}, bf16[2,2,128,512]{3,2,1,0:T(8,128)(2,1)S(1)}, bf16[2,2,128,512]{3,2,1,0:T(8,128)(2,1)S(1)}) custom-call(s32[1024]{0:T(1024)S(1)} %reshape.11.words_ref, bf16[6144,512]{1,0:T(8,128)(2,1)} %table_ref.19, bf16[3,4,2,128,512]{4,3,2,1,0:T(8,128)(2,1)S(1)} %collective-permute-done.2.crossed_ref), custom_call_target="tpu_custom_call" | custom-call | flops 1 | bytes 1 | tf_op jit(solution)/shard_map/pick/pallas_call | solution.py:221
  68.9 3.4 %collective-permute-start.11 = (bf16[2,2,128,512]{3,2,1,0:T(8,128)(2,1)S(1)}, bf16[2,2,128,512]{3,2,1,0:T(8,128)(2,1)S(1)}, u32[]{:S(2)}, u32[]{:S(2)}) collective-permute-start(bf16[2,2,128,512]{3,2,1,0:T(8,128)(2,1)S(1)} %get-tuple-element.106), channel_id=1, source_target_pairs={{0,4},{1,17},{2,6},{3,19},{4,0},{5,21},{6,2},{7,23},{8,12},{9,25},... | collective-permute-start | bytes 1572872 | tf_op jit(solution)/shard_map/ppermute | solution.py:498
  72.7 2.3 %collective-permute-start.10 = (bf16[2,2,128,512]{3,2,1,0:T(8,128)(2,1)S(1)}, bf16[2,2,128,512]{3,2,1,0:T(8,128)(2,1)S(1)}, u32[]{:S(2)}, u32[]{:S(2)}) collective-permute-start(bf16[2,2,128,512]{3,2,1,0:T(8,128)(2,1)S(1)} %get-tuple-element.104), channel_id=1, source_target_pairs={{0,6},{1,25},{2,0},{3,27},{4,2},{5,29},{6,4},{7,31},{8,14},{9,1},{... | collective-permute-start | bytes 1572872 | tf_op jit(solution)/shard_map/ppermute | solution.py:498
  75.1 4.1 %project.7 = (bf16[2,128,1024]{2,1,0:T(8,128)(2,1)S(1)}, bf16[2,128,1024]{2,1,0:T(8,128)(2,1)S(1)}) custom-call(s32[1024]{0:T(1024)S(1)} %reshape.11.words_ref, bf16[6144,512]{1,0:T(8,128)(2,1)} %table_ref.19, bf16[1024,1024]{1,0:T(8,128)(2,1)S(1)} %bitcast.9, bf16[1024,1024]{1,0:T(8,128)(2,1)S(1)} %collective-permute-done.other_basis, ...), custom_call_target="tpu_custom_call" | custom-call | flops 6000000000 | bytes 20000000 | tf_op jit(solution)/shard_map/project/pallas_call | solution.py:339
  79.2 2.7 %collective-permute-start.20 = (bf16[2,128,1024]{2,1,0:T(8,128)(2,1)S(1)}, bf16[2,128,1024]{2,1,0:T(8,128)(2,1)S(1)}, u32[]{:S(2)}, u32[]{:S(2)}) collective-permute-start(bf16[2,128,1024]{2,1,0:T(8,128)(2,1)S(1)} %get-tuple-element.122), channel_id=1, source_target_pairs={{0,96},{1,97},{2,98},{3,99},{4,100},{5,101},{6,102},{7,103},{8,104... | collective-permute-start | bytes 1572872 | tf_op jit(solution)/shard_map/ppermute | solution.py:514
  81.9 3.6 %collective-permute-done.10.rest_1_ = bf16[2,2,128,512]{3,2,1,0:T(8,128)(2,1)S(1)} collective-permute-done((bf16[2,2,128,512]{3,2,1,0:T(8,128)(2,1)S(1)}, bf16[2,2,128,512]{3,2,1,0:T(8,128)(2,1)S(1)}, u32[]{:S(2)}, u32[]{:S(2)}) %collective-permute-start.10) | collective-permute-done | bytes 524320 | tf_op jit(solution)/shard_map/ppermute | solution.py:498
  85.6 3.9 %project.6 = (bf16[2,128,1024]{2,1,0:T(8,128)(2,1)S(1)}, bf16[2,128,1024]{2,1,0:T(8,128)(2,1)S(1)}) custom-call(s32[1024]{0:T(1024)S(1)} %reshape.11.words_ref, bf16[6144,512]{1,0:T(8,128)(2,1)} %table_ref.19, bf16[1024,1024]{1,0:T(8,128)(2,1)S(1)} %bitcast.10, bf16[1024,1024]{1,0:T(8,128)(2,1)S(1)} %collective-permute-done.other_basis, ...), custom_call_target="tpu_custom_call" | custom-call | flops 6000000000 | bytes 20000000 | tf_op jit(solution)/shard_map/project/pallas_call | solution.py:339
  91.8 3.6 %collective-permute-start.21 = (bf16[128,1024]{1,0:T(8,128)(2,1)S(1)}, bf16[128,1024]{1,0:T(8,128)(2,1)S(1)}, u32[]{:S(2)}, u32[]{:S(2)}) collective-permute-start(bf16[128,1024]{1,0:T(8,128)(2,1)S(1)} %get-tuple-element.123), channel_id=1, source_target_pairs={{0,17},{1,2},{2,10},{3,7},{4,21},{5,6},{6,14},{7,3},{8,16},{9,13},... | collective-permute-start | bytes 786440 | tf_op jit(solution)/shard_map/ppermute | solution.py:519
  95.3 4.6 %collective-permute-start.23 = (bf16[128,1024]{1,0:T(8,128)(2,1)S(1)}, bf16[128,1024]{1,0:T(8,128)(2,1)S(1)}, u32[]{:S(2)}, u32[]{:S(2)}) collective-permute-start(bf16[128,1024]{1,0:T(8,128)(2,1)S(1)} %get-tuple-element.125), channel_id=1, source_target_pairs={{0,0},{1,3},{2,11},{3,2},{4,4},{5,7},{6,15},{7,6},{8,17},{9,8},{10... | collective-permute-start | bytes 786440 | tf_op jit(solution)/shard_map/ppermute | solution.py:519
  100.0 5.8 %collective-permute-start.24 = (bf16[128,1024]{1,0:T(8,128)(2,1)S(1)}, bf16[128,1024]{1,0:T(8,128)(2,1)S(1)}, u32[]{:S(2)}, u32[]{:S(2)}) collective-permute-start(bf16[128,1024]{1,0:T(8,128)(2,1)S(1)} %get-tuple-element.126), channel_id=1, source_target_pairs={{0,1},{1,6},{2,26},{3,3},{4,5},{5,2},{6,30},{7,7},{8,0},{9,9},{10,... | collective-permute-start | bytes 786440 | tf_op jit(solution)/shard_map/ppermute | solution.py:519
  105.9 5.5 %collective-permute-done.23.refs_2_ = bf16[128,1024]{1,0:T(8,128)(2,1)S(1)} collective-permute-done((bf16[128,1024]{1,0:T(8,128)(2,1)S(1)}, bf16[128,1024]{1,0:T(8,128)(2,1)S(1)}, u32[]{:S(2)}, u32[]{:S(2)}) %collective-permute-start.23) | collective-permute-done | bytes 262176 | tf_op jit(solution)/shard_map/ppermute | solution.py:519
  (51 shorter events, 13.3 us)
Async XLA Ops:
  0.0 24.3 %collective-permute-start = (bf16[1024,1024]{1,0:T(8,128)(2,1)}, bf16[1024,1024]{1,0:T(8,128)(2,1)S(1)}, u32[]{:S(2)}, u32[]{:S(2)}) collective-permute-start(bf16[1024,1024]{1,0:T(8,128)(2,1)} %bitcast.6), channel_id=1, source_target_pairs={{0,1},{1,0},{2,3},{3,2},{4,5},{5,4},{6,7},{7,6},{8,9},{9,8},{10,11... | collective-permute-start | bytes 6291464 | tf_op jit(solution)/shard_map/ppermute | solution.py:465
  30.0 5.7 %collective-permute-start.2 = (bf16[3,4,2,128,512]{4,3,2,1,0:T(8,128)(2,1)S(1)}, bf16[3,4,2,128,512]{4,3,2,1,0:T(8,128)(2,1)S(1)}, u32[]{:S(2)}, u32[]{:S(2)}) collective-permute-start(bf16[3,4,2,128,512]{4,3,2,1,0:T(8,128)(2,1)S(1)} %cross.3), channel_id=1, source_target_pairs={{0,1},{1,0},{2,3},{3,2},{4,5},{5,4},{6,7},{7,6},{8,9},{9,8},{10,11... | collective-permute-start | bytes 9437192 | tf_op jit(solution)/shard_map/ppermute | solution.py:480
  32.4 15.2 %collective-permute-start.3 = (bf16[2,2,128,512]{3,2,1,0:T(8,128)(2,1)S(1)}, bf16[2,2,128,512]{3,2,1,0:T(8,128)(2,1)S(1)}, u32[]{:S(2)}, u32[]{:S(2)}) collective-permute-start(bf16[2,2,128,512]{3,2,1,0:T(8,128)(2,1)S(1)} %get-tuple-element.74), channel_id=1, source_target_pairs={{0,2},{1,9},{2,4},{3,11},{4,6},{5,13},{6,0},{7,15},{8,10},{9,17},{... | collective-permute-start | bytes 1572872 | tf_op jit(solution)/shard_map/ppermute | solution.py:498
  32.5 15.1 %collective-permute-start.4 = (bf16[2,2,128,512]{3,2,1,0:T(8,128)(2,1)S(1)}, bf16[2,2,128,512]{3,2,1,0:T(8,128)(2,1)S(1)}, u32[]{:S(2)}, u32[]{:S(2)}) collective-permute-start(bf16[2,2,128,512]{3,2,1,0:T(8,128)(2,1)S(1)} %get-tuple-element.75), channel_id=1, source_target_pairs={{0,6},{1,25},{2,0},{3,27},{4,2},{5,29},{6,4},{7,31},{8,14},{9,1},{... | collective-permute-start | bytes 1572872 | tf_op jit(solution)/shard_map/ppermute | solution.py:498
  35.1 12.5 %collective-permute-start.5 = (bf16[2,2,128,512]{3,2,1,0:T(8,128)(2,1)S(1)}, bf16[2,2,128,512]{3,2,1,0:T(8,128)(2,1)S(1)}, u32[]{:S(2)}, u32[]{:S(2)}) collective-permute-start(bf16[2,2,128,512]{3,2,1,0:T(8,128)(2,1)S(1)} %get-tuple-element.76), channel_id=1, source_target_pairs={{0,4},{1,17},{2,6},{3,19},{4,0},{5,21},{6,2},{7,23},{8,12},{9,25},... | collective-permute-start | bytes 1572872 | tf_op jit(solution)/shard_map/ppermute | solution.py:498
  37.7 21.2 %collective-permute-start.6 = (bf16[2,2,128,512]{3,2,1,0:T(8,128)(2,1)S(1)}, bf16[2,2,128,512]{3,2,1,0:T(8,128)(2,1)S(1)}, u32[]{:S(2)}, u32[]{:S(2)}) collective-permute-start(bf16[2,2,128,512]{3,2,1,0:T(8,128)(2,1)S(1)} %get-tuple-element.91), channel_id=1, source_target_pairs={{0,2},{1,9},{2,4},{3,11},{4,6},{5,13},{6,0},{7,15},{8,10},{9,17},{... | collective-permute-start | bytes 1572872 | tf_op jit(solution)/shard_map/ppermute | solution.py:498
  37.9 21.0 %collective-permute-start.7 = (bf16[2,2,128,512]{3,2,1,0:T(8,128)(2,1)S(1)}, bf16[2,2,128,512]{3,2,1,0:T(8,128)(2,1)S(1)}, u32[]{:S(2)}, u32[]{:S(2)}) collective-permute-start(bf16[2,2,128,512]{3,2,1,0:T(8,128)(2,1)S(1)} %get-tuple-element.92), channel_id=1, source_target_pairs={{0,6},{1,25},{2,0},{3,27},{4,2},{5,29},{6,4},{7,31},{8,14},{9,1},{... | collective-permute-start | bytes 1572872 | tf_op jit(solution)/shard_map/ppermute | solution.py:498
  47.6 13.9 %collective-permute-start.8 = (bf16[2,2,128,512]{3,2,1,0:T(8,128)(2,1)S(1)}, bf16[2,2,128,512]{3,2,1,0:T(8,128)(2,1)S(1)}, u32[]{:S(2)}, u32[]{:S(2)}) collective-permute-start(bf16[2,2,128,512]{3,2,1,0:T(8,128)(2,1)S(1)} %get-tuple-element.93), channel_id=1, source_target_pairs={{0,4},{1,17},{2,6},{3,19},{4,0},{5,21},{6,2},{7,23},{8,12},{9,25},... | collective-permute-start | bytes 1572872 | tf_op jit(solution)/shard_map/ppermute | solution.py:498
  50.6 14.5 %collective-permute-start.15 = (bf16[2,128,1024]{2,1,0:T(8,128)(2,1)S(1)}, bf16[2,128,1024]{2,1,0:T(8,128)(2,1)S(1)}, u32[]{:S(2)}, u32[]{:S(2)}) collective-permute-start(bf16[2,128,1024]{2,1,0:T(8,128)(2,1)S(1)} %get-tuple-element.84), channel_id=1, source_target_pairs={{0,32},{1,33},{2,34},{3,35},{4,36},{5,37},{6,38},{7,39},{8,40},{9,... | collective-permute-start | bytes 1572872 | tf_op jit(solution)/shard_map/ppermute | solution.py:514
  50.7 15.0 %collective-permute-start.16 = (bf16[2,128,1024]{2,1,0:T(8,128)(2,1)S(1)}, bf16[2,128,1024]{2,1,0:T(8,128)(2,1)S(1)}, u32[]{:S(2)}, u32[]{:S(2)}) collective-permute-start(bf16[2,128,1024]{2,1,0:T(8,128)(2,1)S(1)} %get-tuple-element.85), channel_id=1, source_target_pairs={{0,96},{1,97},{2,98},{3,99},{4,100},{5,101},{6,102},{7,103},{8,104... | collective-permute-start | bytes 1572872 | tf_op jit(solution)/shard_map/ppermute | solution.py:514
  58.9 10.0 %collective-permute-start.14 = (bf16[2,2,128,512]{3,2,1,0:T(8,128)(2,1)S(1)}, bf16[2,2,128,512]{3,2,1,0:T(8,128)(2,1)S(1)}, u32[]{:S(2)}, u32[]{:S(2)}) collective-permute-start(bf16[2,2,128,512]{3,2,1,0:T(8,128)(2,1)S(1)} %get-tuple-element.113), channel_id=1, source_target_pairs={{0,4},{1,17},{2,6},{3,19},{4,0},{5,21},{6,2},{7,23},{8,12},{9,25},... | collective-permute-start | bytes 1572872 | tf_op jit(solution)/shard_map/ppermute | solution.py:498
  58.9 13.8 %collective-permute-start.13 = (bf16[2,2,128,512]{3,2,1,0:T(8,128)(2,1)S(1)}, bf16[2,2,128,512]{3,2,1,0:T(8,128)(2,1)S(1)}, u32[]{:S(2)}, u32[]{:S(2)}) collective-permute-start(bf16[2,2,128,512]{3,2,1,0:T(8,128)(2,1)S(1)} %get-tuple-element.111), channel_id=1, source_target_pairs={{0,6},{1,25},{2,0},{3,27},{4,2},{5,29},{6,4},{7,31},{8,14},{9,1},{... | collective-permute-start | bytes 1572872 | tf_op jit(solution)/shard_map/ppermute | solution.py:498
  61.5 13.5 %collective-permute-start.12 = (bf16[2,2,128,512]{3,2,1,0:T(8,128)(2,1)S(1)}, bf16[2,2,128,512]{3,2,1,0:T(8,128)(2,1)S(1)}, u32[]{:S(2)}, u32[]{:S(2)}) collective-permute-start(bf16[2,2,128,512]{3,2,1,0:T(8,128)(2,1)S(1)} %get-tuple-element.109), channel_id=1, source_target_pairs={{0,2},{1,9},{2,4},{3,11},{4,6},{5,13},{6,0},{7,15},{8,10},{9,17},{... | collective-permute-start | bytes 1572872 | tf_op jit(solution)/shard_map/ppermute | solution.py:498
  65.1 14.1 %collective-permute-start.18 = (bf16[2,128,1024]{2,1,0:T(8,128)(2,1)S(1)}, bf16[2,128,1024]{2,1,0:T(8,128)(2,1)S(1)}, u32[]{:S(2)}, u32[]{:S(2)}) collective-permute-start(bf16[2,128,1024]{2,1,0:T(8,128)(2,1)S(1)} %get-tuple-element.95), channel_id=1, source_target_pairs={{0,96},{1,97},{2,98},{3,99},{4,100},{5,101},{6,102},{7,103},{8,104... | collective-permute-start | bytes 1572872 | tf_op jit(solution)/shard_map/ppermute | solution.py:514
  65.7 13.4 %collective-permute-start.17 = (bf16[2,128,1024]{2,1,0:T(8,128)(2,1)S(1)}, bf16[2,128,1024]{2,1,0:T(8,128)(2,1)S(1)}, u32[]{:S(2)}, u32[]{:S(2)}) collective-permute-start(bf16[2,128,1024]{2,1,0:T(8,128)(2,1)S(1)} %join.1), channel_id=1, source_target_pairs={{0,32},{1,33},{2,34},{3,35},{4,36},{5,37},{6,38},{7,39},{8,40},{9,... | collective-permute-start | bytes 1572872 | tf_op jit(solution)/shard_map/ppermute | solution.py:514
  68.9 13.0 %collective-permute-start.11 = (bf16[2,2,128,512]{3,2,1,0:T(8,128)(2,1)S(1)}, bf16[2,2,128,512]{3,2,1,0:T(8,128)(2,1)S(1)}, u32[]{:S(2)}, u32[]{:S(2)}) collective-permute-start(bf16[2,2,128,512]{3,2,1,0:T(8,128)(2,1)S(1)} %get-tuple-element.106), channel_id=1, source_target_pairs={{0,4},{1,17},{2,6},{3,19},{4,0},{5,21},{6,2},{7,23},{8,12},{9,25},... | collective-permute-start | bytes 1572872 | tf_op jit(solution)/shard_map/ppermute | solution.py:498
  72.7 12.8 %collective-permute-start.10 = (bf16[2,2,128,512]{3,2,1,0:T(8,128)(2,1)S(1)}, bf16[2,2,128,512]{3,2,1,0:T(8,128)(2,1)S(1)}, u32[]{:S(2)}, u32[]{:S(2)}) collective-permute-start(bf16[2,2,128,512]{3,2,1,0:T(8,128)(2,1)S(1)} %get-tuple-element.104), channel_id=1, source_target_pairs={{0,6},{1,25},{2,0},{3,27},{4,2},{5,29},{6,4},{7,31},{8,14},{9,1},{... | collective-permute-start | bytes 1572872 | tf_op jit(solution)/shard_map/ppermute | solution.py:498
  75.1 10.5 %collective-permute-start.9 = (bf16[2,2,128,512]{3,2,1,0:T(8,128)(2,1)S(1)}, bf16[2,2,128,512]{3,2,1,0:T(8,128)(2,1)S(1)}, u32[]{:S(2)}, u32[]{:S(2)}) collective-permute-start(bf16[2,2,128,512]{3,2,1,0:T(8,128)(2,1)S(1)} %get-tuple-element.102), channel_id=1, source_target_pairs={{0,2},{1,9},{2,4},{3,11},{4,6},{5,13},{6,0},{7,15},{8,10},{9,17},{... | collective-permute-start | bytes 1572872 | tf_op jit(solution)/shard_map/ppermute | solution.py:498
  79.2 12.2 %collective-permute-start.19 = (bf16[2,128,1024]{2,1,0:T(8,128)(2,1)S(1)}, bf16[2,128,1024]{2,1,0:T(8,128)(2,1)S(1)}, u32[]{:S(2)}, u32[]{:S(2)}) collective-permute-start(bf16[2,128,1024]{2,1,0:T(8,128)(2,1)S(1)} %get-tuple-element.121), channel_id=1, source_target_pairs={{0,32},{1,33},{2,34},{3,35},{4,36},{5,37},{6,38},{7,39},{8,40},{9,... | collective-permute-start | bytes 1572872 | tf_op jit(solution)/shard_map/ppermute | solution.py:514
  79.2 12.1 %collective-permute-start.20 = (bf16[2,128,1024]{2,1,0:T(8,128)(2,1)S(1)}, bf16[2,128,1024]{2,1,0:T(8,128)(2,1)S(1)}, u32[]{:S(2)}, u32[]{:S(2)}) collective-permute-start(bf16[2,128,1024]{2,1,0:T(8,128)(2,1)S(1)} %get-tuple-element.122), channel_id=1, source_target_pairs={{0,96},{1,97},{2,98},{3,99},{4,100},{5,101},{6,102},{7,103},{8,104... | collective-permute-start | bytes 1572872 | tf_op jit(solution)/shard_map/ppermute | solution.py:514
  91.8 14.2 %collective-permute-start.21 = (bf16[128,1024]{1,0:T(8,128)(2,1)S(1)}, bf16[128,1024]{1,0:T(8,128)(2,1)S(1)}, u32[]{:S(2)}, u32[]{:S(2)}) collective-permute-start(bf16[128,1024]{1,0:T(8,128)(2,1)S(1)} %get-tuple-element.123), channel_id=1, source_target_pairs={{0,17},{1,2},{2,10},{3,7},{4,21},{5,6},{6,14},{7,3},{8,16},{9,13},... | collective-permute-start | bytes 786440 | tf_op jit(solution)/shard_map/ppermute | solution.py:519
  95.3 10.6 %collective-permute-start.22 = (bf16[128,1024]{1,0:T(8,128)(2,1)S(1)}, bf16[128,1024]{1,0:T(8,128)(2,1)S(1)}, u32[]{:S(2)}, u32[]{:S(2)}) collective-permute-start(bf16[128,1024]{1,0:T(8,128)(2,1)S(1)} %get-tuple-element.124), channel_id=1, source_target_pairs={{0,16},{1,7},{2,27},{3,6},{4,20},{5,3},{6,31},{7,2},{8,1},{9,12},{... | collective-permute-start | bytes 786440 | tf_op jit(solution)/shard_map/ppermute | solution.py:519
  95.3 16.1 %collective-permute-start.23 = (bf16[128,1024]{1,0:T(8,128)(2,1)S(1)}, bf16[128,1024]{1,0:T(8,128)(2,1)S(1)}, u32[]{:S(2)}, u32[]{:S(2)}) collective-permute-start(bf16[128,1024]{1,0:T(8,128)(2,1)S(1)} %get-tuple-element.125), channel_id=1, source_target_pairs={{0,0},{1,3},{2,11},{3,2},{4,4},{5,7},{6,15},{7,6},{8,17},{9,8},{10... | collective-permute-start | bytes 786440 | tf_op jit(solution)/shard_map/ppermute | solution.py:519
  100.0 11.5 %collective-permute-start.24 = (bf16[128,1024]{1,0:T(8,128)(2,1)S(1)}, bf16[128,1024]{1,0:T(8,128)(2,1)S(1)}, u32[]{:S(2)}, u32[]{:S(2)}) collective-permute-start(bf16[128,1024]{1,0:T(8,128)(2,1)S(1)} %get-tuple-element.126), channel_id=1, source_target_pairs={{0,1},{1,6},{2,26},{3,3},{4,5},{5,2},{6,30},{7,7},{8,0},{9,9},{10,... | collective-permute-start | bytes 786440 | tf_op jit(solution)/shard_map/ppermute | solution.py:519
  (4 other events, 37.8 us)

commit v9 on v8

--- a/solution.py
+++ b/solution.py
@@ -299,7 +299,7 @@
                 total[which, half, :, pl.ds(column, width)] += sums
 
     wide = own_basis.shape[1]
-    tile = 256
+    tile = 512
 
     def store(halves, which, here, columns):
         if which in added:

time: 114 us -> 113 us (level)
  Pallas kernels: 30 us -> 27.7 us
  starting transfers between devices: 38.3 us -> 39.5 us
  waiting for transfers between devices: 22.5 us -> 23.7 us
    ppermute x12, waiting for transfers between devices: 14.6 us -> 18 us  [body(): came.append(lax.ppermute(sent, AXES, hop1_pairs(step)))]
    ppermute x4, starting transfers between devices: 13.9 us -> 16.9 us  [body(): lax.ppermute(buf, AXES, hop3_pairs(send))]
    pallas_call x4, Pallas kernels: 14.4 us -> 11.8 us  [project(): pl.pallas_call(functools.partial(project_kernel, chunk, row, added), out_...]
    ppermute x12, starting transfers between devices: 13.9 us -> 12.3 us  [body(): came.append(lax.ppermute(sent, AXES, hop1_pairs(step)))]
  transfers between devices with their start and end apart: 25 -> 25, of which waited for: 8 -> 9; matrix products, arithmetic and copies ran while one was open for 0% -> 0% of each run, Pallas kernels for 24% -> 22%
where the time goes in v9:
time: 113 us; the launch traced here: 112 us
  starting transfers between devices  39.5 us (35%)
  Pallas kernels  27.7 us (25%)
  waiting for transfers between devices  23.7 us (21%)
  blocking collectives  21.1 us (19%)
    all_to_all x1, blocking collectives, body(): lax.all_to_all(sent, 'shard', split_axis=0, concat_axis=0, tiled=True)  21.1 us
    ppermute x12, waiting for transfers between devices, body(): came.append(lax.ppermute(sent, AXES, hop1_pairs(step)))  18 us
    ppermute x4, starting transfers between devices, body(): lax.ppermute(buf, AXES, hop3_pairs(send))  16.9 us
    ppermute x12, starting transfers between devices, body(): came.append(lax.ppermute(sent, AXES, hop1_pairs(step)))  12.3 us
    pallas_call x4, Pallas kernels, project(): pl.pallas_call(functools.partial(project_kernel, chunk, row, added), out_...  11.8 us
    pallas_call x4, Pallas kernels, pick(): pl.pallas_call(functools.partial(pick_kernel, chunk, row), out_shape=[plt...  8.54 us
    ppermute x6, starting transfers between devices, body(): lax.ppermute(p, AXES, hop2_pairs(step))  7.01 us
    ppermute x4, waiting for transfers between devices, body(): lax.ppermute(buf, AXES, hop3_pairs(send))  4.52 us
  transfers between devices with their start and end apart: 25, of which 9 were waited for; matrix products, arithmetic and copies ran while one was open for 0% of the time, Pallas kernels for 22%

profile of v9, /device:TPU:1, one launch (start us, length us, event | category | flops | bytes accessed | tf_op | source)
XLA Modules:
  0.0 112.4 jit_solution(17762789515176839522)
XLA Ops:
  3.0 21.1 %all_to_all.5.notes_ref = s32[64,8,128]{2,1,0:T(8,128)S(1)} all-to-all(s32[64,8,128]{2,1,0:T(8,128)S(1)} %bitcast.4), channel_id=1, replica_groups=mesh['shard'=64,'basis'=2] {'shard'}, dimensions={0} | all-to-all | bytes 524288 | tf_op jit(solution)/shard_map/all_to_all | solution.py:468
  24.3 1.9 %cross.2 = bf16[1,4,2,128,512]{4,3,2,1,0:T(8,128)(2,1)S(1)} custom-call(s32[1024]{0:T(1024)S(1)} %reshape.11.words_ref, bf16[6144,512]{1,0:T(8,128)(2,1)} %table_ref.19), custom_call_target="tpu_custom_call" | custom-call | flops 1 | bytes 1 | tf_op jit(solution)/shard_map/cross/pallas_call | solution.py:193
  27.8 2.2 %cross.3 = bf16[3,4,2,128,512]{4,3,2,1,0:T(8,128)(2,1)S(1)} custom-call(s32[1024]{0:T(1024)S(1)} %reshape.11.words_ref, bf16[6144,512]{1,0:T(8,128)(2,1)} %table_ref.19), custom_call_target="tpu_custom_call" | custom-call | flops 1 | bytes 1 | tf_op jit(solution)/shard_map/cross/pallas_call | solution.py:193
  30.4 2.5 %pick.4 = (bf16[2,2,128,512]{3,2,1,0:T(8,128)(2,1)S(1)}, bf16[2,2,128,512]{3,2,1,0:T(8,128)(2,1)S(1)}, bf16[2,2,128,512]{3,2,1,0:T(8,128)(2,1)S(1)}) custom-call(s32[1024]{0:T(1024)S(1)} %reshape.11.words_ref, bf16[6144,512]{1,0:T(8,128)(2,1)} %table_ref.19, bf16[1,4,2,128,512]{4,3,2,1,0:T(8,128)(2,1)S(1)} %collective-permute-done.1.crossed_ref), custom_call_target="tpu_custom_call" | custom-call | flops 1 | bytes 1 | tf_op jit(solution)/shard_map/pick/pallas_call | solution.py:221
  33.1 2.6 %collective-permute-start.4 = (bf16[2,2,128,512]{3,2,1,0:T(8,128)(2,1)S(1)}, bf16[2,2,128,512]{3,2,1,0:T(8,128)(2,1)S(1)}, u32[]{:S(2)}, u32[]{:S(2)}) collective-permute-start(bf16[2,2,128,512]{3,2,1,0:T(8,128)(2,1)S(1)} %get-tuple-element.75), channel_id=1, source_target_pairs={{0,6},{1,25},{2,0},{3,27},{4,2},{5,29},{6,4},{7,31},{8,14},{9,1},{... | collective-permute-start | bytes 1572872 | tf_op jit(solution)/shard_map/ppermute | solution.py:498
  35.8 2.2 %pick.5 = (bf16[2,2,128,512]{3,2,1,0:T(8,128)(2,1)S(1)}, bf16[2,2,128,512]{3,2,1,0:T(8,128)(2,1)S(1)}, bf16[2,2,128,512]{3,2,1,0:T(8,128)(2,1)S(1)}) custom-call(s32[1024]{0:T(1024)S(1)} %reshape.11.words_ref, bf16[6144,512]{1,0:T(8,128)(2,1)} %table_ref.19, bf16[3,4,2,128,512]{4,3,2,1,0:T(8,128)(2,1)S(1)} %collective-permute-done.2.crossed_ref), custom_call_target="tpu_custom_call" | custom-call | flops 1 | bytes 1 | tf_op jit(solution)/shard_map/pick/pallas_call | solution.py:221
  38.1 2.6 %collective-permute-start.7 = (bf16[2,2,128,512]{3,2,1,0:T(8,128)(2,1)S(1)}, bf16[2,2,128,512]{3,2,1,0:T(8,128)(2,1)S(1)}, u32[]{:S(2)}, u32[]{:S(2)}) collective-permute-start(bf16[2,2,128,512]{3,2,1,0:T(8,128)(2,1)S(1)} %get-tuple-element.92), channel_id=1, source_target_pairs={{0,6},{1,25},{2,0},{3,27},{4,2},{5,29},{6,4},{7,31},{8,14},{9,1},{... | collective-permute-start | bytes 1572872 | tf_op jit(solution)/shard_map/ppermute | solution.py:498
  40.7 7.5 %collective-permute-done.3.rest_0_ = bf16[2,2,128,512]{3,2,1,0:T(8,128)(2,1)S(1)} collective-permute-done((bf16[2,2,128,512]{3,2,1,0:T(8,128)(2,1)S(1)}, bf16[2,2,128,512]{3,2,1,0:T(8,128)(2,1)S(1)}, u32[]{:S(2)}, u32[]{:S(2)}) %collective-permute-start.3) | collective-permute-done | bytes 524320 | tf_op jit(solution)/shard_map/ppermute | solution.py:498
  48.2 3.7 %project.4 = (bf16[2,128,1024]{2,1,0:T(8,128)(2,1)S(1)}, bf16[2,128,1024]{2,1,0:T(8,128)(2,1)S(1)}) custom-call(s32[1024]{0:T(1024)S(1)} %reshape.11.words_ref, bf16[6144,512]{1,0:T(8,128)(2,1)} %table_ref.19, bf16[1024,1024]{1,0:T(8,128)(2,1)S(1)} %bitcast.7, bf16[1024,1024]{1,0:T(8,128)(2,1)S(1)} %collective-permute-done.other_basis, ...), custom_call_target="tpu_custom_call" | custom-call | flops 6000000000 | bytes 20000000 | tf_op jit(solution)/shard_map/project/pallas_call | solution.py:339
  52.0 2.7 %collective-permute-start.16 = (bf16[2,128,1024]{2,1,0:T(8,128)(2,1)S(1)}, bf16[2,128,1024]{2,1,0:T(8,128)(2,1)S(1)}, u32[]{:S(2)}, u32[]{:S(2)}) collective-permute-start(bf16[2,128,1024]{2,1,0:T(8,128)(2,1)S(1)} %get-tuple-element.85), channel_id=1, source_target_pairs={{0,96},{1,97},{2,98},{3,99},{4,100},{5,101},{6,102},{7,103},{8,104... | collective-permute-start | bytes 1572872 | tf_op jit(solution)/shard_map/ppermute | solution.py:514
  56.4 3.0 %collective-permute-done.6.rest_0_ = bf16[2,2,128,512]{3,2,1,0:T(8,128)(2,1)S(1)} collective-permute-done((bf16[2,2,128,512]{3,2,1,0:T(8,128)(2,1)S(1)}, bf16[2,2,128,512]{3,2,1,0:T(8,128)(2,1)S(1)}, u32[]{:S(2)}, u32[]{:S(2)}) %collective-permute-start.6) | collective-permute-done | bytes 524320 | tf_op jit(solution)/shard_map/ppermute | solution.py:498
  59.8 2.3 %collective-permute-start.13 = (bf16[2,2,128,512]{3,2,1,0:T(8,128)(2,1)S(1)}, bf16[2,2,128,512]{3,2,1,0:T(8,128)(2,1)S(1)}, u32[]{:S(2)}, u32[]{:S(2)}) collective-permute-start(bf16[2,2,128,512]{3,2,1,0:T(8,128)(2,1)S(1)} %get-tuple-element.111), channel_id=1, source_target_pairs={{0,6},{1,25},{2,0},{3,27},{4,2},{5,29},{6,4},{7,31},{8,14},{9,1},{... | collective-permute-start | bytes 1572872 | tf_op jit(solution)/shard_map/ppermute | solution.py:498
  62.1 2.4 %project.5 = (f32[2,128,1024]{2,1,0:T(8,128)S(1)}, bf16[2,128,1024]{2,1,0:T(8,128)(2,1)S(1)}) custom-call(s32[1024]{0:T(1024)S(1)} %reshape.11.words_ref, bf16[6144,512]{1,0:T(8,128)(2,1)} %table_ref.19, bf16[1024,1024]{1,0:T(8,128)(2,1)S(1)} %bitcast.8, bf16[1024,1024]{1,0:T(8,128)(2,1)S(1)} %collective-permute-done.other_basis, ...), custom_call_target="tpu_custom_call" | custom-call | flops 6000000000 | bytes 20000000 | tf_op jit(solution)/shard_map/project/pallas_call | solution.py:339
  66.7 2.1 %pick.7 = (bf16[2,2,128,512]{3,2,1,0:T(8,128)(2,1)S(1)}, bf16[2,2,128,512]{3,2,1,0:T(8,128)(2,1)S(1)}, bf16[2,2,128,512]{3,2,1,0:T(8,128)(2,1)S(1)}) custom-call(s32[1024]{0:T(1024)S(1)} %reshape.11.words_ref, bf16[6144,512]{1,0:T(8,128)(2,1)} %table_ref.19, bf16[3,4,2,128,512]{4,3,2,1,0:T(8,128)(2,1)S(1)} %collective-permute-done.2.crossed_ref), custom_call_target="tpu_custom_call" | custom-call | flops 1 | bytes 1 | tf_op jit(solution)/shard_map/pick/pallas_call | solution.py:221
  69.3 1.8 %collective-permute-start.11 = (bf16[2,2,128,512]{3,2,1,0:T(8,128)(2,1)S(1)}, bf16[2,2,128,512]{3,2,1,0:T(8,128)(2,1)S(1)}, u32[]{:S(2)}, u32[]{:S(2)}) collective-permute-start(bf16[2,2,128,512]{3,2,1,0:T(8,128)(2,1)S(1)} %get-tuple-element.106), channel_id=1, source_target_pairs={{0,4},{1,17},{2,6},{3,19},{4,0},{5,21},{6,2},{7,23},{8,12},{9,25},... | collective-permute-start | bytes 1572872 | tf_op jit(solution)/shard_map/ppermute | solution.py:498
  72.9 2.3 %collective-permute-start.10 = (bf16[2,2,128,512]{3,2,1,0:T(8,128)(2,1)S(1)}, bf16[2,2,128,512]{3,2,1,0:T(8,128)(2,1)S(1)}, u32[]{:S(2)}, u32[]{:S(2)}) collective-permute-start(bf16[2,2,128,512]{3,2,1,0:T(8,128)(2,1)S(1)} %get-tuple-element.104), channel_id=1, source_target_pairs={{0,6},{1,25},{2,0},{3,27},{4,2},{5,29},{6,4},{7,31},{8,14},{9,1},{... | collective-permute-start | bytes 1572872 | tf_op jit(solution)/shard_map/ppermute | solution.py:498
  75.2 2.9 %project.7 = (bf16[2,128,1024]{2,1,0:T(8,128)(2,1)S(1)}, bf16[2,128,1024]{2,1,0:T(8,128)(2,1)S(1)}) custom-call(s32[1024]{0:T(1024)S(1)} %reshape.11.words_ref, bf16[6144,512]{1,0:T(8,128)(2,1)} %table_ref.19, bf16[1024,1024]{1,0:T(8,128)(2,1)S(1)} %bitcast.9, bf16[1024,1024]{1,0:T(8,128)(2,1)S(1)} %collective-permute-done.other_basis, ...), custom_call_target="tpu_custom_call" | custom-call | flops 6000000000 | bytes 20000000 | tf_op jit(solution)/shard_map/project/pallas_call | solution.py:339
  78.3 2.7 %collective-permute-start.20 = (bf16[2,128,1024]{2,1,0:T(8,128)(2,1)S(1)}, bf16[2,128,1024]{2,1,0:T(8,128)(2,1)S(1)}, u32[]{:S(2)}, u32[]{:S(2)}) collective-permute-start(bf16[2,128,1024]{2,1,0:T(8,128)(2,1)S(1)} %get-tuple-element.122), channel_id=1, source_target_pairs={{0,96},{1,97},{2,98},{3,99},{4,100},{5,101},{6,102},{7,103},{8,104... | collective-permute-start | bytes 1572872 | tf_op jit(solution)/shard_map/ppermute | solution.py:514
  80.9 4.4 %collective-permute-done.10.rest_1_ = bf16[2,2,128,512]{3,2,1,0:T(8,128)(2,1)S(1)} collective-permute-done((bf16[2,2,128,512]{3,2,1,0:T(8,128)(2,1)S(1)}, bf16[2,2,128,512]{3,2,1,0:T(8,128)(2,1)S(1)}, u32[]{:S(2)}, u32[]{:S(2)}) %collective-permute-start.10) | collective-permute-done | bytes 524320 | tf_op jit(solution)/shard_map/ppermute | solution.py:498
  86.2 2.8 %project.6 = (bf16[2,128,1024]{2,1,0:T(8,128)(2,1)S(1)}, bf16[2,128,1024]{2,1,0:T(8,128)(2,1)S(1)}) custom-call(s32[1024]{0:T(1024)S(1)} %reshape.11.words_ref, bf16[6144,512]{1,0:T(8,128)(2,1)} %table_ref.19, bf16[1024,1024]{1,0:T(8,128)(2,1)S(1)} %bitcast.10, bf16[1024,1024]{1,0:T(8,128)(2,1)S(1)} %collective-permute-done.other_basis, ...), custom_call_target="tpu_custom_call" | custom-call | flops 6000000000 | bytes 20000000 | tf_op jit(solution)/shard_map/project/pallas_call | solution.py:339
  90.0 9.5 %collective-permute-start.21 = (bf16[128,1024]{1,0:T(8,128)(2,1)S(1)}, bf16[128,1024]{1,0:T(8,128)(2,1)S(1)}, u32[]{:S(2)}, u32[]{:S(2)}) collective-permute-start(bf16[128,1024]{1,0:T(8,128)(2,1)S(1)} %get-tuple-element.123), channel_id=1, source_target_pairs={{0,17},{1,2},{2,10},{3,7},{4,21},{5,6},{6,14},{7,3},{8,16},{9,13},... | collective-permute-start | bytes 786440 | tf_op jit(solution)/shard_map/ppermute | solution.py:519
  100.7 1.9 %collective-permute-start.23 = (bf16[128,1024]{1,0:T(8,128)(2,1)S(1)}, bf16[128,1024]{1,0:T(8,128)(2,1)S(1)}, u32[]{:S(2)}, u32[]{:S(2)}) collective-permute-start(bf16[128,1024]{1,0:T(8,128)(2,1)S(1)} %get-tuple-element.125), channel_id=1, source_target_pairs={{0,0},{1,3},{2,11},{3,2},{4,4},{5,7},{6,15},{7,6},{8,17},{9,8},{10... | collective-permute-start | bytes 786440 | tf_op jit(solution)/shard_map/ppermute | solution.py:519
  102.6 4.2 %collective-permute-start.24 = (bf16[128,1024]{1,0:T(8,128)(2,1)S(1)}, bf16[128,1024]{1,0:T(8,128)(2,1)S(1)}, u32[]{:S(2)}, u32[]{:S(2)}) collective-permute-start(bf16[128,1024]{1,0:T(8,128)(2,1)S(1)} %get-tuple-element.126), channel_id=1, source_target_pairs={{0,1},{1,6},{2,26},{3,3},{4,5},{5,2},{6,30},{7,7},{8,0},{9,9},{10,... | collective-permute-start | bytes 786440 | tf_op jit(solution)/shard_map/ppermute | solution.py:519
  107.0 4.5 %collective-permute-done.23.refs_2_ = bf16[128,1024]{1,0:T(8,128)(2,1)S(1)} collective-permute-done((bf16[128,1024]{1,0:T(8,128)(2,1)S(1)}, bf16[128,1024]{1,0:T(8,128)(2,1)S(1)}, u32[]{:S(2)}, u32[]{:S(2)}) %collective-permute-start.23) | collective-permute-done | bytes 262176 | tf_op jit(solution)/shard_map/ppermute | solution.py:519
  (51 shorter events, 16.2 us)
Async XLA Ops:
  0.0 24.3 %collective-permute-start = (bf16[1024,1024]{1,0:T(8,128)(2,1)}, bf16[1024,1024]{1,0:T(8,128)(2,1)S(1)}, u32[]{:S(2)}, u32[]{:S(2)}) collective-permute-start(bf16[1024,1024]{1,0:T(8,128)(2,1)} %bitcast.6), channel_id=1, source_target_pairs={{0,1},{1,0},{2,3},{3,2},{4,5},{5,4},{6,7},{7,6},{8,9},{9,8},{10,11... | collective-permute-start | bytes 6291464 | tf_op jit(solution)/shard_map/ppermute | solution.py:465
  30.1 5.7 %collective-permute-start.2 = (bf16[3,4,2,128,512]{4,3,2,1,0:T(8,128)(2,1)S(1)}, bf16[3,4,2,128,512]{4,3,2,1,0:T(8,128)(2,1)S(1)}, u32[]{:S(2)}, u32[]{:S(2)}) collective-permute-start(bf16[3,4,2,128,512]{4,3,2,1,0:T(8,128)(2,1)S(1)} %cross.3), channel_id=1, source_target_pairs={{0,1},{1,0},{2,3},{3,2},{4,5},{5,4},{6,7},{7,6},{8,9},{9,8},{10,11... | collective-permute-start | bytes 9437192 | tf_op jit(solution)/shard_map/ppermute | solution.py:480
  33.0 15.2 %collective-permute-start.3 = (bf16[2,2,128,512]{3,2,1,0:T(8,128)(2,1)S(1)}, bf16[2,2,128,512]{3,2,1,0:T(8,128)(2,1)S(1)}, u32[]{:S(2)}, u32[]{:S(2)}) collective-permute-start(bf16[2,2,128,512]{3,2,1,0:T(8,128)(2,1)S(1)} %get-tuple-element.74), channel_id=1, source_target_pairs={{0,2},{1,9},{2,4},{3,11},{4,6},{5,13},{6,0},{7,15},{8,10},{9,17},{... | collective-permute-start | bytes 1572872 | tf_op jit(solution)/shard_map/ppermute | solution.py:498
  33.1 15.1 %collective-permute-start.4 = (bf16[2,2,128,512]{3,2,1,0:T(8,128)(2,1)S(1)}, bf16[2,2,128,512]{3,2,1,0:T(8,128)(2,1)S(1)}, u32[]{:S(2)}, u32[]{:S(2)}) collective-permute-start(bf16[2,2,128,512]{3,2,1,0:T(8,128)(2,1)S(1)} %get-tuple-element.75), channel_id=1, source_target_pairs={{0,6},{1,25},{2,0},{3,27},{4,2},{5,29},{6,4},{7,31},{8,14},{9,1},{... | collective-permute-start | bytes 1572872 | tf_op jit(solution)/shard_map/ppermute | solution.py:498
  35.7 12.5 %collective-permute-start.5 = (bf16[2,2,128,512]{3,2,1,0:T(8,128)(2,1)S(1)}, bf16[2,2,128,512]{3,2,1,0:T(8,128)(2,1)S(1)}, u32[]{:S(2)}, u32[]{:S(2)}) collective-permute-start(bf16[2,2,128,512]{3,2,1,0:T(8,128)(2,1)S(1)} %get-tuple-element.76), channel_id=1, source_target_pairs={{0,4},{1,17},{2,6},{3,19},{4,0},{5,21},{6,2},{7,23},{8,12},{9,25},... | collective-permute-start | bytes 1572872 | tf_op jit(solution)/shard_map/ppermute | solution.py:498
  38.0 21.5 %collective-permute-start.6 = (bf16[2,2,128,512]{3,2,1,0:T(8,128)(2,1)S(1)}, bf16[2,2,128,512]{3,2,1,0:T(8,128)(2,1)S(1)}, u32[]{:S(2)}, u32[]{:S(2)}) collective-permute-start(bf16[2,2,128,512]{3,2,1,0:T(8,128)(2,1)S(1)} %get-tuple-element.91), channel_id=1, source_target_pairs={{0,2},{1,9},{2,4},{3,11},{4,6},{5,13},{6,0},{7,15},{8,10},{9,17},{... | collective-permute-start | bytes 1572872 | tf_op jit(solution)/shard_map/ppermute | solution.py:498
  38.1 21.6 %collective-permute-start.7 = (bf16[2,2,128,512]{3,2,1,0:T(8,128)(2,1)S(1)}, bf16[2,2,128,512]{3,2,1,0:T(8,128)(2,1)S(1)}, u32[]{:S(2)}, u32[]{:S(2)}) collective-permute-start(bf16[2,2,128,512]{3,2,1,0:T(8,128)(2,1)S(1)} %get-tuple-element.92), channel_id=1, source_target_pairs={{0,6},{1,25},{2,0},{3,27},{4,2},{5,29},{6,4},{7,31},{8,14},{9,1},{... | collective-permute-start | bytes 1572872 | tf_op jit(solution)/shard_map/ppermute | solution.py:498
  48.2 13.9 %collective-permute-start.8 = (bf16[2,2,128,512]{3,2,1,0:T(8,128)(2,1)S(1)}, bf16[2,2,128,512]{3,2,1,0:T(8,128)(2,1)S(1)}, u32[]{:S(2)}, u32[]{:S(2)}) collective-permute-start(bf16[2,2,128,512]{3,2,1,0:T(8,128)(2,1)S(1)} %get-tuple-element.93), channel_id=1, source_target_pairs={{0,4},{1,17},{2,6},{3,19},{4,0},{5,21},{6,2},{7,23},{8,12},{9,25},... | collective-permute-start | bytes 1572872 | tf_op jit(solution)/shard_map/ppermute | solution.py:498
  51.9 13.1 %collective-permute-start.15 = (bf16[2,128,1024]{2,1,0:T(8,128)(2,1)S(1)}, bf16[2,128,1024]{2,1,0:T(8,128)(2,1)S(1)}, u32[]{:S(2)}, u32[]{:S(2)}) collective-permute-start(bf16[2,128,1024]{2,1,0:T(8,128)(2,1)S(1)} %get-tuple-element.84), channel_id=1, source_target_pairs={{0,32},{1,33},{2,34},{3,35},{4,36},{5,37},{6,38},{7,39},{8,40},{9,... | collective-permute-start | bytes 1572872 | tf_op jit(solution)/shard_map/ppermute | solution.py:514
  52.0 13.7 %collective-permute-start.16 = (bf16[2,128,1024]{2,1,0:T(8,128)(2,1)S(1)}, bf16[2,128,1024]{2,1,0:T(8,128)(2,1)S(1)}, u32[]{:S(2)}, u32[]{:S(2)}) collective-permute-start(bf16[2,128,1024]{2,1,0:T(8,128)(2,1)S(1)} %get-tuple-element.85), channel_id=1, source_target_pairs={{0,96},{1,97},{2,98},{3,99},{4,100},{5,101},{6,102},{7,103},{8,104... | collective-permute-start | bytes 1572872 | tf_op jit(solution)/shard_map/ppermute | solution.py:514
  59.4 9.9 %collective-permute-start.14 = (bf16[2,2,128,512]{3,2,1,0:T(8,128)(2,1)S(1)}, bf16[2,2,128,512]{3,2,1,0:T(8,128)(2,1)S(1)}, u32[]{:S(2)}, u32[]{:S(2)}) collective-permute-start(bf16[2,2,128,512]{3,2,1,0:T(8,128)(2,1)S(1)} %get-tuple-element.113), channel_id=1, source_target_pairs={{0,4},{1,17},{2,6},{3,19},{4,0},{5,21},{6,2},{7,23},{8,12},{9,25},... | collective-permute-start | bytes 1572872 | tf_op jit(solution)/shard_map/ppermute | solution.py:498
  59.8 13.1 %collective-permute-start.13 = (bf16[2,2,128,512]{3,2,1,0:T(8,128)(2,1)S(1)}, bf16[2,2,128,512]{3,2,1,0:T(8,128)(2,1)S(1)}, u32[]{:S(2)}, u32[]{:S(2)}) collective-permute-start(bf16[2,2,128,512]{3,2,1,0:T(8,128)(2,1)S(1)} %get-tuple-element.111), channel_id=1, source_target_pairs={{0,6},{1,25},{2,0},{3,27},{4,2},{5,29},{6,4},{7,31},{8,14},{9,1},{... | collective-permute-start | bytes 1572872 | tf_op jit(solution)/shard_map/ppermute | solution.py:498
  62.1 13.1 %collective-permute-start.12 = (bf16[2,2,128,512]{3,2,1,0:T(8,128)(2,1)S(1)}, bf16[2,2,128,512]{3,2,1,0:T(8,128)(2,1)S(1)}, u32[]{:S(2)}, u32[]{:S(2)}) collective-permute-start(bf16[2,2,128,512]{3,2,1,0:T(8,128)(2,1)S(1)} %get-tuple-element.109), channel_id=1, source_target_pairs={{0,2},{1,9},{2,4},{3,11},{4,6},{5,13},{6,0},{7,15},{8,10},{9,17},{... | collective-permute-start | bytes 1572872 | tf_op jit(solution)/shard_map/ppermute | solution.py:498
  65.0 13.2 %collective-permute-start.18 = (bf16[2,128,1024]{2,1,0:T(8,128)(2,1)S(1)}, bf16[2,128,1024]{2,1,0:T(8,128)(2,1)S(1)}, u32[]{:S(2)}, u32[]{:S(2)}) collective-permute-start(bf16[2,128,1024]{2,1,0:T(8,128)(2,1)S(1)} %get-tuple-element.95), channel_id=1, source_target_pairs={{0,96},{1,97},{2,98},{3,99},{4,100},{5,101},{6,102},{7,103},{8,104... | collective-permute-start | bytes 1572872 | tf_op jit(solution)/shard_map/ppermute | solution.py:514
  65.7 12.5 %collective-permute-start.17 = (bf16[2,128,1024]{2,1,0:T(8,128)(2,1)S(1)}, bf16[2,128,1024]{2,1,0:T(8,128)(2,1)S(1)}, u32[]{:S(2)}, u32[]{:S(2)}) collective-permute-start(bf16[2,128,1024]{2,1,0:T(8,128)(2,1)S(1)} %join.1), channel_id=1, source_target_pairs={{0,32},{1,33},{2,34},{3,35},{4,36},{5,37},{6,38},{7,39},{8,40},{9,... | collective-permute-start | bytes 1572872 | tf_op jit(solution)/shard_map/ppermute | solution.py:514
  69.3 11.6 %collective-permute-start.11 = (bf16[2,2,128,512]{3,2,1,0:T(8,128)(2,1)S(1)}, bf16[2,2,128,512]{3,2,1,0:T(8,128)(2,1)S(1)}, u32[]{:S(2)}, u32[]{:S(2)}) collective-permute-start(bf16[2,2,128,512]{3,2,1,0:T(8,128)(2,1)S(1)} %get-tuple-element.106), channel_id=1, source_target_pairs={{0,4},{1,17},{2,6},{3,19},{4,0},{5,21},{6,2},{7,23},{8,12},{9,25},... | collective-permute-start | bytes 1572872 | tf_op jit(solution)/shard_map/ppermute | solution.py:498
  72.9 12.4 %collective-permute-start.10 = (bf16[2,2,128,512]{3,2,1,0:T(8,128)(2,1)S(1)}, bf16[2,2,128,512]{3,2,1,0:T(8,128)(2,1)S(1)}, u32[]{:S(2)}, u32[]{:S(2)}) collective-permute-start(bf16[2,2,128,512]{3,2,1,0:T(8,128)(2,1)S(1)} %get-tuple-element.104), channel_id=1, source_target_pairs={{0,6},{1,25},{2,0},{3,27},{4,2},{5,29},{6,4},{7,31},{8,14},{9,1},{... | collective-permute-start | bytes 1572872 | tf_op jit(solution)/shard_map/ppermute | solution.py:498
  75.2 10.9 %collective-permute-start.9 = (bf16[2,2,128,512]{3,2,1,0:T(8,128)(2,1)S(1)}, bf16[2,2,128,512]{3,2,1,0:T(8,128)(2,1)S(1)}, u32[]{:S(2)}, u32[]{:S(2)}) collective-permute-start(bf16[2,2,128,512]{3,2,1,0:T(8,128)(2,1)S(1)} %get-tuple-element.102), channel_id=1, source_target_pairs={{0,2},{1,9},{2,4},{3,11},{4,6},{5,13},{6,0},{7,15},{8,10},{9,17},{... | collective-permute-start | bytes 1572872 | tf_op jit(solution)/shard_map/ppermute | solution.py:498
  78.2 11.3 %collective-permute-start.19 = (bf16[2,128,1024]{2,1,0:T(8,128)(2,1)S(1)}, bf16[2,128,1024]{2,1,0:T(8,128)(2,1)S(1)}, u32[]{:S(2)}, u32[]{:S(2)}) collective-permute-start(bf16[2,128,1024]{2,1,0:T(8,128)(2,1)S(1)} %get-tuple-element.121), channel_id=1, source_target_pairs={{0,32},{1,33},{2,34},{3,35},{4,36},{5,37},{6,38},{7,39},{8,40},{9,... | collective-permute-start | bytes 1572872 | tf_op jit(solution)/shard_map/ppermute | solution.py:514
  78.3 11.3 %collective-permute-start.20 = (bf16[2,128,1024]{2,1,0:T(8,128)(2,1)S(1)}, bf16[2,128,1024]{2,1,0:T(8,128)(2,1)S(1)}, u32[]{:S(2)}, u32[]{:S(2)}) collective-permute-start(bf16[2,128,1024]{2,1,0:T(8,128)(2,1)S(1)} %get-tuple-element.122), channel_id=1, source_target_pairs={{0,96},{1,97},{2,98},{3,99},{4,100},{5,101},{6,102},{7,103},{8,104... | collective-permute-start | bytes 1572872 | tf_op jit(solution)/shard_map/ppermute | solution.py:514
  90.0 17.1 %collective-permute-start.21 = (bf16[128,1024]{1,0:T(8,128)(2,1)S(1)}, bf16[128,1024]{1,0:T(8,128)(2,1)S(1)}, u32[]{:S(2)}, u32[]{:S(2)}) collective-permute-start(bf16[128,1024]{1,0:T(8,128)(2,1)S(1)} %get-tuple-element.123), channel_id=1, source_target_pairs={{0,17},{1,2},{2,10},{3,7},{4,21},{5,6},{6,14},{7,3},{8,16},{9,13},... | collective-permute-start | bytes 786440 | tf_op jit(solution)/shard_map/ppermute | solution.py:519
  99.4 7.6 %collective-permute-start.22 = (bf16[128,1024]{1,0:T(8,128)(2,1)S(1)}, bf16[128,1024]{1,0:T(8,128)(2,1)S(1)}, u32[]{:S(2)}, u32[]{:S(2)}) collective-permute-start(bf16[128,1024]{1,0:T(8,128)(2,1)S(1)} %get-tuple-element.124), channel_id=1, source_target_pairs={{0,16},{1,7},{2,27},{3,6},{4,20},{5,3},{6,31},{7,2},{8,1},{9,12},{... | collective-permute-start | bytes 786440 | tf_op jit(solution)/shard_map/ppermute | solution.py:519
  100.7 10.8 %collective-permute-start.23 = (bf16[128,1024]{1,0:T(8,128)(2,1)S(1)}, bf16[128,1024]{1,0:T(8,128)(2,1)S(1)}, u32[]{:S(2)}, u32[]{:S(2)}) collective-permute-start(bf16[128,1024]{1,0:T(8,128)(2,1)S(1)} %get-tuple-element.125), channel_id=1, source_target_pairs={{0,0},{1,3},{2,11},{3,2},{4,4},{5,7},{6,15},{7,6},{8,17},{9,8},{10... | collective-permute-start | bytes 786440 | tf_op jit(solution)/shard_map/ppermute | solution.py:519
  102.6 8.9 %collective-permute-start.24 = (bf16[128,1024]{1,0:T(8,128)(2,1)S(1)}, bf16[128,1024]{1,0:T(8,128)(2,1)S(1)}, u32[]{:S(2)}, u32[]{:S(2)}) collective-permute-start(bf16[128,1024]{1,0:T(8,128)(2,1)S(1)} %get-tuple-element.126), channel_id=1, source_target_pairs={{0,1},{1,6},{2,26},{3,3},{4,5},{5,2},{6,30},{7,7},{8,0},{9,9},{10,... | collective-permute-start | bytes 786440 | tf_op jit(solution)/shard_map/ppermute | solution.py:519
  (4 other events, 39.9 us)
